TPU v7x, 256 devices: a whole 4x4x8 slice. The times are simulated.
256 devices in a mesh: tp: 16 (over z, x_hi), sp: 16 (over y, x_lo, core).
Axes of the slice: x: 4 (x_hi: 2, x_lo: 2; x = x_hi * 2 + x_lo), y: 4, z: 8, core: 2. Of those that a mesh axis runs over, the one named last changes fastest.
Arguments:
- context: bfloat16 [2048, 16384], P('sp', 'tp'), may hold values from -6 to 6
- w_out: bfloat16 [16384, 16384], P('tp', 'sp'), may hold values from -0.046875 to 0.046875
- teacher_resid: bfloat16 [2048, 16384], P('tp', 'sp'), may hold values from -3 to 3
- queries: bfloat16 [2048, 4096], P('sp', 'tp'), may hold values from -5 to 5
- keys: bfloat16 [2048, 4096], P('sp', 'tp'), may hold values from -5 to 5
- values: bfloat16 [2048, 4096], P('sp', 'tp'), may hold values from -6 to 6
- segment_ids: int32 [2048], replicated, may hold values from 0 to 3, never falling along the last dimension, each value on 1 to 1024 neighbouring positions
- proj: bfloat16 [4096, 16384], P('tp', 'sp'), may hold values from -0.75 to 0.75
Outputs:
- proj_grad: bfloat16 [4096, 16384], P('tp', 'sp')
- query_grad: bfloat16 [2048, 4096], P('sp', 'tp')
- key_grad: bfloat16 [2048, 4096], P('sp', 'tp')
- value_grad: bfloat16 [2048, 4096], P('sp', 'tp')
All inputs are finite; a program needn't handle non-finite values.
Results may differ from a plain program's by a relative error of at most 0.02.
Values may be sent and summed in bfloat16 or wider, within the bound.
No kernel may reach another device: no remote copies, remote signals or barrier semaphores. Data moves between devices by JAX's collectives and lax.ppermute only.
A program may use at most 128 MiB of HBM per device.

v0:
```python
import jax
import jax.numpy as jnp
from jax import lax
from jax.sharding import PartitionSpec as P

HEAD_DIM = 128


def body(context, w_out, teacher_resid, queries, keys, values, segment_ids, proj):
    tok_rows, local_width = queries.shape
    head_count = local_width // HEAD_DIM
    scale = HEAD_DIM ** (-0.5)
    total_rows = segment_ids.shape[0]
    context_all = lax.all_gather(context, "sp", axis=0, tiled=True)
    key_all, value_all = (
        lax.all_gather(keys, "sp", axis=0, tiled=True),
        lax.all_gather(values, "sp", axis=0, tiled=True),
    )
    query_split = queries.reshape(tok_rows, head_count, HEAD_DIM)
    key_split = key_all.reshape(total_rows, head_count, HEAD_DIM)
    value_split = value_all.reshape(total_rows, head_count, HEAD_DIM)
    first_row = lax.axis_index("sp") * tok_rows
    query_places = first_row + jnp.arange(tok_rows, dtype=jnp.int32)
    key_places = jnp.arange(total_rows, dtype=jnp.int32)
    query_segments = lax.dynamic_slice_in_dim(segment_ids, first_row, tok_rows, 0)
    allowed = (query_places[:, None] >= key_places[None, :]) & (
        query_segments[:, None] == segment_ids[None, :]
    )
    scores = (
        jnp.einsum("qhd,khd->hqk", query_split, key_split, preferred_element_type=jnp.float32)
        * scale
    )
    scores = jnp.where(allowed[None], scores, -1e30)
    top = jnp.max(scores, axis=-1, keepdims=True)
    expo = jnp.exp(scores - top)
    probs = expo / jnp.sum(expo, axis=-1, keepdims=True)
    probs_low = probs.astype(jnp.bfloat16)
    attn_split = jnp.einsum(
        "hqk,khd->qhd", probs_low, value_split, preferred_element_type=jnp.float32
    ).astype(jnp.bfloat16)
    attn_local = attn_split.reshape(tok_rows, local_width)
    attn_all = lax.all_gather(attn_local, "sp", axis=0, tiled=True)
    rows_part = context_all
    teacher_out = lax.psum_scatter(
        jnp.dot(rows_part, w_out, preferred_element_type=jnp.float32).astype(jnp.bfloat16),
        "tp",
        scatter_dimension=0,
        tiled=True,
    ).astype(jnp.float32)
    rows_part = attn_all
    pred = lax.psum_scatter(
        jnp.dot(rows_part, proj, preferred_element_type=jnp.float32).astype(jnp.bfloat16),
        "tp",
        scatter_dimension=0,
        tiled=True,
    ).astype(jnp.float32)
    diff = pred - (teacher_resid.astype(jnp.float32) + teacher_out)
    dpred = diff.astype(jnp.bfloat16)
    dpred_all = lax.all_gather(dpred, "tp", axis=0, tiled=True)
    proj_grad = lax.dot_general(
        attn_all, dpred_all, (((0,), (0,)), ((), ())), preferred_element_type=jnp.float32
    ).astype(jnp.bfloat16)
    rows_part = dpred_all
    dattn = lax.psum_scatter(
        lax.dot_general(
            rows_part, proj, (((1,), (1,)), ((), ())), preferred_element_type=jnp.float32
        ).astype(jnp.bfloat16),
        "sp",
        scatter_dimension=0,
        tiled=True,
    )
    dattn_split = dattn.reshape(tok_rows, head_count, HEAD_DIM)
    delta = jnp.sum(dattn_split.astype(jnp.float32) * attn_split.astype(jnp.float32), axis=-1)
    dprobs = jnp.einsum(
        "qhd,khd->hqk", dattn_split, value_split, preferred_element_type=jnp.float32
    )
    dscores = (probs * (dprobs - delta.T[:, :, None]) * scale).astype(jnp.bfloat16)
    query_grad = jnp.einsum("hqk,khd->qhd", dscores, key_split, preferred_element_type=jnp.float32)
    query_grad = query_grad.astype(jnp.bfloat16).reshape(tok_rows, local_width)
    key_part = jnp.einsum(
        "hqk,qhd->khd", dscores, query_split, preferred_element_type=jnp.float32
    ).reshape(total_rows, local_width)
    value_part = jnp.einsum(
        "hqk,qhd->khd", probs_low, dattn_split, preferred_element_type=jnp.float32
    ).reshape(total_rows, local_width)
    key_sum, value_total = (
        lax.psum_scatter(
            key_part.astype(jnp.bfloat16), "sp", scatter_dimension=0, tiled=True
        ).astype(jnp.float32),
        lax.psum_scatter(
            value_part.astype(jnp.bfloat16), "sp", scatter_dimension=0, tiled=True
        ).astype(jnp.float32),
    )
    return (proj_grad, query_grad, key_sum.astype(jnp.bfloat16), value_total.astype(jnp.bfloat16))


def solution(mesh):
    in_specs = (
        P("sp", "tp"),
        P("tp", "sp"),
        P("tp", "sp"),
        P("sp", "tp"),
        P("sp", "tp"),
        P("sp", "tp"),
        P(),
        P("tp", "sp"),
    )
    out_specs = (P("tp", "sp"), P("sp", "tp"), P("sp", "tp"), P("sp", "tp"))
    return jax.shard_map(body, mesh=mesh, in_specs=in_specs, out_specs=out_specs, check_vma=False)
```

profile of v0, /device:TPU:4, one launch (start us, length us, event | category | flops | bytes accessed | tf_op | source)
XLA Modules:
  0.0 906.7 jit_solution(4148685454582328317)
XLA Ops:
  7.2 0.0 copy-start
  7.2 0.0 all-gather.6.cloned.1.call-start
  7.2 1.7 copy.22
  8.9 0.0 all-gather.6.cloned.1.call-update
  9.0 0.0 all-gather.8.cloned.1.call-start
  9.0 0.7 all-gather.8.cloned.1.call-update
  9.7 0.0 all-gather.10.cloned.1.call-start
  9.8 1.0 copy.36
  10.7 0.8 dynamic_slice.3
  11.5 1.0 fusion.7
  12.5 37.2 %all-gather.6.cloned.1.call-done = bf16[2048,256]{0,1:T(8,128)(2,1)} async-done(((bf16[128,256]{0,1:T(8,128)(2,1)}), bf16[2048,256]{0,1:T(8,128)(2,1)}) %all-gather.6.cloned.1.call-update) | async-done | bytes 1048592 | tf_op jit(solution)/shard_map/all_gather | solution.py:16
  49.7 3.5 fusion.14
  53.2 33.3 %all-gather.8.cloned.1.call-done = bf16[2048,256]{1,0:T(8,128)(2,1)} async-done(((bf16[128,256]{1,0:T(8,128)(2,1)}), bf16[2048,256]{1,0:T(8,128)(2,1)}) %all-gather.8.cloned.1.call-update) | async-done | bytes 1048592 | tf_op jit(solution)/shard_map/all_gather | solution.py:17
  86.5 1.5 copy.25
  88.0 0.0 copy-start.2
  88.0 3.1 convolution_convert_fusion.7
  91.2 0.0 copy-done.2
  91.2 0.0 all-gather.10.cloned.1.call-update
  91.2 0.0 all-gather.12.cloned.1.call-start
  91.3 0.5 all-gather.12.cloned.1.call-update
  91.8 0.0 reduce-scatter.6.cloned.1.call-start
  91.8 36.2 %all-gather.10.cloned.1.call-done = bf16[2048,256]{0,1:T(8,128)(2,1)} async-done(((bf16[128,256]{0,1:T(8,128)(2,1)}), bf16[2048,256]{0,1:T(8,128)(2,1)}) %all-gather.10.cloned.1.call-update) | async-done | bytes 1048592 | tf_op jit(solution)/shard_map/all_gather | solution.py:42
  128.1 4.6 convolution_convert_fusion
  132.7 0.0 reduce-scatter.6.cloned.1.call-update
  132.7 0.0 reduce-scatter.8.cloned.1.call-start
  132.7 37.0 %all-gather.12.cloned.1.call-done = bf16[2048,1024]{1,0:T(8,128)(2,1)} async-done(((bf16[128,1024]{1,0:T(8,128)(2,1)}), bf16[2048,1024]{1,0:T(8,128)(2,1)}) %all-gather.12.cloned.1.call-update) | async-done | bytes 4194320 | tf_op jit(solution)/shard_map/all_gather | solution.py:14
  169.7 0.0 copy-done
  169.7 8.3 convolution_convert_fusion.1
  178.0 0.0 copy-start.5
  178.0 0.0 copy-start.3
  178.0 0.0 reduce-scatter.8.cloned.1.call-update
  178.0 0.0 all-gather.14.cloned.1.call-start
  178.0 205.9 %reduce-scatter.6.cloned.1.call-done = bf16[128,1024]{1,0:T(8,128)(2,1)} async-done(((bf16[2048,1024]{1,0:T(8,128)(2,1)}), bf16[128,1024]{1,0:T(8,128)(2,1)}) %reduce-scatter.6.cloned.1.call-update) | async-done | bytes 262160 | tf_op jit(solution)/shard_map/reduce_scatter | solution.py:51
  383.9 214.7 %reduce-scatter.8.cloned.1.call-done = bf16[128,1024]{1,0:T(8,128)(2,1)} async-done(((bf16[2048,1024]{1,0:T(8,128)(2,1)}), bf16[128,1024]{1,0:T(8,128)(2,1)}) %reduce-scatter.8.cloned.1.call-update) | async-done | bytes 262160 | tf_op jit(solution)/shard_map/reduce_scatter | solution.py:44
  598.6 0.0 copy-done.5
  598.6 1.9 subtract_convert_fusion
  600.5 0.0 all-gather.14.cloned.1.call-update
  600.5 0.0 reduce-scatter.10.cloned.1.call-start
  600.5 99.0 %all-gather.14.cloned.1.call-done = bf16[2048,1024]{1,0:T(8,128)(2,1)} async-done(((bf16[128,1024]{1,0:T(8,128)(2,1)}), bf16[2048,1024]{1,0:T(8,128)(2,1)}) %all-gather.14.cloned.1.call-update) | async-done | bytes 4194320 | tf_op jit(solution)/shard_map/all_gather | solution.py:59
  699.6 0.0 copy-done.3
  699.6 4.4 convolution_convert_fusion.4
  704.0 0.0 reduce-scatter.10.cloned.1.call-update
  704.0 0.0 reduce-scatter.14.cloned.1.call-start
  704.1 62.9 %reduce-scatter.10.cloned.1.call-done = bf16[128,256]{1,0:T(8,128)(2,1)} async-done(((bf16[2048,256]{1,0:T(8,128)(2,1)}), bf16[128,256]{1,0:T(8,128)(2,1)}) %reduce-scatter.10.cloned.1.call-update) | async-done | bytes 65552 | tf_op jit(solution)/shard_map/reduce_scatter | solution.py:64
  767.0 0.9 copy.26
  767.9 2.1 convolution_convert_fusion.3
  770.0 0.0 copy-start.4
  770.0 1.3 copy.31
  771.3 0.0 reduce-scatter.14.cloned.1.call-update
  771.4 0.0 reduce-scatter.12.cloned.1.call-start
  771.4 0.0 copy-done.4
  771.5 2.5 fusion.6
  774.0 1.4 convolution_convert_fusion.2
  775.4 2.3 copy.30
  777.6 0.0 reduce-scatter.12.cloned.1.call-update
  777.7 0.0 copy-start.1
  777.7 4.6 convolution_convert_fusion.5
  782.3 0.0 copy-done.1
  782.3 0.4 convolution_convert_fusion.6
  782.8 0.7 copy.32
  783.5 50.7 %reduce-scatter.14.cloned.1.call-done = bf16[128,256]{1,0:T(8,128)(2,1)} async-done(((bf16[2048,256]{1,0:T(8,128)(2,1)}), bf16[128,256]{1,0:T(8,128)(2,1)}) %reduce-scatter.14.cloned.1.call-update) | async-done | bytes 65552 | tf_op jit(solution)/shard_map/reduce_scatter | solution.py:90
  834.2 65.7 %reduce-scatter.12.cloned.1.call-done = bf16[128,256]{1,0:T(8,128)(2,1)} async-done(((bf16[2048,256]{1,0:T(8,128)(2,1)}), bf16[128,256]{1,0:T(8,128)(2,1)}) %reduce-scatter.12.cloned.1.call-update) | async-done | bytes 65552 | tf_op jit(solution)/shard_map/reduce_scatter | solution.py:87
  (2 shorter events, 0.0 us)
Async XLA Ops:
  7.2 162.5 %copy-start = (bf16[1024,1024]{1,0:T(8,128)(2,1)S(1)}, bf16[1024,1024]{1,0:T(8,128)(2,1)}, u32[]{:S(2)}) copy-start(bf16[1024,1024]{1,0:T(8,128)(2,1)} %param.9) | copy-start | bytes 6291460
  7.2 42.5 %all-gather.6.cloned.1.call-start = ((), (), s32[]{:S(2)}) async-start(), calls=%async_computation.5 | async-start | bytes 1114112 | tf_op jit(solution)/shard_map/all_gather | solution.py:16
  9.0 77.6 %all-gather.8.cloned.1.call-start = ((), (), s32[]{:S(2)}) async-start(), calls=%async_computation.6 | async-start | bytes 1114112 | tf_op jit(solution)/shard_map/all_gather | solution.py:17
  9.7 118.4 %all-gather.10.cloned.1.call-start = ((), (), s32[]{:S(2)}) async-start(), calls=%async_computation.7 | async-start | bytes 1114112 | tf_op jit(solution)/shard_map/all_gather | solution.py:42
  88.0 3.1 copy-start.2
  91.2 78.5 %all-gather.12.cloned.1.call-start = ((), (), s32[]{:S(2)}) async-start(), calls=%async_computation.9 | async-start | bytes 4456448 | tf_op jit(solution)/shard_map/all_gather | solution.py:14
  91.8 292.1 %reduce-scatter.6.cloned.1.call-start = ((), (), s32[]{:S(2)}) async-start(), calls=%async_computation.8 | async-start | bytes 4456448 | tf_op jit(solution)/shard_map/reduce_scatter | solution.py:51
  132.7 465.9 %reduce-scatter.8.cloned.1.call-start = ((), (), s32[]{:S(2)}) async-start(), calls=%async_computation.10 | async-start | bytes 4456448 | tf_op jit(solution)/shard_map/reduce_scatter | solution.py:44
  178.0 420.6 %copy-start.5 = (bf16[128,1024]{1,0:T(8,128)(2,1)S(1)}, bf16[128,1024]{1,0:T(8,128)(2,1)}, u32[]{:S(2)}) copy-start(bf16[128,1024]{1,0:T(8,128)(2,1)} %param.10) | copy-start | bytes 786436
  178.0 521.6 %copy-start.3 = (bf16[256,1024]{1,0:T(8,128)(2,1)S(1)}, bf16[256,1024]{1,0:T(8,128)(2,1)}, u32[]{:S(2)}) copy-start(bf16[256,1024]{1,0:T(8,128)(2,1)} %param.15) | copy-start | bytes 1572868
  178.0 521.6 %all-gather.14.cloned.1.call-start = ((), (), s32[]{:S(2)}) async-start(), calls=%async_computation.11 | async-start | bytes 4456448 | tf_op jit(solution)/shard_map/all_gather | solution.py:59
  600.5 166.5 %reduce-scatter.10.cloned.1.call-start = ((), (), s32[]{:S(2)}) async-start(), calls=%async_computation.12 | async-start | bytes 1114112 | tf_op jit(solution)/shard_map/reduce_scatter | solution.py:64
  704.0 130.2 %reduce-scatter.14.cloned.1.call-start = ((), (), s32[]{:S(2)}) async-start(), calls=%async_computation.14 | async-start | bytes 1114112 | tf_op jit(solution)/shard_map/reduce_scatter | solution.py:90
  770.0 1.4 copy-start.4
  771.4 128.5 %reduce-scatter.12.cloned.1.call-start = ((), (), s32[]{:S(2)}) async-start(), calls=%async_computation.13 | async-start | bytes 1114112 | tf_op jit(solution)/shard_map/reduce_scatter | solution.py:87
  777.7 4.6 copy-start.1
Sparse Core Ops, SparseCore 0:
  10.4 39.2 all-gather.5
  51.5 34.9 all-gather.7
  91.3 36.6 all-gather.9
  129.8 39.8 all-gather.11
  173.6 210.3 reduce-scatter.5
  388.3 210.2 reduce-scatter.7
  601.8 97.7 all-gather.13
  704.2 62.7 reduce-scatter.9
  771.5 62.6 reduce-scatter.13
  837.1 62.6 reduce-scatter.11
where the time goes:
time: 907 us
  waiting for transfers between devices  844 us (93%)
  matrix products  35 us (4%)
  between operations  14.3 us (2%)
  local copies, waits for them, and re-layouts  10.2 us (1%)
    reduce_scatter x1, waiting for transfers between devices, body(): lax.psum_scatter(jnp.dot(rows_part, w_out, preferred_element_type=jnp.flo...  215 us
    reduce_scatter x1, waiting for transfers between devices, body(): lax.psum_scatter(jnp.dot(rows_part, proj, preferred_element_type=jnp.floa...  206 us
    all_gather x1, waiting for transfers between devices, body(): dpred_all = lax.all_gather(dpred, 'tp', axis=0, tiled=True)  99 us
    reduce_scatter x1, waiting for transfers between devices, body(): lax.psum_scatter(key_part.astype(jnp.bfloat16), 'sp', scatter_dimension=0...  65.7 us
    reduce_scatter x1, waiting for transfers between devices, body(): lax.psum_scatter(lax.dot_general(rows_part, proj, (((1,), (1,)), ((), ())...  62.9 us
    reduce_scatter x1, waiting for transfers between devices, body(): lax.psum_scatter(value_part.astype(jnp.bfloat16), 'sp', scatter_dimension...  50.7 us
    all_gather x1, waiting for transfers between devices, body(): lax.all_gather(keys, 'sp', axis=0, tiled=True)  37.2 us
    all_gather x1, waiting for transfers between devices, body(): context_all = lax.all_gather(context, 'sp', axis=0, tiled=True)  37 us
  transfers between devices with their start and end apart: 10, of which 10 were waited for; matrix products, arithmetic and copies ran while one was open for 3% of the time, Pallas kernels for 0%

commit v1 on v0

v1 whole, which is shorter than its diff:
```python
import functools

import jax
import jax.numpy as jnp
from jax import lax
from jax.experimental import pallas as pl
from jax.experimental.pallas import tpu as pltpu
from jax.sharding import Mesh
from jax.sharding import PartitionSpec as P

HEAD_DIM = 128
SEGMENT_MAX = 1024
TP = ("z", "xh")
SP = ("y", "xl", "core")
F32 = jnp.float32
BF16 = jnp.bfloat16
NT = (((1,), (1,)), ((), ()))
TN = (((0,), (0,)), ((), ()))


def dot(a, b, dims=(((1,), (0,)), ((), ()))):
    return lax.dot_general(a, b, dims, preferred_element_type=F32)


def forward_kernel(q_ref, qseg_ref, kseg_ref, *refs):
    kv_refs, (attn_ref, probs_ref) = refs[:-2], refs[-2:]
    rows, width = q_ref.shape
    keys = rows * len(kv_refs)
    scale = HEAD_DIM ** (-0.5)
    place = lax.broadcasted_iota(jnp.int32, (rows, keys), 0) + (keys - rows)
    allowed = (place >= lax.broadcasted_iota(jnp.int32, (rows, keys), 1)) & (
        qseg_ref[...] == kseg_ref[...]
    )
    for h in range(width // HEAD_DIM):
        cols = slice(h * HEAD_DIM, (h + 1) * HEAD_DIM)
        vcols = slice(width + h * HEAD_DIM, width + (h + 1) * HEAD_DIM)
        key = jnp.concatenate([r[:, cols] for r in kv_refs], axis=0)
        value = jnp.concatenate([r[:, vcols] for r in kv_refs], axis=0)
        scores = jnp.where(allowed, dot(q_ref[:, cols], key, NT) * scale, -1e30)
        expo = jnp.exp(scores - jnp.max(scores, axis=-1, keepdims=True))
        probs = expo / jnp.sum(expo, axis=-1, keepdims=True)
        probs_ref[h] = probs
        attn_ref[:, cols] = dot(probs.astype(BF16), value).astype(BF16)


def backward_kernel(q_ref, attn_ref, dattn_ref, probs_ref, *refs):
    n = (len(refs) - 1) // 2
    kv_refs, dq_ref, dkv_refs = refs[:n], refs[n], refs[n + 1 :]
    rows, width = q_ref.shape
    scale = HEAD_DIM ** (-0.5)
    for h in range(width // HEAD_DIM):
        cols = slice(h * HEAD_DIM, (h + 1) * HEAD_DIM)
        vcols = slice(width + h * HEAD_DIM, width + (h + 1) * HEAD_DIM)
        key = jnp.concatenate([r[:, cols] for r in kv_refs], axis=0)
        value = jnp.concatenate([r[:, vcols] for r in kv_refs], axis=0)
        probs = probs_ref[h]
        dattn = dattn_ref[:, cols]
        delta = jnp.sum(
            dattn.astype(F32) * attn_ref[:, cols].astype(F32), axis=-1, keepdims=True
        )
        dprobs = dot(dattn, value, NT)
        dscores = (probs * (dprobs - delta) * scale).astype(BF16)
        dq_ref[:, cols] = dot(dscores, key).astype(BF16)
        dkey = dot(dscores, q_ref[:, cols], TN).astype(BF16)
        dvalue = dot(probs.astype(BF16), dattn, TN).astype(BF16)
        for i, r in enumerate(dkv_refs):
            r[:, cols] = dkey[i * rows : (i + 1) * rows]
            r[:, vcols] = dvalue[i * rows : (i + 1) * rows]


def call(kernel, out_shape, *args):
    return pl.pallas_call(
        kernel,
        out_shape=out_shape,
        compiler_params=pltpu.CompilerParams(vmem_limit_bytes=40 * 1024 * 1024),
    )(*args)


def body(context, w_out, teacher_resid, queries, keys, values, segment_ids, proj):
    rows, width = queries.shape
    heads = width // HEAD_DIM
    n_sp = lax.axis_size(SP)
    n_xh = lax.axis_size("xh")
    back = -(-(SEGMENT_MAX - 1) // rows)
    back = min(back, n_sp - 1)
    window = (back + 1) * rows
    me = lax.axis_index(SP)
    first_row = me * rows

    def shift(array, by):
        pairs = [(i, i + by) for i in range(n_sp) if 0 <= i + by < n_sp]
        return lax.ppermute(array, SP, pairs)

    def swap(array):
        return lax.ppermute(array, "xh", [(i, i ^ 1) for i in range(n_xh)])

    context_all = lax.all_gather(context, SP, axis=0, tiled=True)

    key_value = jnp.concatenate([keys, values], axis=1)
    blocks = [shift(key_value, k) for k in range(back, 0, -1)] + [key_value]
    padded = jnp.concatenate([jnp.full((window - rows,), -1, jnp.int32), segment_ids])
    window_segments = lax.dynamic_slice_in_dim(padded, first_row, window, 0)
    query_segments = lax.dynamic_slice_in_dim(segment_ids, first_row, rows, 0)
    attn, probs = call(
        forward_kernel,
        (
            jax.ShapeDtypeStruct((rows, width), BF16),
            jax.ShapeDtypeStruct((heads, rows, window), F32),
        ),
        queries,
        query_segments[:, None],
        window_segments[None, :],
        *blocks,
    )
    attn_all = lax.all_to_all(
        jnp.broadcast_to(attn[None], (n_sp, rows, width)), SP, 0, 0, tiled=True
    ).reshape(n_sp * rows, width)

    part = (dot(attn_all, proj) - dot(context_all, w_out)).astype(BF16)
    part = lax.psum_scatter(part, "z", scatter_dimension=0, tiled=True)
    xh = lax.axis_index("xh")
    mine = lax.dynamic_slice_in_dim(part, xh * rows, rows, 0)
    other = lax.dynamic_slice_in_dim(part, (1 - xh) * rows, rows, 0)
    diff = mine.astype(F32) + swap(other).astype(F32) - teacher_resid.astype(F32)
    dpred = diff.astype(BF16)

    theirs = swap(dpred)
    pair = jnp.concatenate(
        [jnp.where(xh == 0, dpred, theirs), jnp.where(xh == 0, theirs, dpred)], axis=0
    )
    dpred_all = lax.all_gather(pair, "z", axis=0, tiled=True)

    dattn_part = dot(dpred_all, proj, NT).astype(BF16).reshape(n_sp, rows, width)
    dattn_parts = lax.all_to_all(dattn_part, SP, 0, 0, tiled=True)
    dattn = jnp.sum(dattn_parts.astype(F32), axis=0).astype(BF16)
    proj_grad = dot(attn_all, dpred_all, TN).astype(BF16)

    query_grad, *grads = call(
        backward_kernel,
        (jax.ShapeDtypeStruct((rows, width), BF16),)
        + (jax.ShapeDtypeStruct((rows, 2 * width), BF16),) * (back + 1),
        queries,
        attn,
        dattn,
        probs,
        *blocks,
    )
    total = grads[back].astype(F32)
    for k in range(1, back + 1):
        total = total + shift(grads[back - k], -k).astype(F32)
    total = total.astype(BF16)
    return proj_grad, query_grad, total[:, :width], total[:, width:]


def solution(mesh):
    fine = Mesh(mesh.devices.reshape(8, 2, 4, 2, 2), TP + SP)
    in_specs = (
        P(SP, TP),
        P(TP, SP),
        P(TP, SP),
        P(SP, TP),
        P(SP, TP),
        P(SP, TP),
        P(),
        P(TP, SP),
    )
    out_specs = (P(TP, SP), P(SP, TP), P(SP, TP), P(SP, TP))
    return jax.shard_map(body, mesh=fine, in_specs=in_specs, out_specs=out_specs, check_vma=False)
```

time: 907 us -> 292 us (0.32)
  waiting for transfers between devices: 844 us -> 150 us
  starting transfers between devices: 0.41 us -> 38.9 us
  blocking collectives: 0 us -> 21.4 us
  local copies, waits for them, and re-layouts: 10.2 us -> 29.4 us
  matrix products: 35 us -> 24.4 us
    reduce_scatter x5 -> x1, waiting for transfers between devices: 600 us -> 56.1 us  [body(): part = lax.psum_scatter(part, 'z', scatter_dimension=0, tiled=True)]
    all_gather x5 -> x2, waiting for transfers between devices: 243 us -> 54.6 us  [the longest x1 53.6 us: body(): dpred_all = lax.all_gather(pair, 'z', axis=0, tiled=True)]
    ppermute x0 -> x18, starting transfers between devices: none -> 32.6 us  [the longest x16 31.5 us: shift(): return lax.ppermute(array, SP, pairs)]
    ppermute x0 -> x18, waiting for transfers between devices: none -> 31.6 us  [the longest x2 17.9 us: swap(): return lax.ppermute(array, 'xh', [(i, i ^ 1) for i in range(n_xh)])]
    all_to_all x0 -> x1, blocking collectives: none -> 21.4 us  [body(): dattn_parts = lax.all_to_all(dattn_part, SP, 0, 0, tiled=True)]
    unnamed x14 -> x57, local copies, waits for them, and re-layouts: 2.49 us -> 22.9 us
    dot_general x9 -> x4, matrix products: 31.5 us -> 24.4 us  [dot(): return lax.dot_general(a, b, dims, preferred_element_type=F32)]
  transfers between devices with their start and end apart: 10 -> 22, of which waited for: 10 -> 11; matrix products, arithmetic and copies ran while one was open for 3% -> 7% of each run, Pallas kernels for 0% -> 0%
where the time goes in v1:
time: 292 us; the launch traced here: 286 us
  waiting for transfers between devices  150 us (51%)
  starting transfers between devices  38.9 us (13%)
  local copies, waits for them, and re-layouts  29.4 us (10%)
  matrix products  24.4 us (8%)
  blocking collectives  21.4 us (7%)
  between operations  14 us (5%)
  other arithmetic  6 us (2%)
    reduce_scatter x1, waiting for transfers between devices, body(): part = lax.psum_scatter(part, 'z', scatter_dimension=0, tiled=True)  56.1 us
    all_gather x1, waiting for transfers between devices, body(): dpred_all = lax.all_gather(pair, 'z', axis=0, tiled=True)  53.6 us
    ppermute x16, starting transfers between devices, shift(): return lax.ppermute(array, SP, pairs)  31.5 us
    dot_general x4, matrix products, dot(): return lax.dot_general(a, b, dims, preferred_element_type=F32)  24.4 us
    unnamed x57, local copies, waits for them, and re-layouts  22.9 us
    all_to_all x1, blocking collectives, body(): dattn_parts = lax.all_to_all(dattn_part, SP, 0, 0, tiled=True)  21.4 us
    ppermute x2, waiting for transfers between devices, swap(): return lax.ppermute(array, 'xh', [(i, i ^ 1) for i in range(n_xh)])  17.9 us
    ppermute x16, waiting for transfers between devices, shift(): return lax.ppermute(array, SP, pairs)  13.7 us
  transfers between devices with their start and end apart: 22, of which 11 were waited for; matrix products, arithmetic and copies ran while one was open for 7% of the time, Pallas kernels for 0%

profile of v1, /device:TPU:4, one launch (start us, length us, event | category | flops | bytes accessed | tf_op | source)
XLA Modules:
  0.0 286.3 jit_solution(2638277059910810275)
XLA Ops:
  7.9 0.8 constant_dynamic-update-slice_fusion.1
  8.8 0.8 constant_dynamic-update-slice_fusion.refs_8_
  9.6 5.1 %collective-permute-start = (bf16[128,512]{1,0:T(8,128)(2,1)S(1)}, bf16[128,512]{1,0:T(8,128)(2,1)S(1)}, u32[]{:S(2)}, u32[]{:S(2)}) collective-permute-start(bf16[128,512]{1,0:T(8,128)(2,1)S(1)} %constant_dynamic-update-slice_fusion.refs_8_), channel_id=1, source_target_pairs={{0,8},{1,9},{2,10},{3,11},{4,12},{5,13},{6,14},{7,15},{16,24},{17,... | collective-permute-start | bytes 393224 | tf_op jit(solution)/shard_map/ppermute | solution.py:92
  14.7 2.4 collective-permute-start.1
  17.1 2.1 collective-permute-start.2
  19.2 1.3 collective-permute-start.3
  20.5 1.6 collective-permute-start.4
  22.2 3.4 %collective-permute-start.5 = (bf16[128,512]{1,0:T(8,128)(2,1)S(1)}, bf16[128,512]{1,0:T(8,128)(2,1)S(1)}, u32[]{:S(2)}, u32[]{:S(2)}) collective-permute-start(bf16[128,512]{1,0:T(8,128)(2,1)S(1)} %constant_dynamic-update-slice_fusion.refs_8_), channel_id=1, source_target_pairs={{0,3},{1,4},{2,5},{3,6},{4,7},{5,8},{6,9},{7,10},{8,11},{9,12},{10... | collective-permute-start | bytes 393224 | tf_op jit(solution)/shard_map/ppermute | solution.py:92
  26.3 1.6 collective-permute-start.6
  28.5 3.6 %collective-permute-start.7 = (bf16[128,512]{1,0:T(8,128)(2,1)S(1)}, bf16[128,512]{1,0:T(8,128)(2,1)S(1)}, u32[]{:S(2)}, u32[]{:S(2)}) collective-permute-start(bf16[128,512]{1,0:T(8,128)(2,1)S(1)} %constant_dynamic-update-slice_fusion.refs_8_), channel_id=1, source_target_pairs={{0,1},{1,2},{2,3},{3,4},{4,5},{5,6},{6,7},{7,8},{8,9},{9,10},{10,1... | collective-permute-start | bytes 393224 | tf_op jit(solution)/shard_map/ppermute | solution.py:92
  32.2 0.8 dynamic-slice_bitcast_fusion
  32.9 0.7 copy.12.qseg_ref
  33.7 0.8 pad_dynamic-slice_fusion
  35.1 5.0 %collective-permute-done.4.refs_4_ = bf16[128,512]{1,0:T(8,128)(2,1)S(1)} collective-permute-done((bf16[128,512]{1,0:T(8,128)(2,1)S(1)}, bf16[128,512]{1,0:T(8,128)(2,1)S(1)}, u32[]{:S(2)}, u32[]{:S(2)}) %collective-permute-start.4) | collective-permute-done | bytes 131104 | tf_op jit(solution)/shard_map/ppermute | solution.py:92
  42.7 0.9 copy-done.2
  43.6 0.9 copy-done.5
  44.5 0.9 copy-done.8
  45.4 0.9 copy-done.11
  46.3 0.9 copy-done.14
  47.2 0.9 copy-done.17
  48.2 0.9 copy-done.20
  49.1 0.8 copy-done.22
  49.9 0.8 copy-done.27
  50.7 1.2 shard_map.111
  51.9 1.1 broadcast_in_dim.15
  53.6 6.2 %all-to-all-start = ((bf16[16,128,256]{2,1,0:T(8,128)(2,1)}), bf16[16,128,256]{2,1,0:T(8,128)(2,1)}, u32[]{:S(2)}, u32[]{:S(2)}) async-start(bf16[16,128,256]{2,1,0:T(8,128)(2,1)} %broadcast_in_dim.15), calls=%async_computation | async-start | bytes 2097152 | tf_op jit(solution)/shard_map/all_to_all | solution.py:115
  59.9 1.0 all-gather.3.cloned.1.call-done
  60.9 9.0 %fusion.1 = f32[2048,1024]{1,0:T(8,128)} fusion(bf16[2048,1024]{1,0:T(8,128)(2,1)} %all-gather.3.cloned.1.call-done, bf16[1024,1024]{1,0:T(8,128)(2,1)S(1)} %copy-done), kind=kOutput, calls=%fused_computation.14 | convolution fusion | flops 4294967296 | bytes 14680064 | tf_op jit(solution)/shard_map/dot_general | solution.py:22
  70.0 6.5 %all-to-all-done = bf16[16,128,256]{2,1,0:T(8,128)(2,1)} async-done(((bf16[16,128,256]{2,1,0:T(8,128)(2,1)}), bf16[16,128,256]{2,1,0:T(8,128)(2,1)}, u32[]{:S(2)}, u32[]{:S(2)}) %all-to-all-start) | async-done | bytes 1048608 | tf_op jit(solution)/shard_map/all_to_all | solution.py:115
  76.5 7.2 %subtract_convert_fusion = bf16[2048,1024]{1,0:T(8,128)(2,1)} fusion(f32[2048,1024]{1,0:T(8,128)} %fusion.1, bf16[2048,256]{1,0:T(8,128)(2,1)} %bitcast.1, bf16[256,1024]{1,0:T(8,128)(2,1)} %param.15), kind=kOutput, calls=%fused_computation | convolution fusion | flops 1077936128 | bytes 14155776 | tf_op jit(solution)/shard_map/dot_general | solution.py:22
  83.8 56.1 %reduce-scatter.2.cloned.1.call-done = bf16[256,1024]{1,0:T(8,128)(2,1)} async-done(((bf16[2048,1024]{1,0:T(8,128)(2,1)}), bf16[256,1024]{1,0:T(8,128)(2,1)}) %reduce-scatter.2.cloned.1.call-update) | async-done | bytes 524304 | tf_op jit(solution)/shard_map/reduce_scatter | solution.py:120
  139.9 1.7 constant_dynamic-slice_fusion
  142.1 9.4 %collective-permute-done.8 = bf16[128,1024]{1,0:T(8,128)(2,1)} collective-permute-done((bf16[128,1024]{1,0:T(8,128)(2,1)}, bf16[128,1024]{1,0:T(8,128)(2,1)}, u32[]{:S(2)}, u32[]{:S(2)}) %collective-permute-start.8) | collective-permute-done | bytes 262176 | tf_op jit(solution)/shard_map/ppermute | solution.py:95
  151.5 1.9 subtract_convert_fusion.1
  154.0 8.5 %collective-permute-done.9 = bf16[128,1024]{1,0:T(8,128)(2,1)} collective-permute-done((bf16[128,1024]{1,0:T(8,128)(2,1)}, bf16[128,1024]{1,0:T(8,128)(2,1)}, u32[]{:S(2)}, u32[]{:S(2)}) %collective-permute-start.9) | collective-permute-done | bytes 262176 | tf_op jit(solution)/shard_map/ppermute | solution.py:95
  162.5 1.1 broadcast_select_fusion.1
  163.5 0.8 pad_maximum_fusion
  164.4 53.6 %all-gather.5.cloned.1.call-done = bf16[2048,1024]{1,0:T(8,128)(2,1)} async-done(((bf16[256,1024]{1,0:T(8,128)(2,1)}), bf16[2048,1024]{1,0:T(8,128)(2,1)}) %all-gather.5.cloned.1.call-update) | async-done | bytes 4194320 | tf_op jit(solution)/shard_map/all_gather | solution.py:131
  218.0 3.6 %convolution_convert_fusion = bf16[2048,256]{1,0:T(8,128)(2,1)S(1)} fusion(bf16[2048,1024]{1,0:T(8,128)(2,1)} %all-gather.5.cloned.1.call-done, bf16[256,1024]{1,0:T(8,128)(2,1)} %param.15), kind=kOutput, calls=%fused_computation.1 | convolution fusion | flops 1074266112 | bytes 5767168 | tf_op jit(solution)/shard_map/dot_general | solution.py:22
  221.6 21.4 %all_to_all.10 = bf16[16,128,256]{2,1,0:T(8,128)(2,1)} all-to-all(bf16[16,128,256]{2,1,0:T(8,128)(2,1)S(1)} %bitcast.12), channel_id=1, replica_groups=mesh['z'=8,'xh'=2,'y'=4,'xl'=2,'core'=2] {'y','xl','core'}, dimensions={0} | all-to-all | bytes 2097152 | tf_op jit(solution)/shard_map/all_to_all | solution.py:134
  243.0 2.0 reduce_sum.12.dattn_ref
  245.0 0.9 copy-done.3
  245.9 0.9 copy-done.6
  246.8 0.9 copy-done.9
  247.7 0.9 copy-done.12
  248.6 0.9 copy-done.15
  249.5 0.9 copy-done.18
  250.4 0.9 copy-done.21
  251.3 0.8 copy-done.23
  252.2 0.8 copy-done.25
  253.0 0.8 copy-done.26
  253.8 1.4 shard_map.112
  255.2 1.3 collective-permute-start.10
  256.5 1.3 collective-permute-start.11
  257.8 1.3 collective-permute-start.12
  259.1 1.3 collective-permute-start.13
  260.4 1.3 collective-permute-start.14
  261.7 1.3 collective-permute-start.15
  263.0 1.6 collective-permute-done.11
  264.6 1.3 collective-permute-start.16
  266.2 1.3 collective-permute-start.17
  267.5 4.6 %convolution_convert_fusion.1 = bf16[256,1024]{1,0:T(8,128)(2,1)} fusion(bf16[2048,256]{1,0:T(8,128)(2,1)} %bitcast.1, bf16[2048,1024]{1,0:T(8,128)(2,1)} %all-gather.5.cloned.1.call-done), kind=kOutput, calls=%fused_computation.2 | convolution fusion | flops 1074003968 | bytes 5767168 | tf_op jit(solution)/shard_map/dot_general | solution.py:22
  272.1 4.5 %collective-permute-done.14 = bf16[128,512]{1,0:T(8,128)(2,1)S(1)} collective-permute-done((bf16[128,512]{1,0:T(8,128)(2,1)S(1)}, bf16[128,512]{1,0:T(8,128)(2,1)S(1)}, u32[]{:S(2)}, u32[]{:S(2)}) %collective-permute-start.14) | collective-permute-done | bytes 131104 | tf_op jit(solution)/shard_map/ppermute | solution.py:92
  276.6 2.4 collective-permute-done.17
  (60 shorter events, 8.3 us)
Async XLA Ops:
  7.2 53.8 %copy-start = (bf16[1024,1024]{1,0:T(8,128)(2,1)S(1)}, bf16[1024,1024]{1,0:T(8,128)(2,1)}, u32[]{:S(2)}) copy-start(bf16[1024,1024]{1,0:T(8,128)(2,1)} %param.9) | copy-start | bytes 6291460
  7.2 53.7 %all-gather.3.cloned.1.call-start = ((), (), s32[]{:S(2)}) async-start(), calls=%async_computation.3 | async-start | bytes 4456448 | tf_op jit(solution)/shard_map/all_gather | solution.py:97
  9.6 12.6 %collective-permute-start = (bf16[128,512]{1,0:T(8,128)(2,1)S(1)}, bf16[128,512]{1,0:T(8,128)(2,1)S(1)}, u32[]{:S(2)}, u32[]{:S(2)}) collective-permute-start(bf16[128,512]{1,0:T(8,128)(2,1)S(1)} %constant_dynamic-update-slice_fusion.refs_8_), channel_id=1, source_target_pairs={{0,8},{1,9},{2,10},{3,11},{4,12},{5,13},{6,14},{7,15},{16,24},{17,... | collective-permute-start | bytes 393224 | tf_op jit(solution)/shard_map/ppermute | solution.py:92
  14.7 10.9 %collective-permute-start.1 = (bf16[128,512]{1,0:T(8,128)(2,1)S(1)}, bf16[128,512]{1,0:T(8,128)(2,1)S(1)}, u32[]{:S(2)}, u32[]{:S(2)}) collective-permute-start(bf16[128,512]{1,0:T(8,128)(2,1)S(1)} %constant_dynamic-update-slice_fusion.refs_8_), channel_id=1, source_target_pairs={{0,7},{1,8},{2,9},{3,10},{4,11},{5,12},{6,13},{7,14},{8,15},{16,23... | collective-permute-start | bytes 393224 | tf_op jit(solution)/shard_map/ppermute | solution.py:92
  17.1 10.8 %collective-permute-start.2 = (bf16[128,512]{1,0:T(8,128)(2,1)S(1)}, bf16[128,512]{1,0:T(8,128)(2,1)S(1)}, u32[]{:S(2)}, u32[]{:S(2)}) collective-permute-start(bf16[128,512]{1,0:T(8,128)(2,1)S(1)} %constant_dynamic-update-slice_fusion.refs_8_), channel_id=1, source_target_pairs={{0,6},{1,7},{2,8},{3,9},{4,10},{5,11},{6,12},{7,13},{8,14},{9,15},... | collective-permute-start | bytes 393224 | tf_op jit(solution)/shard_map/ppermute | solution.py:92
  19.2 15.2 %collective-permute-start.3 = (bf16[128,512]{1,0:T(8,128)(2,1)S(1)}, bf16[128,512]{1,0:T(8,128)(2,1)S(1)}, u32[]{:S(2)}, u32[]{:S(2)}) collective-permute-start(bf16[128,512]{1,0:T(8,128)(2,1)S(1)} %constant_dynamic-update-slice_fusion.refs_8_), channel_id=1, source_target_pairs={{0,5},{1,6},{2,7},{3,8},{4,9},{5,10},{6,11},{7,12},{8,13},{9,14},{... | collective-permute-start | bytes 393224 | tf_op jit(solution)/shard_map/ppermute | solution.py:92
  20.5 19.6 %collective-permute-start.4 = (bf16[128,512]{1,0:T(8,128)(2,1)S(1)}, bf16[128,512]{1,0:T(8,128)(2,1)S(1)}, u32[]{:S(2)}, u32[]{:S(2)}) collective-permute-start(bf16[128,512]{1,0:T(8,128)(2,1)S(1)} %constant_dynamic-update-slice_fusion.refs_8_), channel_id=1, source_target_pairs={{0,4},{1,5},{2,6},{3,7},{4,8},{5,9},{6,10},{7,11},{8,12},{9,13},{1... | collective-permute-start | bytes 393224 | tf_op jit(solution)/shard_map/ppermute | solution.py:92
  22.2 18.6 %collective-permute-start.5 = (bf16[128,512]{1,0:T(8,128)(2,1)S(1)}, bf16[128,512]{1,0:T(8,128)(2,1)S(1)}, u32[]{:S(2)}, u32[]{:S(2)}) collective-permute-start(bf16[128,512]{1,0:T(8,128)(2,1)S(1)} %constant_dynamic-update-slice_fusion.refs_8_), channel_id=1, source_target_pairs={{0,3},{1,4},{2,5},{3,6},{4,7},{5,8},{6,9},{7,10},{8,11},{9,12},{10... | collective-permute-start | bytes 393224 | tf_op jit(solution)/shard_map/ppermute | solution.py:92
  25.6 0.7 copy-start.1
  26.3 15.1 %collective-permute-start.6 = (bf16[128,512]{1,0:T(8,128)(2,1)S(1)}, bf16[128,512]{1,0:T(8,128)(2,1)S(1)}, u32[]{:S(2)}, u32[]{:S(2)}) collective-permute-start(bf16[128,512]{1,0:T(8,128)(2,1)S(1)} %constant_dynamic-update-slice_fusion.refs_8_), channel_id=1, source_target_pairs={{0,2},{1,3},{2,4},{3,5},{4,6},{5,7},{6,8},{7,9},{8,10},{9,11},{10,... | collective-permute-start | bytes 393224 | tf_op jit(solution)/shard_map/ppermute | solution.py:92
  27.9 0.6 copy-start.4
  28.5 13.5 %collective-permute-start.7 = (bf16[128,512]{1,0:T(8,128)(2,1)S(1)}, bf16[128,512]{1,0:T(8,128)(2,1)S(1)}, u32[]{:S(2)}, u32[]{:S(2)}) collective-permute-start(bf16[128,512]{1,0:T(8,128)(2,1)S(1)} %constant_dynamic-update-slice_fusion.refs_8_), channel_id=1, source_target_pairs={{0,1},{1,2},{2,3},{3,4},{4,5},{5,6},{6,7},{7,8},{8,9},{9,10},{10,1... | collective-permute-start | bytes 393224 | tf_op jit(solution)/shard_map/ppermute | solution.py:92
  34.5 0.7 copy-start.7
  40.1 0.7 copy-start.10
  40.8 0.6 copy-start.13
  41.4 0.6 copy-start.16
  42.0 0.7 copy-start.19
  42.7 0.9 copy-start.2
  43.6 0.9 copy-start.5
  44.5 0.9 copy-start.8
  45.4 0.9 copy-start.11
  46.3 0.9 copy-start.14
  47.2 0.9 copy-start.17
  48.2 0.9 copy-start.20
  49.1 0.8 copy-start.22
  49.9 0.8 copy-start.27
  53.0 0.6 copy-start.24
  53.6 22.9 %all-to-all-start = ((bf16[16,128,256]{2,1,0:T(8,128)(2,1)}), bf16[16,128,256]{2,1,0:T(8,128)(2,1)}, u32[]{:S(2)}, u32[]{:S(2)}) async-start(bf16[16,128,256]{2,1,0:T(8,128)(2,1)} %broadcast_in_dim.15), calls=%async_computation | async-start | bytes 2097152 | tf_op jit(solution)/shard_map/all_to_all | solution.py:115
  59.8 80.0 %reduce-scatter.2.cloned.1.call-start = ((), (), s32[]{:S(2)}) async-start(), calls=%async_computation.4 | async-start | bytes 4718592 | tf_op jit(solution)/shard_map/reduce_scatter | solution.py:120
  83.7 134.3 %all-gather.5.cloned.1.call-start = ((), (), s32[]{:S(2)}) async-start(), calls=%async_computation.5 | async-start | bytes 4718592 | tf_op jit(solution)/shard_map/all_gather | solution.py:131
  141.5 9.9 %collective-permute-start.8 = (bf16[128,1024]{1,0:T(8,128)(2,1)}, bf16[128,1024]{1,0:T(8,128)(2,1)}, u32[]{:S(2)}, u32[]{:S(2)}) collective-permute-start(bf16[128,1024]{1,0:T(8,128)(2,1)} %constant_dynamic-slice_fusion), channel_id=1, source_target_pairs={{0,16},{16,0},{1,17},{17,1},{2,18},{18,2},{3,19},{19,3},{4,20},{20... | collective-permute-start | bytes 786440 | tf_op jit(solution)/shard_map/ppermute | solution.py:95
  153.4 9.1 %collective-permute-start.9 = (bf16[128,1024]{1,0:T(8,128)(2,1)}, bf16[128,1024]{1,0:T(8,128)(2,1)}, u32[]{:S(2)}, u32[]{:S(2)}) collective-permute-start(bf16[128,1024]{1,0:T(8,128)(2,1)} %subtract_convert_fusion.1), channel_id=1, source_target_pairs={{0,16},{16,0},{1,17},{17,1},{2,18},{18,2},{3,19},{19,3},{4,20},{20... | collective-permute-start | bytes 786440 | tf_op jit(solution)/shard_map/ppermute | solution.py:95
  245.0 0.9 copy-start.3
  245.9 0.9 copy-start.6
  246.8 0.9 copy-start.9
  247.7 0.9 copy-start.12
  248.6 0.9 copy-start.15
  249.5 0.9 copy-start.18
  250.4 0.9 copy-start.21
  251.3 0.8 copy-start.23
  252.2 0.8 copy-start.25
  253.0 0.8 copy-start.26
  255.2 6.5 %collective-permute-start.10 = (bf16[128,512]{1,0:T(8,128)(2,1)S(1)}, bf16[128,512]{1,0:T(8,128)(2,1)S(1)}, u32[]{:S(2)}, u32[]{:S(2)}) collective-permute-start(bf16[128,512]{1,0:T(8,128)(2,1)S(1)} %get-tuple-element.20), channel_id=1, source_target_pairs={{1,0},{2,1},{3,2},{4,3},{5,4},{6,5},{7,6},{8,7},{9,8},{10,9},{11,1... | collective-permute-start | bytes 393224 | tf_op jit(solution)/shard_map/ppermute | solution.py:92
  256.5 8.1 %collective-permute-start.11 = (bf16[128,512]{1,0:T(8,128)(2,1)S(1)}, bf16[128,512]{1,0:T(8,128)(2,1)S(1)}, u32[]{:S(2)}, u32[]{:S(2)}) collective-permute-start(bf16[128,512]{1,0:T(8,128)(2,1)S(1)} %get-tuple-element.21), channel_id=1, source_target_pairs={{2,0},{3,1},{4,2},{5,3},{6,4},{7,5},{8,6},{9,7},{10,8},{11,9},{12,... | collective-permute-start | bytes 393224 | tf_op jit(solution)/shard_map/ppermute | solution.py:92
  257.8 8.4 %collective-permute-start.12 = (bf16[128,512]{1,0:T(8,128)(2,1)S(1)}, bf16[128,512]{1,0:T(8,128)(2,1)S(1)}, u32[]{:S(2)}, u32[]{:S(2)}) collective-permute-start(bf16[128,512]{1,0:T(8,128)(2,1)S(1)} %get-tuple-element.22), channel_id=1, source_target_pairs={{3,0},{4,1},{5,2},{6,3},{7,4},{8,5},{9,6},{10,7},{11,8},{12,9},{13... | collective-permute-start | bytes 393224 | tf_op jit(solution)/shard_map/ppermute | solution.py:92
  259.1 12.9 %collective-permute-start.13 = (bf16[128,512]{1,0:T(8,128)(2,1)S(1)}, bf16[128,512]{1,0:T(8,128)(2,1)S(1)}, u32[]{:S(2)}, u32[]{:S(2)}) collective-permute-start(bf16[128,512]{1,0:T(8,128)(2,1)S(1)} %get-tuple-element.23), channel_id=1, source_target_pairs={{4,0},{5,1},{6,2},{7,3},{8,4},{9,5},{10,6},{11,7},{12,8},{13,9},{1... | collective-permute-start | bytes 393224 | tf_op jit(solution)/shard_map/ppermute | solution.py:92
  260.4 16.1 %collective-permute-start.14 = (bf16[128,512]{1,0:T(8,128)(2,1)S(1)}, bf16[128,512]{1,0:T(8,128)(2,1)S(1)}, u32[]{:S(2)}, u32[]{:S(2)}) collective-permute-start(bf16[128,512]{1,0:T(8,128)(2,1)S(1)} %get-tuple-element.24), channel_id=1, source_target_pairs={{5,0},{6,1},{7,2},{8,3},{9,4},{10,5},{11,6},{12,7},{13,8},{14,9},{... | collective-permute-start | bytes 393224 | tf_op jit(solution)/shard_map/ppermute | solution.py:92
  261.7 14.8 %collective-permute-start.15 = (bf16[128,512]{1,0:T(8,128)(2,1)S(1)}, bf16[128,512]{1,0:T(8,128)(2,1)S(1)}, u32[]{:S(2)}, u32[]{:S(2)}) collective-permute-start(bf16[128,512]{1,0:T(8,128)(2,1)S(1)} %get-tuple-element.25), channel_id=1, source_target_pairs={{6,0},{7,1},{8,2},{9,3},{10,4},{11,5},{12,6},{13,7},{14,8},{15,9},... | collective-permute-start | bytes 393224 | tf_op jit(solution)/shard_map/ppermute | solution.py:92
  264.6 11.9 %collective-permute-start.16 = (bf16[128,512]{1,0:T(8,128)(2,1)S(1)}, bf16[128,512]{1,0:T(8,128)(2,1)S(1)}, u32[]{:S(2)}, u32[]{:S(2)}) collective-permute-start(bf16[128,512]{1,0:T(8,128)(2,1)S(1)} %get-tuple-element.26), channel_id=1, source_target_pairs={{7,0},{8,1},{9,2},{10,3},{11,4},{12,5},{13,6},{14,7},{15,8},{23,16... | collective-permute-start | bytes 393224 | tf_op jit(solution)/shard_map/ppermute | solution.py:92
  266.2 12.7 %collective-permute-start.17 = (bf16[128,512]{1,0:T(8,128)(2,1)S(1)}, bf16[128,512]{1,0:T(8,128)(2,1)S(1)}, u32[]{:S(2)}, u32[]{:S(2)}) collective-permute-start(bf16[128,512]{1,0:T(8,128)(2,1)S(1)} %get-tuple-element.27), channel_id=1, source_target_pairs={{8,0},{9,1},{10,2},{11,3},{12,4},{13,5},{14,6},{15,7},{24,16},{25,... | collective-permute-start | bytes 393224 | tf_op jit(solution)/shard_map/ppermute | solution.py:92
Sparse Core Ops, SparseCore 0:
  9.9 51.0 all-gather.2
  83.9 55.9 reduce-scatter.1
  164.5 53.4 all-gather.4

commit v2 on v1

v2 whole, which is shorter than its diff:
```python
import functools

import jax
import jax.numpy as jnp
from jax import lax
from jax.experimental import pallas as pl
from jax.experimental.pallas import tpu as pltpu
from jax.sharding import Mesh
from jax.sharding import PartitionSpec as P

HEAD_DIM = 128
SEGMENT_MAX = 1024
TP = ("z", "xh")
SP = ("y", "xl", "core")
F32 = jnp.float32
BF16 = jnp.bfloat16
NT = (((1,), (1,)), ((), ()))
TN = (((0,), (0,)), ((), ()))


def dot(a, b, dims=(((1,), (0,)), ((), ()))):
    return lax.dot_general(a, b, dims, preferred_element_type=F32)


def fetch(sources, targets, sems):
    copies = [
        pltpu.make_async_copy(src, dst, sems.at[i])
        for i, (src, dst) in enumerate(zip(sources, targets, strict=True))
    ]
    for copy in copies:
        copy.start()
    for copy in copies:
        copy.wait()


def forward_kernel(n, qseg_ref, kseg_ref, q_hbm, *refs):
    kv_hbm, (attn_ref, probs_ref, q_ref, kv_ref, sems) = refs[:n], refs[n:]
    rows, width = q_ref.shape
    keys = rows * n
    fetch(
        (q_hbm, *kv_hbm),
        (q_ref, *(kv_ref.at[pl.ds(i * rows, rows)] for i in range(n))),
        sems,
    )
    scale = HEAD_DIM ** (-0.5)
    place = lax.broadcasted_iota(jnp.int32, (rows, keys), 0) + (keys - rows)
    allowed = (place >= lax.broadcasted_iota(jnp.int32, (rows, keys), 1)) & (
        qseg_ref[...] == kseg_ref[...]
    )
    for h in range(width // HEAD_DIM):
        cols = slice(h * HEAD_DIM, (h + 1) * HEAD_DIM)
        vcols = slice(width + h * HEAD_DIM, width + (h + 1) * HEAD_DIM)
        scores = jnp.where(allowed, dot(q_ref[:, cols], kv_ref[:, cols], NT) * scale, -1e30)
        expo = jnp.exp(scores - jnp.max(scores, axis=-1, keepdims=True))
        probs = expo / jnp.sum(expo, axis=-1, keepdims=True)
        probs_ref[h] = probs
        attn_ref[:, cols] = dot(probs.astype(BF16), kv_ref[:, vcols]).astype(BF16)


def backward_kernel(n, dattn_ref, q_hbm, attn_hbm, probs_hbm, *refs):
    kv_hbm, dq_ref, dkv_refs = refs[:n], refs[n], refs[n + 1 : 2 * n + 1]
    q_ref, attn_ref, probs_ref, kv_ref, sems = refs[2 * n + 1 :]
    rows, width = q_ref.shape
    fetch(
        (q_hbm, attn_hbm, probs_hbm, *kv_hbm),
        (q_ref, attn_ref, probs_ref, *(kv_ref.at[pl.ds(i * rows, rows)] for i in range(n))),
        sems,
    )
    scale = HEAD_DIM ** (-0.5)
    for h in range(width // HEAD_DIM):
        cols = slice(h * HEAD_DIM, (h + 1) * HEAD_DIM)
        vcols = slice(width + h * HEAD_DIM, width + (h + 1) * HEAD_DIM)
        probs = probs_ref[h]
        dattn = dattn_ref[:, cols]
        delta = jnp.sum(
            dattn.astype(F32) * attn_ref[:, cols].astype(F32), axis=-1, keepdims=True
        )
        dprobs = dot(dattn, kv_ref[:, vcols], NT)
        dscores = (probs * (dprobs - delta) * scale).astype(BF16)
        dq_ref[:, cols] = dot(dscores, kv_ref[:, cols]).astype(BF16)
        dkey = dot(dscores, q_ref[:, cols], TN).astype(BF16)
        dvalue = dot(probs.astype(BF16), dattn, TN).astype(BF16)
        for i, r in enumerate(dkv_refs):
            r[:, cols] = dkey[i * rows : (i + 1) * rows]
            r[:, vcols] = dvalue[i * rows : (i + 1) * rows]


def dattn_kernel(n, offsets, z_ref, dpred_ref, *refs):
    proj_hbm, (out_ref, *proj_refs, sems) = refs[: len(offsets)], refs[len(offsets) :]
    fetch(proj_hbm, proj_refs, sems)
    first = [0] * n
    for ref, by in zip(proj_refs, offsets, strict=True):
        size = ref.shape[0]
        z = lax.rem(z_ref[0] + by, n)
        out = dot(dpred_ref[...], ref[...], NT).astype(BF16)
        out_ref[z, :, first[by] : first[by] + size] = out
        first[by] += size


def call(kernel, out_shape, in_vmem, in_hbm, scratch, scalars=()):
    return pl.pallas_call(
        kernel,
        out_shape=out_shape,
        in_specs=[pl.BlockSpec(memory_space=pltpu.SMEM)] * len(scalars)
        + [pl.BlockSpec(memory_space=pltpu.VMEM)] * len(in_vmem)
        + [pl.BlockSpec(memory_space=pl.ANY)] * len(in_hbm),
        scratch_shapes=[pltpu.VMEM(s.shape, s.dtype) for s in scratch]
        + [pltpu.SemaphoreType.DMA((len(in_hbm),))],
        compiler_params=pltpu.CompilerParams(vmem_limit_bytes=40 * 1024 * 1024),
    )(*scalars, *in_vmem, *in_hbm)


def body(context, w_out, teacher_resid, queries, keys, values, segment_ids, proj):
    rows, width = queries.shape
    heads = width // HEAD_DIM
    n_sp, n_z, n_xh = lax.axis_size(SP), lax.axis_size("z"), lax.axis_size("xh")
    back = -(-(SEGMENT_MAX - 1) // rows)
    back = min(back, n_sp - 1)
    window = (back + 1) * rows
    first_row = lax.axis_index(SP) * rows
    z, xh = lax.axis_index("z"), lax.axis_index("xh")

    def shift(array, by):
        pairs = [(i, i + by) for i in range(n_sp) if 0 <= i + by < n_sp]
        return lax.ppermute(array, SP, pairs)

    def turn(array, by):
        return lax.ppermute(array, "z", [(i, (i + by) % n_z) for i in range(n_z)])

    def swap(array):
        return lax.ppermute(array, "xh", [(i, i ^ 1) for i in range(n_xh)])

    context_all = lax.all_gather(context, SP, axis=0, tiled=True)

    half = width // 2
    pieces, offsets = [proj], [0]

    def step(up, down):
        k = len(pieces) // 2 + 1
        if k == n_z // 2:
            up, down = up[:half], down[half:]
        offsets.extend([n_z - k, k])
        return turn(up, 1), turn(down, -1)

    key_value = jnp.concatenate([keys, values], axis=1)
    blocks = [shift(key_value, k) for k in range(back, 0, -1)] + [key_value]
    padded = jnp.concatenate([jnp.full((window - rows,), -1, jnp.int32), segment_ids])
    window_segments = lax.dynamic_slice_in_dim(padded, first_row, window, 0)
    query_segments = lax.dynamic_slice_in_dim(segment_ids, first_row, rows, 0)
    block_type = jax.ShapeDtypeStruct((rows, width), BF16)
    window_type = jax.ShapeDtypeStruct((window, 2 * width), BF16)
    probs_type = jax.ShapeDtypeStruct((heads, rows, window), F32)
    up, down = step(proj, proj)
    queries, up, down = lax.optimization_barrier((queries, up, down))
    pieces += [up, down]
    attn, probs = call(
        functools.partial(forward_kernel, back + 1),
        (block_type, probs_type),
        (query_segments[:, None], window_segments[None, :]),
        (queries, *blocks),
        (block_type, window_type),
    )
    attn_all = lax.all_to_all(
        jnp.broadcast_to(attn[None], (n_sp, rows, width)), SP, 0, 0, tiled=True
    ).reshape(n_sp * rows, width)
    up, down = step(up, down)
    attn_all, up, down = lax.optimization_barrier((attn_all, up, down))
    pieces += [up, down]

    resid_other = swap(teacher_resid)
    resid = jnp.concatenate(
        [
            jnp.where(xh == 0, teacher_resid, resid_other),
            jnp.where(xh == 0, resid_other, teacher_resid),
        ],
        axis=0,
    )
    part = (dot(attn_all, proj) - dot(context_all, w_out)).astype(BF16)
    part = lax.psum_scatter(part, "z", scatter_dimension=0, tiled=True)
    while len(pieces) < n_z:
        up, down = step(up, down)
        pieces += [up, down]
    part, resid, up, down = lax.optimization_barrier((part, resid, up, down))
    pieces[-2:] = [up, down]
    diff = (part.astype(F32) + swap(part).astype(F32)) - resid.astype(F32)
    dpred = diff.astype(BF16)

    dattn_part = call(
        functools.partial(dattn_kernel, n_z, offsets),
        jax.ShapeDtypeStruct((n_z, n_xh * rows, width), BF16),
        (dpred,),
        pieces,
        pieces,
        scalars=(z[None],),
    )
    dattn_parts = lax.all_to_all(dattn_part.reshape(n_sp, rows, width), SP, 0, 0, tiled=True)
    dattn = jnp.sum(dattn_parts.astype(F32), axis=0).astype(BF16)
    pairs = []
    for a in range(n_z):
        for x in range(n_xh):
            for b in range(n_z):
                for e in range(n_xh):
                    pairs.append(
                        (
                            (a * n_xh + x) * n_sp + b * n_xh + e,
                            (b * n_xh + x) * n_sp + a * n_xh + e,
                        )
                    )
    dattn = lax.ppermute(dattn, TP + SP, pairs)

    dpred_all = lax.all_gather(dpred, "z", axis=0, tiled=True)
    proj_grad = dot(attn_all, dpred_all, TN).astype(BF16)

    query_grad, *grads = call(
        functools.partial(backward_kernel, back + 1),
        (block_type,) + (jax.ShapeDtypeStruct((rows, 2 * width), BF16),) * (back + 1),
        (dattn,),
        (queries, attn, probs, *blocks),
        (block_type, block_type, probs_type, window_type),
    )
    total = grads[back].astype(F32)
    for k in range(1, back + 1):
        total = total + shift(grads[back - k], -k).astype(F32)
    total = total.astype(BF16)
    return proj_grad, query_grad, total[:, :width], total[:, width:]


def solution(mesh):
    fine = Mesh(mesh.devices.reshape(8, 2, 4, 2, 2), TP + SP)
    in_specs = (
        P(SP, TP),
        P(TP, SP),
        P(TP, SP),
        P(SP, TP),
        P(SP, TP),
        P(SP, TP),
        P(),
        P(TP, SP),
    )
    out_specs = (P(TP, SP), P(SP, TP), P(SP, TP), P(SP, TP))
    return jax.shard_map(body, mesh=fine, in_specs=in_specs, out_specs=out_specs, check_vma=False)
```

time: 292 us -> 262 us (0.90)
  the two profiles are of different devices: /device:TPU:4 before, /device:TPU:10 now
where the time goes in v2:
time: 262 us; the launch traced here: 261 us
  waiting for transfers between devices  95.1 us (36%)
  starting transfers between devices  81.5 us (31%)
  local copies, waits for them, and re-layouts  21.4 us (8%)
  blocking collectives  18.5 us (7%)
  matrix products  15.5 us (6%)
  between operations  14.1 us (5%)
  Pallas kernels  9.31 us (4%)
  other arithmetic  5.09 us (2%)
    ppermute x16, starting transfers between devices, shift(): return lax.ppermute(array, SP, pairs)  41 us
    ppermute x8, waiting for transfers between devices, turn(): return lax.ppermute(array, 'z', [(i, (i + by) % n_z) for i in range(n_z)])  32 us
    reduce_scatter x1, waiting for transfers between devices, body(): part = lax.psum_scatter(part, 'z', scatter_dimension=0, tiled=True)  27.2 us
    all_to_all x1, blocking collectives, body(): lax.all_to_all(dattn_part.reshape(n_sp, rows, width), SP, 0, 0, tiled=True)  18.5 us
    ppermute x16, waiting for transfers between devices, shift(): return lax.ppermute(array, SP, pairs)  17.8 us
    ppermute x8, starting transfers between devices, turn(): return lax.ppermute(array, 'z', [(i, (i + by) % n_z) for i in range(n_z)])  16.7 us
    unnamed x41, local copies, waits for them, and re-layouts  15.5 us
    dot_general x3, matrix products, dot(): return lax.dot_general(a, b, dims, preferred_element_type=F32)  15.5 us
  transfers between devices with their start and end apart: 31, of which 15 were waited for; matrix products, arithmetic and copies ran while one was open for 4% of the time, Pallas kernels for 4%

profile of v2, /device:TPU:10, one launch (start us, length us, event | category | flops | bytes accessed | tf_op | source)
XLA Modules:
  0.0 260.5 jit_solution(17698576864934286496)
XLA Ops:
  7.9 2.0 collective-permute-start
  9.9 4.0 %collective-permute-start.1 = (bf16[256,1024]{1,0:T(8,128)(2,1)}, bf16[256,1024]{1,0:T(8,128)(2,1)S(1)}, u32[]{:S(2)}, u32[]{:S(2)}) collective-permute-start(bf16[256,1024]{1,0:T(8,128)(2,1)} %refs_0_.1), channel_id=1, source_target_pairs={{0,224},{32,0},{64,32},{96,64},{128,96},{160,128},{192,160},{224,1... | collective-permute-start | bytes 1572872 | tf_op jit(solution)/shard_map/ppermute | solution.py:128
  13.9 0.8 constant_dynamic-update-slice_fusion.1
  14.8 0.8 constant_dynamic-update-slice_fusion.refs_8_
  15.6 4.2 %collective-permute-start.2 = (bf16[128,512]{1,0:T(8,128)(2,1)S(1)}, bf16[128,512]{1,0:T(8,128)(2,1)S(1)}, u32[]{:S(2)}, u32[]{:S(2)}) collective-permute-start(bf16[128,512]{1,0:T(8,128)(2,1)S(1)} %constant_dynamic-update-slice_fusion.refs_8_), channel_id=1, source_target_pairs={{0,8},{1,9},{2,10},{3,11},{4,12},{5,13},{6,14},{7,15},{16,24},{17,... | collective-permute-start | bytes 393224 | tf_op jit(solution)/shard_map/ppermute | solution.py:125
  19.8 1.3 collective-permute-start.3
  21.1 1.9 collective-permute-start.4
  23.1 2.7 %collective-permute-start.5 = (bf16[128,512]{1,0:T(8,128)(2,1)S(1)}, bf16[128,512]{1,0:T(8,128)(2,1)}, u32[]{:S(2)}, u32[]{:S(2)}) collective-permute-start(bf16[128,512]{1,0:T(8,128)(2,1)S(1)} %constant_dynamic-update-slice_fusion.refs_8_), channel_id=1, source_target_pairs={{0,5},{1,6},{2,7},{3,8},{4,9},{5,10},{6,11},{7,12},{8,13},{9,14},{... | collective-permute-start | bytes 393224 | tf_op jit(solution)/shard_map/ppermute | solution.py:125
  25.8 7.3 %collective-permute-start.6 = (bf16[128,512]{1,0:T(8,128)(2,1)S(1)}, bf16[128,512]{1,0:T(8,128)(2,1)}, u32[]{:S(2)}, u32[]{:S(2)}) collective-permute-start(bf16[128,512]{1,0:T(8,128)(2,1)S(1)} %constant_dynamic-update-slice_fusion.refs_8_), channel_id=1, source_target_pairs={{0,4},{1,5},{2,6},{3,7},{4,8},{5,9},{6,10},{7,11},{8,12},{9,13},{1... | collective-permute-start | bytes 393224 | tf_op jit(solution)/shard_map/ppermute | solution.py:125
  33.6 1.9 collective-permute-start.7
  35.5 3.5 %collective-permute-start.8 = (bf16[128,512]{1,0:T(8,128)(2,1)S(1)}, bf16[128,512]{1,0:T(8,128)(2,1)}, u32[]{:S(2)}, u32[]{:S(2)}) collective-permute-start(bf16[128,512]{1,0:T(8,128)(2,1)S(1)} %constant_dynamic-update-slice_fusion.refs_8_), channel_id=1, source_target_pairs={{0,2},{1,3},{2,4},{3,5},{4,6},{5,7},{6,8},{7,9},{8,10},{9,11},{10,... | collective-permute-start | bytes 393224 | tf_op jit(solution)/shard_map/ppermute | solution.py:125
  39.1 1.9 collective-permute-start.9
  43.6 1.5 collective-permute-done.7.refs_5_
  45.5 0.8 copy-done.15
  46.3 0.8 copy-done.19
  47.1 2.9 %shard_map.111 = (bf16[128,256]{1,0:T(8,128)(2,1)S(1)}, f32[2,128,1152]{2,1,0:T(8,128)S(1)}) custom-call(s32[128,1]{1,0:T(8,128)S(1)} %copy-done.19, s32[1,1152]{1,0:T(1,128)S(1)} %broadcast_in_dim.17.kseg_ref, bf16[128,256]{1,0:T(8,128)(2,1)S(1)} %copy-done.15, bf16[128,512]{1,0:T(8,128)(2,1)S(1)} %collective-permute-done.2.refs_0_, ...), custom_call_target="tpu_custom_call" | custom-call | tf_op jit(solution)/shard_map/pallas_call | solution.py:101
  50.0 1.0 copy-done.3
  51.1 1.1 broadcast_in_dim.18
  52.8 10.1 %all-to-all-start = ((bf16[16,128,256]{2,1,0:T(8,128)(2,1)}), bf16[16,128,256]{2,1,0:T(8,128)(2,1)}, u32[]{:S(2)}, u32[]{:S(2)}) async-start(bf16[16,128,256]{2,1,0:T(8,128)(2,1)} %broadcast_in_dim.18), calls=%async_computation | async-start | bytes 2097152 | tf_op jit(solution)/shard_map/all_to_all | solution.py:163
  63.1 3.2 %collective-permute-start.11 = (bf16[256,1024]{1,0:T(8,128)(2,1)S(1)}, bf16[256,1024]{1,0:T(8,128)(2,1)}, u32[]{:S(2)}, u32[]{:S(2)}) collective-permute-start(bf16[256,1024]{1,0:T(8,128)(2,1)S(1)} %collective-permute-done.1.refs_2_), channel_id=1, source_target_pairs={{0,224},{32,0},{64,32},{96,64},{128,96},{160,128},{192,160},{224,1... | collective-permute-start | bytes 1572872 | tf_op jit(solution)/shard_map/ppermute | solution.py:128
  66.3 12.0 %collective-permute-done.10.refs_3_ = bf16[256,1024]{1,0:T(8,128)(2,1)S(1)} collective-permute-done((bf16[256,1024]{1,0:T(8,128)(2,1)S(1)}, bf16[256,1024]{1,0:T(8,128)(2,1)S(1)}, u32[]{:S(2)}, u32[]{:S(2)}) %collective-permute-start.10) | collective-permute-done | bytes 524320 | tf_op jit(solution)/shard_map/ppermute | solution.py:128
  78.2 0.8 copy-done.9
  79.1 6.3 %fusion.1 = f32[2048,1024]{1,0:T(8,128)S(1)} fusion(bf16[2048,1024]{1,0:T(8,128)(2,1)} %all-gather.3.cloned.1.call-done, bf16[1024,1024]{1,0:T(8,128)(2,1)S(1)} %copy-done), kind=kOutput, calls=%fused_computation.12 | convolution fusion | flops 4294967296 | bytes 14680064 | tf_op jit(solution)/shard_map/dot_general | solution.py:22
  85.4 4.6 %subtract_convert_fusion = bf16[2048,1024]{1,0:T(8,128)(2,1)} fusion(f32[2048,1024]{1,0:T(8,128)S(1)} %fusion.1, bf16[2048,256]{1,0:T(8,128)(2,1)} %bitcast.1, bf16[256,1024]{1,0:T(8,128)(2,1)S(1)} %copy-done.2), kind=kOutput, calls=%fused_computation | convolution fusion | flops 1077936128 | bytes 14155776 | tf_op jit(solution)/shard_map/dot_general | solution.py:22
  90.2 3.2 %collective-permute-start.15 = (bf16[256,1024]{1,0:T(8,128)(2,1)}, bf16[256,1024]{1,0:T(8,128)(2,1)}, u32[]{:S(2)}, u32[]{:S(2)}) collective-permute-start(bf16[256,1024]{1,0:T(8,128)(2,1)} %collective-permute-done.11.refs_4_), channel_id=1, source_target_pairs={{0,224},{32,0},{64,32},{96,64},{128,96},{160,128},{192,160},{224,1... | collective-permute-start | bytes 1572872 | tf_op jit(solution)/shard_map/ppermute | solution.py:128
  93.4 2.4 collective-permute-start.12
  95.9 8.9 %collective-permute-done.13.refs_5_ = bf16[256,1024]{1,0:T(8,128)(2,1)S(1)} collective-permute-done((bf16[256,1024]{1,0:T(8,128)(2,1)}, bf16[256,1024]{1,0:T(8,128)(2,1)S(1)}, u32[]{:S(2)}, u32[]{:S(2)}) %collective-permute-start.13) | collective-permute-done | bytes 524320 | tf_op jit(solution)/shard_map/ppermute | solution.py:128
  104.9 3.6 %collective-permute-done.15.refs_6_ = bf16[256,1024]{1,0:T(8,128)(2,1)} collective-permute-done((bf16[256,1024]{1,0:T(8,128)(2,1)}, bf16[256,1024]{1,0:T(8,128)(2,1)}, u32[]{:S(2)}, u32[]{:S(2)}) %collective-permute-start.15) | collective-permute-done | bytes 524320 | tf_op jit(solution)/shard_map/ppermute | solution.py:128
  108.5 1.0 slice.17
  109.5 3.9 %collective-permute-start.16 = (bf16[128,1024]{1,0:T(8,128)(2,1)S(1)}, bf16[128,1024]{1,0:T(8,128)(2,1)S(1)}, u32[]{:S(2)}, u32[]{:S(2)}) collective-permute-start(bf16[128,1024]{1,0:T(8,128)(2,1)S(1)} %slice.17), channel_id=1, source_target_pairs={{0,224},{32,0},{64,32},{96,64},{128,96},{160,128},{192,160},{224,1... | collective-permute-start | bytes 786440 | tf_op jit(solution)/shard_map/ppermute | solution.py:128
  113.4 1.1 broadcast_select_fusion.1
  114.5 0.8 pad_maximum_fusion
  115.3 4.6 %collective-permute-done.14.refs_7_ = bf16[128,1024]{1,0:T(8,128)(2,1)S(1)} collective-permute-done((bf16[128,1024]{1,0:T(8,128)(2,1)S(1)}, bf16[128,1024]{1,0:T(8,128)(2,1)S(1)}, u32[]{:S(2)}, u32[]{:S(2)}) %collective-permute-start.14) | collective-permute-done | bytes 262176 | tf_op jit(solution)/shard_map/ppermute | solution.py:128
  120.7 2.9 %collective-permute-done.16.refs_8_ = bf16[128,1024]{1,0:T(8,128)(2,1)S(1)} collective-permute-done((bf16[128,1024]{1,0:T(8,128)(2,1)S(1)}, bf16[128,1024]{1,0:T(8,128)(2,1)S(1)}, u32[]{:S(2)}, u32[]{:S(2)}) %collective-permute-start.16) | collective-permute-done | bytes 262176 | tf_op jit(solution)/shard_map/ppermute | solution.py:128
  124.3 27.2 %reduce-scatter.2.cloned.1.call-done = bf16[256,1024]{1,0:T(8,128)(2,1)} async-done(((bf16[2048,1024]{1,0:T(8,128)(2,1)}), bf16[256,1024]{1,0:T(8,128)(2,1)}) %reduce-scatter.2.cloned.1.call-update) | async-done | bytes 524304 | tf_op jit(solution)/shard_map/reduce_scatter | solution.py:179
  151.6 2.1 collective-permute-start.17
  153.6 13.3 %collective-permute-done.17 = bf16[256,1024]{1,0:T(8,128)(2,1)S(1)} collective-permute-done((bf16[256,1024]{1,0:T(8,128)(2,1)}, bf16[256,1024]{1,0:T(8,128)(2,1)S(1)}, u32[]{:S(2)}, u32[]{:S(2)}) %collective-permute-start.17) | collective-permute-done | bytes 524320 | tf_op jit(solution)/shard_map/ppermute | solution.py:131
  167.0 2.3 subtract_convert_fusion.1.dpred_ref
  169.3 1.0 copy-done.1
  170.3 1.0 copy-done.6
  171.4 1.0 copy-done.8
  172.4 1.0 copy-done.10
  173.5 0.9 copy-done.12
  174.4 0.9 copy-done.14
  175.4 2.9 %shard_map.112 = bf16[8,256,256]{2,1,0:T(8,128)(2,1)S(1)} custom-call(s32[1]{0:T(128)} %bitcast.2.z_ref, bf16[256,1024]{1,0:T(8,128)(2,1)S(1)} %copy-done.1, bf16[256,1024]{1,0:T(8,128)(2,1)S(1)} %copy-done.2, bf16[256,1024]{1,0:T(8,128)(2,1)S(1)} %copy-done.6, bf16[256,1024]{1,0:T(8,128)(2,1)S(1)} %copy-done.8, bf16[256,1024]{1,0:T(8,128)(2,1)S(1)} %copy-done.10, ...), custom_call_target="tpu_custom_call" | custom-call | tf_op jit(solution)/shard_map/pallas_call | solution.py:101
  178.2 18.5 %all_to_all.10 = bf16[16,128,256]{2,1,0:T(8,128)(2,1)S(1)} all-to-all(bf16[16,128,256]{2,1,0:T(8,128)(2,1)S(1)} %bitcast.11), channel_id=1, replica_groups=mesh['z'=8,'xh'=2,'y'=4,'xl'=2,'core'=2] {'y','xl','core'}, dimensions={0} | all-to-all | bytes 2097152 | tf_op jit(solution)/shard_map/all_to_all | solution.py:196
  197.5 9.1 %collective-permute-start.18 = (bf16[128,256]{1,0:T(8,128)(2,1)}, bf16[128,256]{1,0:T(8,128)(2,1)S(1)}, u32[]{:S(2)}, u32[]{:S(2)}) collective-permute-start(bf16[128,256]{1,0:T(8,128)(2,1)} %reduce_sum.12), channel_id=1, source_target_pairs={{0,0},{1,1},{2,32},{3,33},{4,64},{5,65},{6,96},{7,97},{8,128},{9,1... | collective-permute-start | bytes 196616 | tf_op jit(solution)/shard_map/ppermute | solution.py:209
  206.6 4.0 %collective-permute-done.18.dattn_ref = bf16[128,256]{1,0:T(8,128)(2,1)S(1)} collective-permute-done((bf16[128,256]{1,0:T(8,128)(2,1)}, bf16[128,256]{1,0:T(8,128)(2,1)S(1)}, u32[]{:S(2)}, u32[]{:S(2)}) %collective-permute-start.18) | collective-permute-done | bytes 65568 | tf_op jit(solution)/shard_map/ppermute | solution.py:209
  210.6 1.3 copy-done.4
  211.9 0.8 copy-done.16
  212.7 0.8 copy-done.18
  213.6 3.6 %shard_map.113 = (bf16[128,256]{1,0:T(8,128)(2,1)}, bf16[128,512]{1,0:T(8,128)(2,1)S(1)}, bf16[128,512]{1,0:T(8,128)(2,1)S(1)}, bf16[128,512]{1,0:T(8,128)(2,1)S...) custom-call(bf16[128,256]{1,0:T(8,128)(2,1)S(1)} %collective-permute, ...), custom_call_target="tpu_custom_call" | custom-call | tf_op jit(solution)/shard_map/pallas_call | solution.py:101
  217.2 1.9 collective-permute-start.19
  219.1 4.0 %collective-permute-start.20 = (bf16[128,512]{1,0:T(8,128)(2,1)S(1)}, bf16[128,512]{1,0:T(8,128)(2,1)S(1)}, u32[]{:S(2)}, u32[]{:S(2)}) collective-permute-start(bf16[128,512]{1,0:T(8,128)(2,1)S(1)} %get-tuple-element.41), channel_id=1, source_target_pairs={{2,0},{3,1},{4,2},{5,3},{6,4},{7,5},{8,6},{9,7},{10,8},{11,9},{12,... | collective-permute-start | bytes 393224 | tf_op jit(solution)/shard_map/ppermute | solution.py:125
  223.1 1.9 collective-permute-start.21
  225.0 1.9 collective-permute-start.22
  226.9 1.9 collective-permute-start.23
  228.9 1.9 collective-permute-start.24
  230.8 1.3 collective-permute-start.25
  232.1 1.3 collective-permute-start.26
  233.4 2.3 collective-permute-done.22
  235.7 5.8 %collective-permute-done.23 = bf16[128,512]{1,0:T(8,128)(2,1)S(1)} collective-permute-done((bf16[128,512]{1,0:T(8,128)(2,1)S(1)}, bf16[128,512]{1,0:T(8,128)(2,1)S(1)}, u32[]{:S(2)}, u32[]{:S(2)}) %collective-permute-start.23) | collective-permute-done | bytes 131104 | tf_op jit(solution)/shard_map/ppermute | solution.py:125
  241.5 7.1 %collective-permute-done.26 = bf16[128,512]{1,0:T(8,128)(2,1)S(1)} collective-permute-done((bf16[128,512]{1,0:T(8,128)(2,1)S(1)}, bf16[128,512]{1,0:T(8,128)(2,1)S(1)}, u32[]{:S(2)}, u32[]{:S(2)}) %collective-permute-start.26) | collective-permute-done | bytes 131104 | tf_op jit(solution)/shard_map/ppermute | solution.py:125
  249.4 4.6 %convolution_convert_fusion = bf16[256,1024]{1,0:T(8,128)(2,1)} fusion(bf16[2048,256]{1,0:T(8,128)(2,1)} %bitcast.1, bf16[2048,1024]{1,0:T(8,128)(2,1)} %all-gather.5.cloned.1.call-done), kind=kOutput, calls=%fused_computation.1 | convolution fusion | flops 1074003968 | bytes 5767168 | tf_op jit(solution)/shard_map/dot_general | solution.py:22
  (63 shorter events, 8.3 us)
Async XLA Ops:
  7.2 71.9 %copy-start = (bf16[1024,1024]{1,0:T(8,128)(2,1)S(1)}, bf16[1024,1024]{1,0:T(8,128)(2,1)}, u32[]{:S(2)}) copy-start(bf16[1024,1024]{1,0:T(8,128)(2,1)} %param.9) | copy-start | bytes 6291460
  7.2 71.9 %all-gather.3.cloned.1.call-start = ((), (), s32[]{:S(2)}) async-start(), calls=%async_computation.3 | async-start | bytes 4456448 | tf_op jit(solution)/shard_map/all_gather | solution.py:133
  7.9 27.6 %collective-permute-start = (bf16[256,1024]{1,0:T(8,128)(2,1)}, bf16[256,1024]{1,0:T(8,128)(2,1)S(1)}, u32[]{:S(2)}, u32[]{:S(2)}) collective-permute-start(bf16[256,1024]{1,0:T(8,128)(2,1)} %refs_0_.1), channel_id=1, source_target_pairs={{0,32},{32,64},{64,96},{96,128},{128,160},{160,192},{192,224},{224... | collective-permute-start | bytes 1572872 | tf_op jit(solution)/shard_map/ppermute | solution.py:128
  9.9 29.1 %collective-permute-start.1 = (bf16[256,1024]{1,0:T(8,128)(2,1)}, bf16[256,1024]{1,0:T(8,128)(2,1)S(1)}, u32[]{:S(2)}, u32[]{:S(2)}) collective-permute-start(bf16[256,1024]{1,0:T(8,128)(2,1)} %refs_0_.1), channel_id=1, source_target_pairs={{0,224},{32,0},{64,32},{96,64},{128,96},{160,128},{192,160},{224,1... | collective-permute-start | bytes 1572872 | tf_op jit(solution)/shard_map/ppermute | solution.py:128
  15.6 7.4 %collective-permute-start.2 = (bf16[128,512]{1,0:T(8,128)(2,1)S(1)}, bf16[128,512]{1,0:T(8,128)(2,1)S(1)}, u32[]{:S(2)}, u32[]{:S(2)}) collective-permute-start(bf16[128,512]{1,0:T(8,128)(2,1)S(1)} %constant_dynamic-update-slice_fusion.refs_8_), channel_id=1, source_target_pairs={{0,8},{1,9},{2,10},{3,11},{4,12},{5,13},{6,14},{7,15},{16,24},{17,... | collective-permute-start | bytes 393224 | tf_op jit(solution)/shard_map/ppermute | solution.py:125
  19.8 5.9 %collective-permute-start.3 = (bf16[128,512]{1,0:T(8,128)(2,1)S(1)}, bf16[128,512]{1,0:T(8,128)(2,1)S(1)}, u32[]{:S(2)}, u32[]{:S(2)}) collective-permute-start(bf16[128,512]{1,0:T(8,128)(2,1)S(1)} %constant_dynamic-update-slice_fusion.refs_8_), channel_id=1, source_target_pairs={{0,7},{1,8},{2,9},{3,10},{4,11},{5,12},{6,13},{7,14},{8,15},{16,23... | collective-permute-start | bytes 393224 | tf_op jit(solution)/shard_map/ppermute | solution.py:125
  21.1 12.4 %collective-permute-start.4 = (bf16[128,512]{1,0:T(8,128)(2,1)S(1)}, bf16[128,512]{1,0:T(8,128)(2,1)}, u32[]{:S(2)}, u32[]{:S(2)}) collective-permute-start(bf16[128,512]{1,0:T(8,128)(2,1)S(1)} %constant_dynamic-update-slice_fusion.refs_8_), channel_id=1, source_target_pairs={{0,6},{1,7},{2,8},{3,9},{4,10},{5,11},{6,12},{7,13},{8,14},{9,15},... | collective-permute-start | bytes 393224 | tf_op jit(solution)/shard_map/ppermute | solution.py:125
  23.1 20.2 %collective-permute-start.5 = (bf16[128,512]{1,0:T(8,128)(2,1)S(1)}, bf16[128,512]{1,0:T(8,128)(2,1)}, u32[]{:S(2)}, u32[]{:S(2)}) collective-permute-start(bf16[128,512]{1,0:T(8,128)(2,1)S(1)} %constant_dynamic-update-slice_fusion.refs_8_), channel_id=1, source_target_pairs={{0,5},{1,6},{2,7},{3,8},{4,9},{5,10},{6,11},{7,12},{8,13},{9,14},{... | collective-permute-start | bytes 393224 | tf_op jit(solution)/shard_map/ppermute | solution.py:125
  25.8 17.8 %collective-permute-start.6 = (bf16[128,512]{1,0:T(8,128)(2,1)S(1)}, bf16[128,512]{1,0:T(8,128)(2,1)}, u32[]{:S(2)}, u32[]{:S(2)}) collective-permute-start(bf16[128,512]{1,0:T(8,128)(2,1)S(1)} %constant_dynamic-update-slice_fusion.refs_8_), channel_id=1, source_target_pairs={{0,4},{1,5},{2,6},{3,7},{4,8},{5,9},{6,10},{7,11},{8,12},{9,13},{1... | collective-permute-start | bytes 393224 | tf_op jit(solution)/shard_map/ppermute | solution.py:125
  33.6 11.5 %collective-permute-start.7 = (bf16[128,512]{1,0:T(8,128)(2,1)S(1)}, bf16[128,512]{1,0:T(8,128)(2,1)}, u32[]{:S(2)}, u32[]{:S(2)}) collective-permute-start(bf16[128,512]{1,0:T(8,128)(2,1)S(1)} %constant_dynamic-update-slice_fusion.refs_8_), channel_id=1, source_target_pairs={{0,3},{1,4},{2,5},{3,6},{4,7},{5,8},{6,9},{7,10},{8,11},{9,12},{10... | collective-permute-start | bytes 393224 | tf_op jit(solution)/shard_map/ppermute | solution.py:125
  35.5 43.6 %copy-start.5 = (bf16[256,1024]{1,0:T(8,128)(2,1)}, bf16[256,1024]{1,0:T(8,128)(2,1)S(1)}, u32[]{:S(2)}) copy-start(bf16[256,1024]{1,0:T(8,128)(2,1)S(1)} %collective-permute-done.refs_1_) | copy-start | bytes 1572868
  35.5 9.6 %collective-permute-start.8 = (bf16[128,512]{1,0:T(8,128)(2,1)S(1)}, bf16[128,512]{1,0:T(8,128)(2,1)}, u32[]{:S(2)}, u32[]{:S(2)}) collective-permute-start(bf16[128,512]{1,0:T(8,128)(2,1)S(1)} %constant_dynamic-update-slice_fusion.refs_8_), channel_id=1, source_target_pairs={{0,2},{1,3},{2,4},{3,5},{4,6},{5,7},{6,8},{7,9},{8,10},{9,11},{10,... | collective-permute-start | bytes 393224 | tf_op jit(solution)/shard_map/ppermute | solution.py:125
  39.0 46.4 %copy-start.7 = (bf16[256,1024]{1,0:T(8,128)(2,1)}, bf16[256,1024]{1,0:T(8,128)(2,1)S(1)}, u32[]{:S(2)}) copy-start(bf16[256,1024]{1,0:T(8,128)(2,1)S(1)} %collective-permute-done.1.refs_2_) | copy-start | bytes 1572868
  39.1 6.4 %collective-permute-start.9 = (bf16[128,512]{1,0:T(8,128)(2,1)S(1)}, bf16[128,512]{1,0:T(8,128)(2,1)}, u32[]{:S(2)}, u32[]{:S(2)}) collective-permute-start(bf16[128,512]{1,0:T(8,128)(2,1)S(1)} %constant_dynamic-update-slice_fusion.refs_8_), channel_id=1, source_target_pairs={{0,1},{1,2},{2,3},{3,4},{4,5},{5,6},{6,7},{7,8},{8,9},{9,10},{10,1... | collective-permute-start | bytes 393224 | tf_op jit(solution)/shard_map/ppermute | solution.py:125
  45.5 0.8 copy-start.15
  46.3 0.8 copy-start.19
  50.0 1.1 copy-start.3
  52.2 0.6 copy-start.17
  52.8 26.2 %all-to-all-start = ((bf16[16,128,256]{2,1,0:T(8,128)(2,1)}), bf16[16,128,256]{2,1,0:T(8,128)(2,1)}, u32[]{:S(2)}, u32[]{:S(2)}) async-start(bf16[16,128,256]{2,1,0:T(8,128)(2,1)} %broadcast_in_dim.18), calls=%async_computation | async-start | bytes 2097152 | tf_op jit(solution)/shard_map/all_to_all | solution.py:163
  62.9 88.6 %reduce-scatter.2.cloned.1.call-start = ((), (), s32[]{:S(2)}) async-start(), calls=%async_computation.4 | async-start | bytes 4718592 | tf_op jit(solution)/shard_map/reduce_scatter | solution.py:179
  63.0 15.3 %collective-permute-start.10 = (bf16[256,1024]{1,0:T(8,128)(2,1)S(1)}, bf16[256,1024]{1,0:T(8,128)(2,1)S(1)}, u32[]{:S(2)}, u32[]{:S(2)}) collective-permute-start(bf16[256,1024]{1,0:T(8,128)(2,1)S(1)} %collective-permute-done.refs_1_), channel_id=1, source_target_pairs={{0,32},{32,64},{64,96},{96,128},{128,160},{160,192},{192,224},{224... | collective-permute-start | bytes 1572872 | tf_op jit(solution)/shard_map/ppermute | solution.py:128
  63.1 16.0 %collective-permute-start.11 = (bf16[256,1024]{1,0:T(8,128)(2,1)S(1)}, bf16[256,1024]{1,0:T(8,128)(2,1)}, u32[]{:S(2)}, u32[]{:S(2)}) collective-permute-start(bf16[256,1024]{1,0:T(8,128)(2,1)S(1)} %collective-permute-done.1.refs_2_), channel_id=1, source_target_pairs={{0,224},{32,0},{64,32},{96,64},{128,96},{160,128},{192,160},{224,1... | collective-permute-start | bytes 1572872 | tf_op jit(solution)/shard_map/ppermute | solution.py:128
  78.2 0.8 copy-start.9
  79.0 6.4 %copy-start.2 = (bf16[256,1024]{1,0:T(8,128)(2,1)S(1)}, bf16[256,1024]{1,0:T(8,128)(2,1)}, u32[]{:S(2)}) copy-start(bf16[256,1024]{1,0:T(8,128)(2,1)} %refs_0_.1) | copy-start | bytes 1572868
  90.1 159.4 %all-gather.5.cloned.1.call-start = ((), (), s32[]{:S(2)}) async-start(), calls=%async_computation.5 | async-start | bytes 4718592 | tf_op jit(solution)/shard_map/all_gather | solution.py:211
  90.1 14.7 %collective-permute-start.13 = (bf16[256,1024]{1,0:T(8,128)(2,1)}, bf16[256,1024]{1,0:T(8,128)(2,1)S(1)}, u32[]{:S(2)}, u32[]{:S(2)}) collective-permute-start(bf16[256,1024]{1,0:T(8,128)(2,1)} %copy-done.9), channel_id=1, source_target_pairs={{0,32},{32,64},{64,96},{96,128},{128,160},{160,192},{192,224},{224... | collective-permute-start | bytes 1572872 | tf_op jit(solution)/shard_map/ppermute | solution.py:128
  90.2 18.3 %collective-permute-start.15 = (bf16[256,1024]{1,0:T(8,128)(2,1)}, bf16[256,1024]{1,0:T(8,128)(2,1)}, u32[]{:S(2)}, u32[]{:S(2)}) collective-permute-start(bf16[256,1024]{1,0:T(8,128)(2,1)} %collective-permute-done.11.refs_4_), channel_id=1, source_target_pairs={{0,224},{32,0},{64,32},{96,64},{128,96},{160,128},{192,160},{224,1... | collective-permute-start | bytes 1572872 | tf_op jit(solution)/shard_map/ppermute | solution.py:128
  93.4 20.0 %collective-permute-start.12 = (bf16[128,1024]{1,0:T(8,128)(2,1)}, bf16[128,1024]{1,0:T(8,128)(2,1)}, u32[]{:S(2)}, u32[]{:S(2)}) collective-permute-start(bf16[128,1024]{1,0:T(8,128)(2,1)} %param.10), channel_id=1, source_target_pairs={{0,16},{16,0},{1,17},{17,1},{2,18},{18,2},{3,19},{19,3},{4,20},{20... | collective-permute-start | bytes 786440 | tf_op jit(solution)/shard_map/ppermute | solution.py:131
  104.8 15.1 %collective-permute-start.14 = (bf16[128,1024]{1,0:T(8,128)(2,1)S(1)}, bf16[128,1024]{1,0:T(8,128)(2,1)S(1)}, u32[]{:S(2)}, u32[]{:S(2)}) collective-permute-start(bf16[128,1024]{1,0:T(8,128)(2,1)S(1)} %slice.16), channel_id=1, source_target_pairs={{0,32},{32,64},{64,96},{96,128},{128,160},{160,192},{192,224},{224... | collective-permute-start | bytes 786440 | tf_op jit(solution)/shard_map/ppermute | solution.py:128
  109.5 14.1 %collective-permute-start.16 = (bf16[128,1024]{1,0:T(8,128)(2,1)S(1)}, bf16[128,1024]{1,0:T(8,128)(2,1)S(1)}, u32[]{:S(2)}, u32[]{:S(2)}) collective-permute-start(bf16[128,1024]{1,0:T(8,128)(2,1)S(1)} %slice.17), channel_id=1, source_target_pairs={{0,224},{32,0},{64,32},{96,64},{128,96},{160,128},{192,160},{224,1... | collective-permute-start | bytes 786440 | tf_op jit(solution)/shard_map/ppermute | solution.py:128
  119.9 0.7 copy-start.11
  123.6 0.7 copy-start.13
  151.6 15.4 %collective-permute-start.17 = (bf16[256,1024]{1,0:T(8,128)(2,1)}, bf16[256,1024]{1,0:T(8,128)(2,1)S(1)}, u32[]{:S(2)}, u32[]{:S(2)}) collective-permute-start(bf16[256,1024]{1,0:T(8,128)(2,1)} %reduce-scatter.2.cloned.1.call-done), channel_id=1, source_target_pairs={{0,16},{16,0},{1,17},{17,1},{2,18},{18,2},{3,19},{19,3},{4,20},{20... | collective-permute-start | bytes 1572872 | tf_op jit(solution)/shard_map/ppermute | solution.py:131
  169.3 1.0 copy-start.1
  170.3 1.0 copy-start.6
  171.4 1.0 copy-start.8
  172.4 1.0 copy-start.10
  173.5 0.9 copy-start.12
  174.4 0.9 copy-start.14
  197.5 13.1 %collective-permute-start.18 = (bf16[128,256]{1,0:T(8,128)(2,1)}, bf16[128,256]{1,0:T(8,128)(2,1)S(1)}, u32[]{:S(2)}, u32[]{:S(2)}) collective-permute-start(bf16[128,256]{1,0:T(8,128)(2,1)} %reduce_sum.12), channel_id=1, source_target_pairs={{0,0},{1,1},{2,32},{3,33},{4,64},{5,65},{6,96},{7,97},{8,128},{9,1... | collective-permute-start | bytes 196616 | tf_op jit(solution)/shard_map/ppermute | solution.py:209
  210.6 1.3 copy-start.4
  211.9 0.8 copy-start.16
  212.7 0.8 copy-start.18
  217.2 11.7 %collective-permute-start.19 = (bf16[128,512]{1,0:T(8,128)(2,1)S(1)}, bf16[128,512]{1,0:T(8,128)(2,1)S(1)}, u32[]{:S(2)}, u32[]{:S(2)}) collective-permute-start(bf16[128,512]{1,0:T(8,128)(2,1)S(1)} %get-tuple-element.40), channel_id=1, source_target_pairs={{1,0},{2,1},{3,2},{4,3},{5,4},{6,5},{7,6},{8,7},{9,8},{10,9},{11,1... | collective-permute-start | bytes 393224 | tf_op jit(solution)/shard_map/ppermute | solution.py:125
  219.1 11.7 %collective-permute-start.20 = (bf16[128,512]{1,0:T(8,128)(2,1)S(1)}, bf16[128,512]{1,0:T(8,128)(2,1)S(1)}, u32[]{:S(2)}, u32[]{:S(2)}) collective-permute-start(bf16[128,512]{1,0:T(8,128)(2,1)S(1)} %get-tuple-element.41), channel_id=1, source_target_pairs={{2,0},{3,1},{4,2},{5,3},{6,4},{7,5},{8,6},{9,7},{10,8},{11,9},{12,... | collective-permute-start | bytes 393224 | tf_op jit(solution)/shard_map/ppermute | solution.py:125
  223.1 9.0 %collective-permute-start.21 = (bf16[128,512]{1,0:T(8,128)(2,1)S(1)}, bf16[128,512]{1,0:T(8,128)(2,1)S(1)}, u32[]{:S(2)}, u32[]{:S(2)}) collective-permute-start(bf16[128,512]{1,0:T(8,128)(2,1)S(1)} %get-tuple-element.42), channel_id=1, source_target_pairs={{3,0},{4,1},{5,2},{6,3},{7,4},{8,5},{9,6},{10,7},{11,8},{12,9},{13... | collective-permute-start | bytes 393224 | tf_op jit(solution)/shard_map/ppermute | solution.py:125
  225.0 10.7 %collective-permute-start.22 = (bf16[128,512]{1,0:T(8,128)(2,1)S(1)}, bf16[128,512]{1,0:T(8,128)(2,1)S(1)}, u32[]{:S(2)}, u32[]{:S(2)}) collective-permute-start(bf16[128,512]{1,0:T(8,128)(2,1)S(1)} %get-tuple-element.43), channel_id=1, source_target_pairs={{4,0},{5,1},{6,2},{7,3},{8,4},{9,5},{10,6},{11,7},{12,8},{13,9},{1... | collective-permute-start | bytes 393224 | tf_op jit(solution)/shard_map/ppermute | solution.py:125
  226.9 14.6 %collective-permute-start.23 = (bf16[128,512]{1,0:T(8,128)(2,1)S(1)}, bf16[128,512]{1,0:T(8,128)(2,1)S(1)}, u32[]{:S(2)}, u32[]{:S(2)}) collective-permute-start(bf16[128,512]{1,0:T(8,128)(2,1)S(1)} %get-tuple-element.44), channel_id=1, source_target_pairs={{5,0},{6,1},{7,2},{8,3},{9,4},{10,5},{11,6},{12,7},{13,8},{14,9},{... | collective-permute-start | bytes 393224 | tf_op jit(solution)/shard_map/ppermute | solution.py:125
  228.9 12.6 %collective-permute-start.24 = (bf16[128,512]{1,0:T(8,128)(2,1)S(1)}, bf16[128,512]{1,0:T(8,128)(2,1)S(1)}, u32[]{:S(2)}, u32[]{:S(2)}) collective-permute-start(bf16[128,512]{1,0:T(8,128)(2,1)S(1)} %get-tuple-element.45), channel_id=1, source_target_pairs={{6,0},{7,1},{8,2},{9,3},{10,4},{11,5},{12,6},{13,7},{14,8},{15,9},... | collective-permute-start | bytes 393224 | tf_op jit(solution)/shard_map/ppermute | solution.py:125
  230.8 10.7 %collective-permute-start.25 = (bf16[128,512]{1,0:T(8,128)(2,1)S(1)}, bf16[128,512]{1,0:T(8,128)(2,1)S(1)}, u32[]{:S(2)}, u32[]{:S(2)}) collective-permute-start(bf16[128,512]{1,0:T(8,128)(2,1)S(1)} %get-tuple-element.46), channel_id=1, source_target_pairs={{7,0},{8,1},{9,2},{10,3},{11,4},{12,5},{13,6},{14,7},{15,8},{23,16... | collective-permute-start | bytes 393224 | tf_op jit(solution)/shard_map/ppermute | solution.py:125
  232.1 16.5 %collective-permute-start.26 = (bf16[128,512]{1,0:T(8,128)(2,1)S(1)}, bf16[128,512]{1,0:T(8,128)(2,1)S(1)}, u32[]{:S(2)}, u32[]{:S(2)}) collective-permute-start(bf16[128,512]{1,0:T(8,128)(2,1)S(1)} %get-tuple-element.47), channel_id=1, source_target_pairs={{8,0},{9,1},{10,2},{11,3},{12,4},{13,5},{14,6},{15,7},{24,16},{25,... | collective-permute-start | bytes 393224 | tf_op jit(solution)/shard_map/ppermute | solution.py:125
Sparse Core Ops, SparseCore 0:
  9.9 56.4 all-gather.2
  90.2 61.3 reduce-scatter.1
  169.4 54.9 all-gather.4

commit v3 on v2

v3 whole, which is shorter than its diff:
```python
import functools

import jax
import jax.numpy as jnp
from jax import lax
from jax.experimental import pallas as pl
from jax.experimental.pallas import tpu as pltpu
from jax.sharding import Mesh
from jax.sharding import PartitionSpec as P

HEAD_DIM = 128
SEGMENT_MAX = 1024
LSE_TERMS = 3
COPIES = 16
TP = ("z", "xh")
SP = ("y", "xl", "core")
F32 = jnp.float32
BF16 = jnp.bfloat16
NT = (((1,), (1,)), ((), ()))
TN = (((0,), (0,)), ((), ()))


def dot(a, b, dims=(((1,), (0,)), ((), ()))):
    return lax.dot_general(a, b, dims, preferred_element_type=F32)


def fetch(sources, targets, sems):
    copies = [
        pltpu.make_async_copy(src, dst, sems.at[i])
        for i, (src, dst) in enumerate(zip(sources, targets, strict=True))
    ]
    for copy in copies:
        copy.start()
    for copy in copies:
        copy.wait()


def window_parts(core_ref, chips, whole_ref, rows):
    mine, other = [], []
    for i in chips:
        mine.append(whole_ref.at[pl.ds(pl.multiple_of((2 * i + core_ref[0]) * rows, rows), rows)])
        other.append(
            whole_ref.at[pl.ds(pl.multiple_of((2 * i + 1 - core_ref[0]) * rows, rows), rows)]
        )
    return mine + other


def split_parts(n, refs, rows):
    return [*refs[:n], *(refs[n].at[pl.ds(i * rows, rows)] for i in range(n))]


def forward_kernel(n, core_ref, qseg_ref, kseg_ref, q_hbm, *refs):
    kv_hbm, (attn_ref, probs_ref, qx_ref, q_ref, kv_ref, sems) = refs[: n + 1], refs[n + 1 :]
    rows, width = q_ref.shape
    keys = 2 * rows * n
    chips = range(n - 1, -1, -1)
    fetch(
        (q_hbm, *split_parts(n, kv_hbm, rows)),
        (q_ref, *window_parts(core_ref, chips, kv_ref, rows)),
        sems,
    )
    scale = HEAD_DIM ** (-0.5)
    first = keys - 2 * rows + core_ref[0] * rows
    place = lax.broadcasted_iota(jnp.int32, (rows, keys), 0) + first
    allowed = (place >= lax.broadcasted_iota(jnp.int32, (rows, keys), 1)) & (
        qseg_ref[...] == kseg_ref[...]
    )
    lane = lax.broadcasted_iota(jnp.int32, (rows, HEAD_DIM), 1)
    terms = jnp.zeros((rows, HEAD_DIM), F32)
    for h in range(width // HEAD_DIM):
        cols = slice(h * HEAD_DIM, (h + 1) * HEAD_DIM)
        vcols = slice(width + h * HEAD_DIM, width + (h + 1) * HEAD_DIM)
        scores = jnp.where(allowed, dot(q_ref[:, cols], kv_ref[:, cols], NT) * scale, -1e30)
        top = jnp.max(scores, axis=-1, keepdims=True)
        expo = jnp.exp(scores - top)
        total = jnp.sum(expo, axis=-1, keepdims=True)
        probs = expo / total
        probs_ref[h] = probs
        attn_ref[:, cols] = dot(probs.astype(BF16), kv_ref[:, vcols]).astype(BF16)
        rest = top + jnp.log(total)
        for t in range(LSE_TERMS):
            term = rest.astype(BF16).astype(F32)
            rest = rest - term
            terms = jnp.where(lane == h * LSE_TERMS + t, term, terms)
    qx_ref[:, :width] = q_ref[...]
    qx_ref[:, width:] = terms.astype(BF16)


def query_grad_kernel(n, core_ref, dattn_hbm, attn_hbm, probs_hbm, *refs):
    kv_hbm, (dq_ref, dattn_ref, attn_ref, probs_ref, kv_ref, sems) = refs[: n + 1], refs[n + 1 :]
    rows, width = attn_ref.shape
    fetch(
        (dattn_hbm, attn_hbm, probs_hbm, *split_parts(n, kv_hbm, rows)),
        (
            dattn_ref,
            attn_ref,
            probs_ref,
            *window_parts(core_ref, range(n - 1, -1, -1), kv_ref, rows),
        ),
        sems,
    )
    scale = HEAD_DIM ** (-0.5)
    for h in range(width // HEAD_DIM):
        cols = slice(h * HEAD_DIM, (h + 1) * HEAD_DIM)
        vcols = slice(width + h * HEAD_DIM, width + (h + 1) * HEAD_DIM)
        dattn = dattn_ref[:, cols]
        delta = jnp.sum(
            dattn.astype(F32) * attn_ref[:, cols].astype(F32), axis=-1, keepdims=True
        )
        dprobs = dot(dattn, kv_ref[:, vcols], NT)
        dscores = (probs_ref[h] * (dprobs - delta) * scale).astype(BF16)
        dq_ref[:, cols] = dot(dscores, kv_ref[:, cols]).astype(BF16)


def key_grad_kernel(n, core_ref, qseg_ref, kseg_ref, kv_hbm, qx_hbm, attn_hbm, *refs):
    dattn_hbm, refs = refs[: n + 1], refs[n + 1 :]
    dkey_ref, dvalue_ref, kv_ref, qx_ref, attn_ref, dattn_ref, sems = refs
    rows, width = dkey_ref.shape
    queries = 2 * rows * n
    fetch(
        (kv_hbm, qx_hbm, attn_hbm, *split_parts(n, dattn_hbm, rows)),
        (kv_ref, qx_ref, attn_ref, *window_parts(core_ref, range(n), dattn_ref, rows)),
        sems,
    )
    scale = HEAD_DIM ** (-0.5)
    place = lax.broadcasted_iota(jnp.int32, (queries, rows), 1) + core_ref[0] * rows
    allowed = (lax.broadcasted_iota(jnp.int32, (queries, rows), 0) >= place) & (
        qseg_ref[...] == kseg_ref[...]
    )
    for h in range(width // HEAD_DIM):
        cols = slice(h * HEAD_DIM, (h + 1) * HEAD_DIM)
        vcols = slice(width + h * HEAD_DIM, width + (h + 1) * HEAD_DIM)
        terms = qx_ref[:, width : width + HEAD_DIM].astype(F32)
        lse = terms[:, h * LSE_TERMS : h * LSE_TERMS + 1]
        for t in range(1, LSE_TERMS):
            lse = lse + terms[:, h * LSE_TERMS + t : h * LSE_TERMS + t + 1]
        query, dattn = qx_ref[:, cols], dattn_ref[:, cols]
        scores = dot(query, kv_ref[:, cols], NT) * scale
        probs = jnp.exp(jnp.where(allowed, scores - lse, -1e30))
        delta = jnp.sum(
            dattn.astype(F32) * attn_ref[:, cols].astype(F32), axis=-1, keepdims=True
        )
        dprobs = dot(dattn, kv_ref[:, vcols], NT)
        dscores = (probs * (dprobs - delta) * scale).astype(BF16)
        dkey_ref[:, cols] = dot(dscores, query, TN).astype(BF16)
        dvalue_ref[:, cols] = dot(probs.astype(BF16), dattn, TN).astype(BF16)


def dattn_kernel(n, offsets, z_ref, dpred_hbm, *refs):
    proj_hbm, (out_ref, dpred_ref, *proj_refs, sems) = refs[: len(offsets)], refs[len(offsets) :]
    fetch((dpred_hbm, *proj_hbm), (dpred_ref, *proj_refs), sems)
    first = [0] * n
    for ref, by in zip(proj_refs, offsets, strict=True):
        size = ref.shape[0]
        z = lax.rem(z_ref[0] + by, n)
        out = dot(dpred_ref[...], ref[...], NT).astype(BF16)
        out_ref[z, :, first[by] : first[by] + size] = out
        first[by] += size


def call(kernel, out_shape, in_smem, in_vmem, in_hbm, scratch):
    space = pl.BlockSpec
    return pl.pallas_call(
        kernel,
        out_shape=out_shape,
        in_specs=[space(memory_space=pltpu.SMEM)] * len(in_smem)
        + [space(memory_space=pltpu.VMEM)] * len(in_vmem)
        + [space(memory_space=pltpu.HBM)] * len(in_hbm),
        scratch_shapes=[pltpu.VMEM(s.shape, s.dtype) for s in scratch]
        + [pltpu.SemaphoreType.DMA((COPIES,))],
        compiler_params=pltpu.CompilerParams(vmem_limit_bytes=40 * 1024 * 1024),
    )(*in_smem, *in_vmem, *in_hbm)


def body(context, w_out, teacher_resid, queries, keys, values, segment_ids, proj):
    rows, width = queries.shape
    heads = width // HEAD_DIM
    n_sp, n_z, n_xh = lax.axis_size(SP), lax.axis_size("z"), lax.axis_size("xh")
    n_core = lax.axis_size("core")
    n_chip = n_sp // n_core
    near = min(-(-(SEGMENT_MAX - 1) // (n_core * rows)), n_chip - 1) + 1
    window = near * n_core * rows
    sp, core = lax.axis_index(SP), lax.axis_index("core")
    first_row, chip_row = sp * rows, (sp - core) * rows
    z, xh = lax.axis_index("z"), lax.axis_index("xh")
    core_scalar = core[None]

    def shift(array, by):
        by = by * n_core
        pairs = [(i, i + by) for i in range(n_sp) if 0 <= i + by < n_sp]
        return lax.ppermute(array, SP, pairs)

    def other_core(arrays):
        stacked = jnp.concatenate(arrays, axis=0)
        return lax.ppermute(stacked, "core", [(i, i ^ 1) for i in range(n_core)])

    def everywhere(array):
        copies = jnp.broadcast_to(array[None], (n_sp, *array.shape))
        return lax.all_to_all(copies, SP, 0, 0, tiled=True).reshape(-1, array.shape[1])

    def turn(array, by):
        return lax.ppermute(array, "z", [(i, (i + by) % n_z) for i in range(n_z)])

    def swap(array):
        return lax.ppermute(array, "xh", [(i, i ^ 1) for i in range(n_xh)])

    context_all = lax.all_gather(context, SP, axis=0, tiled=True)

    half = width // 2
    pieces, offsets = [proj], [0]

    def step(up, down):
        k = len(pieces) // 2 + 1
        if k == n_z // 2:
            up, down = up[:half], down[half:]
        offsets.extend([n_z - k, k])
        return turn(up, 1), turn(down, -1)

    key_value = jnp.concatenate([keys, values], axis=1)
    shifted = [shift(key_value, k) for k in range(1, near)]
    up, down = step(proj, proj)
    key_value, up, down = lax.optimization_barrier((key_value, up, down))
    pieces += [up, down]
    kv_parts = (key_value, *shifted, other_core([key_value, *shifted]))

    nobody = jnp.full((window - n_core * rows,), -1, jnp.int32)
    key_segments = lax.dynamic_slice_in_dim(
        jnp.concatenate([nobody, segment_ids]), chip_row, window, 0
    )
    query_segments = lax.dynamic_slice_in_dim(
        jnp.concatenate([segment_ids, nobody]), chip_row, window, 0
    )
    own_segments = lax.dynamic_slice_in_dim(segment_ids, first_row, rows, 0)
    block_type = jax.ShapeDtypeStruct((rows, width), BF16)
    window_type = jax.ShapeDtypeStruct((window, width), BF16)
    window_kv_type = jax.ShapeDtypeStruct((window, 2 * width), BF16)
    window_qx_type = jax.ShapeDtypeStruct((window, width + HEAD_DIM), BF16)
    probs_type = jax.ShapeDtypeStruct((heads, rows, window), F32)
    attn, probs, qx = call(
        functools.partial(forward_kernel, near),
        (block_type, probs_type, jax.ShapeDtypeStruct((rows, width + HEAD_DIM), BF16)),
        (core_scalar,),
        (own_segments[:, None], key_segments[None, :]),
        (queries, *kv_parts),
        (block_type, window_kv_type),
    )
    attn_all = everywhere(attn)
    up, down = step(up, down)
    attn_all, qx, up, down = lax.optimization_barrier((attn_all, qx, up, down))
    pieces += [up, down]

    def after(array):
        array = jnp.pad(array, ((0, window - n_core * rows), (0, 0)))
        return lax.dynamic_slice_in_dim(array, chip_row, window, 0)

    qx_after, attn_after = after(everywhere(qx)), after(attn_all)

    resid_other = swap(teacher_resid)
    resid = jnp.concatenate(
        [
            jnp.where(xh == 0, teacher_resid, resid_other),
            jnp.where(xh == 0, resid_other, teacher_resid),
        ],
        axis=0,
    )
    part = (dot(attn_all, proj) - dot(context_all, w_out)).astype(BF16)
    part = lax.psum_scatter(part, "z", scatter_dimension=0, tiled=True)
    while len(pieces) < n_z:
        up, down = step(up, down)
        pieces += [up, down]
    part, resid, up, down, qx_after, attn_after = lax.optimization_barrier(
        (part, resid, up, down, qx_after, attn_after)
    )
    pieces[-2:] = [up, down]
    diff = (part.astype(F32) + swap(part).astype(F32)) - resid.astype(F32)
    dpred = diff.astype(BF16)

    dattn_part = call(
        functools.partial(dattn_kernel, n_z, offsets),
        jax.ShapeDtypeStruct((n_z, n_xh * rows, width), BF16),
        (z[None],),
        (),
        (dpred, *pieces),
        (dpred, *pieces),
    )
    dattn_parts = lax.all_to_all(dattn_part.reshape(n_sp, rows, width), SP, 0, 0, tiled=True)
    dattn = jnp.sum(dattn_parts.astype(F32), axis=0).astype(BF16)
    pairs = []
    for a in range(n_z):
        for x in range(n_xh):
            for b in range(n_z):
                for e in range(n_xh):
                    pairs.append(
                        (
                            (a * n_xh + x) * n_sp + b * n_xh + e,
                            (b * n_xh + x) * n_sp + a * n_xh + e,
                        )
                    )
    dattn = lax.ppermute(dattn, TP + SP, pairs)

    dpred_all = lax.all_gather(dpred, "z", axis=0, tiled=True)
    proj_grad = dot(attn_all, dpred_all, TN).astype(BF16)

    shifted = [shift(dattn, -k) for k in range(1, near)]
    query_grad = call(
        functools.partial(query_grad_kernel, near),
        block_type,
        (core_scalar,),
        (),
        (dattn, attn, probs, *kv_parts),
        (block_type, block_type, probs_type, window_kv_type),
    )
    key_grad, value_grad = call(
        functools.partial(key_grad_kernel, near),
        (block_type, block_type),
        (core_scalar,),
        (query_segments[:, None], own_segments[None, :]),
        (key_value, qx_after, attn_after, dattn, *shifted, other_core([dattn, *shifted])),
        (
            jax.ShapeDtypeStruct((rows, 2 * width), BF16),
            window_qx_type,
            window_type,
            window_type,
        ),
    )
    return proj_grad, query_grad, key_grad, value_grad


def solution(mesh):
    fine = Mesh(mesh.devices.reshape(8, 2, 4, 2, 2), TP + SP)
    in_specs = (
        P(SP, TP),
        P(TP, SP),
        P(TP, SP),
        P(SP, TP),
        P(SP, TP),
        P(SP, TP),
        P(),
        P(TP, SP),
    )
    out_specs = (P(TP, SP), P(SP, TP), P(SP, TP), P(SP, TP))
    return jax.shard_map(body, mesh=fine, in_specs=in_specs, out_specs=out_specs, check_vma=False)
```

time: 262 us -> 255 us (0.973)
  the two profiles are of different devices: /device:TPU:10 before, /device:TPU:4 now
where the time goes in v3:
time: 255 us; the launch traced here: 250 us
  waiting for transfers between devices  95.8 us (38%)
  starting transfers between devices  52.2 us (20%)
  local copies, waits for them, and re-layouts  30.1 us (12%)
  blocking collectives  22.9 us (9%)
  matrix products  15.4 us (6%)
  between operations  14.1 us (6%)
  Pallas kernels  13.9 us (5%)
  other arithmetic  6.09 us (2%)
    ppermute x2, waiting for transfers between devices, swap(): return lax.ppermute(array, 'xh', [(i, i ^ 1) for i in range(n_xh)])  34.4 us
    ppermute x8, waiting for transfers between devices, turn(): return lax.ppermute(array, 'z', [(i, (i + by) % n_z) for i in range(n_z)])  23.3 us
    all_to_all x1, blocking collectives, body(): lax.all_to_all(dattn_part.reshape(n_sp, rows, width), SP, 0, 0, tiled=True)  22.9 us
    ppermute x8, waiting for transfers between devices, shift(): return lax.ppermute(array, SP, pairs)  22 us
    ppermute x8, starting transfers between devices, shift(): return lax.ppermute(array, SP, pairs)  20.6 us
    unnamed x61, local copies, waits for them, and re-layouts  18.5 us
    ppermute x8, starting transfers between devices, turn(): return lax.ppermute(array, 'z', [(i, (i + by) % n_z) for i in range(n_z)])  15.8 us
    dot_general x3, matrix products, dot(): return lax.dot_general(a, b, dims, preferred_element_type=F32)  15.4 us
  transfers between devices with their start and end apart: 26, of which 12 were waited for; matrix products, arithmetic and copies ran while one was open for 8% of the time, Pallas kernels for 6%

profile of v3, /device:TPU:4, one launch (start us, length us, event | category | flops | bytes accessed | tf_op | source)
XLA Modules:
  0.0 250.4 jit_solution(13368674882895227026)
XLA Ops:
  7.9 2.0 collective-permute-start
  9.9 4.0 %collective-permute-start.1 = (bf16[256,1024]{1,0:T(8,128)(2,1)}, bf16[256,1024]{1,0:T(8,128)(2,1)S(1)}, u32[]{:S(2)}, u32[]{:S(2)}) collective-permute-start(bf16[256,1024]{1,0:T(8,128)(2,1)} %refs_0_.1), channel_id=1, source_target_pairs={{0,224},{32,0},{64,32},{96,64},{128,96},{160,128},{192,160},{224,1... | collective-permute-start | bytes 1572872 | tf_op jit(solution)/shard_map/ppermute | solution.py:202
  13.9 0.8 constant_dynamic-update-slice_fusion.1
  14.8 0.8 constant_dynamic-update-slice_fusion.refs_0_.kv_hbm
  15.6 3.1 %collective-permute-start.2 = (bf16[128,512]{1,0:T(8,128)(2,1)S(1)}, bf16[128,512]{1,0:T(8,128)(2,1)S(1)}, u32[]{:S(2)}, u32[]{:S(2)}) collective-permute-start(bf16[128,512]{1,0:T(8,128)(2,1)S(1)} %constant_dynamic-update-slice_fusion.refs_0_.kv_hbm), channel_id=1, source_target_pairs={{0,2},{1,3},{2,4},{3,5},{4,6},{5,7},{6,8},{7,9},{8,10},{9,11},{10,... | collective-permute-start | bytes 393224 | tf_op jit(solution)/shard_map/ppermute | solution.py:191
  18.7 3.5 %collective-permute-start.3 = (bf16[128,512]{1,0:T(8,128)(2,1)S(1)}, bf16[128,512]{1,0:T(8,128)(2,1)S(1)}, u32[]{:S(2)}, u32[]{:S(2)}) collective-permute-start(bf16[128,512]{1,0:T(8,128)(2,1)S(1)} %constant_dynamic-update-slice_fusion.refs_0_.kv_hbm), channel_id=1, source_target_pairs={{0,4},{1,5},{2,6},{3,7},{4,8},{5,9},{6,10},{7,11},{8,12},{9,13},{1... | collective-permute-start | bytes 393224 | tf_op jit(solution)/shard_map/ppermute | solution.py:191
  22.2 4.5 %collective-permute-start.4 = (bf16[128,512]{1,0:T(8,128)(2,1)S(1)}, bf16[128,512]{1,0:T(8,128)(2,1)S(1)}, u32[]{:S(2)}, u32[]{:S(2)}) collective-permute-start(bf16[128,512]{1,0:T(8,128)(2,1)S(1)} %constant_dynamic-update-slice_fusion.refs_0_.kv_hbm), channel_id=1, source_target_pairs={{0,6},{1,7},{2,8},{3,9},{4,10},{5,11},{6,12},{7,13},{8,14},{9,15},... | collective-permute-start | bytes 393224 | tf_op jit(solution)/shard_map/ppermute | solution.py:191
  26.7 4.4 %collective-permute-start.5 = (bf16[128,512]{1,0:T(8,128)(2,1)S(1)}, bf16[128,512]{1,0:T(8,128)(2,1)S(1)}, u32[]{:S(2)}, u32[]{:S(2)}) collective-permute-start(bf16[128,512]{1,0:T(8,128)(2,1)S(1)} %constant_dynamic-update-slice_fusion.refs_0_.kv_hbm), channel_id=1, source_target_pairs={{0,8},{1,9},{2,10},{3,11},{4,12},{5,13},{6,14},{7,15},{16,24},{17,... | collective-permute-start | bytes 393224 | tf_op jit(solution)/shard_map/ppermute | solution.py:191
  33.9 3.7 %collective-permute-done.5.refs_4_ = bf16[128,512]{1,0:T(8,128)(2,1)S(1)} collective-permute-done((bf16[128,512]{1,0:T(8,128)(2,1)S(1)}, bf16[128,512]{1,0:T(8,128)(2,1)S(1)}, u32[]{:S(2)}, u32[]{:S(2)}) %collective-permute-start.5) | collective-permute-done | bytes 131104 | tf_op jit(solution)/shard_map/ppermute | solution.py:191
  38.2 1.4 pad_dynamic-slice_fusion.2
  40.6 0.9 copy-done.23
  41.5 3.2 %shard_map.111 = (bf16[128,256]{1,0:T(8,128)(2,1)S(1)}, f32[2,128,1280]{2,1,0:T(8,128)S(1)}, bf16[128,384]{1,0:T(8,128)(2,1)S(1)}) custom-call(s32[1]{0:T(128)} %bitcast.core_ref, s32[128,1]{1,0:T(8,128)S(1)} %copy.13.qseg_ref, s32[1,1280]{1,0:T(1,128)S(1)} %broadcast_in_dim.33.kseg_ref, bf16[128,256]{1,0:T(8,128)(2,1)S(1)} %copy-done.23, ...), custom_call_target="tpu_custom_call" | custom-call | tf_op jit(solution)/shard_map/pallas_call | solution.py:163
  44.7 1.2 copy-done.7
  46.5 1.1 broadcast_in_dim.34
  47.6 5.8 %all-to-all-start = ((bf16[16,128,256]{2,1,0:T(8,128)(2,1)}), bf16[16,128,256]{2,1,0:T(8,128)(2,1)}, u32[]{:S(2)}, u32[]{:S(2)}) async-start(bf16[16,128,256]{2,1,0:T(8,128)(2,1)} %broadcast_in_dim.34), calls=%async_computation | async-start | bytes 2097152 | tf_op jit(solution)/shard_map/all_to_all | solution.py:199
  53.5 3.2 %collective-permute-start.8 = (bf16[256,1024]{1,0:T(8,128)(2,1)}, bf16[256,1024]{1,0:T(8,128)(2,1)}, u32[]{:S(2)}, u32[]{:S(2)}) collective-permute-start(bf16[256,1024]{1,0:T(8,128)(2,1)} %copy-done.19), channel_id=1, source_target_pairs={{0,224},{32,0},{64,32},{96,64},{128,96},{160,128},{192,160},{224,1... | collective-permute-start | bytes 1572872 | tf_op jit(solution)/shard_map/ppermute | solution.py:202
  56.8 12.5 %collective-permute-done.7.refs_3_ = bf16[256,1024]{1,0:T(8,128)(2,1)} collective-permute-done((bf16[256,1024]{1,0:T(8,128)(2,1)}, bf16[256,1024]{1,0:T(8,128)(2,1)}, u32[]{:S(2)}, u32[]{:S(2)}) %collective-permute-start.7) | collective-permute-done | bytes 524320 | tf_op jit(solution)/shard_map/ppermute | solution.py:202
  69.2 0.8 all-to-all-done
  70.1 6.3 %fusion = f32[2048,1024]{1,0:T(8,128)S(1)} fusion(bf16[2048,1024]{1,0:T(8,128)(2,1)} %all-gather.3.cloned.1.call-done, bf16[1024,1024]{1,0:T(8,128)(2,1)S(1)} %copy-done), kind=kOutput, calls=%fused_computation.24 | convolution fusion | flops 4294967296 | bytes 14680064 | tf_op jit(solution)/shard_map/dot_general | solution.py:24
  76.4 4.5 %subtract_convert_fusion = bf16[2048,1024]{1,0:T(8,128)(2,1)} fusion(f32[2048,1024]{1,0:T(8,128)S(1)} %fusion, bf16[2048,256]{1,0:T(8,128)(2,1)} %bitcast.2, bf16[256,1024]{1,0:T(8,128)(2,1)S(1)} %copy-done.5), kind=kOutput, calls=%fused_computation | convolution fusion | flops 1077936128 | bytes 14155776 | tf_op jit(solution)/shard_map/dot_general | solution.py:24
  81.0 0.9 copy-done.22
  81.9 1.3 broadcast_in_dim.35
  83.2 4.7 %all-to-all-start.1 = ((bf16[16,128,384]{2,1,0:T(8,128)(2,1)}), bf16[16,128,384]{2,1,0:T(8,128)(2,1)}, u32[]{:S(2)}, u32[]{:S(2)}) async-start(bf16[16,128,384]{2,1,0:T(8,128)(2,1)} %broadcast_in_dim.35), calls=%async_computation.2 | async-start | bytes 3145728 | tf_op jit(solution)/shard_map/all_to_all | solution.py:199
  88.0 0.9 collective-permute-start.9
  88.9 3.2 %collective-permute-start.12 = (bf16[256,1024]{1,0:T(8,128)(2,1)}, bf16[256,1024]{1,0:T(8,128)(2,1)S(1)}, u32[]{:S(2)}, u32[]{:S(2)}) collective-permute-start(bf16[256,1024]{1,0:T(8,128)(2,1)} %collective-permute-done.8.refs_4_), channel_id=1, source_target_pairs={{0,224},{32,0},{64,32},{96,64},{128,96},{160,128},{192,160},{224,1... | collective-permute-start | bytes 1572872 | tf_op jit(solution)/shard_map/ppermute | solution.py:202
  92.1 21.9 %collective-permute-done.9 = bf16[128,1024]{1,0:T(8,128)(2,1)} collective-permute-done((bf16[128,1024]{1,0:T(8,128)(2,1)S(1)}, bf16[128,1024]{1,0:T(8,128)(2,1)}, u32[]{:S(2)}, u32[]{:S(2)}) %collective-permute-start.9) | collective-permute-done | bytes 262176 | tf_op jit(solution)/shard_map/ppermute | solution.py:205
  114.0 1.0 broadcast_select_fusion.1
  115.0 0.8 pad_maximum_fusion
  115.8 2.1 pad_dynamic-slice_fusion.1.attn_hbm
  117.9 0.8 slice.8
  119.4 0.8 copy-done.11
  120.2 3.2 %collective-permute-start.13 = (bf16[128,1024]{1,0:T(8,128)(2,1)}, bf16[128,1024]{1,0:T(8,128)(2,1)}, u32[]{:S(2)}, u32[]{:S(2)}) collective-permute-start(bf16[128,1024]{1,0:T(8,128)(2,1)} %slice.9), channel_id=1, source_target_pairs={{0,224},{32,0},{64,32},{96,64},{128,96},{160,128},{192,160},{224,1... | collective-permute-start | bytes 786440 | tf_op jit(solution)/shard_map/ppermute | solution.py:202
  123.4 1.5 pad_dynamic-slice_fusion.qx_hbm
  124.9 9.7 %collective-permute-done.11.refs_7_ = bf16[128,1024]{1,0:T(8,128)(2,1)} collective-permute-done((bf16[128,1024]{1,0:T(8,128)(2,1)}, bf16[128,1024]{1,0:T(8,128)(2,1)}, u32[]{:S(2)}, u32[]{:S(2)}) %collective-permute-start.11) | collective-permute-done | bytes 262176 | tf_op jit(solution)/shard_map/ppermute | solution.py:202
  134.6 1.1 collective-permute-done.13.refs_8_
  135.8 14.5 %reduce-scatter.2.cloned.1.call-done = bf16[256,1024]{1,0:T(8,128)(2,1)} async-done(((bf16[2048,1024]{1,0:T(8,128)(2,1)}), bf16[256,1024]{1,0:T(8,128)(2,1)}) %reduce-scatter.2.cloned.1.call-update) | async-done | bytes 524304 | tf_op jit(solution)/shard_map/reduce_scatter | solution.py:267
  150.2 2.7 %collective-permute-start.14 = (bf16[256,1024]{1,0:T(8,128)(2,1)}, bf16[256,1024]{1,0:T(8,128)(2,1)S(1)}, u32[]{:S(2)}, u32[]{:S(2)}) collective-permute-start(bf16[256,1024]{1,0:T(8,128)(2,1)} %reduce-scatter.2.cloned.1.call-done), channel_id=1, source_target_pairs={{0,16},{16,0},{1,17},{17,1},{2,18},{18,2},{3,19},{19,3},{4,20},{20... | collective-permute-start | bytes 1572872 | tf_op jit(solution)/shard_map/ppermute | solution.py:205
  153.0 12.5 %collective-permute-done.14 = bf16[256,1024]{1,0:T(8,128)(2,1)S(1)} collective-permute-done((bf16[256,1024]{1,0:T(8,128)(2,1)}, bf16[256,1024]{1,0:T(8,128)(2,1)S(1)}, u32[]{:S(2)}, u32[]{:S(2)}) %collective-permute-start.14) | collective-permute-done | bytes 524320 | tf_op jit(solution)/shard_map/ppermute | solution.py:205
  165.5 2.3 subtract_convert_fusion.1.dpred_hbm
  167.8 1.0 copy-done.1
  168.8 1.0 copy-done.6
  169.9 1.0 copy-done.10
  170.9 1.0 copy-done.12
  172.0 1.0 copy-done.18
  173.0 1.0 copy-done.20
  174.0 3.1 %shard_map.112 = bf16[8,256,256]{2,1,0:T(8,128)(2,1)S(1)} custom-call(s32[1]{0:T(128)} %bitcast.4.z_ref, bf16[256,1024]{1,0:T(8,128)(2,1)S(1)} %copy-done.1, bf16[256,1024]{1,0:T(8,128)(2,1)S(1)} %copy-done.6, bf16[256,1024]{1,0:T(8,128)(2,1)S(1)} %copy-done.18, bf16[256,1024]{1,0:T(8,128)(2,1)S(1)} %copy-done.20, ...), custom_call_target="tpu_custom_call" | custom-call | tf_op jit(solution)/shard_map/pallas_call | solution.py:163
  177.1 22.9 %all_to_all.15 = bf16[16,128,256]{2,1,0:T(8,128)(2,1)} all-to-all(bf16[16,128,256]{2,1,0:T(8,128)(2,1)S(1)} %bitcast.15), channel_id=1, replica_groups=mesh['z'=8,'xh'=2,'y'=4,'xl'=2,'core'=2] {'y','xl','core'}, dimensions={0} | all-to-all | bytes 2097152 | tf_op jit(solution)/shard_map/all_to_all | solution.py:286
  200.0 2.0 reduce_sum.12
  202.0 1.6 collective-permute-start.15
  203.6 1.3 collective-permute-start.16
  204.9 1.3 collective-permute-start.17
  206.2 1.3 collective-permute-start.18
  207.5 1.3 collective-permute-start.19
  208.8 9.7 %collective-permute-done.16.refs_1_ = bf16[128,256]{1,0:T(8,128)(2,1)S(1)} collective-permute-done((bf16[128,256]{1,0:T(8,128)(2,1)S(1)}, bf16[128,256]{1,0:T(8,128)(2,1)S(1)}, u32[]{:S(2)}, u32[]{:S(2)}) %collective-permute-start.16) | collective-permute-done | bytes 65568 | tf_op jit(solution)/shard_map/ppermute | solution.py:191
  218.5 4.1 %collective-permute-done.17.refs_2_ = bf16[128,256]{1,0:T(8,128)(2,1)S(1)} collective-permute-done((bf16[128,256]{1,0:T(8,128)(2,1)S(1)}, bf16[128,256]{1,0:T(8,128)(2,1)S(1)}, u32[]{:S(2)}, u32[]{:S(2)}) %collective-permute-start.17) | collective-permute-done | bytes 65568 | tf_op jit(solution)/shard_map/ppermute | solution.py:191
  222.6 1.2 collective-permute-done.18.refs_3_
  223.8 3.4 %collective-permute-done.19.refs_4_ = bf16[128,256]{1,0:T(8,128)(2,1)S(1)} collective-permute-done((bf16[128,256]{1,0:T(8,128)(2,1)S(1)}, bf16[128,256]{1,0:T(8,128)(2,1)S(1)}, u32[]{:S(2)}, u32[]{:S(2)}) %collective-permute-start.19) | collective-permute-done | bytes 65568 | tf_op jit(solution)/shard_map/ppermute | solution.py:191
  227.5 1.1 copy-done.4
  228.5 1.3 copy-done.8
  229.9 0.9 copy-done.14
  230.8 0.9 copy-done.16
  231.7 3.3 %shard_map.113 = bf16[128,256]{1,0:T(8,128)(2,1)} custom-call(s32[1]{0:T(128)} %bitcast.core_ref, bf16[128,256]{1,0:T(8,128)(2,1)S(1)} %collective-permute-done.15.dattn_hbm.refs_0_, bf16[128,256]{1,0:T(8,128)(2,1)S(1)} %get-tuple-element.23.attn_hbm, f32[2,128,1280]{2,1,0:T(8,128)S(1)} %copy-done.8, ...), custom_call_target="tpu_custom_call" | custom-call | tf_op jit(solution)/shard_map/pallas_call | solution.py:163
  235.0 4.3 %shard_map.114 = (bf16[128,256]{1,0:T(8,128)(2,1)}, bf16[128,256]{1,0:T(8,128)(2,1)}) custom-call(s32[1]{0:T(128)} %bitcast.core_ref, s32[1280,1]{1,0:T(8,128)S(1)} %broadcast_in_dim.39.qseg_ref, s32[1,128]{1,0:T(1,128)S(1)} %get-tuple-element.42.kseg_ref, bf16[128,512]{1,0:T(8,128)(2,1)S(1)} %constant_dynamic-update-slice_fusion.refs_0_.kv_hbm, ...), custom_call_target="tpu_custom_call" | custom-call | tf_op jit(solution)/shard_map/pallas_call | solution.py:163
  239.3 4.6 %convolution_convert_fusion = bf16[256,1024]{1,0:T(8,128)(2,1)} fusion(bf16[2048,256]{1,0:T(8,128)(2,1)} %bitcast.2, bf16[2048,1024]{1,0:T(8,128)(2,1)} %all-gather.5.cloned.1.call-done), kind=kOutput, calls=%fused_computation.3 | convolution fusion | flops 1074003968 | bytes 5767168 | tf_op jit(solution)/shard_map/dot_general | solution.py:24
  (78 shorter events, 7.0 us)
Async XLA Ops:
  7.2 62.9 %copy-start = (bf16[1024,1024]{1,0:T(8,128)(2,1)S(1)}, bf16[1024,1024]{1,0:T(8,128)(2,1)}, u32[]{:S(2)}) copy-start(bf16[1024,1024]{1,0:T(8,128)(2,1)} %param.9) | copy-start | bytes 6291460
  7.2 62.9 %all-gather.3.cloned.1.call-start = ((), (), s32[]{:S(2)}) async-start(), calls=%async_computation.4 | async-start | bytes 4456448 | tf_op jit(solution)/shard_map/all_gather | solution.py:207
  7.9 18.8 %collective-permute-start = (bf16[256,1024]{1,0:T(8,128)(2,1)}, bf16[256,1024]{1,0:T(8,128)(2,1)S(1)}, u32[]{:S(2)}, u32[]{:S(2)}) collective-permute-start(bf16[256,1024]{1,0:T(8,128)(2,1)} %refs_0_.1), channel_id=1, source_target_pairs={{0,32},{32,64},{64,96},{96,128},{128,160},{160,192},{192,224},{224... | collective-permute-start | bytes 1572872 | tf_op jit(solution)/shard_map/ppermute | solution.py:202
  9.9 21.2 %collective-permute-start.1 = (bf16[256,1024]{1,0:T(8,128)(2,1)}, bf16[256,1024]{1,0:T(8,128)(2,1)S(1)}, u32[]{:S(2)}, u32[]{:S(2)}) collective-permute-start(bf16[256,1024]{1,0:T(8,128)(2,1)} %refs_0_.1), channel_id=1, source_target_pairs={{0,224},{32,0},{64,32},{96,64},{128,96},{160,128},{192,160},{224,1... | collective-permute-start | bytes 1572872 | tf_op jit(solution)/shard_map/ppermute | solution.py:202
  15.6 16.2 %collective-permute-start.2 = (bf16[128,512]{1,0:T(8,128)(2,1)S(1)}, bf16[128,512]{1,0:T(8,128)(2,1)S(1)}, u32[]{:S(2)}, u32[]{:S(2)}) collective-permute-start(bf16[128,512]{1,0:T(8,128)(2,1)S(1)} %constant_dynamic-update-slice_fusion.refs_0_.kv_hbm), channel_id=1, source_target_pairs={{0,2},{1,3},{2,4},{3,5},{4,6},{5,7},{6,8},{7,9},{8,10},{9,11},{10,... | collective-permute-start | bytes 393224 | tf_op jit(solution)/shard_map/ppermute | solution.py:191
  18.7 13.8 %collective-permute-start.3 = (bf16[128,512]{1,0:T(8,128)(2,1)S(1)}, bf16[128,512]{1,0:T(8,128)(2,1)S(1)}, u32[]{:S(2)}, u32[]{:S(2)}) collective-permute-start(bf16[128,512]{1,0:T(8,128)(2,1)S(1)} %constant_dynamic-update-slice_fusion.refs_0_.kv_hbm), channel_id=1, source_target_pairs={{0,4},{1,5},{2,6},{3,7},{4,8},{5,9},{6,10},{7,11},{8,12},{9,13},{1... | collective-permute-start | bytes 393224 | tf_op jit(solution)/shard_map/ppermute | solution.py:191
  22.2 10.9 %collective-permute-start.4 = (bf16[128,512]{1,0:T(8,128)(2,1)S(1)}, bf16[128,512]{1,0:T(8,128)(2,1)S(1)}, u32[]{:S(2)}, u32[]{:S(2)}) collective-permute-start(bf16[128,512]{1,0:T(8,128)(2,1)S(1)} %constant_dynamic-update-slice_fusion.refs_0_.kv_hbm), channel_id=1, source_target_pairs={{0,6},{1,7},{2,8},{3,9},{4,10},{5,11},{6,12},{7,13},{8,14},{9,15},... | collective-permute-start | bytes 393224 | tf_op jit(solution)/shard_map/ppermute | solution.py:191
  26.7 10.8 %copy-start.17 = (bf16[256,1024]{1,0:T(8,128)(2,1)}, bf16[256,1024]{1,0:T(8,128)(2,1)S(1)}, u32[]{:S(2)}) copy-start(bf16[256,1024]{1,0:T(8,128)(2,1)S(1)} %collective-permute-done.refs_1_) | copy-start | bytes 1572868
  26.7 10.8 %collective-permute-start.5 = (bf16[128,512]{1,0:T(8,128)(2,1)S(1)}, bf16[128,512]{1,0:T(8,128)(2,1)S(1)}, u32[]{:S(2)}, u32[]{:S(2)}) collective-permute-start(bf16[128,512]{1,0:T(8,128)(2,1)S(1)} %constant_dynamic-update-slice_fusion.refs_0_.kv_hbm), channel_id=1, source_target_pairs={{0,8},{1,9},{2,10},{3,11},{4,12},{5,13},{6,14},{7,15},{16,24},{17,... | collective-permute-start | bytes 393224 | tf_op jit(solution)/shard_map/ppermute | solution.py:191
  31.1 7.1 %copy-start.19 = (bf16[256,1024]{1,0:T(8,128)(2,1)}, bf16[256,1024]{1,0:T(8,128)(2,1)S(1)}, u32[]{:S(2)}) copy-start(bf16[256,1024]{1,0:T(8,128)(2,1)S(1)} %collective-permute-done.1.refs_2_) | copy-start | bytes 1572868
  33.1 43.2 %copy-start.13 = (bf16[128,512]{1,0:T(8,128)(2,1)}, bf16[128,512]{1,0:T(8,128)(2,1)S(1)}, u32[]{:S(2)}) copy-start(bf16[128,512]{1,0:T(8,128)(2,1)S(1)} %collective-permute-done.4.refs_3_) | copy-start | bytes 393220
  37.5 38.9 %copy-start.15 = (bf16[128,512]{1,0:T(8,128)(2,1)}, bf16[128,512]{1,0:T(8,128)(2,1)S(1)}, u32[]{:S(2)}) copy-start(bf16[128,512]{1,0:T(8,128)(2,1)S(1)} %collective-permute-done.5.refs_4_) | copy-start | bytes 393220
  38.2 2.3 collective-permute-start.6
  40.6 35.8 %copy-start.3 = (bf16[640,512]{1,0:T(8,128)(2,1)}, bf16[640,512]{1,0:T(8,128)(2,1)S(1)}, u32[]{:S(2)}) copy-start(bf16[640,512]{1,0:T(8,128)(2,1)S(1)} %collective-permute-done.6.refs_5_) | copy-start | bytes 1966084
  40.6 0.9 copy-start.23
  44.7 1.2 copy-start.7
  45.8 0.6 copy-start.21
  47.6 22.5 %all-to-all-start = ((bf16[16,128,256]{2,1,0:T(8,128)(2,1)}), bf16[16,128,256]{2,1,0:T(8,128)(2,1)}, u32[]{:S(2)}, u32[]{:S(2)}) async-start(bf16[16,128,256]{2,1,0:T(8,128)(2,1)} %broadcast_in_dim.34), calls=%async_computation | async-start | bytes 2097152 | tf_op jit(solution)/shard_map/all_to_all | solution.py:199
  53.4 96.9 %reduce-scatter.2.cloned.1.call-start = ((), (), s32[]{:S(2)}) async-start(), calls=%async_computation.5 | async-start | bytes 4718592 | tf_op jit(solution)/shard_map/reduce_scatter | solution.py:267
  53.4 15.8 %collective-permute-start.7 = (bf16[256,1024]{1,0:T(8,128)(2,1)}, bf16[256,1024]{1,0:T(8,128)(2,1)}, u32[]{:S(2)}, u32[]{:S(2)}) collective-permute-start(bf16[256,1024]{1,0:T(8,128)(2,1)} %copy-done.17), channel_id=1, source_target_pairs={{0,32},{32,64},{64,96},{96,128},{128,160},{160,192},{192,224},{224... | collective-permute-start | bytes 1572872 | tf_op jit(solution)/shard_map/ppermute | solution.py:202
  53.5 15.7 %collective-permute-start.8 = (bf16[256,1024]{1,0:T(8,128)(2,1)}, bf16[256,1024]{1,0:T(8,128)(2,1)}, u32[]{:S(2)}, u32[]{:S(2)}) collective-permute-start(bf16[256,1024]{1,0:T(8,128)(2,1)} %copy-done.19), channel_id=1, source_target_pairs={{0,224},{32,0},{64,32},{96,64},{128,96},{160,128},{192,160},{224,1... | collective-permute-start | bytes 1572872 | tf_op jit(solution)/shard_map/ppermute | solution.py:202
  70.1 6.4 %copy-start.5 = (bf16[256,1024]{1,0:T(8,128)(2,1)S(1)}, bf16[256,1024]{1,0:T(8,128)(2,1)}, u32[]{:S(2)}) copy-start(bf16[256,1024]{1,0:T(8,128)(2,1)} %refs_0_.1) | copy-start | bytes 1572868
  81.0 0.9 copy-start.22
  81.0 7.0 %copy-start.24 = (bf16[128,1024]{1,0:T(8,128)(2,1)S(1)}, bf16[128,1024]{1,0:T(8,128)(2,1)}, u32[]{:S(2)}) copy-start(bf16[128,1024]{1,0:T(8,128)(2,1)} %param.10) | copy-start | bytes 786436
  83.2 40.2 %all-to-all-start.1 = ((bf16[16,128,384]{2,1,0:T(8,128)(2,1)}), bf16[16,128,384]{2,1,0:T(8,128)(2,1)}, u32[]{:S(2)}, u32[]{:S(2)}) async-start(bf16[16,128,384]{2,1,0:T(8,128)(2,1)} %broadcast_in_dim.35), calls=%async_computation.2 | async-start | bytes 3145728 | tf_op jit(solution)/shard_map/all_to_all | solution.py:199
  87.9 151.4 %all-gather.5.cloned.1.call-start = ((), (), s32[]{:S(2)}) async-start(), calls=%async_computation.6 | async-start | bytes 4718592 | tf_op jit(solution)/shard_map/all_gather | solution.py:301
  88.0 26.0 %collective-permute-start.9 = (bf16[128,1024]{1,0:T(8,128)(2,1)S(1)}, bf16[128,1024]{1,0:T(8,128)(2,1)}, u32[]{:S(2)}, u32[]{:S(2)}) collective-permute-start(bf16[128,1024]{1,0:T(8,128)(2,1)S(1)} %copy-done.24), channel_id=1, source_target_pairs={{0,16},{16,0},{1,17},{17,1},{2,18},{18,2},{3,19},{19,3},{4,20},{20... | collective-permute-start | bytes 786440 | tf_op jit(solution)/shard_map/ppermute | solution.py:205
  88.9 29.0 %collective-permute-start.10 = (bf16[256,1024]{1,0:T(8,128)(2,1)}, bf16[256,1024]{1,0:T(8,128)(2,1)S(1)}, u32[]{:S(2)}, u32[]{:S(2)}) collective-permute-start(bf16[256,1024]{1,0:T(8,128)(2,1)} %collective-permute-done.7.refs_3_), channel_id=1, source_target_pairs={{0,32},{32,64},{64,96},{96,128},{128,160},{160,192},{192,224},{224... | collective-permute-start | bytes 1572872 | tf_op jit(solution)/shard_map/ppermute | solution.py:202
  88.9 29.8 %collective-permute-start.12 = (bf16[256,1024]{1,0:T(8,128)(2,1)}, bf16[256,1024]{1,0:T(8,128)(2,1)S(1)}, u32[]{:S(2)}, u32[]{:S(2)}) collective-permute-start(bf16[256,1024]{1,0:T(8,128)(2,1)} %collective-permute-done.8.refs_4_), channel_id=1, source_target_pairs={{0,224},{32,0},{64,32},{96,64},{128,96},{160,128},{192,160},{224,1... | collective-permute-start | bytes 1572872 | tf_op jit(solution)/shard_map/ppermute | solution.py:202
  117.9 5.5 %copy-start.9 = (bf16[256,1024]{1,0:T(8,128)(2,1)}, bf16[256,1024]{1,0:T(8,128)(2,1)S(1)}, u32[]{:S(2)}) copy-start(bf16[256,1024]{1,0:T(8,128)(2,1)S(1)} %collective-permute-done.10.refs_5_) | copy-start | bytes 1572868
  118.7 15.9 %collective-permute-start.11 = (bf16[128,1024]{1,0:T(8,128)(2,1)}, bf16[128,1024]{1,0:T(8,128)(2,1)}, u32[]{:S(2)}, u32[]{:S(2)}) collective-permute-start(bf16[128,1024]{1,0:T(8,128)(2,1)} %slice.8), channel_id=1, source_target_pairs={{0,32},{32,64},{64,96},{96,128},{128,160},{160,192},{192,224},{224... | collective-permute-start | bytes 786440 | tf_op jit(solution)/shard_map/ppermute | solution.py:202
  119.4 0.8 copy-start.11
  120.2 15.6 %collective-permute-start.13 = (bf16[128,1024]{1,0:T(8,128)(2,1)}, bf16[128,1024]{1,0:T(8,128)(2,1)}, u32[]{:S(2)}, u32[]{:S(2)}) collective-permute-start(bf16[128,1024]{1,0:T(8,128)(2,1)} %slice.9), channel_id=1, source_target_pairs={{0,224},{32,0},{64,32},{96,64},{128,96},{160,128},{192,160},{224,1... | collective-permute-start | bytes 786440 | tf_op jit(solution)/shard_map/ppermute | solution.py:202
  150.2 15.2 %collective-permute-start.14 = (bf16[256,1024]{1,0:T(8,128)(2,1)}, bf16[256,1024]{1,0:T(8,128)(2,1)S(1)}, u32[]{:S(2)}, u32[]{:S(2)}) collective-permute-start(bf16[256,1024]{1,0:T(8,128)(2,1)} %reduce-scatter.2.cloned.1.call-done), channel_id=1, source_target_pairs={{0,16},{16,0},{1,17},{17,1},{2,18},{18,2},{3,19},{19,3},{4,20},{20... | collective-permute-start | bytes 1572872 | tf_op jit(solution)/shard_map/ppermute | solution.py:205
  167.8 1.0 copy-start.1
  168.8 1.0 copy-start.6
  169.9 1.0 copy-start.10
  170.9 1.0 copy-start.12
  171.9 1.0 copy-start.18
  173.0 1.0 copy-start.20
  174.0 53.2 %copy-start.25 = (s32[1280]{0:T(1024)S(1)}, s32[1280]{0:T(1024)}, u32[]{:S(2)}) copy-start(s32[1280]{0:T(1024)} %get-tuple-element.44) | copy-start | bytes 15364
  202.0 33.0 %copy-start.2 = (bf16[1280,256]{1,0:T(8,128)(2,1)S(1)}, bf16[1280,256]{1,0:T(8,128)(2,1)}, u32[]{:S(2)}) copy-start(bf16[1280,256]{1,0:T(8,128)(2,1)} %pad_dynamic-slice_fusion.1.attn_hbm) | copy-start | bytes 1966084
  202.0 1.6 collective-permute-start.15
  203.6 14.9 %collective-permute-start.16 = (bf16[128,256]{1,0:T(8,128)(2,1)S(1)}, bf16[128,256]{1,0:T(8,128)(2,1)S(1)}, u32[]{:S(2)}, u32[]{:S(2)}) collective-permute-start(bf16[128,256]{1,0:T(8,128)(2,1)S(1)} %collective-permute-done.15.dattn_hbm.refs_0_), channel_id=1, source_target_pairs={{2,0},{3,1},{4,2},{5,3},{6,4},{7,5},{8,6},{9,7},{10,8},{11,9},{12,... | collective-permute-start | bytes 196616 | tf_op jit(solution)/shard_map/ppermute | solution.py:191
  204.9 17.7 %collective-permute-start.17 = (bf16[128,256]{1,0:T(8,128)(2,1)S(1)}, bf16[128,256]{1,0:T(8,128)(2,1)S(1)}, u32[]{:S(2)}, u32[]{:S(2)}) collective-permute-start(bf16[128,256]{1,0:T(8,128)(2,1)S(1)} %collective-permute-done.15.dattn_hbm.refs_0_), channel_id=1, source_target_pairs={{4,0},{5,1},{6,2},{7,3},{8,4},{9,5},{10,6},{11,7},{12,8},{13,9},{1... | collective-permute-start | bytes 196616 | tf_op jit(solution)/shard_map/ppermute | solution.py:191
  206.2 17.6 %collective-permute-start.18 = (bf16[128,256]{1,0:T(8,128)(2,1)S(1)}, bf16[128,256]{1,0:T(8,128)(2,1)S(1)}, u32[]{:S(2)}, u32[]{:S(2)}) collective-permute-start(bf16[128,256]{1,0:T(8,128)(2,1)S(1)} %collective-permute-done.15.dattn_hbm.refs_0_), channel_id=1, source_target_pairs={{6,0},{7,1},{8,2},{9,3},{10,4},{11,5},{12,6},{13,7},{14,8},{15,9},... | collective-permute-start | bytes 196616 | tf_op jit(solution)/shard_map/ppermute | solution.py:191
  207.5 19.7 %collective-permute-start.19 = (bf16[128,256]{1,0:T(8,128)(2,1)S(1)}, bf16[128,256]{1,0:T(8,128)(2,1)S(1)}, u32[]{:S(2)}, u32[]{:S(2)}) collective-permute-start(bf16[128,256]{1,0:T(8,128)(2,1)S(1)} %collective-permute-done.15.dattn_hbm.refs_0_), channel_id=1, source_target_pairs={{8,0},{9,1},{10,2},{11,3},{12,4},{13,5},{14,6},{15,7},{24,16},{25,... | collective-permute-start | bytes 196616 | tf_op jit(solution)/shard_map/ppermute | solution.py:191
  227.2 7.8 %collective-permute-start.20 = (bf16[640,256]{1,0:T(8,128)(2,1)S(1)}, bf16[640,256]{1,0:T(8,128)(2,1)S(1)}, u32[]{:S(2)}, u32[]{:S(2)}) collective-permute-start(bf16[640,256]{1,0:T(8,128)(2,1)S(1)} %constant_dynamic-update-slice_fusion.7), channel_id=1, source_target_pairs={{0,1},{1,0},{2,3},{3,2},{4,5},{5,4},{6,7},{7,6},{8,9},{9,8},{10,11... | collective-permute-start | bytes 983048 | tf_op jit(solution)/shard_map/ppermute | solution.py:195
  227.4 1.1 copy-start.4
  228.5 1.3 copy-start.8
  229.9 0.9 copy-start.14
  230.8 0.9 copy-start.16
Sparse Core Ops, SparseCore 0:
  9.9 47.0 all-gather.2
  81.1 69.0 reduce-scatter.1
  167.9 61.8 all-gather.4

commit v4 on v3

--- a/solution.py
+++ b/solution.py
@@ -158,8 +158,32 @@
         first[by] += size
 
 
+def difference_kernel(attn_ref, proj_ref, teacher_ref, out_ref):
+    out = dot(attn_ref[...], proj_ref[...]) - teacher_ref[...].astype(F32)
+    out_ref[...] = out.astype(BF16)
+
+
+def difference(attn, proj, teacher):
+    tokens, depth = attn.shape
+    features = proj.shape[1]
+    step = tokens // 8
+    return pl.pallas_call(
+        difference_kernel,
+        out_shape=pltpu.HBM((tokens, features), BF16),
+        grid=(tokens // step,),
+        in_specs=[
+            pl.BlockSpec((step, depth), lambda i: (i, 0)),
+            pl.BlockSpec((depth, features), lambda i: (0, 0)),
+            pl.BlockSpec((step, features), lambda i: (i, 0)),
+        ],
+        out_specs=pl.BlockSpec((step, features), lambda i: (i, 0)),
+        compiler_params=pltpu.CompilerParams(vmem_limit_bytes=16 * 1024 * 1024),
+    )(*(pltpu.with_memory_space_constraint(x, pltpu.HBM) for x in (attn, proj, teacher)))
+
+
 def call(kernel, out_shape, in_smem, in_vmem, in_hbm, scratch):
     space = pl.BlockSpec
+    in_hbm = [pltpu.with_memory_space_constraint(x, pltpu.HBM) for x in in_hbm]
     return pl.pallas_call(
         kernel,
         out_shape=out_shape,
@@ -168,7 +192,7 @@
         + [space(memory_space=pltpu.HBM)] * len(in_hbm),
         scratch_shapes=[pltpu.VMEM(s.shape, s.dtype) for s in scratch]
         + [pltpu.SemaphoreType.DMA((COPIES,))],
-        compiler_params=pltpu.CompilerParams(vmem_limit_bytes=40 * 1024 * 1024),
+        compiler_params=pltpu.CompilerParams(vmem_limit_bytes=16 * 1024 * 1024),
     )(*in_smem, *in_vmem, *in_hbm)
 
 
@@ -211,8 +235,6 @@
 
     def step(up, down):
         k = len(pieces) // 2 + 1
-        if k == n_z // 2:
-            up, down = up[:half], down[half:]
         offsets.extend([n_z - k, k])
         return turn(up, 1), turn(down, -1)
 
@@ -246,7 +268,10 @@
     )
     attn_all = everywhere(attn)
     up, down = step(up, down)
-    attn_all, qx, up, down = lax.optimization_barrier((attn_all, qx, up, down))
+    pieces += [up, down]
+    up, down = step(up, down)
+    teacher_part = dot(context_all, w_out).astype(BF16)
+    teacher_part, qx, up, down = lax.optimization_barrier((teacher_part, qx, up, down))
     pieces += [up, down]
 
     def after(array):
@@ -263,16 +288,17 @@
         ],
         axis=0,
     )
-    part = (dot(attn_all, proj) - dot(context_all, w_out)).astype(BF16)
+    part = difference(attn_all, proj, teacher_part)
     part = lax.psum_scatter(part, "z", scatter_dimension=0, tiled=True)
-    while len(pieces) < n_z:
-        up, down = step(up, down)
-        pieces += [up, down]
-    part, resid, up, down, qx_after, attn_after = lax.optimization_barrier(
-        (part, resid, up, down, qx_after, attn_after)
-    )
-    pieces[-2:] = [up, down]
-    diff = (part.astype(F32) + swap(part).astype(F32)) - resid.astype(F32)
+    up, down = up[:half], down[half:]
+    part, resid, qx_after, attn_after, up, down = lax.optimization_barrier(
+        (part, resid, qx_after, attn_after, up, down)
+    )
+    part_other = swap(part)
+    up, down = step(up, down)
+    part_other, up, down = lax.optimization_barrier((part_other, up, down))
+    pieces += [up, down]
+    diff = (part.astype(F32) + part_other.astype(F32)) - resid.astype(F32)
     dpred = diff.astype(BF16)
 
     dattn_part = call(
@@ -310,6 +336,7 @@
         (dattn, attn, probs, *kv_parts),
         (block_type, block_type, probs_type, window_kv_type),
     )
+    key_value, query_grad = lax.optimization_barrier((key_value, query_grad))
     key_grad, value_grad = call(
         functools.partial(key_grad_kernel, near),
         (block_type, block_type),

time: 255 us -> 228 us (0.89)
  waiting for transfers between devices: 95.8 us -> 78.5 us
  local copies, waits for them, and re-layouts: 30.1 us -> 21.1 us
  Pallas kernels: 13.9 us -> 22.2 us
  starting transfers between devices: 52.2 us -> 48.7 us
  matrix products: 15.4 us -> 12.7 us
    unnamed x61 -> x47, local copies, waits for them, and re-layouts: 18.5 us -> 7.86 us
    ppermute x8, waiting for transfers between devices: 23.3 us -> 13.1 us  [turn(): return lax.ppermute(array, 'z', [(i, (i + by) % n_z) for i in range(n_z)])]
    pallas_call x0 -> x1, Pallas kernels: none -> 8.07 us  [difference(): pl.pallas_call(difference_kernel, out_shape=pltpu.HBM((tokens, features),...]
    ppermute x2, waiting for transfers between devices: 34.4 us -> 30.6 us  [swap(): return lax.ppermute(array, 'xh', [(i, i ^ 1) for i in range(n_xh)])]
    reduce_scatter x1, waiting for transfers between devices: 14.5 us -> 11.7 us  [body(): part = lax.psum_scatter(part, 'z', scatter_dimension=0, tiled=True)]
    dot_general x3 -> x2, matrix products: 15.4 us -> 12.7 us  [dot(): return lax.dot_general(a, b, dims, preferred_element_type=F32)]
  transfers between devices with their start and end apart: 26 -> 26, of which waited for: 12 -> 11; matrix products, arithmetic and copies ran while one was open for 8% -> 13% of each run, Pallas kernels for 6% -> 6%
where the time goes in v4:
time: 228 us; the launch traced here: 224 us
  waiting for transfers between devices  78.5 us (34%)
  starting transfers between devices  48.7 us (21%)
  Pallas kernels  22.2 us (10%)
  blocking collectives  21.4 us (9%)
  local copies, waits for them, and re-layouts  21.1 us (9%)
  between operations  14.1 us (6%)
  matrix products  12.7 us (6%)
  other arithmetic  5.46 us (2%)
    ppermute x2, waiting for transfers between devices, swap(): return lax.ppermute(array, 'xh', [(i, i ^ 1) for i in range(n_xh)])  30.6 us
    ppermute x8, waiting for transfers between devices, shift(): return lax.ppermute(array, SP, pairs)  22.5 us
    all_to_all x1, blocking collectives, body(): lax.all_to_all(dattn_part.reshape(n_sp, rows, width), SP, 0, 0, tiled=True)  21.4 us
    ppermute x8, starting transfers between devices, shift(): return lax.ppermute(array, SP, pairs)  20.7 us
    ppermute x8, starting transfers between devices, turn(): return lax.ppermute(array, 'z', [(i, (i + by) % n_z) for i in range(n_z)])  14.5 us
    pallas_call x4, Pallas kernels, call(): pl.pallas_call(kernel, out_shape=out_shape, in_specs=[space(memory_space=...  14.1 us
    ppermute x8, waiting for transfers between devices, turn(): return lax.ppermute(array, 'z', [(i, (i + by) % n_z) for i in range(n_z)])  13.1 us
    dot_general x2, matrix products, dot(): return lax.dot_general(a, b, dims, preferred_element_type=F32)  12.7 us
  transfers between devices with their start and end apart: 26, of which 11 were waited for; matrix products, arithmetic and copies ran while one was open for 13% of the time, Pallas kernels for 6%

profile of v4, /device:TPU:4, one launch (start us, length us, event | category | flops | bytes accessed | tf_op | source)
XLA Modules:
  0.0 224.3 jit_solution(9803330694350181490)
XLA Ops:
  7.2 0.7 all-gather.3.cloned.1.call-update
  7.9 2.0 collective-permute-start
  9.9 4.0 %collective-permute-start.1 = (bf16[256,1024]{1,0:T(8,128)(2,1)}, bf16[256,1024]{1,0:T(8,128)(2,1)}, u32[]{:S(2)}, u32[]{:S(2)}) collective-permute-start(bf16[256,1024]{1,0:T(8,128)(2,1)} %refs_0_.1), channel_id=1, source_target_pairs={{0,224},{32,0},{64,32},{96,64},{128,96},{160,128},{192,160},{224,1... | collective-permute-start | bytes 1572872 | tf_op jit(solution)/shard_map/ppermute | solution.py:226
  13.9 0.8 constant_dynamic-update-slice_fusion.1
  14.8 0.8 constant_dynamic-update-slice_fusion.refs_0_.kv_hbm
  15.6 3.1 %collective-permute-start.2 = (bf16[128,512]{1,0:T(8,128)(2,1)S(1)}, bf16[128,512]{1,0:T(8,128)(2,1)S(1)}, u32[]{:S(2)}, u32[]{:S(2)}) collective-permute-start(bf16[128,512]{1,0:T(8,128)(2,1)S(1)} %constant_dynamic-update-slice_fusion.refs_0_.kv_hbm), channel_id=1, source_target_pairs={{0,2},{1,3},{2,4},{3,5},{4,6},{5,7},{6,8},{7,9},{8,10},{9,11},{10,... | collective-permute-start | bytes 393224 | tf_op jit(solution)/shard_map/ppermute | solution.py:215
  18.7 3.5 %collective-permute-start.3 = (bf16[128,512]{1,0:T(8,128)(2,1)S(1)}, bf16[128,512]{1,0:T(8,128)(2,1)S(1)}, u32[]{:S(2)}, u32[]{:S(2)}) collective-permute-start(bf16[128,512]{1,0:T(8,128)(2,1)S(1)} %constant_dynamic-update-slice_fusion.refs_0_.kv_hbm), channel_id=1, source_target_pairs={{0,4},{1,5},{2,6},{3,7},{4,8},{5,9},{6,10},{7,11},{8,12},{9,13},{1... | collective-permute-start | bytes 393224 | tf_op jit(solution)/shard_map/ppermute | solution.py:215
  22.2 4.5 %collective-permute-start.4 = (bf16[128,512]{1,0:T(8,128)(2,1)S(1)}, bf16[128,512]{1,0:T(8,128)(2,1)S(1)}, u32[]{:S(2)}, u32[]{:S(2)}) collective-permute-start(bf16[128,512]{1,0:T(8,128)(2,1)S(1)} %constant_dynamic-update-slice_fusion.refs_0_.kv_hbm), channel_id=1, source_target_pairs={{0,6},{1,7},{2,8},{3,9},{4,10},{5,11},{6,12},{7,13},{8,14},{9,15},... | collective-permute-start | bytes 393224 | tf_op jit(solution)/shard_map/ppermute | solution.py:215
  26.7 4.5 %collective-permute-start.5 = (bf16[128,512]{1,0:T(8,128)(2,1)S(1)}, bf16[128,512]{1,0:T(8,128)(2,1)S(1)}, u32[]{:S(2)}, u32[]{:S(2)}) collective-permute-start(bf16[128,512]{1,0:T(8,128)(2,1)S(1)} %constant_dynamic-update-slice_fusion.refs_0_.kv_hbm), channel_id=1, source_target_pairs={{0,8},{1,9},{2,10},{3,11},{4,12},{5,13},{6,14},{7,15},{16,24},{17,... | collective-permute-start | bytes 393224 | tf_op jit(solution)/shard_map/ppermute | solution.py:215
  31.2 0.7 constant_dynamic-update-slice_fusion.6
  31.9 0.7 constant_dynamic-update-slice_fusion.5
  32.6 0.7 constant_dynamic-update-slice_fusion.4
  33.3 0.7 constant_dynamic-update-slice_fusion.3
  34.0 3.6 %collective-permute-done.5.refs_4_ = bf16[128,512]{1,0:T(8,128)(2,1)S(1)} collective-permute-done((bf16[128,512]{1,0:T(8,128)(2,1)S(1)}, bf16[128,512]{1,0:T(8,128)(2,1)S(1)}, u32[]{:S(2)}, u32[]{:S(2)}) %collective-permute-start.5) | collective-permute-done | bytes 131104 | tf_op jit(solution)/shard_map/ppermute | solution.py:215
  37.6 0.6 copy-done.10
  38.3 0.7 constant_dynamic-update-slice_fusion.2
  39.0 1.8 collective-permute-start.9
  40.7 0.3 collective-permute-start.7
  41.0 0.8 pad_dynamic-slice_fusion.2
  41.8 0.8 dynamic-slice_bitcast_fusion
  42.8 0.8 copy-done.6
  43.6 2.8 %shard_map.111 = (bf16[128,256]{1,0:T(8,128)(2,1)S(1)}, f32[2,128,1280]{2,1,0:T(8,128)S(1)}, bf16[128,384]{1,0:T(8,128)(2,1)S(1)}) custom-call(s32[1]{0:T(128)} %bitcast.core_ref, s32[128,1]{1,0:T(8,128)S(1)} %copy.13.qseg_ref, s32[1,1280]{1,0:T(1,128)S(1)} %broadcast_in_dim.33.kseg_ref, bf16[128,256]{1,0:T(8,128)(2,1)} %q_hbm.1, ...), custom_call_target="tpu_custom_call" | custom-call | tf_op jit(solution)/shard_map/pallas_call | solution.py:187
  46.4 1.0 copy-done.1
  47.5 1.1 broadcast_in_dim.34
  48.5 5.6 %all-to-all-start = ((bf16[16,128,256]{2,1,0:T(8,128)(2,1)}), bf16[16,128,256]{2,1,0:T(8,128)(2,1)S(1)}, u32[]{:S(2)}, u32[]{:S(2)}) async-start(bf16[16,128,256]{2,1,0:T(8,128)(2,1)} %broadcast_in_dim.34), calls=%async_computation | async-start | bytes 2097152 | tf_op jit(solution)/shard_map/all_to_all | solution.py:223
  54.2 3.2 %collective-permute-start.10 = (bf16[256,1024]{1,0:T(8,128)(2,1)}, bf16[256,1024]{1,0:T(8,128)(2,1)}, u32[]{:S(2)}, u32[]{:S(2)}) collective-permute-start(bf16[256,1024]{1,0:T(8,128)(2,1)} %collective-permute-done.9.refs_4_), channel_id=1, source_target_pairs={{0,224},{32,0},{64,32},{96,64},{128,96},{160,128},{192,160},{224,1... | collective-permute-start | bytes 1572872 | tf_op jit(solution)/shard_map/ppermute | solution.py:226
  57.4 8.4 %convolution_convert_fusion.teacher_ref = bf16[2048,1024]{1,0:T(8,128)(2,1)} fusion(bf16[2048,1024]{1,0:T(8,128)(2,1)} %all-gather.3.cloned.1.call-done, bf16[1024,1024]{1,0:T(8,128)(2,1)S(1)} %copy-done), kind=kOutput, calls=%fused_computation | convolution fusion | flops 4297064448 | bytes 10485760 | tf_op jit(solution)/shard_map/dot_general | solution.py:24
  65.9 3.6 %collective-permute-done.10.refs_6_ = bf16[256,1024]{1,0:T(8,128)(2,1)} collective-permute-done((bf16[256,1024]{1,0:T(8,128)(2,1)}, bf16[256,1024]{1,0:T(8,128)(2,1)}, u32[]{:S(2)}, u32[]{:S(2)}) %collective-permute-start.10) | collective-permute-done | bytes 524320 | tf_op jit(solution)/shard_map/ppermute | solution.py:226
  69.5 3.4 %collective-permute-done.8.refs_5_ = bf16[256,1024]{1,0:T(8,128)(2,1)} collective-permute-done((bf16[256,1024]{1,0:T(8,128)(2,1)}, bf16[256,1024]{1,0:T(8,128)(2,1)}, u32[]{:S(2)}, u32[]{:S(2)}) %collective-permute-start.8) | collective-permute-done | bytes 524320 | tf_op jit(solution)/shard_map/ppermute | solution.py:226
  72.9 1.0 copy-done.3
  73.9 8.1 %shard_map.112 = bf16[2048,1024]{1,0:T(8,128)(2,1)} custom-call(bf16[2048,256]{1,0:T(8,128)(2,1)} %bitcast.14, bf16[256,1024]{1,0:T(8,128)(2,1)} %refs_0_.1, bf16[2048,1024]{1,0:T(8,128)(2,1)} %convolution_convert_fusion.teacher_ref), custom_call_target="tpu_custom_call" | custom-call | tf_op jit(solution)/shard_map/pallas_call | solution.py:170
  82.0 1.4 broadcast_in_dim.35
  83.4 5.5 %all-to-all-start.1 = ((bf16[16,128,384]{2,1,0:T(8,128)(2,1)}), bf16[16,128,384]{2,1,0:T(8,128)(2,1)}, u32[]{:S(2)}, u32[]{:S(2)}) async-start(bf16[16,128,384]{2,1,0:T(8,128)(2,1)} %broadcast_in_dim.35), calls=%async_computation.2 | async-start | bytes 3145728 | tf_op jit(solution)/shard_map/all_to_all | solution.py:223
  88.9 1.0 collective-permute-start.11
  90.0 24.9 %collective-permute-done.11 = bf16[128,1024]{1,0:T(8,128)(2,1)} collective-permute-done((bf16[128,1024]{1,0:T(8,128)(2,1)S(1)}, bf16[128,1024]{1,0:T(8,128)(2,1)}, u32[]{:S(2)}, u32[]{:S(2)}) %collective-permute-start.11) | collective-permute-done | bytes 262176 | tf_op jit(solution)/shard_map/ppermute | solution.py:229
  114.9 1.0 broadcast_select_fusion.1
  115.9 0.8 pad_maximum_fusion
  116.7 1.6 pad_dynamic-slice_fusion.1.attn_hbm
  118.2 1.7 slice.6
  119.9 1.7 slice.7
  121.6 2.5 %pad_dynamic-slice_fusion.qx_hbm = bf16[1280,384]{1,0:T(8,128)(2,1)} fusion(s32[]{:T(128)S(6)} %select_n.22, bf16[2048,384]{1,0:T(8,128)(2,1)} %bitcast.3), kind=kLoop, calls=%fused_computation.1 | loop fusion | bytes 2555908 | tf_op jit(solution)/shard_map/dynamic_slice | solution.py:279
  124.1 11.7 %reduce-scatter.2.cloned.1.call-done = bf16[256,1024]{1,0:T(8,128)(2,1)} async-done(((bf16[2048,1024]{1,0:T(8,128)(2,1)}), bf16[256,1024]{1,0:T(8,128)(2,1)}) %reduce-scatter.2.cloned.1.call-update) | async-done | bytes 524304 | tf_op jit(solution)/shard_map/reduce_scatter | solution.py:292
  135.8 0.6 collective-permute-start.12
  136.3 3.2 %collective-permute-start.14 = (bf16[128,1024]{1,0:T(8,128)(2,1)}, bf16[128,1024]{1,0:T(8,128)(2,1)}, u32[]{:S(2)}, u32[]{:S(2)}) collective-permute-start(bf16[128,1024]{1,0:T(8,128)(2,1)} %slice.7), channel_id=1, source_target_pairs={{0,224},{32,0},{64,32},{96,64},{128,96},{160,128},{192,160},{224,1... | collective-permute-start | bytes 786440 | tf_op jit(solution)/shard_map/ppermute | solution.py:226
  139.6 6.0 %collective-permute-done.13.refs_7_ = bf16[128,1024]{1,0:T(8,128)(2,1)S(1)} collective-permute-done((bf16[128,1024]{1,0:T(8,128)(2,1)}, bf16[128,1024]{1,0:T(8,128)(2,1)S(1)}, u32[]{:S(2)}, u32[]{:S(2)}) %collective-permute-start.13) | collective-permute-done | bytes 262176 | tf_op jit(solution)/shard_map/ppermute | solution.py:226
  145.6 5.7 %collective-permute-done.12 = bf16[256,1024]{1,0:T(8,128)(2,1)S(1)} collective-permute-done((bf16[256,1024]{1,0:T(8,128)(2,1)}, bf16[256,1024]{1,0:T(8,128)(2,1)S(1)}, u32[]{:S(2)}, u32[]{:S(2)}) %collective-permute-start.12) | collective-permute-done | bytes 524320 | tf_op jit(solution)/shard_map/ppermute | solution.py:229
  151.2 2.3 %subtract_convert_fusion.dpred_hbm = bf16[256,1024]{1,0:T(8,128)(2,1)} fusion(bf16[256,1024]{1,0:T(8,128)(2,1)} %pad_maximum_fusion, bf16[256,1024]{1,0:T(8,128)(2,1)S(1)} %collective-permute-done.12, bf16[256,1024]{1,0:T(8,128)(2,1)} %reduce-scatter.2.cloned.1.call-done), kind=kLoop, calls=%fused_computation.4 | loop fusion | flops 1572864 | bytes 2097152 | tf_op jit(solution)/shard_map/convert_element_type | solution.py:302
  153.5 3.9 %shard_map.113 = bf16[8,256,256]{2,1,0:T(8,128)(2,1)S(1)} custom-call(s32[1]{0:T(128)} %bitcast.4.z_ref, bf16[256,1024]{1,0:T(8,128)(2,1)} %subtract_convert_fusion.dpred_hbm, bf16[256,1024]{1,0:T(8,128)(2,1)} %refs_0_.1, bf16[256,1024]{1,0:T(8,128)(2,1)} %collective-permute-done.refs_1_, bf16[256,1024]{1,0:T(8,128)(2,1)} %collective-permute-done.1.refs_2_, ...), custom_call_target="tpu_custom_call" | custom-call | tf_op jit(solution)/shard_map/pallas_call | solution.py:187
  157.4 21.4 %all_to_all.15 = bf16[16,128,256]{2,1,0:T(8,128)(2,1)} all-to-all(bf16[16,128,256]{2,1,0:T(8,128)(2,1)S(1)} %bitcast.13), channel_id=1, replica_groups=mesh['z'=8,'xh'=2,'y'=4,'xl'=2,'core'=2] {'y','xl','core'}, dimensions={0} | all-to-all | bytes 2097152 | tf_op jit(solution)/shard_map/all_to_all | solution.py:312
  178.8 1.4 reduce_sum.12
  180.2 0.7 collective-permute-start.15
  180.8 1.3 collective-permute-start.16
  182.1 1.3 collective-permute-start.17
  183.4 1.3 collective-permute-start.18
  184.7 1.3 collective-permute-start.19
  186.1 10.2 %collective-permute-done.16.refs_1_ = bf16[128,256]{1,0:T(8,128)(2,1)S(1)} collective-permute-done((bf16[128,256]{1,0:T(8,128)(2,1)S(1)}, bf16[128,256]{1,0:T(8,128)(2,1)S(1)}, u32[]{:S(2)}, u32[]{:S(2)}) %collective-permute-start.16) | collective-permute-done | bytes 65568 | tf_op jit(solution)/shard_map/ppermute | solution.py:215
  196.3 3.4 %collective-permute-done.17.refs_2_ = bf16[128,256]{1,0:T(8,128)(2,1)S(1)} collective-permute-done((bf16[128,256]{1,0:T(8,128)(2,1)S(1)}, bf16[128,256]{1,0:T(8,128)(2,1)S(1)}, u32[]{:S(2)}, u32[]{:S(2)}) %collective-permute-start.17) | collective-permute-done | bytes 65568 | tf_op jit(solution)/shard_map/ppermute | solution.py:215
  199.7 1.9 collective-permute-done.18.refs_3_
  201.6 3.3 %collective-permute-done.19.refs_4_ = bf16[128,256]{1,0:T(8,128)(2,1)S(1)} collective-permute-done((bf16[128,256]{1,0:T(8,128)(2,1)S(1)}, bf16[128,256]{1,0:T(8,128)(2,1)S(1)}, u32[]{:S(2)}, u32[]{:S(2)}) %collective-permute-start.19) | collective-permute-done | bytes 65568 | tf_op jit(solution)/shard_map/ppermute | solution.py:215
  205.1 0.2 broadcast_in_dim.39.qseg_ref
  205.3 3.1 %shard_map.114 = bf16[128,256]{1,0:T(8,128)(2,1)} custom-call(s32[1]{0:T(128)} %bitcast.core_ref, bf16[128,256]{1,0:T(8,128)(2,1)} %copy-done.11, bf16[128,256]{1,0:T(8,128)(2,1)} %copy-done.2, f32[2,128,1280]{2,1,0:T(8,128)} %copy-done.1, bf16[128,512]{1,0:T(8,128)(2,1)} %copy-done.5, bf16[128,512]{1,0:T(8,128)(2,1)} %copy-done.7, ...), custom_call_target="tpu_custom_call" | custom-call | tf_op jit(solution)/shard_map/pallas_call | solution.py:187
  208.5 0.7 copy-done.12
  209.2 4.3 %shard_map.115 = (bf16[128,256]{1,0:T(8,128)(2,1)}, bf16[128,256]{1,0:T(8,128)(2,1)}) custom-call(s32[1]{0:T(128)} %bitcast.core_ref, s32[1280,1]{1,0:T(8,128)S(1)} %broadcast_in_dim.39.qseg_ref, s32[1,128]{1,0:T(1,128)S(1)} %get-tuple-element.52.kseg_ref, bf16[128,512]{1,0:T(8,128)(2,1)} %copy-done.5, bf16[1280,384]{1,0:T(8,128)(2,1)} %pad_dynamic-slice_fusion.qx_hbm, ...), custom_call_target="tpu_custom_call" | custom-call | tf_op jit(solution)/shard_map/pallas_call | solution.py:187
  213.5 4.3 %convolution_convert_fusion.1 = bf16[256,1024]{1,0:T(8,128)(2,1)} fusion(bf16[2048,256]{1,0:T(8,128)(2,1)S(1)} %bitcast.16, bf16[2048,1024]{1,0:T(8,128)(2,1)} %all-gather.5.cloned.1.call-done), kind=kOutput, calls=%fused_computation.3 | convolution fusion | flops 1074003968 | bytes 5767168 | tf_op jit(solution)/shard_map/dot_general | solution.py:24
  (64 shorter events, 0.5 us)
Async XLA Ops:
  7.2 50.3 %copy-start = (bf16[1024,1024]{1,0:T(8,128)(2,1)S(1)}, bf16[1024,1024]{1,0:T(8,128)(2,1)}, u32[]{:S(2)}) copy-start(bf16[1024,1024]{1,0:T(8,128)(2,1)} %param.9) | copy-start | bytes 6291460
  7.2 50.3 %all-gather.3.cloned.1.call-start = ((), (), s32[]{:S(2)}) async-start(), calls=%async_computation.4 | async-start | bytes 4456448 | tf_op jit(solution)/shard_map/all_gather | solution.py:231
  7.9 18.8 %collective-permute-start = (bf16[256,1024]{1,0:T(8,128)(2,1)}, bf16[256,1024]{1,0:T(8,128)(2,1)}, u32[]{:S(2)}, u32[]{:S(2)}) collective-permute-start(bf16[256,1024]{1,0:T(8,128)(2,1)} %refs_0_.1), channel_id=1, source_target_pairs={{0,32},{32,64},{64,96},{96,128},{128,160},{160,192},{192,224},{224... | collective-permute-start | bytes 1572872 | tf_op jit(solution)/shard_map/ppermute | solution.py:226
  9.9 21.3 %collective-permute-start.1 = (bf16[256,1024]{1,0:T(8,128)(2,1)}, bf16[256,1024]{1,0:T(8,128)(2,1)}, u32[]{:S(2)}, u32[]{:S(2)}) collective-permute-start(bf16[256,1024]{1,0:T(8,128)(2,1)} %refs_0_.1), channel_id=1, source_target_pairs={{0,224},{32,0},{64,32},{96,64},{128,96},{160,128},{192,160},{224,1... | collective-permute-start | bytes 1572872 | tf_op jit(solution)/shard_map/ppermute | solution.py:226
  15.6 27.1 %copy-start.5 = (bf16[128,512]{1,0:T(8,128)(2,1)}, bf16[128,512]{1,0:T(8,128)(2,1)S(1)}, u32[]{:S(2)}) copy-start(bf16[128,512]{1,0:T(8,128)(2,1)S(1)} %constant_dynamic-update-slice_fusion.refs_0_.kv_hbm) | copy-start | bytes 393220
  15.6 16.3 %collective-permute-start.2 = (bf16[128,512]{1,0:T(8,128)(2,1)S(1)}, bf16[128,512]{1,0:T(8,128)(2,1)S(1)}, u32[]{:S(2)}, u32[]{:S(2)}) collective-permute-start(bf16[128,512]{1,0:T(8,128)(2,1)S(1)} %constant_dynamic-update-slice_fusion.refs_0_.kv_hbm), channel_id=1, source_target_pairs={{0,2},{1,3},{2,4},{3,5},{4,6},{5,7},{6,8},{7,9},{8,10},{9,11},{10,... | collective-permute-start | bytes 393224 | tf_op jit(solution)/shard_map/ppermute | solution.py:215
  18.7 13.9 %collective-permute-start.3 = (bf16[128,512]{1,0:T(8,128)(2,1)S(1)}, bf16[128,512]{1,0:T(8,128)(2,1)S(1)}, u32[]{:S(2)}, u32[]{:S(2)}) collective-permute-start(bf16[128,512]{1,0:T(8,128)(2,1)S(1)} %constant_dynamic-update-slice_fusion.refs_0_.kv_hbm), channel_id=1, source_target_pairs={{0,4},{1,5},{2,6},{3,7},{4,8},{5,9},{6,10},{7,11},{8,12},{9,13},{1... | collective-permute-start | bytes 393224 | tf_op jit(solution)/shard_map/ppermute | solution.py:215
  22.2 11.1 %collective-permute-start.4 = (bf16[128,512]{1,0:T(8,128)(2,1)S(1)}, bf16[128,512]{1,0:T(8,128)(2,1)S(1)}, u32[]{:S(2)}, u32[]{:S(2)}) collective-permute-start(bf16[128,512]{1,0:T(8,128)(2,1)S(1)} %constant_dynamic-update-slice_fusion.refs_0_.kv_hbm), channel_id=1, source_target_pairs={{0,6},{1,7},{2,8},{3,9},{4,10},{5,11},{6,12},{7,13},{8,14},{9,15},... | collective-permute-start | bytes 393224 | tf_op jit(solution)/shard_map/ppermute | solution.py:215
  26.7 10.9 %collective-permute-start.5 = (bf16[128,512]{1,0:T(8,128)(2,1)S(1)}, bf16[128,512]{1,0:T(8,128)(2,1)S(1)}, u32[]{:S(2)}, u32[]{:S(2)}) collective-permute-start(bf16[128,512]{1,0:T(8,128)(2,1)S(1)} %constant_dynamic-update-slice_fusion.refs_0_.kv_hbm), channel_id=1, source_target_pairs={{0,8},{1,9},{2,10},{3,11},{4,12},{5,13},{6,14},{7,15},{16,24},{17,... | collective-permute-start | bytes 393224 | tf_op jit(solution)/shard_map/ppermute | solution.py:215
  31.9 10.9 %copy-start.7 = (bf16[128,512]{1,0:T(8,128)(2,1)}, bf16[128,512]{1,0:T(8,128)(2,1)S(1)}, u32[]{:S(2)}) copy-start(bf16[128,512]{1,0:T(8,128)(2,1)S(1)} %collective-permute-done.2.refs_1_) | copy-start | bytes 393220
  32.6 10.1 %copy-start.8 = (bf16[128,512]{1,0:T(8,128)(2,1)}, bf16[128,512]{1,0:T(8,128)(2,1)S(1)}, u32[]{:S(2)}) copy-start(bf16[128,512]{1,0:T(8,128)(2,1)S(1)} %collective-permute-done.3.refs_2_) | copy-start | bytes 393220
  33.3 9.4 %copy-start.9 = (bf16[128,512]{1,0:T(8,128)(2,1)}, bf16[128,512]{1,0:T(8,128)(2,1)S(1)}, u32[]{:S(2)}) copy-start(bf16[128,512]{1,0:T(8,128)(2,1)S(1)} %collective-permute-done.4.refs_3_) | copy-start | bytes 393220
  37.6 0.6 copy-start.10
  38.9 3.8 %collective-permute-start.6 = (bf16[640,512]{1,0:T(8,128)(2,1)}, bf16[640,512]{1,0:T(8,128)(2,1)S(1)}, u32[]{:S(2)}, u32[]{:S(2)}) collective-permute-start(bf16[640,512]{1,0:T(8,128)(2,1)} %constant_dynamic-update-slice_fusion.2), channel_id=1, source_target_pairs={{0,1},{1,0},{2,3},{3,2},{4,5},{5,4},{6,7},{7,6},{8,9},{9,8},{10,11... | collective-permute-start | bytes 1966088 | tf_op jit(solution)/shard_map/ppermute | solution.py:219
  39.0 15.2 %collective-permute-start.9 = (bf16[256,1024]{1,0:T(8,128)(2,1)}, bf16[256,1024]{1,0:T(8,128)(2,1)}, u32[]{:S(2)}, u32[]{:S(2)}) collective-permute-start(bf16[256,1024]{1,0:T(8,128)(2,1)} %collective-permute-done.1.refs_2_), channel_id=1, source_target_pairs={{0,224},{32,0},{64,32},{96,64},{128,96},{160,128},{192,160},{224,1... | collective-permute-start | bytes 1572872 | tf_op jit(solution)/shard_map/ppermute | solution.py:226
  40.7 16.7 %collective-permute-start.7 = (bf16[256,1024]{1,0:T(8,128)(2,1)}, bf16[256,1024]{1,0:T(8,128)(2,1)}, u32[]{:S(2)}, u32[]{:S(2)}) collective-permute-start(bf16[256,1024]{1,0:T(8,128)(2,1)} %collective-permute-done.refs_1_), channel_id=1, source_target_pairs={{0,32},{32,64},{64,96},{96,128},{128,160},{160,192},{192,224},{224... | collective-permute-start | bytes 1572872 | tf_op jit(solution)/shard_map/ppermute | solution.py:226
  42.7 0.8 copy-start.6
  46.4 1.0 copy-start.1
  47.5 18.4 %copy-start.2 = (bf16[128,256]{1,0:T(8,128)(2,1)}, bf16[128,256]{1,0:T(8,128)(2,1)S(1)}, u32[]{:S(2)}) copy-start(bf16[128,256]{1,0:T(8,128)(2,1)S(1)} %get-tuple-element.28.attn_hbm) | copy-start | bytes 196612
  48.5 24.4 %all-to-all-start = ((bf16[16,128,256]{2,1,0:T(8,128)(2,1)}), bf16[16,128,256]{2,1,0:T(8,128)(2,1)S(1)}, u32[]{:S(2)}, u32[]{:S(2)}) async-start(bf16[16,128,256]{2,1,0:T(8,128)(2,1)} %broadcast_in_dim.34), calls=%async_computation | async-start | bytes 2097152 | tf_op jit(solution)/shard_map/all_to_all | solution.py:223
  54.1 81.6 %reduce-scatter.2.cloned.1.call-start = ((), (), s32[]{:S(2)}) async-start(), calls=%async_computation.5 | async-start | bytes 4718592 | tf_op jit(solution)/shard_map/reduce_scatter | solution.py:292
  54.2 15.3 %collective-permute-start.10 = (bf16[256,1024]{1,0:T(8,128)(2,1)}, bf16[256,1024]{1,0:T(8,128)(2,1)}, u32[]{:S(2)}, u32[]{:S(2)}) collective-permute-start(bf16[256,1024]{1,0:T(8,128)(2,1)} %collective-permute-done.9.refs_4_), channel_id=1, source_target_pairs={{0,224},{32,0},{64,32},{96,64},{128,96},{160,128},{192,160},{224,1... | collective-permute-start | bytes 1572872 | tf_op jit(solution)/shard_map/ppermute | solution.py:226
  57.4 15.5 %collective-permute-start.8 = (bf16[256,1024]{1,0:T(8,128)(2,1)}, bf16[256,1024]{1,0:T(8,128)(2,1)}, u32[]{:S(2)}, u32[]{:S(2)}) collective-permute-start(bf16[256,1024]{1,0:T(8,128)(2,1)} %collective-permute-done.7.refs_3_), channel_id=1, source_target_pairs={{0,32},{32,64},{64,96},{96,128},{128,160},{160,192},{192,224},{224... | collective-permute-start | bytes 1572872 | tf_op jit(solution)/shard_map/ppermute | solution.py:226
  72.9 1.0 copy-start.3
  82.0 6.9 %copy-start.18 = (bf16[128,1024]{1,0:T(8,128)(2,1)S(1)}, bf16[128,1024]{1,0:T(8,128)(2,1)}, u32[]{:S(2)}) copy-start(bf16[128,1024]{1,0:T(8,128)(2,1)} %param.10) | copy-start | bytes 786436
  82.0 34.7 %copy-start.4 = (bf16[16,128,256]{2,1,0:T(8,128)(2,1)S(1)}, bf16[16,128,256]{2,1,0:T(8,128)(2,1)}, u32[]{:S(2)}) copy-start(bf16[16,128,256]{2,1,0:T(8,128)(2,1)} %copy-done.3) | copy-start | bytes 3145732
  83.4 38.2 %all-to-all-start.1 = ((bf16[16,128,384]{2,1,0:T(8,128)(2,1)}), bf16[16,128,384]{2,1,0:T(8,128)(2,1)}, u32[]{:S(2)}, u32[]{:S(2)}) async-start(bf16[16,128,384]{2,1,0:T(8,128)(2,1)} %broadcast_in_dim.35), calls=%async_computation.2 | async-start | bytes 3145728 | tf_op jit(solution)/shard_map/all_to_all | solution.py:223
  88.9 124.6 %all-gather.5.cloned.1.call-start = ((), (), s32[]{:S(2)}) async-start(), calls=%async_computation.6 | async-start | bytes 4718592 | tf_op jit(solution)/shard_map/all_gather | solution.py:327
  88.9 25.9 %collective-permute-start.11 = (bf16[128,1024]{1,0:T(8,128)(2,1)S(1)}, bf16[128,1024]{1,0:T(8,128)(2,1)}, u32[]{:S(2)}, u32[]{:S(2)}) collective-permute-start(bf16[128,1024]{1,0:T(8,128)(2,1)S(1)} %copy-done.18), channel_id=1, source_target_pairs={{0,16},{16,0},{1,17},{17,1},{2,18},{18,2},{3,19},{19,3},{4,20},{20... | collective-permute-start | bytes 786440 | tf_op jit(solution)/shard_map/ppermute | solution.py:229
  135.8 15.4 %collective-permute-start.12 = (bf16[256,1024]{1,0:T(8,128)(2,1)}, bf16[256,1024]{1,0:T(8,128)(2,1)S(1)}, u32[]{:S(2)}, u32[]{:S(2)}) collective-permute-start(bf16[256,1024]{1,0:T(8,128)(2,1)} %reduce-scatter.2.cloned.1.call-done), channel_id=1, source_target_pairs={{0,16},{16,0},{1,17},{17,1},{2,18},{18,2},{3,19},{19,3},{4,20},{20... | collective-permute-start | bytes 1572872 | tf_op jit(solution)/shard_map/ppermute | solution.py:229
  136.3 9.2 %collective-permute-start.13 = (bf16[128,1024]{1,0:T(8,128)(2,1)}, bf16[128,1024]{1,0:T(8,128)(2,1)S(1)}, u32[]{:S(2)}, u32[]{:S(2)}) collective-permute-start(bf16[128,1024]{1,0:T(8,128)(2,1)} %slice.6), channel_id=1, source_target_pairs={{0,32},{32,64},{64,96},{96,128},{128,160},{160,192},{192,224},{224... | collective-permute-start | bytes 786440 | tf_op jit(solution)/shard_map/ppermute | solution.py:226
  136.3 9.2 %collective-permute-start.14 = (bf16[128,1024]{1,0:T(8,128)(2,1)}, bf16[128,1024]{1,0:T(8,128)(2,1)}, u32[]{:S(2)}, u32[]{:S(2)}) collective-permute-start(bf16[128,1024]{1,0:T(8,128)(2,1)} %slice.7), channel_id=1, source_target_pairs={{0,224},{32,0},{64,32},{96,64},{128,96},{160,128},{192,160},{224,1... | collective-permute-start | bytes 786440 | tf_op jit(solution)/shard_map/ppermute | solution.py:226
  145.6 8.0 %copy-start.13 = (bf16[128,1024]{1,0:T(8,128)(2,1)}, bf16[128,1024]{1,0:T(8,128)(2,1)S(1)}, u32[]{:S(2)}) copy-start(bf16[128,1024]{1,0:T(8,128)(2,1)S(1)} %collective-permute-done.13.refs_7_) | copy-start | bytes 786436
  180.2 0.7 collective-permute-start.15
  180.8 24.5 %copy-start.11 = (bf16[128,256]{1,0:T(8,128)(2,1)}, bf16[128,256]{1,0:T(8,128)(2,1)S(1)}, u32[]{:S(2)}) copy-start(bf16[128,256]{1,0:T(8,128)(2,1)S(1)} %collective-permute-done.15.dattn_hbm.refs_0_) | copy-start | bytes 196612
  180.8 15.4 %collective-permute-start.16 = (bf16[128,256]{1,0:T(8,128)(2,1)S(1)}, bf16[128,256]{1,0:T(8,128)(2,1)S(1)}, u32[]{:S(2)}, u32[]{:S(2)}) collective-permute-start(bf16[128,256]{1,0:T(8,128)(2,1)S(1)} %collective-permute-done.15.dattn_hbm.refs_0_), channel_id=1, source_target_pairs={{2,0},{3,1},{4,2},{5,3},{6,4},{7,5},{8,6},{9,7},{10,8},{11,9},{12,... | collective-permute-start | bytes 196616 | tf_op jit(solution)/shard_map/ppermute | solution.py:215
  182.1 17.5 %collective-permute-start.17 = (bf16[128,256]{1,0:T(8,128)(2,1)S(1)}, bf16[128,256]{1,0:T(8,128)(2,1)S(1)}, u32[]{:S(2)}, u32[]{:S(2)}) collective-permute-start(bf16[128,256]{1,0:T(8,128)(2,1)S(1)} %collective-permute-done.15.dattn_hbm.refs_0_), channel_id=1, source_target_pairs={{4,0},{5,1},{6,2},{7,3},{8,4},{9,5},{10,6},{11,7},{12,8},{13,9},{1... | collective-permute-start | bytes 196616 | tf_op jit(solution)/shard_map/ppermute | solution.py:215
  183.4 18.1 %collective-permute-start.18 = (bf16[128,256]{1,0:T(8,128)(2,1)S(1)}, bf16[128,256]{1,0:T(8,128)(2,1)S(1)}, u32[]{:S(2)}, u32[]{:S(2)}) collective-permute-start(bf16[128,256]{1,0:T(8,128)(2,1)S(1)} %collective-permute-done.15.dattn_hbm.refs_0_), channel_id=1, source_target_pairs={{6,0},{7,1},{8,2},{9,3},{10,4},{11,5},{12,6},{13,7},{14,8},{15,9},... | collective-permute-start | bytes 196616 | tf_op jit(solution)/shard_map/ppermute | solution.py:215
  184.7 20.2 %collective-permute-start.19 = (bf16[128,256]{1,0:T(8,128)(2,1)S(1)}, bf16[128,256]{1,0:T(8,128)(2,1)S(1)}, u32[]{:S(2)}, u32[]{:S(2)}) collective-permute-start(bf16[128,256]{1,0:T(8,128)(2,1)S(1)} %collective-permute-done.15.dattn_hbm.refs_0_), channel_id=1, source_target_pairs={{8,0},{9,1},{10,2},{11,3},{12,4},{13,5},{14,6},{15,7},{24,16},{25,... | collective-permute-start | bytes 196616 | tf_op jit(solution)/shard_map/ppermute | solution.py:215
  196.3 12.2 %copy-start.14 = (bf16[128,256]{1,0:T(8,128)(2,1)}, bf16[128,256]{1,0:T(8,128)(2,1)S(1)}, u32[]{:S(2)}) copy-start(bf16[128,256]{1,0:T(8,128)(2,1)S(1)} %collective-permute-done.16.refs_1_) | copy-start | bytes 196612
  199.7 8.8 %copy-start.15 = (bf16[128,256]{1,0:T(8,128)(2,1)}, bf16[128,256]{1,0:T(8,128)(2,1)S(1)}, u32[]{:S(2)}) copy-start(bf16[128,256]{1,0:T(8,128)(2,1)S(1)} %collective-permute-done.17.refs_2_) | copy-start | bytes 196612
  201.6 6.9 %copy-start.16 = (bf16[128,256]{1,0:T(8,128)(2,1)}, bf16[128,256]{1,0:T(8,128)(2,1)S(1)}, u32[]{:S(2)}) copy-start(bf16[128,256]{1,0:T(8,128)(2,1)S(1)} %collective-permute-done.18.refs_3_) | copy-start | bytes 196612
  204.9 3.5 %copy-start.17 = (bf16[128,256]{1,0:T(8,128)(2,1)}, bf16[128,256]{1,0:T(8,128)(2,1)S(1)}, u32[]{:S(2)}) copy-start(bf16[128,256]{1,0:T(8,128)(2,1)S(1)} %collective-permute-done.19.refs_4_) | copy-start | bytes 196612
  205.0 3.5 %collective-permute-start.20 = (bf16[640,256]{1,0:T(8,128)(2,1)S(1)}, bf16[640,256]{1,0:T(8,128)(2,1)S(1)}, u32[]{:S(2)}, u32[]{:S(2)}) collective-permute-start(bf16[640,256]{1,0:T(8,128)(2,1)S(1)} %constant_dynamic-update-slice_fusion.7), channel_id=1, source_target_pairs={{0,1},{1,0},{2,3},{3,2},{4,5},{5,4},{6,7},{7,6},{8,9},{9,8},{10,11... | collective-permute-start | bytes 983048 | tf_op jit(solution)/shard_map/ppermute | solution.py:219
  208.4 0.7 copy-start.12
Sparse Core Ops, SparseCore 0:
  9.9 47.0 all-gather.2
  82.1 53.5 reduce-scatter.1
  153.6 59.0 all-gather.4

commit v5 on v4

--- a/solution.py
+++ b/solution.py
@@ -158,26 +158,51 @@
         first[by] += size
 
 
-def difference_kernel(attn_ref, proj_ref, teacher_ref, out_ref):
-    out = dot(attn_ref[...], proj_ref[...]) - teacher_ref[...].astype(F32)
-    out_ref[...] = out.astype(BF16)
+def difference_kernel(n, attn_hbm, proj_hbm, teacher_hbm, out_hbm, *refs):
+    attn_ref, proj_ref, teacher_ref, out_ref, sems = refs
+    rows = attn_ref.shape[0] // n
+    parts = [pl.ds(i * rows, rows) for i in range(n)]
+    first = [
+        pltpu.make_async_copy(attn_hbm, attn_ref, sems.at[2 * n]),
+        pltpu.make_async_copy(proj_hbm, proj_ref, sems.at[2 * n + 1]),
+    ]
+    reads = [
+        pltpu.make_async_copy(teacher_hbm.at[p], teacher_ref.at[p], sems.at[i])
+        for i, p in enumerate(parts)
+    ]
+    writes = [
+        pltpu.make_async_copy(out_ref.at[p], out_hbm.at[p], sems.at[n + i])
+        for i, p in enumerate(parts)
+    ]
+    for copy in first + reads:
+        copy.start()
+    for copy in first:
+        copy.wait()
+    for i, p in enumerate(parts):
+        reads[i].wait()
+        out = dot(attn_ref[p, :], proj_ref[...]) - teacher_ref[p, :].astype(F32)
+        out_ref[p, :] = out.astype(BF16)
+        writes[i].start()
+    for copy in writes:
+        copy.wait()
 
 
 def difference(attn, proj, teacher):
-    tokens, depth = attn.shape
-    features = proj.shape[1]
-    step = tokens // 8
+    n = 8
+    hbm = pl.BlockSpec(memory_space=pltpu.HBM)
     return pl.pallas_call(
-        difference_kernel,
-        out_shape=pltpu.HBM((tokens, features), BF16),
-        grid=(tokens // step,),
-        in_specs=[
-            pl.BlockSpec((step, depth), lambda i: (i, 0)),
-            pl.BlockSpec((depth, features), lambda i: (0, 0)),
-            pl.BlockSpec((step, features), lambda i: (i, 0)),
+        functools.partial(difference_kernel, n),
+        out_shape=pltpu.HBM(teacher.shape, BF16),
+        in_specs=[hbm, hbm, hbm],
+        out_specs=hbm,
+        scratch_shapes=[
+            pltpu.VMEM(attn.shape, BF16),
+            pltpu.VMEM(proj.shape, BF16),
+            pltpu.VMEM(teacher.shape, BF16),
+            pltpu.VMEM(teacher.shape, BF16),
+            pltpu.SemaphoreType.DMA((2 * n + 2,)),
         ],
-        out_specs=pl.BlockSpec((step, features), lambda i: (i, 0)),
-        compiler_params=pltpu.CompilerParams(vmem_limit_bytes=16 * 1024 * 1024),
+        compiler_params=pltpu.CompilerParams(vmem_limit_bytes=24 * 1024 * 1024),
     )(*(pltpu.with_memory_space_constraint(x, pltpu.HBM) for x in (attn, proj, teacher)))
 
 

time: 228 us -> 225 us (0.987)
  Pallas kernels: 22.2 us -> 19.1 us
    pallas_call x1, Pallas kernels: 8.07 us -> 4.92 us  [difference(): pl.pallas_call(functools.partial(difference_kernel, n), out_shape=pltpu.H...]
where the time goes in v5:
time: 225 us; the launch traced here: 221 us
  waiting for transfers between devices  78.5 us (35%)
  starting transfers between devices  48.8 us (22%)
  blocking collectives  21.4 us (10%)
  local copies, waits for them, and re-layouts  21.1 us (9%)
  Pallas kernels  19.1 us (8%)
  between operations  14.2 us (6%)
  matrix products  12.7 us (6%)
  other arithmetic  5.46 us (2%)
    ppermute x2, waiting for transfers between devices, swap(): return lax.ppermute(array, 'xh', [(i, i ^ 1) for i in range(n_xh)])  30.6 us
    ppermute x8, waiting for transfers between devices, shift(): return lax.ppermute(array, SP, pairs)  22.5 us
    all_to_all x1, blocking collectives, body(): lax.all_to_all(dattn_part.reshape(n_sp, rows, width), SP, 0, 0, tiled=True)  21.4 us
    ppermute x8, starting transfers between devices, shift(): return lax.ppermute(array, SP, pairs)  20.7 us
    ppermute x8, starting transfers between devices, turn(): return lax.ppermute(array, 'z', [(i, (i + by) % n_z) for i in range(n_z)])  14.5 us
    pallas_call x4, Pallas kernels, call(): pl.pallas_call(kernel, out_shape=out_shape, in_specs=[space(memory_space=...  14.1 us
    ppermute x8, waiting for transfers between devices, turn(): return lax.ppermute(array, 'z', [(i, (i + by) % n_z) for i in range(n_z)])  13.1 us
    dot_general x2, matrix products, dot(): return lax.dot_general(a, b, dims, preferred_element_type=F32)  12.7 us
  transfers between devices with their start and end apart: 26, of which 11 were waited for; matrix products, arithmetic and copies ran while one was open for 13% of the time, Pallas kernels for 6%

profile of v5, /device:TPU:4, one launch (start us, length us, event | category | flops | bytes accessed | tf_op | source)
XLA Modules:
  0.0 221.1 jit_solution(5157009585043032243)
XLA Ops:
  7.2 0.7 all-gather.3.cloned.1.call-update
  7.9 2.0 collective-permute-start
  9.9 4.0 %collective-permute-start.1 = (bf16[256,1024]{1,0:T(8,128)(2,1)}, bf16[256,1024]{1,0:T(8,128)(2,1)}, u32[]{:S(2)}, u32[]{:S(2)}) collective-permute-start(bf16[256,1024]{1,0:T(8,128)(2,1)} %refs_0_.1), channel_id=1, source_target_pairs={{0,224},{32,0},{64,32},{96,64},{128,96},{160,128},{192,160},{224,1... | collective-permute-start | bytes 1572872 | tf_op jit(solution)/shard_map/ppermute | solution.py:251
  13.9 0.8 constant_dynamic-update-slice_fusion.1
  14.8 0.8 constant_dynamic-update-slice_fusion.refs_0_.kv_hbm
  15.6 3.1 %collective-permute-start.2 = (bf16[128,512]{1,0:T(8,128)(2,1)S(1)}, bf16[128,512]{1,0:T(8,128)(2,1)S(1)}, u32[]{:S(2)}, u32[]{:S(2)}) collective-permute-start(bf16[128,512]{1,0:T(8,128)(2,1)S(1)} %constant_dynamic-update-slice_fusion.refs_0_.kv_hbm), channel_id=1, source_target_pairs={{0,2},{1,3},{2,4},{3,5},{4,6},{5,7},{6,8},{7,9},{8,10},{9,11},{10,... | collective-permute-start | bytes 393224 | tf_op jit(solution)/shard_map/ppermute | solution.py:240
  18.7 3.5 %collective-permute-start.3 = (bf16[128,512]{1,0:T(8,128)(2,1)S(1)}, bf16[128,512]{1,0:T(8,128)(2,1)S(1)}, u32[]{:S(2)}, u32[]{:S(2)}) collective-permute-start(bf16[128,512]{1,0:T(8,128)(2,1)S(1)} %constant_dynamic-update-slice_fusion.refs_0_.kv_hbm), channel_id=1, source_target_pairs={{0,4},{1,5},{2,6},{3,7},{4,8},{5,9},{6,10},{7,11},{8,12},{9,13},{1... | collective-permute-start | bytes 393224 | tf_op jit(solution)/shard_map/ppermute | solution.py:240
  22.2 4.5 %collective-permute-start.4 = (bf16[128,512]{1,0:T(8,128)(2,1)S(1)}, bf16[128,512]{1,0:T(8,128)(2,1)S(1)}, u32[]{:S(2)}, u32[]{:S(2)}) collective-permute-start(bf16[128,512]{1,0:T(8,128)(2,1)S(1)} %constant_dynamic-update-slice_fusion.refs_0_.kv_hbm), channel_id=1, source_target_pairs={{0,6},{1,7},{2,8},{3,9},{4,10},{5,11},{6,12},{7,13},{8,14},{9,15},... | collective-permute-start | bytes 393224 | tf_op jit(solution)/shard_map/ppermute | solution.py:240
  26.7 4.5 %collective-permute-start.5 = (bf16[128,512]{1,0:T(8,128)(2,1)S(1)}, bf16[128,512]{1,0:T(8,128)(2,1)S(1)}, u32[]{:S(2)}, u32[]{:S(2)}) collective-permute-start(bf16[128,512]{1,0:T(8,128)(2,1)S(1)} %constant_dynamic-update-slice_fusion.refs_0_.kv_hbm), channel_id=1, source_target_pairs={{0,8},{1,9},{2,10},{3,11},{4,12},{5,13},{6,14},{7,15},{16,24},{17,... | collective-permute-start | bytes 393224 | tf_op jit(solution)/shard_map/ppermute | solution.py:240
  31.2 0.7 constant_dynamic-update-slice_fusion.6
  31.9 0.7 constant_dynamic-update-slice_fusion.5
  32.6 0.7 constant_dynamic-update-slice_fusion.4
  33.3 0.7 constant_dynamic-update-slice_fusion.3
  34.0 3.6 %collective-permute-done.5.refs_4_ = bf16[128,512]{1,0:T(8,128)(2,1)S(1)} collective-permute-done((bf16[128,512]{1,0:T(8,128)(2,1)S(1)}, bf16[128,512]{1,0:T(8,128)(2,1)S(1)}, u32[]{:S(2)}, u32[]{:S(2)}) %collective-permute-start.5) | collective-permute-done | bytes 131104 | tf_op jit(solution)/shard_map/ppermute | solution.py:240
  37.6 0.6 copy-done.10
  38.3 0.7 constant_dynamic-update-slice_fusion.2
  39.0 1.8 collective-permute-start.9
  40.7 0.3 collective-permute-start.7
  41.0 0.8 pad_dynamic-slice_fusion.2
  41.8 0.8 dynamic-slice_bitcast_fusion
  42.8 0.8 copy-done.6
  43.6 2.8 %shard_map.111 = (bf16[128,256]{1,0:T(8,128)(2,1)S(1)}, f32[2,128,1280]{2,1,0:T(8,128)S(1)}, bf16[128,384]{1,0:T(8,128)(2,1)S(1)}) custom-call(s32[1]{0:T(128)} %bitcast.core_ref, s32[128,1]{1,0:T(8,128)S(1)} %copy.13.qseg_ref, s32[1,1280]{1,0:T(1,128)S(1)} %broadcast_in_dim.33.kseg_ref, bf16[128,256]{1,0:T(8,128)(2,1)} %q_hbm.1, ...), custom_call_target="tpu_custom_call" | custom-call | tf_op jit(solution)/shard_map/pallas_call | solution.py:212
  46.4 1.0 copy-done.1
  47.5 1.1 broadcast_in_dim.34
  48.5 5.6 %all-to-all-start = ((bf16[16,128,256]{2,1,0:T(8,128)(2,1)}), bf16[16,128,256]{2,1,0:T(8,128)(2,1)S(1)}, u32[]{:S(2)}, u32[]{:S(2)}) async-start(bf16[16,128,256]{2,1,0:T(8,128)(2,1)} %broadcast_in_dim.34), calls=%async_computation | async-start | bytes 2097152 | tf_op jit(solution)/shard_map/all_to_all | solution.py:248
  54.2 3.2 %collective-permute-start.10 = (bf16[256,1024]{1,0:T(8,128)(2,1)}, bf16[256,1024]{1,0:T(8,128)(2,1)}, u32[]{:S(2)}, u32[]{:S(2)}) collective-permute-start(bf16[256,1024]{1,0:T(8,128)(2,1)} %collective-permute-done.9.refs_4_), channel_id=1, source_target_pairs={{0,224},{32,0},{64,32},{96,64},{128,96},{160,128},{192,160},{224,1... | collective-permute-start | bytes 1572872 | tf_op jit(solution)/shard_map/ppermute | solution.py:251
  57.4 8.4 %convolution_convert_fusion.teacher_hbm = bf16[2048,1024]{1,0:T(8,128)(2,1)} fusion(bf16[2048,1024]{1,0:T(8,128)(2,1)} %all-gather.3.cloned.1.call-done, bf16[1024,1024]{1,0:T(8,128)(2,1)S(1)} %copy-done), kind=kOutput, calls=%fused_computation | convolution fusion | flops 4297064448 | bytes 10485760 | tf_op jit(solution)/shard_map/dot_general | solution.py:24
  65.9 3.6 %collective-permute-done.10.refs_6_ = bf16[256,1024]{1,0:T(8,128)(2,1)} collective-permute-done((bf16[256,1024]{1,0:T(8,128)(2,1)}, bf16[256,1024]{1,0:T(8,128)(2,1)}, u32[]{:S(2)}, u32[]{:S(2)}) %collective-permute-start.10) | collective-permute-done | bytes 524320 | tf_op jit(solution)/shard_map/ppermute | solution.py:251
  69.5 3.4 %collective-permute-done.8.refs_5_ = bf16[256,1024]{1,0:T(8,128)(2,1)} collective-permute-done((bf16[256,1024]{1,0:T(8,128)(2,1)}, bf16[256,1024]{1,0:T(8,128)(2,1)}, u32[]{:S(2)}, u32[]{:S(2)}) %collective-permute-start.8) | collective-permute-done | bytes 524320 | tf_op jit(solution)/shard_map/ppermute | solution.py:251
  72.9 1.0 copy-done.3
  73.9 4.9 %shard_map.112 = bf16[2048,1024]{1,0:T(8,128)(2,1)} custom-call(bf16[2048,256]{1,0:T(8,128)(2,1)} %bitcast.14, bf16[256,1024]{1,0:T(8,128)(2,1)} %refs_0_.1, bf16[2048,1024]{1,0:T(8,128)(2,1)} %convolution_convert_fusion.teacher_hbm), custom_call_target="tpu_custom_call" | custom-call | tf_op jit(solution)/shard_map/pallas_call | solution.py:193
  78.9 1.4 broadcast_in_dim.35
  80.2 5.5 %all-to-all-start.1 = ((bf16[16,128,384]{2,1,0:T(8,128)(2,1)}), bf16[16,128,384]{2,1,0:T(8,128)(2,1)}, u32[]{:S(2)}, u32[]{:S(2)}) async-start(bf16[16,128,384]{2,1,0:T(8,128)(2,1)} %broadcast_in_dim.35), calls=%async_computation.2 | async-start | bytes 3145728 | tf_op jit(solution)/shard_map/all_to_all | solution.py:248
  85.8 1.0 collective-permute-start.11
  86.8 24.9 %collective-permute-done.11 = bf16[128,1024]{1,0:T(8,128)(2,1)} collective-permute-done((bf16[128,1024]{1,0:T(8,128)(2,1)S(1)}, bf16[128,1024]{1,0:T(8,128)(2,1)}, u32[]{:S(2)}, u32[]{:S(2)}) %collective-permute-start.11) | collective-permute-done | bytes 262176 | tf_op jit(solution)/shard_map/ppermute | solution.py:254
  111.7 1.0 broadcast_select_fusion.1
  112.7 0.8 pad_maximum_fusion
  113.6 1.6 pad_dynamic-slice_fusion.1.attn_hbm
  115.1 1.7 slice.6
  116.8 1.7 slice.7
  118.5 2.5 %pad_dynamic-slice_fusion.qx_hbm = bf16[1280,384]{1,0:T(8,128)(2,1)} fusion(s32[]{:T(128)S(6)} %select_n.22, bf16[2048,384]{1,0:T(8,128)(2,1)} %bitcast.3), kind=kLoop, calls=%fused_computation.1 | loop fusion | bytes 2555908 | tf_op jit(solution)/shard_map/dynamic_slice | solution.py:304
  120.9 11.7 %reduce-scatter.2.cloned.1.call-done = bf16[256,1024]{1,0:T(8,128)(2,1)} async-done(((bf16[2048,1024]{1,0:T(8,128)(2,1)}), bf16[256,1024]{1,0:T(8,128)(2,1)}) %reduce-scatter.2.cloned.1.call-update) | async-done | bytes 524304 | tf_op jit(solution)/shard_map/reduce_scatter | solution.py:317
  132.6 0.6 collective-permute-start.12
  133.2 3.2 %collective-permute-start.14 = (bf16[128,1024]{1,0:T(8,128)(2,1)}, bf16[128,1024]{1,0:T(8,128)(2,1)}, u32[]{:S(2)}, u32[]{:S(2)}) collective-permute-start(bf16[128,1024]{1,0:T(8,128)(2,1)} %slice.7), channel_id=1, source_target_pairs={{0,224},{32,0},{64,32},{96,64},{128,96},{160,128},{192,160},{224,1... | collective-permute-start | bytes 786440 | tf_op jit(solution)/shard_map/ppermute | solution.py:251
  136.4 6.0 %collective-permute-done.13.refs_7_ = bf16[128,1024]{1,0:T(8,128)(2,1)S(1)} collective-permute-done((bf16[128,1024]{1,0:T(8,128)(2,1)}, bf16[128,1024]{1,0:T(8,128)(2,1)S(1)}, u32[]{:S(2)}, u32[]{:S(2)}) %collective-permute-start.13) | collective-permute-done | bytes 262176 | tf_op jit(solution)/shard_map/ppermute | solution.py:251
  142.4 5.7 %collective-permute-done.12 = bf16[256,1024]{1,0:T(8,128)(2,1)S(1)} collective-permute-done((bf16[256,1024]{1,0:T(8,128)(2,1)}, bf16[256,1024]{1,0:T(8,128)(2,1)S(1)}, u32[]{:S(2)}, u32[]{:S(2)}) %collective-permute-start.12) | collective-permute-done | bytes 524320 | tf_op jit(solution)/shard_map/ppermute | solution.py:254
  148.1 2.3 %subtract_convert_fusion.dpred_hbm = bf16[256,1024]{1,0:T(8,128)(2,1)} fusion(bf16[256,1024]{1,0:T(8,128)(2,1)} %pad_maximum_fusion, bf16[256,1024]{1,0:T(8,128)(2,1)S(1)} %collective-permute-done.12, bf16[256,1024]{1,0:T(8,128)(2,1)} %reduce-scatter.2.cloned.1.call-done), kind=kLoop, calls=%fused_computation.4 | loop fusion | flops 1572864 | bytes 2097152 | tf_op jit(solution)/shard_map/convert_element_type | solution.py:327
  150.4 3.9 %shard_map.113 = bf16[8,256,256]{2,1,0:T(8,128)(2,1)S(1)} custom-call(s32[1]{0:T(128)} %bitcast.4.z_ref, bf16[256,1024]{1,0:T(8,128)(2,1)} %subtract_convert_fusion.dpred_hbm, bf16[256,1024]{1,0:T(8,128)(2,1)} %refs_0_.1, bf16[256,1024]{1,0:T(8,128)(2,1)} %collective-permute-done.refs_1_, bf16[256,1024]{1,0:T(8,128)(2,1)} %collective-permute-done.1.refs_2_, ...), custom_call_target="tpu_custom_call" | custom-call | tf_op jit(solution)/shard_map/pallas_call | solution.py:212
  154.3 21.4 %all_to_all.15 = bf16[16,128,256]{2,1,0:T(8,128)(2,1)} all-to-all(bf16[16,128,256]{2,1,0:T(8,128)(2,1)S(1)} %bitcast.13), channel_id=1, replica_groups=mesh['z'=8,'xh'=2,'y'=4,'xl'=2,'core'=2] {'y','xl','core'}, dimensions={0} | all-to-all | bytes 2097152 | tf_op jit(solution)/shard_map/all_to_all | solution.py:337
  175.7 1.4 reduce_sum.12
  177.0 0.7 collective-permute-start.15
  177.7 1.3 collective-permute-start.16
  179.0 1.3 collective-permute-start.17
  180.3 1.3 collective-permute-start.18
  181.6 1.3 collective-permute-start.19
  182.9 10.2 %collective-permute-done.16.refs_1_ = bf16[128,256]{1,0:T(8,128)(2,1)S(1)} collective-permute-done((bf16[128,256]{1,0:T(8,128)(2,1)S(1)}, bf16[128,256]{1,0:T(8,128)(2,1)S(1)}, u32[]{:S(2)}, u32[]{:S(2)}) %collective-permute-start.16) | collective-permute-done | bytes 65568 | tf_op jit(solution)/shard_map/ppermute | solution.py:240
  193.2 3.4 %collective-permute-done.17.refs_2_ = bf16[128,256]{1,0:T(8,128)(2,1)S(1)} collective-permute-done((bf16[128,256]{1,0:T(8,128)(2,1)S(1)}, bf16[128,256]{1,0:T(8,128)(2,1)S(1)}, u32[]{:S(2)}, u32[]{:S(2)}) %collective-permute-start.17) | collective-permute-done | bytes 65568 | tf_op jit(solution)/shard_map/ppermute | solution.py:240
  196.5 1.9 collective-permute-done.18.refs_3_
  198.5 3.3 %collective-permute-done.19.refs_4_ = bf16[128,256]{1,0:T(8,128)(2,1)S(1)} collective-permute-done((bf16[128,256]{1,0:T(8,128)(2,1)S(1)}, bf16[128,256]{1,0:T(8,128)(2,1)S(1)}, u32[]{:S(2)}, u32[]{:S(2)}) %collective-permute-start.19) | collective-permute-done | bytes 65568 | tf_op jit(solution)/shard_map/ppermute | solution.py:240
  201.9 0.2 broadcast_in_dim.39.qseg_ref
  202.2 3.1 %shard_map.114 = bf16[128,256]{1,0:T(8,128)(2,1)} custom-call(s32[1]{0:T(128)} %bitcast.core_ref, bf16[128,256]{1,0:T(8,128)(2,1)} %copy-done.11, bf16[128,256]{1,0:T(8,128)(2,1)} %copy-done.2, f32[2,128,1280]{2,1,0:T(8,128)} %copy-done.1, bf16[128,512]{1,0:T(8,128)(2,1)} %copy-done.5, bf16[128,512]{1,0:T(8,128)(2,1)} %copy-done.7, ...), custom_call_target="tpu_custom_call" | custom-call | tf_op jit(solution)/shard_map/pallas_call | solution.py:212
  205.4 0.7 copy-done.12
  206.0 4.3 %shard_map.115 = (bf16[128,256]{1,0:T(8,128)(2,1)}, bf16[128,256]{1,0:T(8,128)(2,1)}) custom-call(s32[1]{0:T(128)} %bitcast.core_ref, s32[1280,1]{1,0:T(8,128)S(1)} %broadcast_in_dim.39.qseg_ref, s32[1,128]{1,0:T(1,128)S(1)} %get-tuple-element.52.kseg_ref, bf16[128,512]{1,0:T(8,128)(2,1)} %copy-done.5, bf16[1280,384]{1,0:T(8,128)(2,1)} %pad_dynamic-slice_fusion.qx_hbm, ...), custom_call_target="tpu_custom_call" | custom-call | tf_op jit(solution)/shard_map/pallas_call | solution.py:212
  210.4 4.3 %convolution_convert_fusion.1 = bf16[256,1024]{1,0:T(8,128)(2,1)} fusion(bf16[2048,256]{1,0:T(8,128)(2,1)S(1)} %bitcast.16, bf16[2048,1024]{1,0:T(8,128)(2,1)} %all-gather.5.cloned.1.call-done), kind=kOutput, calls=%fused_computation.3 | convolution fusion | flops 1074003968 | bytes 5767168 | tf_op jit(solution)/shard_map/dot_general | solution.py:24
  (64 shorter events, 0.5 us)
Async XLA Ops:
  7.2 50.3 %copy-start = (bf16[1024,1024]{1,0:T(8,128)(2,1)S(1)}, bf16[1024,1024]{1,0:T(8,128)(2,1)}, u32[]{:S(2)}) copy-start(bf16[1024,1024]{1,0:T(8,128)(2,1)} %param.9) | copy-start | bytes 6291460
  7.2 50.3 %all-gather.3.cloned.1.call-start = ((), (), s32[]{:S(2)}) async-start(), calls=%async_computation.4 | async-start | bytes 4456448 | tf_op jit(solution)/shard_map/all_gather | solution.py:256
  7.9 18.8 %collective-permute-start = (bf16[256,1024]{1,0:T(8,128)(2,1)}, bf16[256,1024]{1,0:T(8,128)(2,1)}, u32[]{:S(2)}, u32[]{:S(2)}) collective-permute-start(bf16[256,1024]{1,0:T(8,128)(2,1)} %refs_0_.1), channel_id=1, source_target_pairs={{0,32},{32,64},{64,96},{96,128},{128,160},{160,192},{192,224},{224... | collective-permute-start | bytes 1572872 | tf_op jit(solution)/shard_map/ppermute | solution.py:251
  9.9 21.3 %collective-permute-start.1 = (bf16[256,1024]{1,0:T(8,128)(2,1)}, bf16[256,1024]{1,0:T(8,128)(2,1)}, u32[]{:S(2)}, u32[]{:S(2)}) collective-permute-start(bf16[256,1024]{1,0:T(8,128)(2,1)} %refs_0_.1), channel_id=1, source_target_pairs={{0,224},{32,0},{64,32},{96,64},{128,96},{160,128},{192,160},{224,1... | collective-permute-start | bytes 1572872 | tf_op jit(solution)/shard_map/ppermute | solution.py:251
  15.6 27.1 %copy-start.5 = (bf16[128,512]{1,0:T(8,128)(2,1)}, bf16[128,512]{1,0:T(8,128)(2,1)S(1)}, u32[]{:S(2)}) copy-start(bf16[128,512]{1,0:T(8,128)(2,1)S(1)} %constant_dynamic-update-slice_fusion.refs_0_.kv_hbm) | copy-start | bytes 393220
  15.6 16.3 %collective-permute-start.2 = (bf16[128,512]{1,0:T(8,128)(2,1)S(1)}, bf16[128,512]{1,0:T(8,128)(2,1)S(1)}, u32[]{:S(2)}, u32[]{:S(2)}) collective-permute-start(bf16[128,512]{1,0:T(8,128)(2,1)S(1)} %constant_dynamic-update-slice_fusion.refs_0_.kv_hbm), channel_id=1, source_target_pairs={{0,2},{1,3},{2,4},{3,5},{4,6},{5,7},{6,8},{7,9},{8,10},{9,11},{10,... | collective-permute-start | bytes 393224 | tf_op jit(solution)/shard_map/ppermute | solution.py:240
  18.7 13.9 %collective-permute-start.3 = (bf16[128,512]{1,0:T(8,128)(2,1)S(1)}, bf16[128,512]{1,0:T(8,128)(2,1)S(1)}, u32[]{:S(2)}, u32[]{:S(2)}) collective-permute-start(bf16[128,512]{1,0:T(8,128)(2,1)S(1)} %constant_dynamic-update-slice_fusion.refs_0_.kv_hbm), channel_id=1, source_target_pairs={{0,4},{1,5},{2,6},{3,7},{4,8},{5,9},{6,10},{7,11},{8,12},{9,13},{1... | collective-permute-start | bytes 393224 | tf_op jit(solution)/shard_map/ppermute | solution.py:240
  22.2 11.1 %collective-permute-start.4 = (bf16[128,512]{1,0:T(8,128)(2,1)S(1)}, bf16[128,512]{1,0:T(8,128)(2,1)S(1)}, u32[]{:S(2)}, u32[]{:S(2)}) collective-permute-start(bf16[128,512]{1,0:T(8,128)(2,1)S(1)} %constant_dynamic-update-slice_fusion.refs_0_.kv_hbm), channel_id=1, source_target_pairs={{0,6},{1,7},{2,8},{3,9},{4,10},{5,11},{6,12},{7,13},{8,14},{9,15},... | collective-permute-start | bytes 393224 | tf_op jit(solution)/shard_map/ppermute | solution.py:240
  26.7 10.9 %collective-permute-start.5 = (bf16[128,512]{1,0:T(8,128)(2,1)S(1)}, bf16[128,512]{1,0:T(8,128)(2,1)S(1)}, u32[]{:S(2)}, u32[]{:S(2)}) collective-permute-start(bf16[128,512]{1,0:T(8,128)(2,1)S(1)} %constant_dynamic-update-slice_fusion.refs_0_.kv_hbm), channel_id=1, source_target_pairs={{0,8},{1,9},{2,10},{3,11},{4,12},{5,13},{6,14},{7,15},{16,24},{17,... | collective-permute-start | bytes 393224 | tf_op jit(solution)/shard_map/ppermute | solution.py:240
  31.9 10.9 %copy-start.7 = (bf16[128,512]{1,0:T(8,128)(2,1)}, bf16[128,512]{1,0:T(8,128)(2,1)S(1)}, u32[]{:S(2)}) copy-start(bf16[128,512]{1,0:T(8,128)(2,1)S(1)} %collective-permute-done.2.refs_1_) | copy-start | bytes 393220
  32.6 10.1 %copy-start.8 = (bf16[128,512]{1,0:T(8,128)(2,1)}, bf16[128,512]{1,0:T(8,128)(2,1)S(1)}, u32[]{:S(2)}) copy-start(bf16[128,512]{1,0:T(8,128)(2,1)S(1)} %collective-permute-done.3.refs_2_) | copy-start | bytes 393220
  33.3 9.4 %copy-start.9 = (bf16[128,512]{1,0:T(8,128)(2,1)}, bf16[128,512]{1,0:T(8,128)(2,1)S(1)}, u32[]{:S(2)}) copy-start(bf16[128,512]{1,0:T(8,128)(2,1)S(1)} %collective-permute-done.4.refs_3_) | copy-start | bytes 393220
  37.6 0.6 copy-start.10
  38.9 3.8 %collective-permute-start.6 = (bf16[640,512]{1,0:T(8,128)(2,1)}, bf16[640,512]{1,0:T(8,128)(2,1)S(1)}, u32[]{:S(2)}, u32[]{:S(2)}) collective-permute-start(bf16[640,512]{1,0:T(8,128)(2,1)} %constant_dynamic-update-slice_fusion.2), channel_id=1, source_target_pairs={{0,1},{1,0},{2,3},{3,2},{4,5},{5,4},{6,7},{7,6},{8,9},{9,8},{10,11... | collective-permute-start | bytes 1966088 | tf_op jit(solution)/shard_map/ppermute | solution.py:244
  39.0 15.2 %collective-permute-start.9 = (bf16[256,1024]{1,0:T(8,128)(2,1)}, bf16[256,1024]{1,0:T(8,128)(2,1)}, u32[]{:S(2)}, u32[]{:S(2)}) collective-permute-start(bf16[256,1024]{1,0:T(8,128)(2,1)} %collective-permute-done.1.refs_2_), channel_id=1, source_target_pairs={{0,224},{32,0},{64,32},{96,64},{128,96},{160,128},{192,160},{224,1... | collective-permute-start | bytes 1572872 | tf_op jit(solution)/shard_map/ppermute | solution.py:251
  40.7 16.7 %collective-permute-start.7 = (bf16[256,1024]{1,0:T(8,128)(2,1)}, bf16[256,1024]{1,0:T(8,128)(2,1)}, u32[]{:S(2)}, u32[]{:S(2)}) collective-permute-start(bf16[256,1024]{1,0:T(8,128)(2,1)} %collective-permute-done.refs_1_), channel_id=1, source_target_pairs={{0,32},{32,64},{64,96},{96,128},{128,160},{160,192},{192,224},{224... | collective-permute-start | bytes 1572872 | tf_op jit(solution)/shard_map/ppermute | solution.py:251
  42.7 0.8 copy-start.6
  46.4 1.0 copy-start.1
  47.5 18.4 %copy-start.2 = (bf16[128,256]{1,0:T(8,128)(2,1)}, bf16[128,256]{1,0:T(8,128)(2,1)S(1)}, u32[]{:S(2)}) copy-start(bf16[128,256]{1,0:T(8,128)(2,1)S(1)} %get-tuple-element.28.attn_hbm) | copy-start | bytes 196612
  48.5 24.4 %all-to-all-start = ((bf16[16,128,256]{2,1,0:T(8,128)(2,1)}), bf16[16,128,256]{2,1,0:T(8,128)(2,1)S(1)}, u32[]{:S(2)}, u32[]{:S(2)}) async-start(bf16[16,128,256]{2,1,0:T(8,128)(2,1)} %broadcast_in_dim.34), calls=%async_computation | async-start | bytes 2097152 | tf_op jit(solution)/shard_map/all_to_all | solution.py:248
  54.1 78.5 %reduce-scatter.2.cloned.1.call-start = ((), (), s32[]{:S(2)}) async-start(), calls=%async_computation.5 | async-start | bytes 4718592 | tf_op jit(solution)/shard_map/reduce_scatter | solution.py:317
  54.2 15.3 %collective-permute-start.10 = (bf16[256,1024]{1,0:T(8,128)(2,1)}, bf16[256,1024]{1,0:T(8,128)(2,1)}, u32[]{:S(2)}, u32[]{:S(2)}) collective-permute-start(bf16[256,1024]{1,0:T(8,128)(2,1)} %collective-permute-done.9.refs_4_), channel_id=1, source_target_pairs={{0,224},{32,0},{64,32},{96,64},{128,96},{160,128},{192,160},{224,1... | collective-permute-start | bytes 1572872 | tf_op jit(solution)/shard_map/ppermute | solution.py:251
  57.4 15.5 %collective-permute-start.8 = (bf16[256,1024]{1,0:T(8,128)(2,1)}, bf16[256,1024]{1,0:T(8,128)(2,1)}, u32[]{:S(2)}, u32[]{:S(2)}) collective-permute-start(bf16[256,1024]{1,0:T(8,128)(2,1)} %collective-permute-done.7.refs_3_), channel_id=1, source_target_pairs={{0,32},{32,64},{64,96},{96,128},{128,160},{160,192},{192,224},{224... | collective-permute-start | bytes 1572872 | tf_op jit(solution)/shard_map/ppermute | solution.py:251
  72.9 1.0 copy-start.3
  78.8 6.9 %copy-start.18 = (bf16[128,1024]{1,0:T(8,128)(2,1)S(1)}, bf16[128,1024]{1,0:T(8,128)(2,1)}, u32[]{:S(2)}) copy-start(bf16[128,1024]{1,0:T(8,128)(2,1)} %param.10) | copy-start | bytes 786436
  78.9 34.7 %copy-start.4 = (bf16[16,128,256]{2,1,0:T(8,128)(2,1)S(1)}, bf16[16,128,256]{2,1,0:T(8,128)(2,1)}, u32[]{:S(2)}) copy-start(bf16[16,128,256]{2,1,0:T(8,128)(2,1)} %copy-done.3) | copy-start | bytes 3145732
  80.2 38.2 %all-to-all-start.1 = ((bf16[16,128,384]{2,1,0:T(8,128)(2,1)}), bf16[16,128,384]{2,1,0:T(8,128)(2,1)}, u32[]{:S(2)}, u32[]{:S(2)}) async-start(bf16[16,128,384]{2,1,0:T(8,128)(2,1)} %broadcast_in_dim.35), calls=%async_computation.2 | async-start | bytes 3145728 | tf_op jit(solution)/shard_map/all_to_all | solution.py:248
  85.7 124.6 %all-gather.5.cloned.1.call-start = ((), (), s32[]{:S(2)}) async-start(), calls=%async_computation.6 | async-start | bytes 4718592 | tf_op jit(solution)/shard_map/all_gather | solution.py:352
  85.8 25.9 %collective-permute-start.11 = (bf16[128,1024]{1,0:T(8,128)(2,1)S(1)}, bf16[128,1024]{1,0:T(8,128)(2,1)}, u32[]{:S(2)}, u32[]{:S(2)}) collective-permute-start(bf16[128,1024]{1,0:T(8,128)(2,1)S(1)} %copy-done.18), channel_id=1, source_target_pairs={{0,16},{16,0},{1,17},{17,1},{2,18},{18,2},{3,19},{19,3},{4,20},{20... | collective-permute-start | bytes 786440 | tf_op jit(solution)/shard_map/ppermute | solution.py:254
  132.6 15.5 %collective-permute-start.12 = (bf16[256,1024]{1,0:T(8,128)(2,1)}, bf16[256,1024]{1,0:T(8,128)(2,1)S(1)}, u32[]{:S(2)}, u32[]{:S(2)}) collective-permute-start(bf16[256,1024]{1,0:T(8,128)(2,1)} %reduce-scatter.2.cloned.1.call-done), channel_id=1, source_target_pairs={{0,16},{16,0},{1,17},{17,1},{2,18},{18,2},{3,19},{19,3},{4,20},{20... | collective-permute-start | bytes 1572872 | tf_op jit(solution)/shard_map/ppermute | solution.py:254
  133.2 9.2 %collective-permute-start.13 = (bf16[128,1024]{1,0:T(8,128)(2,1)}, bf16[128,1024]{1,0:T(8,128)(2,1)S(1)}, u32[]{:S(2)}, u32[]{:S(2)}) collective-permute-start(bf16[128,1024]{1,0:T(8,128)(2,1)} %slice.6), channel_id=1, source_target_pairs={{0,32},{32,64},{64,96},{96,128},{128,160},{160,192},{192,224},{224... | collective-permute-start | bytes 786440 | tf_op jit(solution)/shard_map/ppermute | solution.py:251
  133.2 9.2 %collective-permute-start.14 = (bf16[128,1024]{1,0:T(8,128)(2,1)}, bf16[128,1024]{1,0:T(8,128)(2,1)}, u32[]{:S(2)}, u32[]{:S(2)}) collective-permute-start(bf16[128,1024]{1,0:T(8,128)(2,1)} %slice.7), channel_id=1, source_target_pairs={{0,224},{32,0},{64,32},{96,64},{128,96},{160,128},{192,160},{224,1... | collective-permute-start | bytes 786440 | tf_op jit(solution)/shard_map/ppermute | solution.py:251
  142.4 8.0 %copy-start.13 = (bf16[128,1024]{1,0:T(8,128)(2,1)}, bf16[128,1024]{1,0:T(8,128)(2,1)S(1)}, u32[]{:S(2)}) copy-start(bf16[128,1024]{1,0:T(8,128)(2,1)S(1)} %collective-permute-done.13.refs_7_) | copy-start | bytes 786436
  177.0 0.7 collective-permute-start.15
  177.7 24.5 %copy-start.11 = (bf16[128,256]{1,0:T(8,128)(2,1)}, bf16[128,256]{1,0:T(8,128)(2,1)S(1)}, u32[]{:S(2)}) copy-start(bf16[128,256]{1,0:T(8,128)(2,1)S(1)} %collective-permute-done.15.dattn_hbm.refs_0_) | copy-start | bytes 196612
  177.7 15.4 %collective-permute-start.16 = (bf16[128,256]{1,0:T(8,128)(2,1)S(1)}, bf16[128,256]{1,0:T(8,128)(2,1)S(1)}, u32[]{:S(2)}, u32[]{:S(2)}) collective-permute-start(bf16[128,256]{1,0:T(8,128)(2,1)S(1)} %collective-permute-done.15.dattn_hbm.refs_0_), channel_id=1, source_target_pairs={{2,0},{3,1},{4,2},{5,3},{6,4},{7,5},{8,6},{9,7},{10,8},{11,9},{12,... | collective-permute-start | bytes 196616 | tf_op jit(solution)/shard_map/ppermute | solution.py:240
  179.0 17.5 %collective-permute-start.17 = (bf16[128,256]{1,0:T(8,128)(2,1)S(1)}, bf16[128,256]{1,0:T(8,128)(2,1)S(1)}, u32[]{:S(2)}, u32[]{:S(2)}) collective-permute-start(bf16[128,256]{1,0:T(8,128)(2,1)S(1)} %collective-permute-done.15.dattn_hbm.refs_0_), channel_id=1, source_target_pairs={{4,0},{5,1},{6,2},{7,3},{8,4},{9,5},{10,6},{11,7},{12,8},{13,9},{1... | collective-permute-start | bytes 196616 | tf_op jit(solution)/shard_map/ppermute | solution.py:240
  180.3 18.1 %collective-permute-start.18 = (bf16[128,256]{1,0:T(8,128)(2,1)S(1)}, bf16[128,256]{1,0:T(8,128)(2,1)S(1)}, u32[]{:S(2)}, u32[]{:S(2)}) collective-permute-start(bf16[128,256]{1,0:T(8,128)(2,1)S(1)} %collective-permute-done.15.dattn_hbm.refs_0_), channel_id=1, source_target_pairs={{6,0},{7,1},{8,2},{9,3},{10,4},{11,5},{12,6},{13,7},{14,8},{15,9},... | collective-permute-start | bytes 196616 | tf_op jit(solution)/shard_map/ppermute | solution.py:240
  181.6 20.2 %collective-permute-start.19 = (bf16[128,256]{1,0:T(8,128)(2,1)S(1)}, bf16[128,256]{1,0:T(8,128)(2,1)S(1)}, u32[]{:S(2)}, u32[]{:S(2)}) collective-permute-start(bf16[128,256]{1,0:T(8,128)(2,1)S(1)} %collective-permute-done.15.dattn_hbm.refs_0_), channel_id=1, source_target_pairs={{8,0},{9,1},{10,2},{11,3},{12,4},{13,5},{14,6},{15,7},{24,16},{25,... | collective-permute-start | bytes 196616 | tf_op jit(solution)/shard_map/ppermute | solution.py:240
  193.2 12.2 %copy-start.14 = (bf16[128,256]{1,0:T(8,128)(2,1)}, bf16[128,256]{1,0:T(8,128)(2,1)S(1)}, u32[]{:S(2)}) copy-start(bf16[128,256]{1,0:T(8,128)(2,1)S(1)} %collective-permute-done.16.refs_1_) | copy-start | bytes 196612
  196.5 8.8 %copy-start.15 = (bf16[128,256]{1,0:T(8,128)(2,1)}, bf16[128,256]{1,0:T(8,128)(2,1)S(1)}, u32[]{:S(2)}) copy-start(bf16[128,256]{1,0:T(8,128)(2,1)S(1)} %collective-permute-done.17.refs_2_) | copy-start | bytes 196612
  198.5 6.9 %copy-start.16 = (bf16[128,256]{1,0:T(8,128)(2,1)}, bf16[128,256]{1,0:T(8,128)(2,1)S(1)}, u32[]{:S(2)}) copy-start(bf16[128,256]{1,0:T(8,128)(2,1)S(1)} %collective-permute-done.18.refs_3_) | copy-start | bytes 196612
  201.8 3.5 %copy-start.17 = (bf16[128,256]{1,0:T(8,128)(2,1)}, bf16[128,256]{1,0:T(8,128)(2,1)S(1)}, u32[]{:S(2)}) copy-start(bf16[128,256]{1,0:T(8,128)(2,1)S(1)} %collective-permute-done.19.refs_4_) | copy-start | bytes 196612
  201.8 3.5 %collective-permute-start.20 = (bf16[640,256]{1,0:T(8,128)(2,1)S(1)}, bf16[640,256]{1,0:T(8,128)(2,1)S(1)}, u32[]{:S(2)}, u32[]{:S(2)}) collective-permute-start(bf16[640,256]{1,0:T(8,128)(2,1)S(1)} %constant_dynamic-update-slice_fusion.7), channel_id=1, source_target_pairs={{0,1},{1,0},{2,3},{3,2},{4,5},{5,4},{6,7},{7,6},{8,9},{9,8},{10,11... | collective-permute-start | bytes 983048 | tf_op jit(solution)/shard_map/ppermute | solution.py:244
  205.3 0.7 copy-start.12
Sparse Core Ops, SparseCore 0:
  9.9 47.0 all-gather.2
  79.0 53.5 reduce-scatter.1
  150.5 59.0 all-gather.4

commit v6 on v3

--- a/solution.py
+++ b/solution.py
@@ -11,7 +11,7 @@
 HEAD_DIM = 128
 SEGMENT_MAX = 1024
 LSE_TERMS = 3
-COPIES = 16
+COPIES = 24
 TP = ("z", "xh")
 SP = ("y", "xl", "core")
 F32 = jnp.float32
@@ -24,15 +24,23 @@
     return lax.dot_general(a, b, dims, preferred_element_type=F32)
 
 
-def fetch(sources, targets, sems):
+def begin(sources, targets, sems, first=0):
     copies = [
-        pltpu.make_async_copy(src, dst, sems.at[i])
+        pltpu.make_async_copy(src, dst, sems.at[first + i])
         for i, (src, dst) in enumerate(zip(sources, targets, strict=True))
     ]
     for copy in copies:
         copy.start()
+    return copies
+
+
+def finish(copies):
     for copy in copies:
         copy.wait()
+
+
+def fetch(sources, targets, sems):
+    finish(begin(sources, targets, sems))
 
 
 def window_parts(core_ref, chips, whole_ref, rows):
@@ -50,7 +58,9 @@
 
 
 def forward_kernel(n, core_ref, qseg_ref, kseg_ref, q_hbm, *refs):
-    kv_hbm, (attn_ref, probs_ref, qx_ref, q_ref, kv_ref, sems) = refs[: n + 1], refs[n + 1 :]
+    kv_hbm, refs = refs[: n + 1], refs[n + 1 :]
+    attn_ref, probs_hbm, qx_ref, q_ref, kv_ref, probs_ref, sems = refs
+    out = []
     rows, width = q_ref.shape
     keys = 2 * rows * n
     chips = range(n - 1, -1, -1)
@@ -76,6 +86,7 @@
         total = jnp.sum(expo, axis=-1, keepdims=True)
         probs = expo / total
         probs_ref[h] = probs
+        out += begin([probs_ref.at[h]], [probs_hbm.at[h]], sems, h)
         attn_ref[:, cols] = dot(probs.astype(BF16), kv_ref[:, vcols]).astype(BF16)
         rest = top + jnp.log(total)
         for t in range(LSE_TERMS):
@@ -84,6 +95,7 @@
             terms = jnp.where(lane == h * LSE_TERMS + t, term, terms)
     qx_ref[:, :width] = q_ref[...]
     qx_ref[:, width:] = terms.astype(BF16)
+    finish(out)
 
 
 def query_grad_kernel(n, core_ref, dattn_hbm, attn_hbm, probs_hbm, *refs):
@@ -146,9 +158,20 @@
         dvalue_ref[:, cols] = dot(probs.astype(BF16), dattn, TN).astype(BF16)
 
 
-def dattn_kernel(n, offsets, z_ref, dpred_hbm, *refs):
-    proj_hbm, (out_ref, dpred_ref, *proj_refs, sems) = refs[: len(offsets)], refs[len(offsets) :]
-    fetch((dpred_hbm, *proj_hbm), (dpred_ref, *proj_refs), sems)
+def loss_kernel(n, offsets, z_ref, *refs):
+    terms_hbm, proj_hbm, refs = refs[:4], refs[4 : 4 + len(offsets)], refs[4 + len(offsets) :]
+    out_ref, dpred_hbm, *terms_refs, dpred_ref = refs[:7]
+    *proj_refs, sems = refs[7:]
+    terms = begin(terms_hbm, terms_refs, sems)
+    copies = begin(proj_hbm, proj_refs, sems, len(terms))
+    finish(terms)
+    first = 0
+    for mine, other in (terms_refs[:2], terms_refs[2:]):
+        diff = (mine[...].astype(F32) + other[...].astype(F32)).astype(BF16)
+        dpred_ref[:, first : first + diff.shape[1]] = diff
+        first += diff.shape[1]
+    copies += begin([dpred_ref], [dpred_hbm], sems, len(terms) + len(copies))
+    finish(copies[:-1])
     first = [0] * n
     for ref, by in zip(proj_refs, offsets, strict=True):
         size = ref.shape[0]
@@ -156,19 +179,77 @@
         out = dot(dpred_ref[...], ref[...], NT).astype(BF16)
         out_ref[z, :, first[by] : first[by] + size] = out
         first[by] += size
-
-
-def call(kernel, out_shape, in_smem, in_vmem, in_hbm, scratch):
+    finish(copies[-1:])
+
+
+def proj_grad_kernel(n, attn_hbm, dpred_hbm, out_hbm, attn_ref, dpred_ref, out_ref, sems):
+    rows = dpred_ref.shape[0] // n
+    parts = [pl.ds(i * rows, rows) for i in range(n)]
+    attn = begin([attn_hbm], [attn_ref], sems)
+    dpred = begin([dpred_hbm.at[p] for p in parts], [dpred_ref.at[p] for p in parts], sems, 1)
+    finish(attn)
+    total = None
+    for p, copy in zip(parts, dpred, strict=True):
+        copy.wait()
+        term = dot(attn_ref[p, :], dpred_ref[p, :], TN)
+        total = term if total is None else total + term
+    out_ref[...] = total.astype(BF16)
+    fetch([out_ref], [out_hbm], sems)
+
+
+def difference_kernel(n, z_ref, xh_ref, attn_hbm, proj_hbm, resid_hbm, teacher_hbm, sum_hbm, *refs):
+    ring_refs, refs = refs[:n], refs[n:]
+    attn_ref, proj_ref, resid_ref, teacher_ref, sum_ref, sems = refs
+    rows = attn_ref.shape[0] // n
+    split = sum_ref.shape[1]
+
+    def at(r):
+        return pl.ds(pl.multiple_of(lax.rem(z_ref[0] + r, n) * rows, rows), rows)
+
+    own = [pl.ds(r * rows, rows) for r in range(n)]
+    first = begin((attn_hbm, proj_hbm, resid_hbm), (attn_ref, proj_ref, resid_ref), sems)
+    reads = begin(
+        [teacher_hbm.at[at(r)] for r in range(n)], [teacher_ref.at[p] for p in own], sems, 3
+    )
+    finish(first)
+    writes = []
+    for r in range(n):
+        reads[r].wait()
+        out = dot(attn_ref[at(r), :], proj_ref[...]) - teacher_ref[own[r], :].astype(F32)
+        if r == 0:
+            resid = resid_ref[...].astype(F32)
+            place = lax.broadcasted_iota(jnp.int32, out.shape, 0) // resid.shape[0]
+            pair = jnp.concatenate([resid] * (rows // resid.shape[0]), axis=0)
+            out = out - jnp.where(place == xh_ref[0], pair, 0.0)
+        out = out.astype(BF16)
+        sum_ref[own[r], :] = out[:, :split]
+        writes += begin([sum_ref.at[own[r]]], [sum_hbm.at[at(r)]], sems, 3 + n + r)
+        ring_refs[r][...] = out[:, split:]
+    finish(writes)
+
+
+def call(kernel, out_shape, in_smem, in_vmem, in_hbm, scratch, loose=()):
     space = pl.BlockSpec
+    out_specs = jax.tree.map(
+        lambda x: space(
+            memory_space=pltpu.VMEM if isinstance(x, jax.ShapeDtypeStruct) else pltpu.HBM
+        ),
+        out_shape,
+    )
+    in_hbm = [
+        x if i in loose else pltpu.with_memory_space_constraint(x, pltpu.HBM)
+        for i, x in enumerate(in_hbm)
+    ]
     return pl.pallas_call(
         kernel,
         out_shape=out_shape,
+        out_specs=out_specs,
         in_specs=[space(memory_space=pltpu.SMEM)] * len(in_smem)
         + [space(memory_space=pltpu.VMEM)] * len(in_vmem)
         + [space(memory_space=pltpu.HBM)] * len(in_hbm),
         scratch_shapes=[pltpu.VMEM(s.shape, s.dtype) for s in scratch]
         + [pltpu.SemaphoreType.DMA((COPIES,))],
-        compiler_params=pltpu.CompilerParams(vmem_limit_bytes=40 * 1024 * 1024),
+        compiler_params=pltpu.CompilerParams(vmem_limit_bytes=20 * 1024 * 1024),
     )(*in_smem, *in_vmem, *in_hbm)
 
 
@@ -211,8 +292,6 @@
 
     def step(up, down):
         k = len(pieces) // 2 + 1
-        if k == n_z // 2:
-            up, down = up[:half], down[half:]
         offsets.extend([n_z - k, k])
         return turn(up, 1), turn(down, -1)
 
@@ -238,15 +317,22 @@
     probs_type = jax.ShapeDtypeStruct((heads, rows, window), F32)
     attn, probs, qx = call(
         functools.partial(forward_kernel, near),
-        (block_type, probs_type, jax.ShapeDtypeStruct((rows, width + HEAD_DIM), BF16)),
+        (
+            block_type,
+            pltpu.HBM(probs_type.shape, F32),
+            jax.ShapeDtypeStruct((rows, width + HEAD_DIM), BF16),
+        ),
         (core_scalar,),
         (own_segments[:, None], key_segments[None, :]),
         (queries, *kv_parts),
-        (block_type, window_kv_type),
+        (block_type, window_kv_type, probs_type),
     )
     attn_all = everywhere(attn)
     up, down = step(up, down)
-    attn_all, qx, up, down = lax.optimization_barrier((attn_all, qx, up, down))
+    pieces += [up, down]
+    up, down = step(up, down)
+    teacher_part = dot(context_all, w_out).astype(BF16)
+    teacher_part, qx, up, down = lax.optimization_barrier((teacher_part, qx, up, down))
     pieces += [up, down]
 
     def after(array):
@@ -255,33 +341,55 @@
 
     qx_after, attn_after = after(everywhere(qx)), after(attn_all)
 
-    resid_other = swap(teacher_resid)
-    resid = jnp.concatenate(
-        [
-            jnp.where(xh == 0, teacher_resid, resid_other),
-            jnp.where(xh == 0, resid_other, teacher_resid),
-        ],
-        axis=0,
-    )
-    part = (dot(attn_all, proj) - dot(context_all, w_out)).astype(BF16)
+    tokens, features = teacher_part.shape
+    split = features * 3 // 4 // 128 * 128
+    pair = n_xh * rows
+    part, *ring = call(
+        functools.partial(difference_kernel, n_z),
+        (
+            pltpu.HBM((tokens, split), BF16),
+            *[jax.ShapeDtypeStruct((pair, features - split), BF16)] * n_z,
+        ),
+        (z[None], xh[None]),
+        (),
+        (attn_all, proj, teacher_resid, teacher_part),
+        (attn_all, proj, teacher_resid, teacher_part, jax.ShapeDtypeStruct((tokens, split), BF16)),
+    )
     part = lax.psum_scatter(part, "z", scatter_dimension=0, tiled=True)
-    while len(pieces) < n_z:
-        up, down = step(up, down)
-        pieces += [up, down]
-    part, resid, up, down, qx_after, attn_after = lax.optimization_barrier(
-        (part, resid, up, down, qx_after, attn_after)
-    )
-    pieces[-2:] = [up, down]
-    diff = (part.astype(F32) + swap(part).astype(F32)) - resid.astype(F32)
-    dpred = diff.astype(BF16)
-
-    dattn_part = call(
-        functools.partial(dattn_kernel, n_z, offsets),
-        jax.ShapeDtypeStruct((n_z, n_xh * rows, width), BF16),
+
+    def plus(*arrays):
+        return sum(x.astype(F32) for x in arrays).astype(BF16)
+
+    right, left = turn(ring[n_z // 2], 1), turn(ring[n_z // 2 + 1], -1)
+    for r in range(n_z // 2 - 1, 0, -1):
+        right = turn(plus(ring[r], right), 1)
+        if r > 1:
+            left = turn(plus(ring[n_z - r + 1], left), -1)
+    ring_sum = plus(ring[0], right, left)
+    ring_other = swap(ring_sum)
+    up, down = up[:half], down[half:]
+    part, ring_other, qx_after, attn_after, up, down = lax.optimization_barrier(
+        (part, ring_other, qx_after, attn_after, up, down)
+    )
+    part_other = swap(part)
+    up, down = step(up, down)
+    part_other, up, down = lax.optimization_barrier((part_other, up, down))
+    pieces += [up, down]
+    dattn_part, dpred = call(
+        functools.partial(loss_kernel, n_z, offsets),
+        (
+            jax.ShapeDtypeStruct((n_z, pair, width), BF16),
+            pltpu.HBM((pair, features), BF16),
+        ),
         (z[None],),
         (),
-        (dpred, *pieces),
-        (dpred, *pieces),
+        (part, part_other, ring_sum, ring_other, *pieces),
+        (
+            *(part, part_other, ring_sum, ring_other),
+            jax.ShapeDtypeStruct((pair, features), BF16),
+            *pieces,
+        ),
+        loose=(1, 2, 3, 4 + len(pieces) - 2, 4 + len(pieces) - 1),
     )
     dattn_parts = lax.all_to_all(dattn_part.reshape(n_sp, rows, width), SP, 0, 0, tiled=True)
     dattn = jnp.sum(dattn_parts.astype(F32), axis=0).astype(BF16)
@@ -299,7 +407,14 @@
     dattn = lax.ppermute(dattn, TP + SP, pairs)
 
     dpred_all = lax.all_gather(dpred, "z", axis=0, tiled=True)
-    proj_grad = dot(attn_all, dpred_all, TN).astype(BF16)
+    proj_grad = call(
+        functools.partial(proj_grad_kernel, 4),
+        pltpu.HBM(proj.shape, BF16),
+        (),
+        (),
+        (attn_all, dpred_all),
+        (attn_all, dpred_all, proj),
+    )
 
     shifted = [shift(dattn, -k) for k in range(1, near)]
     query_grad = call(
@@ -309,7 +424,9 @@
         (),
         (dattn, attn, probs, *kv_parts),
         (block_type, block_type, probs_type, window_kv_type),
-    )
+        loose=(0,),
+    )
+    key_value, query_grad = lax.optimization_barrier((key_value, query_grad))
     key_grad, value_grad = call(
         functools.partial(key_grad_kernel, near),
         (block_type, block_type),
@@ -322,6 +439,7 @@
             window_type,
             window_type,
         ),
+        loose=range(3, 5 + near),
     )
     return proj_grad, query_grad, key_grad, value_grad
 

time: 255 us -> 219 us (0.86)
  waiting for transfers between devices: 95.8 us -> 71.6 us
  local copies, waits for them, and re-layouts: 30.1 us -> 15.8 us
  Pallas kernels: 13.9 us -> 24.8 us
  matrix products: 15.4 us -> 8.4 us
  starting transfers between devices: 52.2 us -> 59 us
  other arithmetic: 6.09 us -> 1.62 us
    ppermute x2, waiting for transfers between devices: 34.4 us -> 6.22 us  [swap(): return lax.ppermute(array, 'xh', [(i, i ^ 1) for i in range(n_xh)])]
    unnamed x61 -> x33, local copies, waits for them, and re-layouts: 18.5 us -> 5.3 us
    pallas_call x4 -> x6, Pallas kernels: 13.9 us -> 24.8 us  [call(): pl.pallas_call(kernel, out_shape=out_shape, out_specs=out_specs, in_specs...]
    ppermute x8 -> x15, waiting for transfers between devices: 23.3 us -> 32.7 us  [turn(): return lax.ppermute(array, 'z', [(i, (i + by) % n_z) for i in range(n_z)])]
    reduce_scatter x1, waiting for transfers between devices: 14.5 us -> 5.25 us  [body(): part = lax.psum_scatter(part, 'z', scatter_dimension=0, tiled=True)]
    ppermute x8 -> x15, starting transfers between devices: 15.8 us -> 24.8 us  [turn(): return lax.ppermute(array, 'z', [(i, (i + by) % n_z) for i in range(n_z)])]
    dot_general x3 -> x1, matrix products: 15.4 us -> 8.4 us  [dot(): return lax.dot_general(a, b, dims, preferred_element_type=F32)]
    all_gather x1, waiting for transfers between devices: 0.02 us -> 3.8 us  [body(): dpred_all = lax.all_gather(dpred, 'z', axis=0, tiled=True)]
  transfers between devices with their start and end apart: 26 -> 33, of which waited for: 12 -> 16; matrix products, arithmetic and copies ran while one was open for 8% -> 11% of each run, Pallas kernels for 6% -> 5%
where the time goes in v6:
time: 219 us; the launch traced here: 217 us
  waiting for transfers between devices  71.6 us (33%)
  starting transfers between devices  59 us (27%)
  Pallas kernels  24.8 us (11%)
  blocking collectives  21.3 us (10%)
  local copies, waits for them, and re-layouts  15.8 us (7%)
  between operations  14.2 us (6%)
  matrix products  8.4 us (4%)
    ppermute x15, waiting for transfers between devices, turn(): return lax.ppermute(array, 'z', [(i, (i + by) % n_z) for i in range(n_z)])  32.7 us
    ppermute x15, starting transfers between devices, turn(): return lax.ppermute(array, 'z', [(i, (i + by) % n_z) for i in range(n_z)])  24.8 us
    pallas_call x6, Pallas kernels, call(): pl.pallas_call(kernel, out_shape=out_shape, out_specs=out_specs, in_specs...  24.8 us
    ppermute x8, waiting for transfers between devices, shift(): return lax.ppermute(array, SP, pairs)  22.5 us
    all_to_all x1, blocking collectives, body(): lax.all_to_all(dattn_part.reshape(n_sp, rows, width), SP, 0, 0, tiled=True)  21.3 us
    ppermute x8, starting transfers between devices, shift(): return lax.ppermute(array, SP, pairs)  20.7 us
    all_to_all x2, starting transfers between devices, everywhere(): lax.all_to_all(copies, SP, 0, 0, tiled=True).reshape(-1, array.shape[1])  11.2 us
    dot_general x1, matrix products, dot(): return lax.dot_general(a, b, dims, preferred_element_type=F32)  8.4 us
  transfers between devices with their start and end apart: 33, of which 16 were waited for; matrix products, arithmetic and copies ran while one was open for 11% of the time, Pallas kernels for 5%

profile of v6, /device:TPU:4, one launch (start us, length us, event | category | flops | bytes accessed | tf_op | source)
XLA Modules:
  0.0 216.7 jit_solution(3894449570074251781)
XLA Ops:
  7.2 0.7 all-gather.3.cloned.1.call-update
  7.9 2.0 collective-permute-start
  9.9 4.0 %collective-permute-start.1 = (bf16[256,1024]{1,0:T(8,128)(2,1)}, bf16[256,1024]{1,0:T(8,128)(2,1)}, u32[]{:S(2)}, u32[]{:S(2)}) collective-permute-start(bf16[256,1024]{1,0:T(8,128)(2,1)} %refs_4_.1), channel_id=1, source_target_pairs={{0,224},{32,0},{64,32},{96,64},{128,96},{160,128},{192,160},{224,1... | collective-permute-start | bytes 1572872 | tf_op jit(solution)/shard_map/ppermute | solution.py:283
  13.9 0.8 constant_dynamic-update-slice_fusion.1
  14.8 0.8 constant_dynamic-update-slice_fusion.refs_0_.kv_hbm
  15.6 3.1 %collective-permute-start.2 = (bf16[128,512]{1,0:T(8,128)(2,1)S(1)}, bf16[128,512]{1,0:T(8,128)(2,1)S(1)}, u32[]{:S(2)}, u32[]{:S(2)}) collective-permute-start(bf16[128,512]{1,0:T(8,128)(2,1)S(1)} %constant_dynamic-update-slice_fusion.refs_0_.kv_hbm), channel_id=1, source_target_pairs={{0,2},{1,3},{2,4},{3,5},{4,6},{5,7},{6,8},{7,9},{8,10},{9,11},{10,... | collective-permute-start | bytes 393224 | tf_op jit(solution)/shard_map/ppermute | solution.py:272
  18.7 3.5 %collective-permute-start.3 = (bf16[128,512]{1,0:T(8,128)(2,1)S(1)}, bf16[128,512]{1,0:T(8,128)(2,1)S(1)}, u32[]{:S(2)}, u32[]{:S(2)}) collective-permute-start(bf16[128,512]{1,0:T(8,128)(2,1)S(1)} %constant_dynamic-update-slice_fusion.refs_0_.kv_hbm), channel_id=1, source_target_pairs={{0,4},{1,5},{2,6},{3,7},{4,8},{5,9},{6,10},{7,11},{8,12},{9,13},{1... | collective-permute-start | bytes 393224 | tf_op jit(solution)/shard_map/ppermute | solution.py:272
  22.2 4.5 %collective-permute-start.4 = (bf16[128,512]{1,0:T(8,128)(2,1)S(1)}, bf16[128,512]{1,0:T(8,128)(2,1)S(1)}, u32[]{:S(2)}, u32[]{:S(2)}) collective-permute-start(bf16[128,512]{1,0:T(8,128)(2,1)S(1)} %constant_dynamic-update-slice_fusion.refs_0_.kv_hbm), channel_id=1, source_target_pairs={{0,6},{1,7},{2,8},{3,9},{4,10},{5,11},{6,12},{7,13},{8,14},{9,15},... | collective-permute-start | bytes 393224 | tf_op jit(solution)/shard_map/ppermute | solution.py:272
  26.7 4.5 %collective-permute-start.5 = (bf16[128,512]{1,0:T(8,128)(2,1)S(1)}, bf16[128,512]{1,0:T(8,128)(2,1)S(1)}, u32[]{:S(2)}, u32[]{:S(2)}) collective-permute-start(bf16[128,512]{1,0:T(8,128)(2,1)S(1)} %constant_dynamic-update-slice_fusion.refs_0_.kv_hbm), channel_id=1, source_target_pairs={{0,8},{1,9},{2,10},{3,11},{4,12},{5,13},{6,14},{7,15},{16,24},{17,... | collective-permute-start | bytes 393224 | tf_op jit(solution)/shard_map/ppermute | solution.py:272
  31.2 0.7 constant_dynamic-update-slice_fusion.6
  31.9 0.7 constant_dynamic-update-slice_fusion.5
  32.6 0.7 constant_dynamic-update-slice_fusion.4
  33.3 0.7 constant_dynamic-update-slice_fusion.3
  34.0 3.6 %collective-permute-done.5.refs_4_ = bf16[128,512]{1,0:T(8,128)(2,1)S(1)} collective-permute-done((bf16[128,512]{1,0:T(8,128)(2,1)S(1)}, bf16[128,512]{1,0:T(8,128)(2,1)S(1)}, u32[]{:S(2)}, u32[]{:S(2)}) %collective-permute-start.5) | collective-permute-done | bytes 131104 | tf_op jit(solution)/shard_map/ppermute | solution.py:272
  37.6 0.7 constant_dynamic-update-slice_fusion.2
  38.3 1.8 collective-permute-start.9
  40.1 0.3 collective-permute-start.7
  40.4 0.8 pad_dynamic-slice_fusion.2
  41.2 0.8 dynamic-slice_bitcast_fusion
  42.1 0.8 copy-done.3
  43.0 3.5 %shard_map.111 = (bf16[128,256]{1,0:T(8,128)(2,1)S(1)}, f32[2,128,1280]{2,1,0:T(8,128)}, bf16[128,384]{1,0:T(8,128)(2,1)S(1)}) custom-call(s32[1]{0:T(128)} %bitcast.core_ref, s32[128,1]{1,0:T(8,128)S(1)} %copy.13.qseg_ref, s32[1,1280]{1,0:T(1,128)S(1)} %broadcast_in_dim.37.kseg_ref, bf16[128,256]{1,0:T(8,128)(2,1)} %q_hbm.1, bf16[128,512]{1,0:T(8,128)(2,1)} %copy-done.2, ...), custom_call_target="tpu_custom_call" | custom-call | tf_op jit(solution)/shard_map/pallas_call | solution.py:243
  46.5 1.1 broadcast_in_dim.38
  47.6 5.7 %all-to-all-start = ((bf16[16,128,256]{2,1,0:T(8,128)(2,1)}), bf16[16,128,256]{2,1,0:T(8,128)(2,1)}, u32[]{:S(2)}, u32[]{:S(2)}) async-start(bf16[16,128,256]{2,1,0:T(8,128)(2,1)} %broadcast_in_dim.38), calls=%async_computation | async-start | bytes 2097152 | tf_op jit(solution)/shard_map/all_to_all | solution.py:280
  53.4 3.2 %collective-permute-start.10 = (bf16[256,1024]{1,0:T(8,128)(2,1)}, bf16[256,1024]{1,0:T(8,128)(2,1)S(1)}, u32[]{:S(2)}, u32[]{:S(2)}) collective-permute-start(bf16[256,1024]{1,0:T(8,128)(2,1)} %collective-permute-done.9.refs_8_), channel_id=1, source_target_pairs={{0,224},{32,0},{64,32},{96,64},{128,96},{160,128},{192,160},{224,1... | collective-permute-start | bytes 1572872 | tf_op jit(solution)/shard_map/ppermute | solution.py:283
  56.6 0.4 all-gather.3.cloned.1.call-done
  56.9 8.4 %convolution_convert_fusion.teacher_hbm = bf16[2048,1024]{1,0:T(8,128)(2,1)} fusion(bf16[2048,1024]{1,0:T(8,128)(2,1)} %all-gather.3.cloned.1.call-done, bf16[1024,1024]{1,0:T(8,128)(2,1)S(1)} %copy-done), kind=kOutput, calls=%fused_computation | convolution fusion | flops 4297064448 | bytes 10485760 | tf_op jit(solution)/shard_map/dot_general | solution.py:24
  65.3 3.2 %collective-permute-done.10.refs_10_ = bf16[256,1024]{1,0:T(8,128)(2,1)S(1)} collective-permute-done((bf16[256,1024]{1,0:T(8,128)(2,1)}, bf16[256,1024]{1,0:T(8,128)(2,1)S(1)}, u32[]{:S(2)}, u32[]{:S(2)}) %collective-permute-start.10) | collective-permute-done | bytes 524320 | tf_op jit(solution)/shard_map/ppermute | solution.py:283
  68.6 3.3 %collective-permute-done.8.refs_9_ = bf16[256,1024]{1,0:T(8,128)(2,1)S(1)} collective-permute-done((bf16[256,1024]{1,0:T(8,128)(2,1)}, bf16[256,1024]{1,0:T(8,128)(2,1)S(1)}, u32[]{:S(2)}, u32[]{:S(2)}) %collective-permute-start.8) | collective-permute-done | bytes 524320 | tf_op jit(solution)/shard_map/ppermute | solution.py:283
  71.9 0.8 copy-done.10
  72.7 5.1 %shard_map.112 = (bf16[2048,768]{1,0:T(8,128)(2,1)}, bf16[256,256]{1,0:T(8,128)(2,1)S(1)}, bf16[256,256]{1,0:T(8,128)(2,1)S(1)}, bf16[256,256]{1,0:T(8,128)(2,1)...) custom-call(s32[1]{0:T(128)} %bitcast.3.z_ref, ...), custom_call_target="tpu_custom_call" | custom-call | tf_op jit(solution)/shard_map/pallas_call | solution.py:243
  77.8 0.3 collective-permute-start.11
  78.0 3.2 %collective-permute-start.15 = (bf16[256,256]{1,0:T(8,128)(2,1)S(1)}, bf16[256,256]{1,0:T(8,128)(2,1)S(1)}, u32[]{:S(2)}, u32[]{:S(2)}) collective-permute-start(bf16[256,256]{1,0:T(8,128)(2,1)S(1)} %get-tuple-element.52), channel_id=1, source_target_pairs={{0,224},{32,0},{64,32},{96,64},{128,96},{160,128},{192,160},{224,1... | collective-permute-start | bytes 393224 | tf_op jit(solution)/shard_map/ppermute | solution.py:283
  81.3 1.4 broadcast_in_dim.41
  82.6 5.5 %all-to-all-start.1 = ((bf16[16,128,384]{2,1,0:T(8,128)(2,1)}), bf16[16,128,384]{2,1,0:T(8,128)(2,1)}, u32[]{:S(2)}, u32[]{:S(2)}) async-start(bf16[16,128,384]{2,1,0:T(8,128)(2,1)} %broadcast_in_dim.41), calls=%async_computation.2 | async-start | bytes 3145728 | tf_op jit(solution)/shard_map/all_to_all | solution.py:280
  88.4 3.3 %collective-permute-start.16 = (bf16[256,256]{1,0:T(8,128)(2,1)S(1)}, bf16[256,256]{1,0:T(8,128)(2,1)S(1)}, u32[]{:S(2)}, u32[]{:S(2)}) collective-permute-start(bf16[256,256]{1,0:T(8,128)(2,1)S(1)} %add_convert_fusion.2), channel_id=1, source_target_pairs={{0,224},{32,0},{64,32},{96,64},{128,96},{160,128},{192,160},{224,1... | collective-permute-start | bytes 393224 | tf_op jit(solution)/shard_map/ppermute | solution.py:283
  91.7 6.7 %collective-permute-done.12 = bf16[256,256]{1,0:T(8,128)(2,1)S(1)} collective-permute-done((bf16[256,256]{1,0:T(8,128)(2,1)S(1)}, bf16[256,256]{1,0:T(8,128)(2,1)S(1)}, u32[]{:S(2)}, u32[]{:S(2)}) %collective-permute-start.12) | collective-permute-done | bytes 131104 | tf_op jit(solution)/shard_map/ppermute | solution.py:283
  98.5 3.3 %collective-permute-start.17 = (bf16[256,256]{1,0:T(8,128)(2,1)S(1)}, bf16[256,256]{1,0:T(8,128)(2,1)S(1)}, u32[]{:S(2)}, u32[]{:S(2)}) collective-permute-start(bf16[256,256]{1,0:T(8,128)(2,1)S(1)} %add_convert_fusion.1), channel_id=1, source_target_pairs={{0,224},{32,0},{64,32},{96,64},{128,96},{160,128},{192,160},{224,1... | collective-permute-start | bytes 393224 | tf_op jit(solution)/shard_map/ppermute | solution.py:283
  101.8 6.7 %collective-permute-done.13 = bf16[256,256]{1,0:T(8,128)(2,1)S(1)} collective-permute-done((bf16[256,256]{1,0:T(8,128)(2,1)S(1)}, bf16[256,256]{1,0:T(8,128)(2,1)S(1)}, u32[]{:S(2)}, u32[]{:S(2)}) %collective-permute-start.13) | collective-permute-done | bytes 131104 | tf_op jit(solution)/shard_map/ppermute | solution.py:283
  108.7 2.1 pad_dynamic-slice_fusion.1.attn_hbm
  110.9 7.6 %collective-permute-done.14 = bf16[256,256]{1,0:T(8,128)(2,1)S(1)} collective-permute-done((bf16[256,256]{1,0:T(8,128)(2,1)S(1)}, bf16[256,256]{1,0:T(8,128)(2,1)S(1)}, u32[]{:S(2)}, u32[]{:S(2)}) %collective-permute-start.14) | collective-permute-done | bytes 131104 | tf_op jit(solution)/shard_map/ppermute | solution.py:283
  118.5 0.9 collective-permute-start.18
  119.5 2.4 %pad_dynamic-slice_fusion.qx_hbm = bf16[1280,384]{1,0:T(8,128)(2,1)} fusion(s32[]{:T(128)S(6)} %select_n.10, bf16[2048,384]{1,0:T(8,128)(2,1)} %bitcast.5), kind=kLoop, calls=%fused_computation.1 | loop fusion | bytes 2555908 | tf_op jit(solution)/shard_map/dynamic_slice | solution.py:340
  121.9 3.2 %collective-permute-done.18.refs_3_ = bf16[256,256]{1,0:T(8,128)(2,1)S(1)} collective-permute-done((bf16[256,256]{1,0:T(8,128)(2,1)S(1)}, bf16[256,256]{1,0:T(8,128)(2,1)S(1)}, u32[]{:S(2)}, u32[]{:S(2)}) %collective-permute-start.18) | collective-permute-done | bytes 131104 | tf_op jit(solution)/shard_map/ppermute | solution.py:286
  125.1 5.2 %reduce-scatter.2.cloned.1.call-done.refs_0_ = bf16[256,768]{1,0:T(8,128)(2,1)} async-done(((bf16[2048,768]{1,0:T(8,128)(2,1)}), bf16[256,768]{1,0:T(8,128)(2,1)}) %reduce-scatter.2.cloned.1.call-update) | async-done | bytes 393232 | tf_op jit(solution)/shard_map/reduce_scatter | solution.py:358
  130.3 0.6 collective-permute-start.19
  131.1 3.0 %collective-permute-start.21 = (bf16[128,1024]{1,0:T(8,128)(2,1)S(1)}, bf16[128,1024]{1,0:T(8,128)(2,1)S(1)}, u32[]{:S(2)}, u32[]{:S(2)}) collective-permute-start(bf16[128,1024]{1,0:T(8,128)(2,1)S(1)} %slice.7), channel_id=1, source_target_pairs={{0,224},{32,0},{64,32},{96,64},{128,96},{160,128},{192,160},{224,1... | collective-permute-start | bytes 786440 | tf_op jit(solution)/shard_map/ppermute | solution.py:283
  134.1 5.2 %collective-permute-done.20.refs_11_ = bf16[128,1024]{1,0:T(8,128)(2,1)S(1)} collective-permute-done((bf16[128,1024]{1,0:T(8,128)(2,1)S(1)}, bf16[128,1024]{1,0:T(8,128)(2,1)S(1)}, u32[]{:S(2)}, u32[]{:S(2)}) %collective-permute-start.20) | collective-permute-done | bytes 262176 | tf_op jit(solution)/shard_map/ppermute | solution.py:283
  139.3 3.0 %collective-permute-done.19.refs_1_ = bf16[256,768]{1,0:T(8,128)(2,1)S(1)} collective-permute-done((bf16[256,768]{1,0:T(8,128)(2,1)}, bf16[256,768]{1,0:T(8,128)(2,1)S(1)}, u32[]{:S(2)}, u32[]{:S(2)}) %collective-permute-start.19) | collective-permute-done | bytes 393248 | tf_op jit(solution)/shard_map/ppermute | solution.py:286
  142.3 4.4 %shard_map.113 = (bf16[8,256,256]{2,1,0:T(8,128)(2,1)S(1)}, bf16[256,1024]{1,0:T(8,128)(2,1)}) custom-call(s32[1]{0:T(128)} %bitcast.3.z_ref, bf16[256,768]{1,0:T(8,128)(2,1)} %reduce-scatter.2.cloned.1.call-done.refs_0_, bf16[256,768]{1,0:T(8,128)(2,1)S(1)} %collective-permute-done.19.refs_1_, bf16[256,256]{1,0:T(8,128)(2,1)S(1)} %add_convert_fusion.refs_2_, ...), custom_call_target="tpu_custom_call" | custom-call | tf_op jit(solution)/shard_map/pallas_call | solution.py:243
  146.7 21.3 %all_to_all.15 = bf16[16,128,256]{2,1,0:T(8,128)(2,1)} all-to-all(bf16[16,128,256]{2,1,0:T(8,128)(2,1)S(1)} %bitcast.12), channel_id=1, replica_groups=mesh['z'=8,'xh'=2,'y'=4,'xl'=2,'core'=2] {'y','xl','core'}, dimensions={0} | all-to-all | bytes 2097152 | tf_op jit(solution)/shard_map/all_to_all | solution.py:394
  168.1 1.4 reduce_sum.12
  169.5 0.7 collective-permute-start.22
  170.1 1.3 collective-permute-start.23
  171.4 1.3 collective-permute-start.24
  172.7 1.3 collective-permute-start.25
  174.0 1.3 collective-permute-start.26
  175.4 10.2 %collective-permute-done.23.refs_1_ = bf16[128,256]{1,0:T(8,128)(2,1)S(1)} collective-permute-done((bf16[128,256]{1,0:T(8,128)(2,1)S(1)}, bf16[128,256]{1,0:T(8,128)(2,1)S(1)}, u32[]{:S(2)}, u32[]{:S(2)}) %collective-permute-start.23) | collective-permute-done | bytes 65568 | tf_op jit(solution)/shard_map/ppermute | solution.py:272
  185.6 3.4 %collective-permute-done.24.refs_2_ = bf16[128,256]{1,0:T(8,128)(2,1)S(1)} collective-permute-done((bf16[128,256]{1,0:T(8,128)(2,1)S(1)}, bf16[128,256]{1,0:T(8,128)(2,1)S(1)}, u32[]{:S(2)}, u32[]{:S(2)}) %collective-permute-start.24) | collective-permute-done | bytes 65568 | tf_op jit(solution)/shard_map/ppermute | solution.py:272
  189.0 1.9 collective-permute-done.25.refs_3_
  190.9 3.4 %collective-permute-done.26.refs_4_ = bf16[128,256]{1,0:T(8,128)(2,1)S(1)} collective-permute-done((bf16[128,256]{1,0:T(8,128)(2,1)S(1)}, bf16[128,256]{1,0:T(8,128)(2,1)S(1)}, u32[]{:S(2)}, u32[]{:S(2)}) %collective-permute-start.26) | collective-permute-done | bytes 65568 | tf_op jit(solution)/shard_map/ppermute | solution.py:272
  194.5 3.3 %shard_map.115 = bf16[128,256]{1,0:T(8,128)(2,1)} custom-call(s32[1]{0:T(128)} %bitcast.core_ref, bf16[128,256]{1,0:T(8,128)(2,1)S(1)} %collective-permute-done.22.dattn_hbm.refs_0_, bf16[128,256]{1,0:T(8,128)(2,1)} %copy-done.1, f32[2,128,1280]{2,1,0:T(8,128)} %get-tuple-element.65.probs_hbm, bf16[128,512]{1,0:T(8,128)(2,1)} %copy-done.2, ...), custom_call_target="tpu_custom_call" | custom-call | tf_op jit(solution)/shard_map/pallas_call | solution.py:243
  197.8 4.3 %shard_map.116 = (bf16[128,256]{1,0:T(8,128)(2,1)}, bf16[128,256]{1,0:T(8,128)(2,1)}) custom-call(s32[1]{0:T(128)} %bitcast.core_ref, s32[1280,1]{1,0:T(8,128)S(1)} %broadcast_in_dim.44.qseg_ref, s32[1,128]{1,0:T(1,128)S(1)} %get-tuple-element.72.kseg_ref, bf16[128,512]{1,0:T(8,128)(2,1)} %copy-done.2, bf16[1280,384]{1,0:T(8,128)(2,1)} %pad_dynamic-slice_fusion.qx_hbm, ...), custom_call_target="tpu_custom_call" | custom-call | tf_op jit(solution)/shard_map/pallas_call | solution.py:243
  202.1 3.8 %all-gather.5.cloned.1.call-done.dpred_hbm = bf16[2048,1024]{1,0:T(8,128)(2,1)} async-done(((bf16[256,1024]{1,0:T(8,128)(2,1)}), bf16[2048,1024]{1,0:T(8,128)(2,1)}) %all-gather.5.cloned.1.call-update) | async-done | bytes 4194320 | tf_op jit(solution)/shard_map/all_gather | solution.py:409
  205.9 4.3 %shard_map.114 = bf16[256,1024]{1,0:T(8,128)(2,1)} custom-call(bf16[2048,256]{1,0:T(8,128)(2,1)} %bitcast.2.attn_hbm, bf16[2048,1024]{1,0:T(8,128)(2,1)} %all-gather.5.cloned.1.call-done.dpred_hbm), custom_call_target="tpu_custom_call" | custom-call | tf_op jit(solution)/shard_map/pallas_call | solution.py:243
  (67 shorter events, 1.4 us)
Async XLA Ops:
  7.2 49.8 %copy-start = (bf16[1024,1024]{1,0:T(8,128)(2,1)S(1)}, bf16[1024,1024]{1,0:T(8,128)(2,1)}, u32[]{:S(2)}) copy-start(bf16[1024,1024]{1,0:T(8,128)(2,1)} %param.9) | copy-start | bytes 6291460
  7.2 49.8 %all-gather.3.cloned.1.call-start = ((), (), s32[]{:S(2)}) async-start(), calls=%async_computation.4 | async-start | bytes 4456448 | tf_op jit(solution)/shard_map/all_gather | solution.py:288
  7.9 18.8 %collective-permute-start = (bf16[256,1024]{1,0:T(8,128)(2,1)}, bf16[256,1024]{1,0:T(8,128)(2,1)}, u32[]{:S(2)}, u32[]{:S(2)}) collective-permute-start(bf16[256,1024]{1,0:T(8,128)(2,1)} %refs_4_.1), channel_id=1, source_target_pairs={{0,32},{32,64},{64,96},{96,128},{128,160},{160,192},{192,224},{224... | collective-permute-start | bytes 1572872 | tf_op jit(solution)/shard_map/ppermute | solution.py:283
  9.9 21.3 %collective-permute-start.1 = (bf16[256,1024]{1,0:T(8,128)(2,1)}, bf16[256,1024]{1,0:T(8,128)(2,1)}, u32[]{:S(2)}, u32[]{:S(2)}) collective-permute-start(bf16[256,1024]{1,0:T(8,128)(2,1)} %refs_4_.1), channel_id=1, source_target_pairs={{0,224},{32,0},{64,32},{96,64},{128,96},{160,128},{192,160},{224,1... | collective-permute-start | bytes 1572872 | tf_op jit(solution)/shard_map/ppermute | solution.py:283
  15.6 26.5 %copy-start.2 = (bf16[128,512]{1,0:T(8,128)(2,1)}, bf16[128,512]{1,0:T(8,128)(2,1)S(1)}, u32[]{:S(2)}) copy-start(bf16[128,512]{1,0:T(8,128)(2,1)S(1)} %constant_dynamic-update-slice_fusion.refs_0_.kv_hbm) | copy-start | bytes 393220
  15.6 16.2 %collective-permute-start.2 = (bf16[128,512]{1,0:T(8,128)(2,1)S(1)}, bf16[128,512]{1,0:T(8,128)(2,1)S(1)}, u32[]{:S(2)}, u32[]{:S(2)}) collective-permute-start(bf16[128,512]{1,0:T(8,128)(2,1)S(1)} %constant_dynamic-update-slice_fusion.refs_0_.kv_hbm), channel_id=1, source_target_pairs={{0,2},{1,3},{2,4},{3,5},{4,6},{5,7},{6,8},{7,9},{8,10},{9,11},{10,... | collective-permute-start | bytes 393224 | tf_op jit(solution)/shard_map/ppermute | solution.py:272
  18.7 13.8 %collective-permute-start.3 = (bf16[128,512]{1,0:T(8,128)(2,1)S(1)}, bf16[128,512]{1,0:T(8,128)(2,1)S(1)}, u32[]{:S(2)}, u32[]{:S(2)}) collective-permute-start(bf16[128,512]{1,0:T(8,128)(2,1)S(1)} %constant_dynamic-update-slice_fusion.refs_0_.kv_hbm), channel_id=1, source_target_pairs={{0,4},{1,5},{2,6},{3,7},{4,8},{5,9},{6,10},{7,11},{8,12},{9,13},{1... | collective-permute-start | bytes 393224 | tf_op jit(solution)/shard_map/ppermute | solution.py:272
  22.2 11.0 %collective-permute-start.4 = (bf16[128,512]{1,0:T(8,128)(2,1)S(1)}, bf16[128,512]{1,0:T(8,128)(2,1)S(1)}, u32[]{:S(2)}, u32[]{:S(2)}) collective-permute-start(bf16[128,512]{1,0:T(8,128)(2,1)S(1)} %constant_dynamic-update-slice_fusion.refs_0_.kv_hbm), channel_id=1, source_target_pairs={{0,6},{1,7},{2,8},{3,9},{4,10},{5,11},{6,12},{7,13},{8,14},{9,15},... | collective-permute-start | bytes 393224 | tf_op jit(solution)/shard_map/ppermute | solution.py:272
  26.7 10.9 %collective-permute-start.5 = (bf16[128,512]{1,0:T(8,128)(2,1)S(1)}, bf16[128,512]{1,0:T(8,128)(2,1)S(1)}, u32[]{:S(2)}, u32[]{:S(2)}) collective-permute-start(bf16[128,512]{1,0:T(8,128)(2,1)S(1)} %constant_dynamic-update-slice_fusion.refs_0_.kv_hbm), channel_id=1, source_target_pairs={{0,8},{1,9},{2,10},{3,11},{4,12},{5,13},{6,14},{7,15},{16,24},{17,... | collective-permute-start | bytes 393224 | tf_op jit(solution)/shard_map/ppermute | solution.py:272
  31.9 10.3 %copy-start.4 = (bf16[128,512]{1,0:T(8,128)(2,1)}, bf16[128,512]{1,0:T(8,128)(2,1)S(1)}, u32[]{:S(2)}) copy-start(bf16[128,512]{1,0:T(8,128)(2,1)S(1)} %collective-permute-done.2.refs_1_) | copy-start | bytes 393220
  32.6 9.6 %copy-start.5 = (bf16[128,512]{1,0:T(8,128)(2,1)}, bf16[128,512]{1,0:T(8,128)(2,1)S(1)}, u32[]{:S(2)}) copy-start(bf16[128,512]{1,0:T(8,128)(2,1)S(1)} %collective-permute-done.3.refs_2_) | copy-start | bytes 393220
  33.3 4.4 %copy-start.6 = (bf16[128,512]{1,0:T(8,128)(2,1)}, bf16[128,512]{1,0:T(8,128)(2,1)S(1)}, u32[]{:S(2)}) copy-start(bf16[128,512]{1,0:T(8,128)(2,1)S(1)} %collective-permute-done.4.refs_3_) | copy-start | bytes 393220
  37.6 0.7 copy-start.7
  38.3 3.8 %collective-permute-start.6 = (bf16[640,512]{1,0:T(8,128)(2,1)}, bf16[640,512]{1,0:T(8,128)(2,1)S(1)}, u32[]{:S(2)}, u32[]{:S(2)}) collective-permute-start(bf16[640,512]{1,0:T(8,128)(2,1)} %constant_dynamic-update-slice_fusion.2), channel_id=1, source_target_pairs={{0,1},{1,0},{2,3},{3,2},{4,5},{5,4},{6,7},{7,6},{8,9},{9,8},{10,11... | collective-permute-start | bytes 1966088 | tf_op jit(solution)/shard_map/ppermute | solution.py:276
  38.3 15.0 %collective-permute-start.9 = (bf16[256,1024]{1,0:T(8,128)(2,1)}, bf16[256,1024]{1,0:T(8,128)(2,1)}, u32[]{:S(2)}, u32[]{:S(2)}) collective-permute-start(bf16[256,1024]{1,0:T(8,128)(2,1)} %collective-permute-done.1.refs_6_), channel_id=1, source_target_pairs={{0,224},{32,0},{64,32},{96,64},{128,96},{160,128},{192,160},{224,1... | collective-permute-start | bytes 1572872 | tf_op jit(solution)/shard_map/ppermute | solution.py:283
  40.1 16.5 %collective-permute-start.7 = (bf16[256,1024]{1,0:T(8,128)(2,1)}, bf16[256,1024]{1,0:T(8,128)(2,1)}, u32[]{:S(2)}, u32[]{:S(2)}) collective-permute-start(bf16[256,1024]{1,0:T(8,128)(2,1)} %collective-permute-done.refs_5_), channel_id=1, source_target_pairs={{0,32},{32,64},{64,96},{96,128},{128,160},{160,192},{192,224},{224... | collective-permute-start | bytes 1572872 | tf_op jit(solution)/shard_map/ppermute | solution.py:283
  42.1 0.9 copy-start.3
  46.5 18.9 %copy-start.1 = (bf16[128,256]{1,0:T(8,128)(2,1)}, bf16[128,256]{1,0:T(8,128)(2,1)S(1)}, u32[]{:S(2)}) copy-start(bf16[128,256]{1,0:T(8,128)(2,1)S(1)} %get-tuple-element.39.attn_hbm) | copy-start | bytes 196612
  47.6 24.3 %all-to-all-start = ((bf16[16,128,256]{2,1,0:T(8,128)(2,1)}), bf16[16,128,256]{2,1,0:T(8,128)(2,1)}, u32[]{:S(2)}, u32[]{:S(2)}) async-start(bf16[16,128,256]{2,1,0:T(8,128)(2,1)} %broadcast_in_dim.38), calls=%async_computation | async-start | bytes 2097152 | tf_op jit(solution)/shard_map/all_to_all | solution.py:280
  53.3 77.0 %reduce-scatter.2.cloned.1.call-start = ((), (), s32[]{:S(2)}) async-start(), calls=%async_computation.5 | async-start | bytes 3538944 | tf_op jit(solution)/shard_map/reduce_scatter | solution.py:358
  53.4 15.2 %collective-permute-start.10 = (bf16[256,1024]{1,0:T(8,128)(2,1)}, bf16[256,1024]{1,0:T(8,128)(2,1)S(1)}, u32[]{:S(2)}, u32[]{:S(2)}) collective-permute-start(bf16[256,1024]{1,0:T(8,128)(2,1)} %collective-permute-done.9.refs_8_), channel_id=1, source_target_pairs={{0,224},{32,0},{64,32},{96,64},{128,96},{160,128},{192,160},{224,1... | collective-permute-start | bytes 1572872 | tf_op jit(solution)/shard_map/ppermute | solution.py:283
  56.6 15.3 %collective-permute-start.8 = (bf16[256,1024]{1,0:T(8,128)(2,1)}, bf16[256,1024]{1,0:T(8,128)(2,1)S(1)}, u32[]{:S(2)}, u32[]{:S(2)}) collective-permute-start(bf16[256,1024]{1,0:T(8,128)(2,1)} %collective-permute-done.7.refs_7_), channel_id=1, source_target_pairs={{0,32},{32,64},{64,96},{96,128},{128,160},{160,192},{192,224},{224... | collective-permute-start | bytes 1572872 | tf_op jit(solution)/shard_map/ppermute | solution.py:283
  68.6 3.3 %copy-start.8 = (bf16[256,1024]{1,0:T(8,128)(2,1)}, bf16[256,1024]{1,0:T(8,128)(2,1)S(1)}, u32[]{:S(2)}) copy-start(bf16[256,1024]{1,0:T(8,128)(2,1)S(1)} %collective-permute-done.10.refs_10_) | copy-start | bytes 1572868
  71.9 0.8 copy-start.10
  77.8 10.4 %collective-permute-start.11 = (bf16[256,256]{1,0:T(8,128)(2,1)S(1)}, bf16[256,256]{1,0:T(8,128)(2,1)S(1)}, u32[]{:S(2)}, u32[]{:S(2)}) collective-permute-start(bf16[256,256]{1,0:T(8,128)(2,1)S(1)} %get-tuple-element.49), channel_id=1, source_target_pairs={{0,32},{32,64},{64,96},{96,128},{128,160},{160,192},{192,224},{224... | collective-permute-start | bytes 393224 | tf_op jit(solution)/shard_map/ppermute | solution.py:283
  78.0 10.3 %collective-permute-start.15 = (bf16[256,256]{1,0:T(8,128)(2,1)S(1)}, bf16[256,256]{1,0:T(8,128)(2,1)S(1)}, u32[]{:S(2)}, u32[]{:S(2)}) collective-permute-start(bf16[256,256]{1,0:T(8,128)(2,1)S(1)} %get-tuple-element.52), channel_id=1, source_target_pairs={{0,224},{32,0},{64,32},{96,64},{128,96},{160,128},{192,160},{224,1... | collective-permute-start | bytes 393224 | tf_op jit(solution)/shard_map/ppermute | solution.py:283
  82.6 36.8 %all-to-all-start.1 = ((bf16[16,128,384]{2,1,0:T(8,128)(2,1)}), bf16[16,128,384]{2,1,0:T(8,128)(2,1)}, u32[]{:S(2)}, u32[]{:S(2)}) async-start(bf16[16,128,384]{2,1,0:T(8,128)(2,1)} %broadcast_in_dim.41), calls=%async_computation.2 | async-start | bytes 3145728 | tf_op jit(solution)/shard_map/all_to_all | solution.py:280
  88.1 117.8 %all-gather.5.cloned.1.call-start = ((), (), s32[]{:S(2)}) async-start(), calls=%async_computation.6 | async-start | bytes 4718592 | tf_op jit(solution)/shard_map/all_gather | solution.py:409
  88.2 22.6 %copy-start.11 = (bf16[256,1024]{1,0:T(8,128)(2,1)S(1)}, bf16[256,1024]{1,0:T(8,128)(2,1)}, u32[]{:S(2)}) copy-start(bf16[256,1024]{1,0:T(8,128)(2,1)} %copy-done.10) | copy-start | bytes 1572868
  88.2 22.6 %copy-start.9 = (bf16[256,1024]{1,0:T(8,128)(2,1)S(1)}, bf16[256,1024]{1,0:T(8,128)(2,1)}, u32[]{:S(2)}) copy-start(bf16[256,1024]{1,0:T(8,128)(2,1)} %copy-done.8) | copy-start | bytes 1572868
  88.2 10.1 %collective-permute-start.12 = (bf16[256,256]{1,0:T(8,128)(2,1)S(1)}, bf16[256,256]{1,0:T(8,128)(2,1)S(1)}, u32[]{:S(2)}, u32[]{:S(2)}) collective-permute-start(bf16[256,256]{1,0:T(8,128)(2,1)S(1)} %add_convert_fusion.5), channel_id=1, source_target_pairs={{0,32},{32,64},{64,96},{96,128},{128,160},{160,192},{192,224},{224... | collective-permute-start | bytes 393224 | tf_op jit(solution)/shard_map/ppermute | solution.py:283
  88.4 10.1 %collective-permute-start.16 = (bf16[256,256]{1,0:T(8,128)(2,1)S(1)}, bf16[256,256]{1,0:T(8,128)(2,1)S(1)}, u32[]{:S(2)}, u32[]{:S(2)}) collective-permute-start(bf16[256,256]{1,0:T(8,128)(2,1)S(1)} %add_convert_fusion.2), channel_id=1, source_target_pairs={{0,224},{32,0},{64,32},{96,64},{128,96},{160,128},{192,160},{224,1... | collective-permute-start | bytes 393224 | tf_op jit(solution)/shard_map/ppermute | solution.py:283
  98.4 10.2 %collective-permute-start.13 = (bf16[256,256]{1,0:T(8,128)(2,1)S(1)}, bf16[256,256]{1,0:T(8,128)(2,1)S(1)}, u32[]{:S(2)}, u32[]{:S(2)}) collective-permute-start(bf16[256,256]{1,0:T(8,128)(2,1)S(1)} %add_convert_fusion.4), channel_id=1, source_target_pairs={{0,32},{32,64},{64,96},{96,128},{128,160},{160,192},{192,224},{224... | collective-permute-start | bytes 393224 | tf_op jit(solution)/shard_map/ppermute | solution.py:283
  98.5 12.3 %collective-permute-start.17 = (bf16[256,256]{1,0:T(8,128)(2,1)S(1)}, bf16[256,256]{1,0:T(8,128)(2,1)S(1)}, u32[]{:S(2)}, u32[]{:S(2)}) collective-permute-start(bf16[256,256]{1,0:T(8,128)(2,1)S(1)} %add_convert_fusion.1), channel_id=1, source_target_pairs={{0,224},{32,0},{64,32},{96,64},{128,96},{160,128},{192,160},{224,1... | collective-permute-start | bytes 393224 | tf_op jit(solution)/shard_map/ppermute | solution.py:283
  108.6 9.9 %collective-permute-start.14 = (bf16[256,256]{1,0:T(8,128)(2,1)S(1)}, bf16[256,256]{1,0:T(8,128)(2,1)S(1)}, u32[]{:S(2)}, u32[]{:S(2)}) collective-permute-start(bf16[256,256]{1,0:T(8,128)(2,1)S(1)} %add_convert_fusion.3), channel_id=1, source_target_pairs={{0,32},{32,64},{64,96},{96,128},{128,160},{160,192},{192,224},{224... | collective-permute-start | bytes 393224 | tf_op jit(solution)/shard_map/ppermute | solution.py:283
  118.5 6.6 %collective-permute-start.18 = (bf16[256,256]{1,0:T(8,128)(2,1)S(1)}, bf16[256,256]{1,0:T(8,128)(2,1)S(1)}, u32[]{:S(2)}, u32[]{:S(2)}) collective-permute-start(bf16[256,256]{1,0:T(8,128)(2,1)S(1)} %add_convert_fusion.refs_2_), channel_id=1, source_target_pairs={{0,16},{16,0},{1,17},{17,1},{2,18},{18,2},{3,19},{19,3},{4,20},{20... | collective-permute-start | bytes 393224 | tf_op jit(solution)/shard_map/ppermute | solution.py:286
  130.3 12.0 %collective-permute-start.19 = (bf16[256,768]{1,0:T(8,128)(2,1)}, bf16[256,768]{1,0:T(8,128)(2,1)S(1)}, u32[]{:S(2)}, u32[]{:S(2)}) collective-permute-start(bf16[256,768]{1,0:T(8,128)(2,1)} %reduce-scatter.2.cloned.1.call-done.refs_0_), channel_id=1, source_target_pairs={{0,16},{16,0},{1,17},{17,1},{2,18},{18,2},{3,19},{19,3},{4,20},{20... | collective-permute-start | bytes 1179656 | tf_op jit(solution)/shard_map/ppermute | solution.py:286
  130.9 8.4 %collective-permute-start.20 = (bf16[128,1024]{1,0:T(8,128)(2,1)S(1)}, bf16[128,1024]{1,0:T(8,128)(2,1)S(1)}, u32[]{:S(2)}, u32[]{:S(2)}) collective-permute-start(bf16[128,1024]{1,0:T(8,128)(2,1)S(1)} %slice.6), channel_id=1, source_target_pairs={{0,32},{32,64},{64,96},{96,128},{128,160},{160,192},{192,224},{224... | collective-permute-start | bytes 786440 | tf_op jit(solution)/shard_map/ppermute | solution.py:283
  131.1 8.2 %collective-permute-start.21 = (bf16[128,1024]{1,0:T(8,128)(2,1)S(1)}, bf16[128,1024]{1,0:T(8,128)(2,1)S(1)}, u32[]{:S(2)}, u32[]{:S(2)}) collective-permute-start(bf16[128,1024]{1,0:T(8,128)(2,1)S(1)} %slice.7), channel_id=1, source_target_pairs={{0,224},{32,0},{64,32},{96,64},{128,96},{160,128},{192,160},{224,1... | collective-permute-start | bytes 786440 | tf_op jit(solution)/shard_map/ppermute | solution.py:283
  169.5 0.7 collective-permute-start.22
  170.1 15.4 %collective-permute-start.23 = (bf16[128,256]{1,0:T(8,128)(2,1)S(1)}, bf16[128,256]{1,0:T(8,128)(2,1)S(1)}, u32[]{:S(2)}, u32[]{:S(2)}) collective-permute-start(bf16[128,256]{1,0:T(8,128)(2,1)S(1)} %collective-permute-done.22.dattn_hbm.refs_0_), channel_id=1, source_target_pairs={{2,0},{3,1},{4,2},{5,3},{6,4},{7,5},{8,6},{9,7},{10,8},{11,9},{12,... | collective-permute-start | bytes 196616 | tf_op jit(solution)/shard_map/ppermute | solution.py:272
  171.4 17.5 %collective-permute-start.24 = (bf16[128,256]{1,0:T(8,128)(2,1)S(1)}, bf16[128,256]{1,0:T(8,128)(2,1)S(1)}, u32[]{:S(2)}, u32[]{:S(2)}) collective-permute-start(bf16[128,256]{1,0:T(8,128)(2,1)S(1)} %collective-permute-done.22.dattn_hbm.refs_0_), channel_id=1, source_target_pairs={{4,0},{5,1},{6,2},{7,3},{8,4},{9,5},{10,6},{11,7},{12,8},{13,9},{1... | collective-permute-start | bytes 196616 | tf_op jit(solution)/shard_map/ppermute | solution.py:272
  172.7 18.1 %collective-permute-start.25 = (bf16[128,256]{1,0:T(8,128)(2,1)S(1)}, bf16[128,256]{1,0:T(8,128)(2,1)S(1)}, u32[]{:S(2)}, u32[]{:S(2)}) collective-permute-start(bf16[128,256]{1,0:T(8,128)(2,1)S(1)} %collective-permute-done.22.dattn_hbm.refs_0_), channel_id=1, source_target_pairs={{6,0},{7,1},{8,2},{9,3},{10,4},{11,5},{12,6},{13,7},{14,8},{15,9},... | collective-permute-start | bytes 196616 | tf_op jit(solution)/shard_map/ppermute | solution.py:272
  174.0 20.2 %collective-permute-start.26 = (bf16[128,256]{1,0:T(8,128)(2,1)S(1)}, bf16[128,256]{1,0:T(8,128)(2,1)S(1)}, u32[]{:S(2)}, u32[]{:S(2)}) collective-permute-start(bf16[128,256]{1,0:T(8,128)(2,1)S(1)} %collective-permute-done.22.dattn_hbm.refs_0_), channel_id=1, source_target_pairs={{8,0},{9,1},{10,2},{11,3},{12,4},{13,5},{14,6},{15,7},{24,16},{25,... | collective-permute-start | bytes 196616 | tf_op jit(solution)/shard_map/ppermute | solution.py:272
  194.2 3.5 %collective-permute-start.27 = (bf16[640,256]{1,0:T(8,128)(2,1)S(1)}, bf16[640,256]{1,0:T(8,128)(2,1)S(1)}, u32[]{:S(2)}, u32[]{:S(2)}) collective-permute-start(bf16[640,256]{1,0:T(8,128)(2,1)S(1)} %constant_dynamic-update-slice_fusion.7), channel_id=1, source_target_pairs={{0,1},{1,0},{2,3},{3,2},{4,5},{5,4},{6,7},{7,6},{8,9},{9,8},{10,11... | collective-permute-start | bytes 983048 | tf_op jit(solution)/shard_map/ppermute | solution.py:276
Sparse Core Ops, SparseCore 0:
  9.9 47.0 all-gather.2
  77.9 52.3 reduce-scatter.1
  146.8 58.9 all-gather.4

commit v7 on v6

--- a/solution.py
+++ b/solution.py
@@ -158,20 +158,25 @@
         dvalue_ref[:, cols] = dot(probs.astype(BF16), dattn, TN).astype(BF16)
 
 
-def loss_kernel(n, offsets, z_ref, *refs):
-    terms_hbm, proj_hbm, refs = refs[:4], refs[4 : 4 + len(offsets)], refs[4 + len(offsets) :]
-    out_ref, dpred_hbm, *terms_refs, dpred_ref = refs[:7]
-    *proj_refs, sems = refs[7:]
+def loss_kernel(*refs):
+    n = (len(refs) - 3) // 4
+    terms_hbm, dpred_hbm, terms_refs = refs[: 2 * n], refs[2 * n], refs[2 * n + 1 : 4 * n + 1]
+    dpred_ref, sems = refs[4 * n + 1 :]
     terms = begin(terms_hbm, terms_refs, sems)
-    copies = begin(proj_hbm, proj_refs, sems, len(terms))
-    finish(terms)
-    first = 0
-    for mine, other in (terms_refs[:2], terms_refs[2:]):
-        diff = (mine[...].astype(F32) + other[...].astype(F32)).astype(BF16)
-        dpred_ref[:, first : first + diff.shape[1]] = diff
-        first += diff.shape[1]
-    copies += begin([dpred_ref], [dpred_hbm], sems, len(terms) + len(copies))
-    finish(copies[:-1])
+    first, out = 0, []
+    for i in range(n):
+        finish(terms[2 * i : 2 * i + 2])
+        mine, other = terms_refs[2 * i : 2 * i + 2]
+        here = pl.ds(first, mine.shape[1])
+        dpred_ref[:, here] = (mine[...].astype(F32) + other[...].astype(F32)).astype(BF16)
+        out += begin([dpred_ref.at[:, here]], [dpred_hbm.at[:, here]], sems, 2 * n + i)
+        first += mine.shape[1]
+    finish(out)
+
+
+def dattn_kernel(n, offsets, z_ref, dpred_hbm, *refs):
+    proj_hbm, (out_ref, dpred_ref, *proj_refs, sems) = refs[: len(offsets)], refs[len(offsets) :]
+    fetch((dpred_hbm, *proj_hbm), (dpred_ref, *proj_refs), sems)
     first = [0] * n
     for ref, by in zip(proj_refs, offsets, strict=True):
         size = ref.shape[0]
@@ -179,7 +184,6 @@
         out = dot(dpred_ref[...], ref[...], NT).astype(BF16)
         out_ref[z, :, first[by] : first[by] + size] = out
         first[by] += size
-    finish(copies[-1:])
 
 
 def proj_grad_kernel(n, attn_hbm, dpred_hbm, out_hbm, attn_ref, dpred_ref, out_ref, sems):
@@ -201,7 +205,7 @@
     ring_refs, refs = refs[:n], refs[n:]
     attn_ref, proj_ref, resid_ref, teacher_ref, sum_ref, sems = refs
     rows = attn_ref.shape[0] // n
-    split = sum_ref.shape[1]
+    last = proj_ref.shape[1] - sum_ref.shape[1]
 
     def at(r):
         return pl.ds(pl.multiple_of(lax.rem(z_ref[0] + r, n) * rows, rows), rows)
@@ -222,9 +226,9 @@
             pair = jnp.concatenate([resid] * (rows // resid.shape[0]), axis=0)
             out = out - jnp.where(place == xh_ref[0], pair, 0.0)
         out = out.astype(BF16)
-        sum_ref[own[r], :] = out[:, :split]
+        sum_ref[own[r], :] = out[:, last:]
         writes += begin([sum_ref.at[own[r]]], [sum_hbm.at[at(r)]], sems, 3 + n + r)
-        ring_refs[r][...] = out[:, split:]
+        ring_refs[r][...] = out[:, :last]
     finish(writes)
 
 
@@ -249,7 +253,7 @@
         + [space(memory_space=pltpu.HBM)] * len(in_hbm),
         scratch_shapes=[pltpu.VMEM(s.shape, s.dtype) for s in scratch]
         + [pltpu.SemaphoreType.DMA((COPIES,))],
-        compiler_params=pltpu.CompilerParams(vmem_limit_bytes=20 * 1024 * 1024),
+        compiler_params=pltpu.CompilerParams(vmem_limit_bytes=14 * 1024 * 1024),
     )(*in_smem, *in_vmem, *in_hbm)
 
 
@@ -326,6 +330,7 @@
         (own_segments[:, None], key_segments[None, :]),
         (queries, *kv_parts),
         (block_type, window_kv_type, probs_type),
+        loose=range(1, 2 + near),
     )
     attn_all = everywhere(attn)
     up, down = step(up, down)
@@ -375,21 +380,24 @@
     up, down = step(up, down)
     part_other, up, down = lax.optimization_barrier((part_other, up, down))
     pieces += [up, down]
-    dattn_part, dpred = call(
-        functools.partial(loss_kernel, n_z, offsets),
-        (
-            jax.ShapeDtypeStruct((n_z, pair, width), BF16),
-            pltpu.HBM((pair, features), BF16),
-        ),
+    pair_type = jax.ShapeDtypeStruct((pair, features), BF16)
+    dpred = call(
+        loss_kernel,
+        pltpu.HBM(pair_type.shape, BF16),
+        (),
+        (),
+        (ring_sum, ring_other, part, part_other),
+        (ring_sum, ring_other, part, part_other, pair_type),
+        loose=(0, 1, 3),
+    )
+    dattn_part = call(
+        functools.partial(dattn_kernel, n_z, offsets),
+        jax.ShapeDtypeStruct((n_z, pair, width), BF16),
         (z[None],),
         (),
-        (part, part_other, ring_sum, ring_other, *pieces),
-        (
-            *(part, part_other, ring_sum, ring_other),
-            jax.ShapeDtypeStruct((pair, features), BF16),
-            *pieces,
-        ),
-        loose=(1, 2, 3, 4 + len(pieces) - 2, 4 + len(pieces) - 1),
+        (dpred, *pieces),
+        (dpred, *pieces),
+        loose=(len(pieces) - 1, len(pieces)),
     )
     dattn_parts = lax.all_to_all(dattn_part.reshape(n_sp, rows, width), SP, 0, 0, tiled=True)
     dattn = jnp.sum(dattn_parts.astype(F32), axis=0).astype(BF16)

time: 219 us -> 217 us (level)
  waiting for transfers between devices: 71.6 us -> 67.1 us
    all_gather x1, waiting for transfers between devices: 3.8 us -> 1.18 us  [body(): dpred_all = lax.all_gather(dpred, 'z', axis=0, tiled=True)]
    pallas_call x6 -> x7, Pallas kernels: 24.8 us -> 26.9 us  [call(): pl.pallas_call(kernel, out_shape=out_shape, out_specs=out_specs, in_specs...]
    unnamed x33 -> x31, local copies, waits for them, and re-layouts: 5.3 us -> 4.34 us
  transfers between devices with their start and end apart: 33 -> 33, of which waited for: 16 -> 15; matrix products, arithmetic and copies ran while one was open for 11% -> 12% of each run, Pallas kernels for 5% -> 7%
where the time goes in v7:
time: 217 us; the launch traced here: 215 us
  waiting for transfers between devices  67.1 us (31%)
  starting transfers between devices  58.9 us (27%)
  Pallas kernels  26.9 us (12%)
  blocking collectives  21.3 us (10%)
  local copies, waits for them, and re-layouts  17.4 us (8%)
  between operations  14.2 us (7%)
  matrix products  8.41 us (4%)
    ppermute x15, waiting for transfers between devices, turn(): return lax.ppermute(array, 'z', [(i, (i + by) % n_z) for i in range(n_z)])  31.4 us
    pallas_call x7, Pallas kernels, call(): pl.pallas_call(kernel, out_shape=out_shape, out_specs=out_specs, in_specs...  26.9 us
    ppermute x15, starting transfers between devices, turn(): return lax.ppermute(array, 'z', [(i, (i + by) % n_z) for i in range(n_z)])  24.8 us
    ppermute x8, waiting for transfers between devices, shift(): return lax.ppermute(array, SP, pairs)  22.5 us
    all_to_all x1, blocking collectives, body(): lax.all_to_all(dattn_part.reshape(n_sp, rows, width), SP, 0, 0, tiled=True)  21.3 us
    ppermute x8, starting transfers between devices, shift(): return lax.ppermute(array, SP, pairs)  20.7 us
    all_to_all x2, starting transfers between devices, everywhere(): lax.all_to_all(copies, SP, 0, 0, tiled=True).reshape(-1, array.shape[1])  11.2 us
    dot_general x1, matrix products, dot(): return lax.dot_general(a, b, dims, preferred_element_type=F32)  8.41 us
  transfers between devices with their start and end apart: 33, of which 15 were waited for; matrix products, arithmetic and copies ran while one was open for 12% of the time, Pallas kernels for 7%

profile of v7, /device:TPU:4, one launch (start us, length us, event | category | flops | bytes accessed | tf_op | source)
XLA Modules:
  0.0 214.6 jit_solution(18402253116979146577)
XLA Ops:
  7.2 0.7 all-gather.3.cloned.1.call-update
  7.9 2.0 collective-permute-start
  9.9 4.0 %collective-permute-start.1 = (bf16[256,1024]{1,0:T(8,128)(2,1)}, bf16[256,1024]{1,0:T(8,128)(2,1)}, u32[]{:S(2)}, u32[]{:S(2)}) collective-permute-start(bf16[256,1024]{1,0:T(8,128)(2,1)} %refs_0_.1), channel_id=1, source_target_pairs={{0,224},{32,0},{64,32},{96,64},{128,96},{160,128},{192,160},{224,1... | collective-permute-start | bytes 1572872 | tf_op jit(solution)/shard_map/ppermute | solution.py:287
  13.9 0.8 constant_dynamic-update-slice_fusion.1
  14.8 0.8 constant_dynamic-update-slice_fusion.refs_0_.kv_hbm
  15.6 3.1 %collective-permute-start.2 = (bf16[128,512]{1,0:T(8,128)(2,1)S(1)}, bf16[128,512]{1,0:T(8,128)(2,1)S(1)}, u32[]{:S(2)}, u32[]{:S(2)}) collective-permute-start(bf16[128,512]{1,0:T(8,128)(2,1)S(1)} %constant_dynamic-update-slice_fusion.refs_0_.kv_hbm), channel_id=1, source_target_pairs={{0,2},{1,3},{2,4},{3,5},{4,6},{5,7},{6,8},{7,9},{8,10},{9,11},{10,... | collective-permute-start | bytes 393224 | tf_op jit(solution)/shard_map/ppermute | solution.py:276
  18.7 3.5 %collective-permute-start.3 = (bf16[128,512]{1,0:T(8,128)(2,1)S(1)}, bf16[128,512]{1,0:T(8,128)(2,1)S(1)}, u32[]{:S(2)}, u32[]{:S(2)}) collective-permute-start(bf16[128,512]{1,0:T(8,128)(2,1)S(1)} %constant_dynamic-update-slice_fusion.refs_0_.kv_hbm), channel_id=1, source_target_pairs={{0,4},{1,5},{2,6},{3,7},{4,8},{5,9},{6,10},{7,11},{8,12},{9,13},{1... | collective-permute-start | bytes 393224 | tf_op jit(solution)/shard_map/ppermute | solution.py:276
  22.2 4.5 %collective-permute-start.4 = (bf16[128,512]{1,0:T(8,128)(2,1)S(1)}, bf16[128,512]{1,0:T(8,128)(2,1)S(1)}, u32[]{:S(2)}, u32[]{:S(2)}) collective-permute-start(bf16[128,512]{1,0:T(8,128)(2,1)S(1)} %constant_dynamic-update-slice_fusion.refs_0_.kv_hbm), channel_id=1, source_target_pairs={{0,6},{1,7},{2,8},{3,9},{4,10},{5,11},{6,12},{7,13},{8,14},{9,15},... | collective-permute-start | bytes 393224 | tf_op jit(solution)/shard_map/ppermute | solution.py:276
  26.7 4.5 %collective-permute-start.5 = (bf16[128,512]{1,0:T(8,128)(2,1)S(1)}, bf16[128,512]{1,0:T(8,128)(2,1)S(1)}, u32[]{:S(2)}, u32[]{:S(2)}) collective-permute-start(bf16[128,512]{1,0:T(8,128)(2,1)S(1)} %constant_dynamic-update-slice_fusion.refs_0_.kv_hbm), channel_id=1, source_target_pairs={{0,8},{1,9},{2,10},{3,11},{4,12},{5,13},{6,14},{7,15},{16,24},{17,... | collective-permute-start | bytes 393224 | tf_op jit(solution)/shard_map/ppermute | solution.py:276
  31.2 0.7 constant_dynamic-update-slice_fusion.6
  31.9 0.7 constant_dynamic-update-slice_fusion.5
  32.6 0.7 constant_dynamic-update-slice_fusion.4
  33.3 0.7 constant_dynamic-update-slice_fusion.3
  34.0 3.6 %collective-permute-done.5.refs_4_ = bf16[128,512]{1,0:T(8,128)(2,1)S(1)} collective-permute-done((bf16[128,512]{1,0:T(8,128)(2,1)S(1)}, bf16[128,512]{1,0:T(8,128)(2,1)S(1)}, u32[]{:S(2)}, u32[]{:S(2)}) %collective-permute-start.5) | collective-permute-done | bytes 131104 | tf_op jit(solution)/shard_map/ppermute | solution.py:276
  37.6 0.7 constant_dynamic-update-slice_fusion.2
  38.4 1.8 collective-permute-start.9
  40.1 0.3 collective-permute-start.7
  40.4 1.4 pad_dynamic-slice_fusion.2
  41.8 0.8 dynamic-slice_bitcast_fusion
  42.7 3.8 %shard_map.111 = (bf16[128,256]{1,0:T(8,128)(2,1)S(1)}, f32[2,128,1280]{2,1,0:T(8,128)}, bf16[128,384]{1,0:T(8,128)(2,1)S(1)}) custom-call(s32[1]{0:T(128)} %bitcast.core_ref, s32[128,1]{1,0:T(8,128)S(1)} %copy.13.qseg_ref, s32[1,1280]{1,0:T(1,128)S(1)} %broadcast_in_dim.37.kseg_ref, bf16[128,256]{1,0:T(8,128)(2,1)} %q_hbm.1, ...), custom_call_target="tpu_custom_call" | custom-call | tf_op jit(solution)/shard_map/pallas_call | solution.py:247
  46.6 0.6 copy-done.8
  47.2 1.1 broadcast_in_dim.38
  48.3 5.7 %all-to-all-start = ((bf16[16,128,256]{2,1,0:T(8,128)(2,1)}), bf16[16,128,256]{2,1,0:T(8,128)(2,1)}, u32[]{:S(2)}, u32[]{:S(2)}) async-start(bf16[16,128,256]{2,1,0:T(8,128)(2,1)} %broadcast_in_dim.38), calls=%async_computation | async-start | bytes 2097152 | tf_op jit(solution)/shard_map/all_to_all | solution.py:284
  54.1 3.2 %collective-permute-start.10 = (bf16[256,1024]{1,0:T(8,128)(2,1)}, bf16[256,1024]{1,0:T(8,128)(2,1)}, u32[]{:S(2)}, u32[]{:S(2)}) collective-permute-start(bf16[256,1024]{1,0:T(8,128)(2,1)} %collective-permute-done.9.refs_4_), channel_id=1, source_target_pairs={{0,224},{32,0},{64,32},{96,64},{128,96},{160,128},{192,160},{224,1... | collective-permute-start | bytes 1572872 | tf_op jit(solution)/shard_map/ppermute | solution.py:287
  57.3 8.4 %convolution_convert_fusion.teacher_hbm = bf16[2048,1024]{1,0:T(8,128)(2,1)} fusion(bf16[2048,1024]{1,0:T(8,128)(2,1)} %all-gather.3.cloned.1.call-done, bf16[1024,1024]{1,0:T(8,128)(2,1)S(1)} %copy-done), kind=kOutput, calls=%fused_computation | convolution fusion | flops 4297064448 | bytes 10485760 | tf_op jit(solution)/shard_map/dot_general | solution.py:24
  65.7 3.6 %collective-permute-done.10.refs_6_ = bf16[256,1024]{1,0:T(8,128)(2,1)} collective-permute-done((bf16[256,1024]{1,0:T(8,128)(2,1)}, bf16[256,1024]{1,0:T(8,128)(2,1)}, u32[]{:S(2)}, u32[]{:S(2)}) %collective-permute-start.10) | collective-permute-done | bytes 524320 | tf_op jit(solution)/shard_map/ppermute | solution.py:287
  69.3 3.4 %collective-permute-done.8.refs_5_ = bf16[256,1024]{1,0:T(8,128)(2,1)} collective-permute-done((bf16[256,1024]{1,0:T(8,128)(2,1)}, bf16[256,1024]{1,0:T(8,128)(2,1)}, u32[]{:S(2)}, u32[]{:S(2)}) %collective-permute-start.8) | collective-permute-done | bytes 524320 | tf_op jit(solution)/shard_map/ppermute | solution.py:287
  72.7 5.1 %shard_map.112 = (bf16[2048,768]{1,0:T(8,128)(2,1)}, bf16[256,256]{1,0:T(8,128)(2,1)S(1)}, bf16[256,256]{1,0:T(8,128)(2,1)S(1)}, bf16[256,256]{1,0:T(8,128)(2,1)...) custom-call(s32[1]{0:T(128)} %bitcast.3.z_ref, ...), custom_call_target="tpu_custom_call" | custom-call | tf_op jit(solution)/shard_map/pallas_call | solution.py:247
  77.8 0.3 collective-permute-start.11
  78.1 3.2 %collective-permute-start.15 = (bf16[256,256]{1,0:T(8,128)(2,1)S(1)}, bf16[256,256]{1,0:T(8,128)(2,1)S(1)}, u32[]{:S(2)}, u32[]{:S(2)}) collective-permute-start(bf16[256,256]{1,0:T(8,128)(2,1)S(1)} %get-tuple-element.49), channel_id=1, source_target_pairs={{0,224},{32,0},{64,32},{96,64},{128,96},{160,128},{192,160},{224,1... | collective-permute-start | bytes 393224 | tf_op jit(solution)/shard_map/ppermute | solution.py:287
  81.3 1.4 broadcast_in_dim.41
  82.7 5.5 %all-to-all-start.1 = ((bf16[16,128,384]{2,1,0:T(8,128)(2,1)}), bf16[16,128,384]{2,1,0:T(8,128)(2,1)}, u32[]{:S(2)}, u32[]{:S(2)}) async-start(bf16[16,128,384]{2,1,0:T(8,128)(2,1)} %broadcast_in_dim.41), calls=%async_computation.2 | async-start | bytes 3145728 | tf_op jit(solution)/shard_map/all_to_all | solution.py:284
  88.4 3.3 %collective-permute-start.16 = (bf16[256,256]{1,0:T(8,128)(2,1)S(1)}, bf16[256,256]{1,0:T(8,128)(2,1)S(1)}, u32[]{:S(2)}, u32[]{:S(2)}) collective-permute-start(bf16[256,256]{1,0:T(8,128)(2,1)S(1)} %add_convert_fusion.2), channel_id=1, source_target_pairs={{0,224},{32,0},{64,32},{96,64},{128,96},{160,128},{192,160},{224,1... | collective-permute-start | bytes 393224 | tf_op jit(solution)/shard_map/ppermute | solution.py:287
  91.8 6.7 %collective-permute-done.12 = bf16[256,256]{1,0:T(8,128)(2,1)S(1)} collective-permute-done((bf16[256,256]{1,0:T(8,128)(2,1)S(1)}, bf16[256,256]{1,0:T(8,128)(2,1)S(1)}, u32[]{:S(2)}, u32[]{:S(2)}) %collective-permute-start.12) | collective-permute-done | bytes 131104 | tf_op jit(solution)/shard_map/ppermute | solution.py:287
  98.6 3.3 %collective-permute-start.17 = (bf16[256,256]{1,0:T(8,128)(2,1)S(1)}, bf16[256,256]{1,0:T(8,128)(2,1)S(1)}, u32[]{:S(2)}, u32[]{:S(2)}) collective-permute-start(bf16[256,256]{1,0:T(8,128)(2,1)S(1)} %add_convert_fusion.1), channel_id=1, source_target_pairs={{0,224},{32,0},{64,32},{96,64},{128,96},{160,128},{192,160},{224,1... | collective-permute-start | bytes 393224 | tf_op jit(solution)/shard_map/ppermute | solution.py:287
  101.9 6.7 %collective-permute-done.13 = bf16[256,256]{1,0:T(8,128)(2,1)S(1)} collective-permute-done((bf16[256,256]{1,0:T(8,128)(2,1)S(1)}, bf16[256,256]{1,0:T(8,128)(2,1)S(1)}, u32[]{:S(2)}, u32[]{:S(2)}) %collective-permute-start.13) | collective-permute-done | bytes 131104 | tf_op jit(solution)/shard_map/ppermute | solution.py:287
  108.7 2.1 pad_dynamic-slice_fusion.1.attn_hbm
  110.9 1.0 slice.6
  111.8 1.0 slice.7
  112.8 5.7 %collective-permute-done.14 = bf16[256,256]{1,0:T(8,128)(2,1)S(1)} collective-permute-done((bf16[256,256]{1,0:T(8,128)(2,1)S(1)}, bf16[256,256]{1,0:T(8,128)(2,1)S(1)}, u32[]{:S(2)}, u32[]{:S(2)}) %collective-permute-start.14) | collective-permute-done | bytes 131104 | tf_op jit(solution)/shard_map/ppermute | solution.py:287
  118.6 0.9 collective-permute-start.18
  119.5 2.5 %pad_dynamic-slice_fusion.qx_hbm = bf16[1280,384]{1,0:T(8,128)(2,1)} fusion(s32[]{:T(128)S(6)} %select_n.10, bf16[2048,384]{1,0:T(8,128)(2,1)} %bitcast.5), kind=kLoop, calls=%fused_computation.1 | loop fusion | bytes 2555908 | tf_op jit(solution)/shard_map/dynamic_slice | solution.py:345
  122.0 3.2 %collective-permute-done.18.refs_1_ = bf16[256,256]{1,0:T(8,128)(2,1)S(1)} collective-permute-done((bf16[256,256]{1,0:T(8,128)(2,1)S(1)}, bf16[256,256]{1,0:T(8,128)(2,1)S(1)}, u32[]{:S(2)}, u32[]{:S(2)}) %collective-permute-start.18) | collective-permute-done | bytes 131104 | tf_op jit(solution)/shard_map/ppermute | solution.py:290
  125.2 5.1 %reduce-scatter.2.cloned.1.call-done.refs_2_ = bf16[256,768]{1,0:T(8,128)(2,1)} async-done(((bf16[2048,768]{1,0:T(8,128)(2,1)}), bf16[256,768]{1,0:T(8,128)(2,1)}) %reduce-scatter.2.cloned.1.call-update) | async-done | bytes 393232 | tf_op jit(solution)/shard_map/reduce_scatter | solution.py:363
  130.3 0.5 collective-permute-start.19
  131.1 3.0 %collective-permute-start.21 = (bf16[128,1024]{1,0:T(8,128)(2,1)S(1)}, bf16[128,1024]{1,0:T(8,128)(2,1)S(1)}, u32[]{:S(2)}, u32[]{:S(2)}) collective-permute-start(bf16[128,1024]{1,0:T(8,128)(2,1)S(1)} %slice.7), channel_id=1, source_target_pairs={{0,224},{32,0},{64,32},{96,64},{128,96},{160,128},{192,160},{224,1... | collective-permute-start | bytes 786440 | tf_op jit(solution)/shard_map/ppermute | solution.py:287
  134.1 5.2 %collective-permute-done.20.refs_7_ = bf16[128,1024]{1,0:T(8,128)(2,1)S(1)} collective-permute-done((bf16[128,1024]{1,0:T(8,128)(2,1)S(1)}, bf16[128,1024]{1,0:T(8,128)(2,1)S(1)}, u32[]{:S(2)}, u32[]{:S(2)}) %collective-permute-start.20) | collective-permute-done | bytes 262176 | tf_op jit(solution)/shard_map/ppermute | solution.py:287
  139.3 3.0 %collective-permute-done.19.refs_3_ = bf16[256,768]{1,0:T(8,128)(2,1)S(1)} collective-permute-done((bf16[256,768]{1,0:T(8,128)(2,1)}, bf16[256,768]{1,0:T(8,128)(2,1)S(1)}, u32[]{:S(2)}, u32[]{:S(2)}) %collective-permute-start.19) | collective-permute-done | bytes 393248 | tf_op jit(solution)/shard_map/ppermute | solution.py:290
  142.3 2.4 %shard_map.113.dpred_hbm = bf16[256,1024]{1,0:T(8,128)(2,1)} custom-call(bf16[256,256]{1,0:T(8,128)(2,1)S(1)} %add_convert_fusion.refs_0_, bf16[256,256]{1,0:T(8,128)(2,1)S(1)} %collective-permute-done.18.refs_1_, bf16[256,768]{1,0:T(8,128)(2,1)} %reduce-scatter.2.cloned.1.call-done.refs_2_, bf16[256,768]{1,0:T(8,128)(2,1)S(1)} %collective-permute-done.19.refs_3_), custom_call_target="tpu_custom_call" | custom-call | tf_op jit(solution)/shard_map/pallas_call | solution.py:247
  144.7 3.8 %shard_map.115 = bf16[8,256,256]{2,1,0:T(8,128)(2,1)S(1)} custom-call(s32[1]{0:T(128)} %bitcast.3.z_ref, bf16[256,1024]{1,0:T(8,128)(2,1)} %shard_map.113.dpred_hbm, bf16[256,1024]{1,0:T(8,128)(2,1)} %refs_0_.1, bf16[256,1024]{1,0:T(8,128)(2,1)} %collective-permute-done.refs_1_, bf16[256,1024]{1,0:T(8,128)(2,1)} %collective-permute-done.1.refs_2_, ...), custom_call_target="tpu_custom_call" | custom-call | tf_op jit(solution)/shard_map/pallas_call | solution.py:247
  148.5 21.3 %all_to_all.15 = bf16[16,128,256]{2,1,0:T(8,128)(2,1)S(1)} all-to-all(bf16[16,128,256]{2,1,0:T(8,128)(2,1)S(1)} %bitcast.12), channel_id=1, replica_groups=mesh['z'=8,'xh'=2,'y'=4,'xl'=2,'core'=2] {'y','xl','core'}, dimensions={0} | all-to-all | bytes 2097152 | tf_op jit(solution)/shard_map/all_to_all | solution.py:402
  169.9 0.7 collective-permute-start.22
  170.6 1.3 collective-permute-start.23
  171.9 1.3 collective-permute-start.24
  173.2 1.3 collective-permute-start.25
  174.5 1.3 collective-permute-start.26
  175.8 10.3 %collective-permute-done.23.refs_1_ = bf16[128,256]{1,0:T(8,128)(2,1)S(1)} collective-permute-done((bf16[128,256]{1,0:T(8,128)(2,1)S(1)}, bf16[128,256]{1,0:T(8,128)(2,1)S(1)}, u32[]{:S(2)}, u32[]{:S(2)}) %collective-permute-start.23) | collective-permute-done | bytes 65568 | tf_op jit(solution)/shard_map/ppermute | solution.py:276
  186.1 3.4 %collective-permute-done.24.refs_2_ = bf16[128,256]{1,0:T(8,128)(2,1)S(1)} collective-permute-done((bf16[128,256]{1,0:T(8,128)(2,1)S(1)}, bf16[128,256]{1,0:T(8,128)(2,1)S(1)}, u32[]{:S(2)}, u32[]{:S(2)}) %collective-permute-start.24) | collective-permute-done | bytes 65568 | tf_op jit(solution)/shard_map/ppermute | solution.py:276
  189.5 1.9 collective-permute-done.25.refs_3_
  191.4 3.4 %collective-permute-done.26.refs_4_ = bf16[128,256]{1,0:T(8,128)(2,1)S(1)} collective-permute-done((bf16[128,256]{1,0:T(8,128)(2,1)S(1)}, bf16[128,256]{1,0:T(8,128)(2,1)S(1)}, u32[]{:S(2)}, u32[]{:S(2)}) %collective-permute-start.26) | collective-permute-done | bytes 65568 | tf_op jit(solution)/shard_map/ppermute | solution.py:276
  195.0 3.3 %shard_map.116 = bf16[128,256]{1,0:T(8,128)(2,1)} custom-call(s32[1]{0:T(128)} %bitcast.core_ref, bf16[128,256]{1,0:T(8,128)(2,1)S(1)} %collective-permute-done.22.dattn_hbm.refs_0_, bf16[128,256]{1,0:T(8,128)(2,1)} %copy-done.7, f32[2,128,1280]{2,1,0:T(8,128)} %get-tuple-element.61.probs_hbm, bf16[128,512]{1,0:T(8,128)(2,1)} %copy-done.1, ...), custom_call_target="tpu_custom_call" | custom-call | tf_op jit(solution)/shard_map/pallas_call | solution.py:247
  198.3 4.3 %shard_map.117 = (bf16[128,256]{1,0:T(8,128)(2,1)}, bf16[128,256]{1,0:T(8,128)(2,1)}) custom-call(s32[1]{0:T(128)} %bitcast.core_ref, s32[1280,1]{1,0:T(8,128)S(1)} %broadcast_in_dim.44.qseg_ref, s32[1,128]{1,0:T(1,128)S(1)} %get-tuple-element.68.kseg_ref, bf16[128,512]{1,0:T(8,128)(2,1)} %copy-done.1, bf16[1280,384]{1,0:T(8,128)(2,1)} %pad_dynamic-slice_fusion.qx_hbm, ...), custom_call_target="tpu_custom_call" | custom-call | tf_op jit(solution)/shard_map/pallas_call | solution.py:247
  202.6 1.2 all-gather.5.cloned.1.call-done.dpred_hbm
  203.8 4.3 %shard_map.114 = bf16[256,1024]{1,0:T(8,128)(2,1)} custom-call(bf16[2048,256]{1,0:T(8,128)(2,1)} %bitcast.2.attn_hbm, bf16[2048,1024]{1,0:T(8,128)(2,1)} %all-gather.5.cloned.1.call-done.dpred_hbm), custom_call_target="tpu_custom_call" | custom-call | tf_op jit(solution)/shard_map/pallas_call | solution.py:247
  (66 shorter events, 1.5 us)
Async XLA Ops:
  7.2 50.1 %copy-start = (bf16[1024,1024]{1,0:T(8,128)(2,1)S(1)}, bf16[1024,1024]{1,0:T(8,128)(2,1)}, u32[]{:S(2)}) copy-start(bf16[1024,1024]{1,0:T(8,128)(2,1)} %param.9) | copy-start | bytes 6291460
  7.2 50.1 %all-gather.3.cloned.1.call-start = ((), (), s32[]{:S(2)}) async-start(), calls=%async_computation.4 | async-start | bytes 4456448 | tf_op jit(solution)/shard_map/all_gather | solution.py:292
  7.9 18.8 %collective-permute-start = (bf16[256,1024]{1,0:T(8,128)(2,1)}, bf16[256,1024]{1,0:T(8,128)(2,1)}, u32[]{:S(2)}, u32[]{:S(2)}) collective-permute-start(bf16[256,1024]{1,0:T(8,128)(2,1)} %refs_0_.1), channel_id=1, source_target_pairs={{0,32},{32,64},{64,96},{96,128},{128,160},{160,192},{192,224},{224... | collective-permute-start | bytes 1572872 | tf_op jit(solution)/shard_map/ppermute | solution.py:287
  9.9 21.3 %collective-permute-start.1 = (bf16[256,1024]{1,0:T(8,128)(2,1)}, bf16[256,1024]{1,0:T(8,128)(2,1)}, u32[]{:S(2)}, u32[]{:S(2)}) collective-permute-start(bf16[256,1024]{1,0:T(8,128)(2,1)} %refs_0_.1), channel_id=1, source_target_pairs={{0,224},{32,0},{64,32},{96,64},{128,96},{160,128},{192,160},{224,1... | collective-permute-start | bytes 1572872 | tf_op jit(solution)/shard_map/ppermute | solution.py:287
  15.6 32.7 %copy-start.1 = (bf16[128,512]{1,0:T(8,128)(2,1)}, bf16[128,512]{1,0:T(8,128)(2,1)S(1)}, u32[]{:S(2)}) copy-start(bf16[128,512]{1,0:T(8,128)(2,1)S(1)} %constant_dynamic-update-slice_fusion.refs_0_.kv_hbm) | copy-start | bytes 393220
  15.6 16.2 %collective-permute-start.2 = (bf16[128,512]{1,0:T(8,128)(2,1)S(1)}, bf16[128,512]{1,0:T(8,128)(2,1)S(1)}, u32[]{:S(2)}, u32[]{:S(2)}) collective-permute-start(bf16[128,512]{1,0:T(8,128)(2,1)S(1)} %constant_dynamic-update-slice_fusion.refs_0_.kv_hbm), channel_id=1, source_target_pairs={{0,2},{1,3},{2,4},{3,5},{4,6},{5,7},{6,8},{7,9},{8,10},{9,11},{10,... | collective-permute-start | bytes 393224 | tf_op jit(solution)/shard_map/ppermute | solution.py:276
  18.7 13.9 %collective-permute-start.3 = (bf16[128,512]{1,0:T(8,128)(2,1)S(1)}, bf16[128,512]{1,0:T(8,128)(2,1)S(1)}, u32[]{:S(2)}, u32[]{:S(2)}) collective-permute-start(bf16[128,512]{1,0:T(8,128)(2,1)S(1)} %constant_dynamic-update-slice_fusion.refs_0_.kv_hbm), channel_id=1, source_target_pairs={{0,4},{1,5},{2,6},{3,7},{4,8},{5,9},{6,10},{7,11},{8,12},{9,13},{1... | collective-permute-start | bytes 393224 | tf_op jit(solution)/shard_map/ppermute | solution.py:276
  22.2 11.1 %collective-permute-start.4 = (bf16[128,512]{1,0:T(8,128)(2,1)S(1)}, bf16[128,512]{1,0:T(8,128)(2,1)S(1)}, u32[]{:S(2)}, u32[]{:S(2)}) collective-permute-start(bf16[128,512]{1,0:T(8,128)(2,1)S(1)} %constant_dynamic-update-slice_fusion.refs_0_.kv_hbm), channel_id=1, source_target_pairs={{0,6},{1,7},{2,8},{3,9},{4,10},{5,11},{6,12},{7,13},{8,14},{9,15},... | collective-permute-start | bytes 393224 | tf_op jit(solution)/shard_map/ppermute | solution.py:276
  26.7 10.9 %collective-permute-start.5 = (bf16[128,512]{1,0:T(8,128)(2,1)S(1)}, bf16[128,512]{1,0:T(8,128)(2,1)S(1)}, u32[]{:S(2)}, u32[]{:S(2)}) collective-permute-start(bf16[128,512]{1,0:T(8,128)(2,1)S(1)} %constant_dynamic-update-slice_fusion.refs_0_.kv_hbm), channel_id=1, source_target_pairs={{0,8},{1,9},{2,10},{3,11},{4,12},{5,13},{6,14},{7,15},{16,24},{17,... | collective-permute-start | bytes 393224 | tf_op jit(solution)/shard_map/ppermute | solution.py:276
  31.9 16.4 %copy-start.3 = (bf16[128,512]{1,0:T(8,128)(2,1)}, bf16[128,512]{1,0:T(8,128)(2,1)S(1)}, u32[]{:S(2)}) copy-start(bf16[128,512]{1,0:T(8,128)(2,1)S(1)} %collective-permute-done.2.refs_1_) | copy-start | bytes 393220
  32.6 15.7 %copy-start.4 = (bf16[128,512]{1,0:T(8,128)(2,1)}, bf16[128,512]{1,0:T(8,128)(2,1)S(1)}, u32[]{:S(2)}) copy-start(bf16[128,512]{1,0:T(8,128)(2,1)S(1)} %collective-permute-done.3.refs_2_) | copy-start | bytes 393220
  33.3 15.0 %copy-start.5 = (bf16[128,512]{1,0:T(8,128)(2,1)}, bf16[128,512]{1,0:T(8,128)(2,1)S(1)}, u32[]{:S(2)}) copy-start(bf16[128,512]{1,0:T(8,128)(2,1)S(1)} %collective-permute-done.4.refs_3_) | copy-start | bytes 393220
  37.6 10.7 %copy-start.6 = (bf16[128,512]{1,0:T(8,128)(2,1)}, bf16[128,512]{1,0:T(8,128)(2,1)S(1)}, u32[]{:S(2)}) copy-start(bf16[128,512]{1,0:T(8,128)(2,1)S(1)} %collective-permute-done.5.refs_4_) | copy-start | bytes 393220
  38.4 4.4 %collective-permute-start.6 = (bf16[640,512]{1,0:T(8,128)(2,1)}, bf16[640,512]{1,0:T(8,128)(2,1)S(1)}, u32[]{:S(2)}, u32[]{:S(2)}) collective-permute-start(bf16[640,512]{1,0:T(8,128)(2,1)} %constant_dynamic-update-slice_fusion.2), channel_id=1, source_target_pairs={{0,1},{1,0},{2,3},{3,2},{4,5},{5,4},{6,7},{7,6},{8,9},{9,8},{10,11... | collective-permute-start | bytes 1966088 | tf_op jit(solution)/shard_map/ppermute | solution.py:280
  38.4 15.7 %collective-permute-start.9 = (bf16[256,1024]{1,0:T(8,128)(2,1)}, bf16[256,1024]{1,0:T(8,128)(2,1)}, u32[]{:S(2)}, u32[]{:S(2)}) collective-permute-start(bf16[256,1024]{1,0:T(8,128)(2,1)} %collective-permute-done.1.refs_2_), channel_id=1, source_target_pairs={{0,224},{32,0},{64,32},{96,64},{128,96},{160,128},{192,160},{224,1... | collective-permute-start | bytes 1572872 | tf_op jit(solution)/shard_map/ppermute | solution.py:287
  40.1 17.2 %collective-permute-start.7 = (bf16[256,1024]{1,0:T(8,128)(2,1)}, bf16[256,1024]{1,0:T(8,128)(2,1)}, u32[]{:S(2)}, u32[]{:S(2)}) collective-permute-start(bf16[256,1024]{1,0:T(8,128)(2,1)} %collective-permute-done.refs_1_), channel_id=1, source_target_pairs={{0,32},{32,64},{64,96},{96,128},{128,160},{160,192},{192,224},{224... | collective-permute-start | bytes 1572872 | tf_op jit(solution)/shard_map/ppermute | solution.py:287
  42.7 23.0 %copy-start.2 = (bf16[640,512]{1,0:T(8,128)(2,1)}, bf16[640,512]{1,0:T(8,128)(2,1)S(1)}, u32[]{:S(2)}) copy-start(bf16[640,512]{1,0:T(8,128)(2,1)S(1)} %collective-permute-done.6.refs_5_) | copy-start | bytes 1966084
  46.6 0.6 copy-start.8
  47.2 18.5 %copy-start.7 = (bf16[128,256]{1,0:T(8,128)(2,1)}, bf16[128,256]{1,0:T(8,128)(2,1)S(1)}, u32[]{:S(2)}) copy-start(bf16[128,256]{1,0:T(8,128)(2,1)S(1)} %get-tuple-element.37.attn_hbm) | copy-start | bytes 196612
  48.3 24.4 %all-to-all-start = ((bf16[16,128,256]{2,1,0:T(8,128)(2,1)}), bf16[16,128,256]{2,1,0:T(8,128)(2,1)}, u32[]{:S(2)}, u32[]{:S(2)}) async-start(bf16[16,128,256]{2,1,0:T(8,128)(2,1)} %broadcast_in_dim.38), calls=%async_computation | async-start | bytes 2097152 | tf_op jit(solution)/shard_map/all_to_all | solution.py:284
  54.0 76.3 %reduce-scatter.2.cloned.1.call-start = ((), (), s32[]{:S(2)}) async-start(), calls=%async_computation.5 | async-start | bytes 3538944 | tf_op jit(solution)/shard_map/reduce_scatter | solution.py:363
  54.1 15.2 %collective-permute-start.10 = (bf16[256,1024]{1,0:T(8,128)(2,1)}, bf16[256,1024]{1,0:T(8,128)(2,1)}, u32[]{:S(2)}, u32[]{:S(2)}) collective-permute-start(bf16[256,1024]{1,0:T(8,128)(2,1)} %collective-permute-done.9.refs_4_), channel_id=1, source_target_pairs={{0,224},{32,0},{64,32},{96,64},{128,96},{160,128},{192,160},{224,1... | collective-permute-start | bytes 1572872 | tf_op jit(solution)/shard_map/ppermute | solution.py:287
  57.3 15.4 %collective-permute-start.8 = (bf16[256,1024]{1,0:T(8,128)(2,1)}, bf16[256,1024]{1,0:T(8,128)(2,1)}, u32[]{:S(2)}, u32[]{:S(2)}) collective-permute-start(bf16[256,1024]{1,0:T(8,128)(2,1)} %collective-permute-done.7.refs_3_), channel_id=1, source_target_pairs={{0,32},{32,64},{64,96},{96,128},{128,160},{160,192},{192,224},{224... | collective-permute-start | bytes 1572872 | tf_op jit(solution)/shard_map/ppermute | solution.py:287
  77.8 3.5 %copy-start.9 = (bf16[128,384]{1,0:T(8,128)(2,1)S(1)}, bf16[128,384]{1,0:T(8,128)(2,1)}, u32[]{:S(2)}) copy-start(bf16[128,384]{1,0:T(8,128)(2,1)} %copy-done.8) | copy-start | bytes 294916
  77.8 10.4 %collective-permute-start.11 = (bf16[256,256]{1,0:T(8,128)(2,1)S(1)}, bf16[256,256]{1,0:T(8,128)(2,1)S(1)}, u32[]{:S(2)}, u32[]{:S(2)}) collective-permute-start(bf16[256,256]{1,0:T(8,128)(2,1)S(1)} %get-tuple-element.46), channel_id=1, source_target_pairs={{0,32},{32,64},{64,96},{96,128},{128,160},{160,192},{192,224},{224... | collective-permute-start | bytes 393224 | tf_op jit(solution)/shard_map/ppermute | solution.py:287
  78.1 10.3 %collective-permute-start.15 = (bf16[256,256]{1,0:T(8,128)(2,1)S(1)}, bf16[256,256]{1,0:T(8,128)(2,1)S(1)}, u32[]{:S(2)}, u32[]{:S(2)}) collective-permute-start(bf16[256,256]{1,0:T(8,128)(2,1)S(1)} %get-tuple-element.49), channel_id=1, source_target_pairs={{0,224},{32,0},{64,32},{96,64},{128,96},{160,128},{192,160},{224,1... | collective-permute-start | bytes 393224 | tf_op jit(solution)/shard_map/ppermute | solution.py:287
  82.7 36.8 %all-to-all-start.1 = ((bf16[16,128,384]{2,1,0:T(8,128)(2,1)}), bf16[16,128,384]{2,1,0:T(8,128)(2,1)}, u32[]{:S(2)}, u32[]{:S(2)}) async-start(bf16[16,128,384]{2,1,0:T(8,128)(2,1)} %broadcast_in_dim.41), calls=%async_computation.2 | async-start | bytes 3145728 | tf_op jit(solution)/shard_map/all_to_all | solution.py:284
  88.2 115.6 %all-gather.5.cloned.1.call-start = ((), (), s32[]{:S(2)}) async-start(), calls=%async_computation.6 | async-start | bytes 4718592 | tf_op jit(solution)/shard_map/all_gather | solution.py:417
  88.3 10.1 %collective-permute-start.12 = (bf16[256,256]{1,0:T(8,128)(2,1)S(1)}, bf16[256,256]{1,0:T(8,128)(2,1)S(1)}, u32[]{:S(2)}, u32[]{:S(2)}) collective-permute-start(bf16[256,256]{1,0:T(8,128)(2,1)S(1)} %add_convert_fusion.5), channel_id=1, source_target_pairs={{0,32},{32,64},{64,96},{96,128},{128,160},{160,192},{192,224},{224... | collective-permute-start | bytes 393224 | tf_op jit(solution)/shard_map/ppermute | solution.py:287
  88.4 10.1 %collective-permute-start.16 = (bf16[256,256]{1,0:T(8,128)(2,1)S(1)}, bf16[256,256]{1,0:T(8,128)(2,1)S(1)}, u32[]{:S(2)}, u32[]{:S(2)}) collective-permute-start(bf16[256,256]{1,0:T(8,128)(2,1)S(1)} %add_convert_fusion.2), channel_id=1, source_target_pairs={{0,224},{32,0},{64,32},{96,64},{128,96},{160,128},{192,160},{224,1... | collective-permute-start | bytes 393224 | tf_op jit(solution)/shard_map/ppermute | solution.py:287
  98.5 10.1 %collective-permute-start.13 = (bf16[256,256]{1,0:T(8,128)(2,1)S(1)}, bf16[256,256]{1,0:T(8,128)(2,1)S(1)}, u32[]{:S(2)}, u32[]{:S(2)}) collective-permute-start(bf16[256,256]{1,0:T(8,128)(2,1)S(1)} %add_convert_fusion.4), channel_id=1, source_target_pairs={{0,32},{32,64},{64,96},{96,128},{128,160},{160,192},{192,224},{224... | collective-permute-start | bytes 393224 | tf_op jit(solution)/shard_map/ppermute | solution.py:287
  98.6 14.2 %collective-permute-start.17 = (bf16[256,256]{1,0:T(8,128)(2,1)S(1)}, bf16[256,256]{1,0:T(8,128)(2,1)S(1)}, u32[]{:S(2)}, u32[]{:S(2)}) collective-permute-start(bf16[256,256]{1,0:T(8,128)(2,1)S(1)} %add_convert_fusion.1), channel_id=1, source_target_pairs={{0,224},{32,0},{64,32},{96,64},{128,96},{160,128},{192,160},{224,1... | collective-permute-start | bytes 393224 | tf_op jit(solution)/shard_map/ppermute | solution.py:287
  108.7 9.9 %collective-permute-start.14 = (bf16[256,256]{1,0:T(8,128)(2,1)S(1)}, bf16[256,256]{1,0:T(8,128)(2,1)S(1)}, u32[]{:S(2)}, u32[]{:S(2)}) collective-permute-start(bf16[256,256]{1,0:T(8,128)(2,1)S(1)} %add_convert_fusion.3), channel_id=1, source_target_pairs={{0,32},{32,64},{64,96},{96,128},{128,160},{160,192},{192,224},{224... | collective-permute-start | bytes 393224 | tf_op jit(solution)/shard_map/ppermute | solution.py:287
  118.6 6.6 %collective-permute-start.18 = (bf16[256,256]{1,0:T(8,128)(2,1)S(1)}, bf16[256,256]{1,0:T(8,128)(2,1)S(1)}, u32[]{:S(2)}, u32[]{:S(2)}) collective-permute-start(bf16[256,256]{1,0:T(8,128)(2,1)S(1)} %add_convert_fusion.refs_0_), channel_id=1, source_target_pairs={{0,16},{16,0},{1,17},{17,1},{2,18},{18,2},{3,19},{19,3},{4,20},{20... | collective-permute-start | bytes 393224 | tf_op jit(solution)/shard_map/ppermute | solution.py:290
  130.3 12.0 %collective-permute-start.19 = (bf16[256,768]{1,0:T(8,128)(2,1)}, bf16[256,768]{1,0:T(8,128)(2,1)S(1)}, u32[]{:S(2)}, u32[]{:S(2)}) collective-permute-start(bf16[256,768]{1,0:T(8,128)(2,1)} %reduce-scatter.2.cloned.1.call-done.refs_2_), channel_id=1, source_target_pairs={{0,16},{16,0},{1,17},{17,1},{2,18},{18,2},{3,19},{19,3},{4,20},{20... | collective-permute-start | bytes 1179656 | tf_op jit(solution)/shard_map/ppermute | solution.py:290
  130.8 8.5 %collective-permute-start.20 = (bf16[128,1024]{1,0:T(8,128)(2,1)S(1)}, bf16[128,1024]{1,0:T(8,128)(2,1)S(1)}, u32[]{:S(2)}, u32[]{:S(2)}) collective-permute-start(bf16[128,1024]{1,0:T(8,128)(2,1)S(1)} %slice.6), channel_id=1, source_target_pairs={{0,32},{32,64},{64,96},{96,128},{128,160},{160,192},{192,224},{224... | collective-permute-start | bytes 786440 | tf_op jit(solution)/shard_map/ppermute | solution.py:287
  131.1 8.2 %collective-permute-start.21 = (bf16[128,1024]{1,0:T(8,128)(2,1)S(1)}, bf16[128,1024]{1,0:T(8,128)(2,1)S(1)}, u32[]{:S(2)}, u32[]{:S(2)}) collective-permute-start(bf16[128,1024]{1,0:T(8,128)(2,1)S(1)} %slice.7), channel_id=1, source_target_pairs={{0,224},{32,0},{64,32},{96,64},{128,96},{160,128},{192,160},{224,1... | collective-permute-start | bytes 786440 | tf_op jit(solution)/shard_map/ppermute | solution.py:287
  148.5 46.3 %copy-start.10 = (s32[1280]{0:T(1024)S(1)}, s32[1280]{0:T(1024)}, u32[]{:S(2)}) copy-start(s32[1280]{0:T(1024)} %get-tuple-element.70) | copy-start | bytes 15364
  169.9 0.7 collective-permute-start.22
  170.6 15.5 %collective-permute-start.23 = (bf16[128,256]{1,0:T(8,128)(2,1)S(1)}, bf16[128,256]{1,0:T(8,128)(2,1)S(1)}, u32[]{:S(2)}, u32[]{:S(2)}) collective-permute-start(bf16[128,256]{1,0:T(8,128)(2,1)S(1)} %collective-permute-done.22.dattn_hbm.refs_0_), channel_id=1, source_target_pairs={{2,0},{3,1},{4,2},{5,3},{6,4},{7,5},{8,6},{9,7},{10,8},{11,9},{12,... | collective-permute-start | bytes 196616 | tf_op jit(solution)/shard_map/ppermute | solution.py:276
  171.9 17.6 %collective-permute-start.24 = (bf16[128,256]{1,0:T(8,128)(2,1)S(1)}, bf16[128,256]{1,0:T(8,128)(2,1)S(1)}, u32[]{:S(2)}, u32[]{:S(2)}) collective-permute-start(bf16[128,256]{1,0:T(8,128)(2,1)S(1)} %collective-permute-done.22.dattn_hbm.refs_0_), channel_id=1, source_target_pairs={{4,0},{5,1},{6,2},{7,3},{8,4},{9,5},{10,6},{11,7},{12,8},{13,9},{1... | collective-permute-start | bytes 196616 | tf_op jit(solution)/shard_map/ppermute | solution.py:276
  173.2 18.2 %collective-permute-start.25 = (bf16[128,256]{1,0:T(8,128)(2,1)S(1)}, bf16[128,256]{1,0:T(8,128)(2,1)S(1)}, u32[]{:S(2)}, u32[]{:S(2)}) collective-permute-start(bf16[128,256]{1,0:T(8,128)(2,1)S(1)} %collective-permute-done.22.dattn_hbm.refs_0_), channel_id=1, source_target_pairs={{6,0},{7,1},{8,2},{9,3},{10,4},{11,5},{12,6},{13,7},{14,8},{15,9},... | collective-permute-start | bytes 196616 | tf_op jit(solution)/shard_map/ppermute | solution.py:276
  174.5 20.2 %collective-permute-start.26 = (bf16[128,256]{1,0:T(8,128)(2,1)S(1)}, bf16[128,256]{1,0:T(8,128)(2,1)S(1)}, u32[]{:S(2)}, u32[]{:S(2)}) collective-permute-start(bf16[128,256]{1,0:T(8,128)(2,1)S(1)} %collective-permute-done.22.dattn_hbm.refs_0_), channel_id=1, source_target_pairs={{8,0},{9,1},{10,2},{11,3},{12,4},{13,5},{14,6},{15,7},{24,16},{25,... | collective-permute-start | bytes 196616 | tf_op jit(solution)/shard_map/ppermute | solution.py:276
  194.8 3.5 %collective-permute-start.27 = (bf16[640,256]{1,0:T(8,128)(2,1)S(1)}, bf16[640,256]{1,0:T(8,128)(2,1)S(1)}, u32[]{:S(2)}, u32[]{:S(2)}) collective-permute-start(bf16[640,256]{1,0:T(8,128)(2,1)S(1)} %constant_dynamic-update-slice_fusion.7), channel_id=1, source_target_pairs={{0,1},{1,0},{2,3},{3,2},{4,5},{5,4},{6,7},{7,6},{8,9},{9,8},{10,11... | collective-permute-start | bytes 983048 | tf_op jit(solution)/shard_map/ppermute | solution.py:280
Sparse Core Ops, SparseCore 0:
  9.9 47.0 all-gather.2
  77.9 52.3 reduce-scatter.1
  144.8 58.9 all-gather.4

commit v8 on v7

--- a/solution.py
+++ b/solution.py
@@ -187,18 +187,17 @@
 
 
 def proj_grad_kernel(n, attn_hbm, dpred_hbm, out_hbm, attn_ref, dpred_ref, out_ref, sems):
-    rows = dpred_ref.shape[0] // n
+    rows, columns = dpred_ref.shape[0] // n, dpred_ref.shape[1] // 2
     parts = [pl.ds(i * rows, rows) for i in range(n)]
-    attn = begin([attn_hbm], [attn_ref], sems)
-    dpred = begin([dpred_hbm.at[p] for p in parts], [dpred_ref.at[p] for p in parts], sems, 1)
-    finish(attn)
-    total = None
-    for p, copy in zip(parts, dpred, strict=True):
-        copy.wait()
-        term = dot(attn_ref[p, :], dpred_ref[p, :], TN)
-        total = term if total is None else total + term
-    out_ref[...] = total.astype(BF16)
-    fetch([out_ref], [out_hbm], sems)
+    copies = begin([attn_hbm], [attn_ref], sems)
+    copies += begin([dpred_hbm.at[p] for p in parts], [dpred_ref.at[p] for p in parts], sems, 1)
+    finish(copies)
+    writes = []
+    for half in range(2):
+        here = pl.ds(half * columns, columns)
+        out_ref[:, here] = dot(attn_ref[...], dpred_ref[:, here], TN).astype(BF16)
+        writes += begin([out_ref.at[:, here]], [out_hbm.at[:, here]], sems, 1 + n + half)
+    finish(writes)
 
 
 def difference_kernel(n, z_ref, xh_ref, attn_hbm, proj_hbm, resid_hbm, teacher_hbm, sum_hbm, *refs):

time: 217 us -> 217 us (level)
  no operation moved by 1% of the time
where the time goes in v8:
time: 217 us; the launch traced here: 215 us
  waiting for transfers between devices  67.1 us (31%)
  starting transfers between devices  58.9 us (27%)
  Pallas kernels  27.3 us (13%)
  blocking collectives  21.3 us (10%)
  local copies, waits for them, and re-layouts  17.4 us (8%)
  between operations  14.2 us (7%)
  matrix products  8.41 us (4%)
    ppermute x15, waiting for transfers between devices, turn(): return lax.ppermute(array, 'z', [(i, (i + by) % n_z) for i in range(n_z)])  31.4 us
    pallas_call x7, Pallas kernels, call(): pl.pallas_call(kernel, out_shape=out_shape, out_specs=out_specs, in_specs...  27.3 us
    ppermute x15, starting transfers between devices, turn(): return lax.ppermute(array, 'z', [(i, (i + by) % n_z) for i in range(n_z)])  24.8 us
    ppermute x8, waiting for transfers between devices, shift(): return lax.ppermute(array, SP, pairs)  22.5 us
    all_to_all x1, blocking collectives, body(): lax.all_to_all(dattn_part.reshape(n_sp, rows, width), SP, 0, 0, tiled=True)  21.3 us
    ppermute x8, starting transfers between devices, shift(): return lax.ppermute(array, SP, pairs)  20.7 us
    all_to_all x2, starting transfers between devices, everywhere(): lax.all_to_all(copies, SP, 0, 0, tiled=True).reshape(-1, array.shape[1])  11.2 us
    dot_general x1, matrix products, dot(): return lax.dot_general(a, b, dims, preferred_element_type=F32)  8.41 us
  transfers between devices with their start and end apart: 33, of which 15 were waited for; matrix products, arithmetic and copies ran while one was open for 12% of the time, Pallas kernels for 7%

profile of v8, /device:TPU:4, one launch (start us, length us, event | category | flops | bytes accessed | tf_op | source)
XLA Modules:
  0.0 215.0 jit_solution(10719020912350156372)
XLA Ops:
  7.2 0.7 all-gather.3.cloned.1.call-update
  7.9 2.0 collective-permute-start
  9.9 4.0 %collective-permute-start.1 = (bf16[256,1024]{1,0:T(8,128)(2,1)}, bf16[256,1024]{1,0:T(8,128)(2,1)}, u32[]{:S(2)}, u32[]{:S(2)}) collective-permute-start(bf16[256,1024]{1,0:T(8,128)(2,1)} %refs_0_.1), channel_id=1, source_target_pairs={{0,224},{32,0},{64,32},{96,64},{128,96},{160,128},{192,160},{224,1... | collective-permute-start | bytes 1572872 | tf_op jit(solution)/shard_map/ppermute | solution.py:286
  13.9 0.8 constant_dynamic-update-slice_fusion.1
  14.8 0.8 constant_dynamic-update-slice_fusion.refs_0_.kv_hbm
  15.6 3.1 %collective-permute-start.2 = (bf16[128,512]{1,0:T(8,128)(2,1)S(1)}, bf16[128,512]{1,0:T(8,128)(2,1)S(1)}, u32[]{:S(2)}, u32[]{:S(2)}) collective-permute-start(bf16[128,512]{1,0:T(8,128)(2,1)S(1)} %constant_dynamic-update-slice_fusion.refs_0_.kv_hbm), channel_id=1, source_target_pairs={{0,2},{1,3},{2,4},{3,5},{4,6},{5,7},{6,8},{7,9},{8,10},{9,11},{10,... | collective-permute-start | bytes 393224 | tf_op jit(solution)/shard_map/ppermute | solution.py:275
  18.7 3.5 %collective-permute-start.3 = (bf16[128,512]{1,0:T(8,128)(2,1)S(1)}, bf16[128,512]{1,0:T(8,128)(2,1)S(1)}, u32[]{:S(2)}, u32[]{:S(2)}) collective-permute-start(bf16[128,512]{1,0:T(8,128)(2,1)S(1)} %constant_dynamic-update-slice_fusion.refs_0_.kv_hbm), channel_id=1, source_target_pairs={{0,4},{1,5},{2,6},{3,7},{4,8},{5,9},{6,10},{7,11},{8,12},{9,13},{1... | collective-permute-start | bytes 393224 | tf_op jit(solution)/shard_map/ppermute | solution.py:275
  22.2 4.5 %collective-permute-start.4 = (bf16[128,512]{1,0:T(8,128)(2,1)S(1)}, bf16[128,512]{1,0:T(8,128)(2,1)S(1)}, u32[]{:S(2)}, u32[]{:S(2)}) collective-permute-start(bf16[128,512]{1,0:T(8,128)(2,1)S(1)} %constant_dynamic-update-slice_fusion.refs_0_.kv_hbm), channel_id=1, source_target_pairs={{0,6},{1,7},{2,8},{3,9},{4,10},{5,11},{6,12},{7,13},{8,14},{9,15},... | collective-permute-start | bytes 393224 | tf_op jit(solution)/shard_map/ppermute | solution.py:275
  26.7 4.5 %collective-permute-start.5 = (bf16[128,512]{1,0:T(8,128)(2,1)S(1)}, bf16[128,512]{1,0:T(8,128)(2,1)S(1)}, u32[]{:S(2)}, u32[]{:S(2)}) collective-permute-start(bf16[128,512]{1,0:T(8,128)(2,1)S(1)} %constant_dynamic-update-slice_fusion.refs_0_.kv_hbm), channel_id=1, source_target_pairs={{0,8},{1,9},{2,10},{3,11},{4,12},{5,13},{6,14},{7,15},{16,24},{17,... | collective-permute-start | bytes 393224 | tf_op jit(solution)/shard_map/ppermute | solution.py:275
  31.2 0.7 constant_dynamic-update-slice_fusion.6
  31.9 0.7 constant_dynamic-update-slice_fusion.5
  32.6 0.7 constant_dynamic-update-slice_fusion.4
  33.3 0.7 constant_dynamic-update-slice_fusion.3
  34.0 3.6 %collective-permute-done.5.refs_4_ = bf16[128,512]{1,0:T(8,128)(2,1)S(1)} collective-permute-done((bf16[128,512]{1,0:T(8,128)(2,1)S(1)}, bf16[128,512]{1,0:T(8,128)(2,1)S(1)}, u32[]{:S(2)}, u32[]{:S(2)}) %collective-permute-start.5) | collective-permute-done | bytes 131104 | tf_op jit(solution)/shard_map/ppermute | solution.py:275
  37.6 0.7 constant_dynamic-update-slice_fusion.2
  38.4 1.8 collective-permute-start.9
  40.1 0.3 collective-permute-start.7
  40.4 1.4 pad_dynamic-slice_fusion.2
  41.8 0.8 dynamic-slice_bitcast_fusion
  42.7 3.8 %shard_map.111 = (bf16[128,256]{1,0:T(8,128)(2,1)S(1)}, f32[2,128,1280]{2,1,0:T(8,128)}, bf16[128,384]{1,0:T(8,128)(2,1)S(1)}) custom-call(s32[1]{0:T(128)} %bitcast.core_ref, s32[128,1]{1,0:T(8,128)S(1)} %copy.13.qseg_ref, s32[1,1280]{1,0:T(1,128)S(1)} %broadcast_in_dim.37.kseg_ref, bf16[128,256]{1,0:T(8,128)(2,1)} %q_hbm.1, ...), custom_call_target="tpu_custom_call" | custom-call | tf_op jit(solution)/shard_map/pallas_call | solution.py:246
  46.6 0.6 copy-done.8
  47.2 1.1 broadcast_in_dim.38
  48.3 5.7 %all-to-all-start = ((bf16[16,128,256]{2,1,0:T(8,128)(2,1)}), bf16[16,128,256]{2,1,0:T(8,128)(2,1)}, u32[]{:S(2)}, u32[]{:S(2)}) async-start(bf16[16,128,256]{2,1,0:T(8,128)(2,1)} %broadcast_in_dim.38), calls=%async_computation | async-start | bytes 2097152 | tf_op jit(solution)/shard_map/all_to_all | solution.py:283
  54.1 3.2 %collective-permute-start.10 = (bf16[256,1024]{1,0:T(8,128)(2,1)}, bf16[256,1024]{1,0:T(8,128)(2,1)}, u32[]{:S(2)}, u32[]{:S(2)}) collective-permute-start(bf16[256,1024]{1,0:T(8,128)(2,1)} %collective-permute-done.9.refs_4_), channel_id=1, source_target_pairs={{0,224},{32,0},{64,32},{96,64},{128,96},{160,128},{192,160},{224,1... | collective-permute-start | bytes 1572872 | tf_op jit(solution)/shard_map/ppermute | solution.py:286
  57.3 8.4 %convolution_convert_fusion.teacher_hbm = bf16[2048,1024]{1,0:T(8,128)(2,1)} fusion(bf16[2048,1024]{1,0:T(8,128)(2,1)} %all-gather.3.cloned.1.call-done, bf16[1024,1024]{1,0:T(8,128)(2,1)S(1)} %copy-done), kind=kOutput, calls=%fused_computation | convolution fusion | flops 4297064448 | bytes 10485760 | tf_op jit(solution)/shard_map/dot_general | solution.py:24
  65.7 3.6 %collective-permute-done.10.refs_6_ = bf16[256,1024]{1,0:T(8,128)(2,1)} collective-permute-done((bf16[256,1024]{1,0:T(8,128)(2,1)}, bf16[256,1024]{1,0:T(8,128)(2,1)}, u32[]{:S(2)}, u32[]{:S(2)}) %collective-permute-start.10) | collective-permute-done | bytes 524320 | tf_op jit(solution)/shard_map/ppermute | solution.py:286
  69.3 3.4 %collective-permute-done.8.refs_5_ = bf16[256,1024]{1,0:T(8,128)(2,1)} collective-permute-done((bf16[256,1024]{1,0:T(8,128)(2,1)}, bf16[256,1024]{1,0:T(8,128)(2,1)}, u32[]{:S(2)}, u32[]{:S(2)}) %collective-permute-start.8) | collective-permute-done | bytes 524320 | tf_op jit(solution)/shard_map/ppermute | solution.py:286
  72.7 5.1 %shard_map.112 = (bf16[2048,768]{1,0:T(8,128)(2,1)}, bf16[256,256]{1,0:T(8,128)(2,1)S(1)}, bf16[256,256]{1,0:T(8,128)(2,1)S(1)}, bf16[256,256]{1,0:T(8,128)(2,1)...) custom-call(s32[1]{0:T(128)} %bitcast.3.z_ref, ...), custom_call_target="tpu_custom_call" | custom-call | tf_op jit(solution)/shard_map/pallas_call | solution.py:246
  77.8 0.3 collective-permute-start.11
  78.1 3.2 %collective-permute-start.15 = (bf16[256,256]{1,0:T(8,128)(2,1)S(1)}, bf16[256,256]{1,0:T(8,128)(2,1)S(1)}, u32[]{:S(2)}, u32[]{:S(2)}) collective-permute-start(bf16[256,256]{1,0:T(8,128)(2,1)S(1)} %get-tuple-element.49), channel_id=1, source_target_pairs={{0,224},{32,0},{64,32},{96,64},{128,96},{160,128},{192,160},{224,1... | collective-permute-start | bytes 393224 | tf_op jit(solution)/shard_map/ppermute | solution.py:286
  81.3 1.4 broadcast_in_dim.41
  82.7 5.5 %all-to-all-start.1 = ((bf16[16,128,384]{2,1,0:T(8,128)(2,1)}), bf16[16,128,384]{2,1,0:T(8,128)(2,1)}, u32[]{:S(2)}, u32[]{:S(2)}) async-start(bf16[16,128,384]{2,1,0:T(8,128)(2,1)} %broadcast_in_dim.41), calls=%async_computation.2 | async-start | bytes 3145728 | tf_op jit(solution)/shard_map/all_to_all | solution.py:283
  88.4 3.3 %collective-permute-start.16 = (bf16[256,256]{1,0:T(8,128)(2,1)S(1)}, bf16[256,256]{1,0:T(8,128)(2,1)S(1)}, u32[]{:S(2)}, u32[]{:S(2)}) collective-permute-start(bf16[256,256]{1,0:T(8,128)(2,1)S(1)} %add_convert_fusion.2), channel_id=1, source_target_pairs={{0,224},{32,0},{64,32},{96,64},{128,96},{160,128},{192,160},{224,1... | collective-permute-start | bytes 393224 | tf_op jit(solution)/shard_map/ppermute | solution.py:286
  91.8 6.7 %collective-permute-done.12 = bf16[256,256]{1,0:T(8,128)(2,1)S(1)} collective-permute-done((bf16[256,256]{1,0:T(8,128)(2,1)S(1)}, bf16[256,256]{1,0:T(8,128)(2,1)S(1)}, u32[]{:S(2)}, u32[]{:S(2)}) %collective-permute-start.12) | collective-permute-done | bytes 131104 | tf_op jit(solution)/shard_map/ppermute | solution.py:286
  98.6 3.3 %collective-permute-start.17 = (bf16[256,256]{1,0:T(8,128)(2,1)S(1)}, bf16[256,256]{1,0:T(8,128)(2,1)S(1)}, u32[]{:S(2)}, u32[]{:S(2)}) collective-permute-start(bf16[256,256]{1,0:T(8,128)(2,1)S(1)} %add_convert_fusion.1), channel_id=1, source_target_pairs={{0,224},{32,0},{64,32},{96,64},{128,96},{160,128},{192,160},{224,1... | collective-permute-start | bytes 393224 | tf_op jit(solution)/shard_map/ppermute | solution.py:286
  101.9 6.7 %collective-permute-done.13 = bf16[256,256]{1,0:T(8,128)(2,1)S(1)} collective-permute-done((bf16[256,256]{1,0:T(8,128)(2,1)S(1)}, bf16[256,256]{1,0:T(8,128)(2,1)S(1)}, u32[]{:S(2)}, u32[]{:S(2)}) %collective-permute-start.13) | collective-permute-done | bytes 131104 | tf_op jit(solution)/shard_map/ppermute | solution.py:286
  108.7 2.1 pad_dynamic-slice_fusion.1.attn_hbm
  110.9 1.0 slice.6
  111.8 1.0 slice.7
  112.8 5.7 %collective-permute-done.14 = bf16[256,256]{1,0:T(8,128)(2,1)S(1)} collective-permute-done((bf16[256,256]{1,0:T(8,128)(2,1)S(1)}, bf16[256,256]{1,0:T(8,128)(2,1)S(1)}, u32[]{:S(2)}, u32[]{:S(2)}) %collective-permute-start.14) | collective-permute-done | bytes 131104 | tf_op jit(solution)/shard_map/ppermute | solution.py:286
  118.6 0.9 collective-permute-start.18
  119.5 2.5 %pad_dynamic-slice_fusion.qx_hbm = bf16[1280,384]{1,0:T(8,128)(2,1)} fusion(s32[]{:T(128)S(6)} %select_n.10, bf16[2048,384]{1,0:T(8,128)(2,1)} %bitcast.5), kind=kLoop, calls=%fused_computation.1 | loop fusion | bytes 2555908 | tf_op jit(solution)/shard_map/dynamic_slice | solution.py:344
  122.0 3.2 %collective-permute-done.18.refs_1_ = bf16[256,256]{1,0:T(8,128)(2,1)S(1)} collective-permute-done((bf16[256,256]{1,0:T(8,128)(2,1)S(1)}, bf16[256,256]{1,0:T(8,128)(2,1)S(1)}, u32[]{:S(2)}, u32[]{:S(2)}) %collective-permute-start.18) | collective-permute-done | bytes 131104 | tf_op jit(solution)/shard_map/ppermute | solution.py:289
  125.2 5.1 %reduce-scatter.2.cloned.1.call-done.refs_2_ = bf16[256,768]{1,0:T(8,128)(2,1)} async-done(((bf16[2048,768]{1,0:T(8,128)(2,1)}), bf16[256,768]{1,0:T(8,128)(2,1)}) %reduce-scatter.2.cloned.1.call-update) | async-done | bytes 393232 | tf_op jit(solution)/shard_map/reduce_scatter | solution.py:362
  130.3 0.5 collective-permute-start.19
  131.1 3.0 %collective-permute-start.21 = (bf16[128,1024]{1,0:T(8,128)(2,1)S(1)}, bf16[128,1024]{1,0:T(8,128)(2,1)S(1)}, u32[]{:S(2)}, u32[]{:S(2)}) collective-permute-start(bf16[128,1024]{1,0:T(8,128)(2,1)S(1)} %slice.7), channel_id=1, source_target_pairs={{0,224},{32,0},{64,32},{96,64},{128,96},{160,128},{192,160},{224,1... | collective-permute-start | bytes 786440 | tf_op jit(solution)/shard_map/ppermute | solution.py:286
  134.1 5.2 %collective-permute-done.20.refs_7_ = bf16[128,1024]{1,0:T(8,128)(2,1)S(1)} collective-permute-done((bf16[128,1024]{1,0:T(8,128)(2,1)S(1)}, bf16[128,1024]{1,0:T(8,128)(2,1)S(1)}, u32[]{:S(2)}, u32[]{:S(2)}) %collective-permute-start.20) | collective-permute-done | bytes 262176 | tf_op jit(solution)/shard_map/ppermute | solution.py:286
  139.3 3.0 %collective-permute-done.19.refs_3_ = bf16[256,768]{1,0:T(8,128)(2,1)S(1)} collective-permute-done((bf16[256,768]{1,0:T(8,128)(2,1)}, bf16[256,768]{1,0:T(8,128)(2,1)S(1)}, u32[]{:S(2)}, u32[]{:S(2)}) %collective-permute-start.19) | collective-permute-done | bytes 393248 | tf_op jit(solution)/shard_map/ppermute | solution.py:289
  142.3 2.4 %shard_map.113.dpred_hbm = bf16[256,1024]{1,0:T(8,128)(2,1)} custom-call(bf16[256,256]{1,0:T(8,128)(2,1)S(1)} %add_convert_fusion.refs_0_, bf16[256,256]{1,0:T(8,128)(2,1)S(1)} %collective-permute-done.18.refs_1_, bf16[256,768]{1,0:T(8,128)(2,1)} %reduce-scatter.2.cloned.1.call-done.refs_2_, bf16[256,768]{1,0:T(8,128)(2,1)S(1)} %collective-permute-done.19.refs_3_), custom_call_target="tpu_custom_call" | custom-call | tf_op jit(solution)/shard_map/pallas_call | solution.py:246
  144.7 3.8 %shard_map.115 = bf16[8,256,256]{2,1,0:T(8,128)(2,1)S(1)} custom-call(s32[1]{0:T(128)} %bitcast.3.z_ref, bf16[256,1024]{1,0:T(8,128)(2,1)} %shard_map.113.dpred_hbm, bf16[256,1024]{1,0:T(8,128)(2,1)} %refs_0_.1, bf16[256,1024]{1,0:T(8,128)(2,1)} %collective-permute-done.refs_1_, bf16[256,1024]{1,0:T(8,128)(2,1)} %collective-permute-done.1.refs_2_, ...), custom_call_target="tpu_custom_call" | custom-call | tf_op jit(solution)/shard_map/pallas_call | solution.py:246
  148.5 21.3 %all_to_all.15 = bf16[16,128,256]{2,1,0:T(8,128)(2,1)S(1)} all-to-all(bf16[16,128,256]{2,1,0:T(8,128)(2,1)S(1)} %bitcast.12), channel_id=1, replica_groups=mesh['z'=8,'xh'=2,'y'=4,'xl'=2,'core'=2] {'y','xl','core'}, dimensions={0} | all-to-all | bytes 2097152 | tf_op jit(solution)/shard_map/all_to_all | solution.py:401
  169.9 0.7 collective-permute-start.22
  170.6 1.3 collective-permute-start.23
  171.9 1.3 collective-permute-start.24
  173.2 1.3 collective-permute-start.25
  174.5 1.3 collective-permute-start.26
  175.8 10.3 %collective-permute-done.23.refs_1_ = bf16[128,256]{1,0:T(8,128)(2,1)S(1)} collective-permute-done((bf16[128,256]{1,0:T(8,128)(2,1)S(1)}, bf16[128,256]{1,0:T(8,128)(2,1)S(1)}, u32[]{:S(2)}, u32[]{:S(2)}) %collective-permute-start.23) | collective-permute-done | bytes 65568 | tf_op jit(solution)/shard_map/ppermute | solution.py:275
  186.1 3.4 %collective-permute-done.24.refs_2_ = bf16[128,256]{1,0:T(8,128)(2,1)S(1)} collective-permute-done((bf16[128,256]{1,0:T(8,128)(2,1)S(1)}, bf16[128,256]{1,0:T(8,128)(2,1)S(1)}, u32[]{:S(2)}, u32[]{:S(2)}) %collective-permute-start.24) | collective-permute-done | bytes 65568 | tf_op jit(solution)/shard_map/ppermute | solution.py:275
  189.5 1.9 collective-permute-done.25.refs_3_
  191.4 3.4 %collective-permute-done.26.refs_4_ = bf16[128,256]{1,0:T(8,128)(2,1)S(1)} collective-permute-done((bf16[128,256]{1,0:T(8,128)(2,1)S(1)}, bf16[128,256]{1,0:T(8,128)(2,1)S(1)}, u32[]{:S(2)}, u32[]{:S(2)}) %collective-permute-start.26) | collective-permute-done | bytes 65568 | tf_op jit(solution)/shard_map/ppermute | solution.py:275
  195.0 3.3 %shard_map.116 = bf16[128,256]{1,0:T(8,128)(2,1)} custom-call(s32[1]{0:T(128)} %bitcast.core_ref, bf16[128,256]{1,0:T(8,128)(2,1)S(1)} %collective-permute-done.22.dattn_hbm.refs_0_, bf16[128,256]{1,0:T(8,128)(2,1)} %copy-done.7, f32[2,128,1280]{2,1,0:T(8,128)} %get-tuple-element.61.probs_hbm, bf16[128,512]{1,0:T(8,128)(2,1)} %copy-done.1, ...), custom_call_target="tpu_custom_call" | custom-call | tf_op jit(solution)/shard_map/pallas_call | solution.py:246
  198.3 4.3 %shard_map.117 = (bf16[128,256]{1,0:T(8,128)(2,1)}, bf16[128,256]{1,0:T(8,128)(2,1)}) custom-call(s32[1]{0:T(128)} %bitcast.core_ref, s32[1280,1]{1,0:T(8,128)S(1)} %broadcast_in_dim.44.qseg_ref, s32[1,128]{1,0:T(1,128)S(1)} %get-tuple-element.68.kseg_ref, bf16[128,512]{1,0:T(8,128)(2,1)} %copy-done.1, bf16[1280,384]{1,0:T(8,128)(2,1)} %pad_dynamic-slice_fusion.qx_hbm, ...), custom_call_target="tpu_custom_call" | custom-call | tf_op jit(solution)/shard_map/pallas_call | solution.py:246
  202.6 1.2 all-gather.5.cloned.1.call-done.dpred_hbm
  203.8 4.7 %shard_map.114 = bf16[256,1024]{1,0:T(8,128)(2,1)} custom-call(bf16[2048,256]{1,0:T(8,128)(2,1)} %bitcast.2.attn_hbm, bf16[2048,1024]{1,0:T(8,128)(2,1)} %all-gather.5.cloned.1.call-done.dpred_hbm), custom_call_target="tpu_custom_call" | custom-call | tf_op jit(solution)/shard_map/pallas_call | solution.py:246
  (66 shorter events, 1.5 us)
Async XLA Ops:
  7.2 50.1 %copy-start = (bf16[1024,1024]{1,0:T(8,128)(2,1)S(1)}, bf16[1024,1024]{1,0:T(8,128)(2,1)}, u32[]{:S(2)}) copy-start(bf16[1024,1024]{1,0:T(8,128)(2,1)} %param.9) | copy-start | bytes 6291460
  7.2 50.1 %all-gather.3.cloned.1.call-start = ((), (), s32[]{:S(2)}) async-start(), calls=%async_computation.4 | async-start | bytes 4456448 | tf_op jit(solution)/shard_map/all_gather | solution.py:291
  7.9 18.8 %collective-permute-start = (bf16[256,1024]{1,0:T(8,128)(2,1)}, bf16[256,1024]{1,0:T(8,128)(2,1)}, u32[]{:S(2)}, u32[]{:S(2)}) collective-permute-start(bf16[256,1024]{1,0:T(8,128)(2,1)} %refs_0_.1), channel_id=1, source_target_pairs={{0,32},{32,64},{64,96},{96,128},{128,160},{160,192},{192,224},{224... | collective-permute-start | bytes 1572872 | tf_op jit(solution)/shard_map/ppermute | solution.py:286
  9.9 21.3 %collective-permute-start.1 = (bf16[256,1024]{1,0:T(8,128)(2,1)}, bf16[256,1024]{1,0:T(8,128)(2,1)}, u32[]{:S(2)}, u32[]{:S(2)}) collective-permute-start(bf16[256,1024]{1,0:T(8,128)(2,1)} %refs_0_.1), channel_id=1, source_target_pairs={{0,224},{32,0},{64,32},{96,64},{128,96},{160,128},{192,160},{224,1... | collective-permute-start | bytes 1572872 | tf_op jit(solution)/shard_map/ppermute | solution.py:286
  15.6 32.7 %copy-start.1 = (bf16[128,512]{1,0:T(8,128)(2,1)}, bf16[128,512]{1,0:T(8,128)(2,1)S(1)}, u32[]{:S(2)}) copy-start(bf16[128,512]{1,0:T(8,128)(2,1)S(1)} %constant_dynamic-update-slice_fusion.refs_0_.kv_hbm) | copy-start | bytes 393220
  15.6 16.2 %collective-permute-start.2 = (bf16[128,512]{1,0:T(8,128)(2,1)S(1)}, bf16[128,512]{1,0:T(8,128)(2,1)S(1)}, u32[]{:S(2)}, u32[]{:S(2)}) collective-permute-start(bf16[128,512]{1,0:T(8,128)(2,1)S(1)} %constant_dynamic-update-slice_fusion.refs_0_.kv_hbm), channel_id=1, source_target_pairs={{0,2},{1,3},{2,4},{3,5},{4,6},{5,7},{6,8},{7,9},{8,10},{9,11},{10,... | collective-permute-start | bytes 393224 | tf_op jit(solution)/shard_map/ppermute | solution.py:275
  18.7 13.9 %collective-permute-start.3 = (bf16[128,512]{1,0:T(8,128)(2,1)S(1)}, bf16[128,512]{1,0:T(8,128)(2,1)S(1)}, u32[]{:S(2)}, u32[]{:S(2)}) collective-permute-start(bf16[128,512]{1,0:T(8,128)(2,1)S(1)} %constant_dynamic-update-slice_fusion.refs_0_.kv_hbm), channel_id=1, source_target_pairs={{0,4},{1,5},{2,6},{3,7},{4,8},{5,9},{6,10},{7,11},{8,12},{9,13},{1... | collective-permute-start | bytes 393224 | tf_op jit(solution)/shard_map/ppermute | solution.py:275
  22.2 11.1 %collective-permute-start.4 = (bf16[128,512]{1,0:T(8,128)(2,1)S(1)}, bf16[128,512]{1,0:T(8,128)(2,1)S(1)}, u32[]{:S(2)}, u32[]{:S(2)}) collective-permute-start(bf16[128,512]{1,0:T(8,128)(2,1)S(1)} %constant_dynamic-update-slice_fusion.refs_0_.kv_hbm), channel_id=1, source_target_pairs={{0,6},{1,7},{2,8},{3,9},{4,10},{5,11},{6,12},{7,13},{8,14},{9,15},... | collective-permute-start | bytes 393224 | tf_op jit(solution)/shard_map/ppermute | solution.py:275
  26.7 10.9 %collective-permute-start.5 = (bf16[128,512]{1,0:T(8,128)(2,1)S(1)}, bf16[128,512]{1,0:T(8,128)(2,1)S(1)}, u32[]{:S(2)}, u32[]{:S(2)}) collective-permute-start(bf16[128,512]{1,0:T(8,128)(2,1)S(1)} %constant_dynamic-update-slice_fusion.refs_0_.kv_hbm), channel_id=1, source_target_pairs={{0,8},{1,9},{2,10},{3,11},{4,12},{5,13},{6,14},{7,15},{16,24},{17,... | collective-permute-start | bytes 393224 | tf_op jit(solution)/shard_map/ppermute | solution.py:275
  31.9 16.4 %copy-start.3 = (bf16[128,512]{1,0:T(8,128)(2,1)}, bf16[128,512]{1,0:T(8,128)(2,1)S(1)}, u32[]{:S(2)}) copy-start(bf16[128,512]{1,0:T(8,128)(2,1)S(1)} %collective-permute-done.2.refs_1_) | copy-start | bytes 393220
  32.6 15.7 %copy-start.4 = (bf16[128,512]{1,0:T(8,128)(2,1)}, bf16[128,512]{1,0:T(8,128)(2,1)S(1)}, u32[]{:S(2)}) copy-start(bf16[128,512]{1,0:T(8,128)(2,1)S(1)} %collective-permute-done.3.refs_2_) | copy-start | bytes 393220
  33.3 15.0 %copy-start.5 = (bf16[128,512]{1,0:T(8,128)(2,1)}, bf16[128,512]{1,0:T(8,128)(2,1)S(1)}, u32[]{:S(2)}) copy-start(bf16[128,512]{1,0:T(8,128)(2,1)S(1)} %collective-permute-done.4.refs_3_) | copy-start | bytes 393220
  37.6 10.7 %copy-start.6 = (bf16[128,512]{1,0:T(8,128)(2,1)}, bf16[128,512]{1,0:T(8,128)(2,1)S(1)}, u32[]{:S(2)}) copy-start(bf16[128,512]{1,0:T(8,128)(2,1)S(1)} %collective-permute-done.5.refs_4_) | copy-start | bytes 393220
  38.4 4.4 %collective-permute-start.6 = (bf16[640,512]{1,0:T(8,128)(2,1)}, bf16[640,512]{1,0:T(8,128)(2,1)S(1)}, u32[]{:S(2)}, u32[]{:S(2)}) collective-permute-start(bf16[640,512]{1,0:T(8,128)(2,1)} %constant_dynamic-update-slice_fusion.2), channel_id=1, source_target_pairs={{0,1},{1,0},{2,3},{3,2},{4,5},{5,4},{6,7},{7,6},{8,9},{9,8},{10,11... | collective-permute-start | bytes 1966088 | tf_op jit(solution)/shard_map/ppermute | solution.py:279
  38.4 15.7 %collective-permute-start.9 = (bf16[256,1024]{1,0:T(8,128)(2,1)}, bf16[256,1024]{1,0:T(8,128)(2,1)}, u32[]{:S(2)}, u32[]{:S(2)}) collective-permute-start(bf16[256,1024]{1,0:T(8,128)(2,1)} %collective-permute-done.1.refs_2_), channel_id=1, source_target_pairs={{0,224},{32,0},{64,32},{96,64},{128,96},{160,128},{192,160},{224,1... | collective-permute-start | bytes 1572872 | tf_op jit(solution)/shard_map/ppermute | solution.py:286
  40.1 17.2 %collective-permute-start.7 = (bf16[256,1024]{1,0:T(8,128)(2,1)}, bf16[256,1024]{1,0:T(8,128)(2,1)}, u32[]{:S(2)}, u32[]{:S(2)}) collective-permute-start(bf16[256,1024]{1,0:T(8,128)(2,1)} %collective-permute-done.refs_1_), channel_id=1, source_target_pairs={{0,32},{32,64},{64,96},{96,128},{128,160},{160,192},{192,224},{224... | collective-permute-start | bytes 1572872 | tf_op jit(solution)/shard_map/ppermute | solution.py:286
  42.7 23.0 %copy-start.2 = (bf16[640,512]{1,0:T(8,128)(2,1)}, bf16[640,512]{1,0:T(8,128)(2,1)S(1)}, u32[]{:S(2)}) copy-start(bf16[640,512]{1,0:T(8,128)(2,1)S(1)} %collective-permute-done.6.refs_5_) | copy-start | bytes 1966084
  46.6 0.6 copy-start.8
  47.2 18.5 %copy-start.7 = (bf16[128,256]{1,0:T(8,128)(2,1)}, bf16[128,256]{1,0:T(8,128)(2,1)S(1)}, u32[]{:S(2)}) copy-start(bf16[128,256]{1,0:T(8,128)(2,1)S(1)} %get-tuple-element.37.attn_hbm) | copy-start | bytes 196612
  48.3 24.4 %all-to-all-start = ((bf16[16,128,256]{2,1,0:T(8,128)(2,1)}), bf16[16,128,256]{2,1,0:T(8,128)(2,1)}, u32[]{:S(2)}, u32[]{:S(2)}) async-start(bf16[16,128,256]{2,1,0:T(8,128)(2,1)} %broadcast_in_dim.38), calls=%async_computation | async-start | bytes 2097152 | tf_op jit(solution)/shard_map/all_to_all | solution.py:283
  54.0 76.3 %reduce-scatter.2.cloned.1.call-start = ((), (), s32[]{:S(2)}) async-start(), calls=%async_computation.5 | async-start | bytes 3538944 | tf_op jit(solution)/shard_map/reduce_scatter | solution.py:362
  54.1 15.2 %collective-permute-start.10 = (bf16[256,1024]{1,0:T(8,128)(2,1)}, bf16[256,1024]{1,0:T(8,128)(2,1)}, u32[]{:S(2)}, u32[]{:S(2)}) collective-permute-start(bf16[256,1024]{1,0:T(8,128)(2,1)} %collective-permute-done.9.refs_4_), channel_id=1, source_target_pairs={{0,224},{32,0},{64,32},{96,64},{128,96},{160,128},{192,160},{224,1... | collective-permute-start | bytes 1572872 | tf_op jit(solution)/shard_map/ppermute | solution.py:286
  57.3 15.4 %collective-permute-start.8 = (bf16[256,1024]{1,0:T(8,128)(2,1)}, bf16[256,1024]{1,0:T(8,128)(2,1)}, u32[]{:S(2)}, u32[]{:S(2)}) collective-permute-start(bf16[256,1024]{1,0:T(8,128)(2,1)} %collective-permute-done.7.refs_3_), channel_id=1, source_target_pairs={{0,32},{32,64},{64,96},{96,128},{128,160},{160,192},{192,224},{224... | collective-permute-start | bytes 1572872 | tf_op jit(solution)/shard_map/ppermute | solution.py:286
  77.8 3.5 %copy-start.9 = (bf16[128,384]{1,0:T(8,128)(2,1)S(1)}, bf16[128,384]{1,0:T(8,128)(2,1)}, u32[]{:S(2)}) copy-start(bf16[128,384]{1,0:T(8,128)(2,1)} %copy-done.8) | copy-start | bytes 294916
  77.8 10.4 %collective-permute-start.11 = (bf16[256,256]{1,0:T(8,128)(2,1)S(1)}, bf16[256,256]{1,0:T(8,128)(2,1)S(1)}, u32[]{:S(2)}, u32[]{:S(2)}) collective-permute-start(bf16[256,256]{1,0:T(8,128)(2,1)S(1)} %get-tuple-element.46), channel_id=1, source_target_pairs={{0,32},{32,64},{64,96},{96,128},{128,160},{160,192},{192,224},{224... | collective-permute-start | bytes 393224 | tf_op jit(solution)/shard_map/ppermute | solution.py:286
  78.1 10.3 %collective-permute-start.15 = (bf16[256,256]{1,0:T(8,128)(2,1)S(1)}, bf16[256,256]{1,0:T(8,128)(2,1)S(1)}, u32[]{:S(2)}, u32[]{:S(2)}) collective-permute-start(bf16[256,256]{1,0:T(8,128)(2,1)S(1)} %get-tuple-element.49), channel_id=1, source_target_pairs={{0,224},{32,0},{64,32},{96,64},{128,96},{160,128},{192,160},{224,1... | collective-permute-start | bytes 393224 | tf_op jit(solution)/shard_map/ppermute | solution.py:286
  82.7 36.8 %all-to-all-start.1 = ((bf16[16,128,384]{2,1,0:T(8,128)(2,1)}), bf16[16,128,384]{2,1,0:T(8,128)(2,1)}, u32[]{:S(2)}, u32[]{:S(2)}) async-start(bf16[16,128,384]{2,1,0:T(8,128)(2,1)} %broadcast_in_dim.41), calls=%async_computation.2 | async-start | bytes 3145728 | tf_op jit(solution)/shard_map/all_to_all | solution.py:283
  88.2 115.6 %all-gather.5.cloned.1.call-start = ((), (), s32[]{:S(2)}) async-start(), calls=%async_computation.6 | async-start | bytes 4718592 | tf_op jit(solution)/shard_map/all_gather | solution.py:416
  88.3 10.1 %collective-permute-start.12 = (bf16[256,256]{1,0:T(8,128)(2,1)S(1)}, bf16[256,256]{1,0:T(8,128)(2,1)S(1)}, u32[]{:S(2)}, u32[]{:S(2)}) collective-permute-start(bf16[256,256]{1,0:T(8,128)(2,1)S(1)} %add_convert_fusion.5), channel_id=1, source_target_pairs={{0,32},{32,64},{64,96},{96,128},{128,160},{160,192},{192,224},{224... | collective-permute-start | bytes 393224 | tf_op jit(solution)/shard_map/ppermute | solution.py:286
  88.4 10.1 %collective-permute-start.16 = (bf16[256,256]{1,0:T(8,128)(2,1)S(1)}, bf16[256,256]{1,0:T(8,128)(2,1)S(1)}, u32[]{:S(2)}, u32[]{:S(2)}) collective-permute-start(bf16[256,256]{1,0:T(8,128)(2,1)S(1)} %add_convert_fusion.2), channel_id=1, source_target_pairs={{0,224},{32,0},{64,32},{96,64},{128,96},{160,128},{192,160},{224,1... | collective-permute-start | bytes 393224 | tf_op jit(solution)/shard_map/ppermute | solution.py:286
  98.5 10.1 %collective-permute-start.13 = (bf16[256,256]{1,0:T(8,128)(2,1)S(1)}, bf16[256,256]{1,0:T(8,128)(2,1)S(1)}, u32[]{:S(2)}, u32[]{:S(2)}) collective-permute-start(bf16[256,256]{1,0:T(8,128)(2,1)S(1)} %add_convert_fusion.4), channel_id=1, source_target_pairs={{0,32},{32,64},{64,96},{96,128},{128,160},{160,192},{192,224},{224... | collective-permute-start | bytes 393224 | tf_op jit(solution)/shard_map/ppermute | solution.py:286
  98.6 14.2 %collective-permute-start.17 = (bf16[256,256]{1,0:T(8,128)(2,1)S(1)}, bf16[256,256]{1,0:T(8,128)(2,1)S(1)}, u32[]{:S(2)}, u32[]{:S(2)}) collective-permute-start(bf16[256,256]{1,0:T(8,128)(2,1)S(1)} %add_convert_fusion.1), channel_id=1, source_target_pairs={{0,224},{32,0},{64,32},{96,64},{128,96},{160,128},{192,160},{224,1... | collective-permute-start | bytes 393224 | tf_op jit(solution)/shard_map/ppermute | solution.py:286
  108.7 9.9 %collective-permute-start.14 = (bf16[256,256]{1,0:T(8,128)(2,1)S(1)}, bf16[256,256]{1,0:T(8,128)(2,1)S(1)}, u32[]{:S(2)}, u32[]{:S(2)}) collective-permute-start(bf16[256,256]{1,0:T(8,128)(2,1)S(1)} %add_convert_fusion.3), channel_id=1, source_target_pairs={{0,32},{32,64},{64,96},{96,128},{128,160},{160,192},{192,224},{224... | collective-permute-start | bytes 393224 | tf_op jit(solution)/shard_map/ppermute | solution.py:286
  118.6 6.6 %collective-permute-start.18 = (bf16[256,256]{1,0:T(8,128)(2,1)S(1)}, bf16[256,256]{1,0:T(8,128)(2,1)S(1)}, u32[]{:S(2)}, u32[]{:S(2)}) collective-permute-start(bf16[256,256]{1,0:T(8,128)(2,1)S(1)} %add_convert_fusion.refs_0_), channel_id=1, source_target_pairs={{0,16},{16,0},{1,17},{17,1},{2,18},{18,2},{3,19},{19,3},{4,20},{20... | collective-permute-start | bytes 393224 | tf_op jit(solution)/shard_map/ppermute | solution.py:289
  130.3 12.0 %collective-permute-start.19 = (bf16[256,768]{1,0:T(8,128)(2,1)}, bf16[256,768]{1,0:T(8,128)(2,1)S(1)}, u32[]{:S(2)}, u32[]{:S(2)}) collective-permute-start(bf16[256,768]{1,0:T(8,128)(2,1)} %reduce-scatter.2.cloned.1.call-done.refs_2_), channel_id=1, source_target_pairs={{0,16},{16,0},{1,17},{17,1},{2,18},{18,2},{3,19},{19,3},{4,20},{20... | collective-permute-start | bytes 1179656 | tf_op jit(solution)/shard_map/ppermute | solution.py:289
  130.8 8.5 %collective-permute-start.20 = (bf16[128,1024]{1,0:T(8,128)(2,1)S(1)}, bf16[128,1024]{1,0:T(8,128)(2,1)S(1)}, u32[]{:S(2)}, u32[]{:S(2)}) collective-permute-start(bf16[128,1024]{1,0:T(8,128)(2,1)S(1)} %slice.6), channel_id=1, source_target_pairs={{0,32},{32,64},{64,96},{96,128},{128,160},{160,192},{192,224},{224... | collective-permute-start | bytes 786440 | tf_op jit(solution)/shard_map/ppermute | solution.py:286
  131.1 8.2 %collective-permute-start.21 = (bf16[128,1024]{1,0:T(8,128)(2,1)S(1)}, bf16[128,1024]{1,0:T(8,128)(2,1)S(1)}, u32[]{:S(2)}, u32[]{:S(2)}) collective-permute-start(bf16[128,1024]{1,0:T(8,128)(2,1)S(1)} %slice.7), channel_id=1, source_target_pairs={{0,224},{32,0},{64,32},{96,64},{128,96},{160,128},{192,160},{224,1... | collective-permute-start | bytes 786440 | tf_op jit(solution)/shard_map/ppermute | solution.py:286
  148.5 46.3 %copy-start.10 = (s32[1280]{0:T(1024)S(1)}, s32[1280]{0:T(1024)}, u32[]{:S(2)}) copy-start(s32[1280]{0:T(1024)} %get-tuple-element.70) | copy-start | bytes 15364
  169.9 0.7 collective-permute-start.22
  170.6 15.5 %collective-permute-start.23 = (bf16[128,256]{1,0:T(8,128)(2,1)S(1)}, bf16[128,256]{1,0:T(8,128)(2,1)S(1)}, u32[]{:S(2)}, u32[]{:S(2)}) collective-permute-start(bf16[128,256]{1,0:T(8,128)(2,1)S(1)} %collective-permute-done.22.dattn_hbm.refs_0_), channel_id=1, source_target_pairs={{2,0},{3,1},{4,2},{5,3},{6,4},{7,5},{8,6},{9,7},{10,8},{11,9},{12,... | collective-permute-start | bytes 196616 | tf_op jit(solution)/shard_map/ppermute | solution.py:275
  171.9 17.6 %collective-permute-start.24 = (bf16[128,256]{1,0:T(8,128)(2,1)S(1)}, bf16[128,256]{1,0:T(8,128)(2,1)S(1)}, u32[]{:S(2)}, u32[]{:S(2)}) collective-permute-start(bf16[128,256]{1,0:T(8,128)(2,1)S(1)} %collective-permute-done.22.dattn_hbm.refs_0_), channel_id=1, source_target_pairs={{4,0},{5,1},{6,2},{7,3},{8,4},{9,5},{10,6},{11,7},{12,8},{13,9},{1... | collective-permute-start | bytes 196616 | tf_op jit(solution)/shard_map/ppermute | solution.py:275
  173.2 18.2 %collective-permute-start.25 = (bf16[128,256]{1,0:T(8,128)(2,1)S(1)}, bf16[128,256]{1,0:T(8,128)(2,1)S(1)}, u32[]{:S(2)}, u32[]{:S(2)}) collective-permute-start(bf16[128,256]{1,0:T(8,128)(2,1)S(1)} %collective-permute-done.22.dattn_hbm.refs_0_), channel_id=1, source_target_pairs={{6,0},{7,1},{8,2},{9,3},{10,4},{11,5},{12,6},{13,7},{14,8},{15,9},... | collective-permute-start | bytes 196616 | tf_op jit(solution)/shard_map/ppermute | solution.py:275
  174.5 20.2 %collective-permute-start.26 = (bf16[128,256]{1,0:T(8,128)(2,1)S(1)}, bf16[128,256]{1,0:T(8,128)(2,1)S(1)}, u32[]{:S(2)}, u32[]{:S(2)}) collective-permute-start(bf16[128,256]{1,0:T(8,128)(2,1)S(1)} %collective-permute-done.22.dattn_hbm.refs_0_), channel_id=1, source_target_pairs={{8,0},{9,1},{10,2},{11,3},{12,4},{13,5},{14,6},{15,7},{24,16},{25,... | collective-permute-start | bytes 196616 | tf_op jit(solution)/shard_map/ppermute | solution.py:275
  194.8 3.5 %collective-permute-start.27 = (bf16[640,256]{1,0:T(8,128)(2,1)S(1)}, bf16[640,256]{1,0:T(8,128)(2,1)S(1)}, u32[]{:S(2)}, u32[]{:S(2)}) collective-permute-start(bf16[640,256]{1,0:T(8,128)(2,1)S(1)} %constant_dynamic-update-slice_fusion.7), channel_id=1, source_target_pairs={{0,1},{1,0},{2,3},{3,2},{4,5},{5,4},{6,7},{7,6},{8,9},{9,8},{10,11... | collective-permute-start | bytes 983048 | tf_op jit(solution)/shard_map/ppermute | solution.py:279
Sparse Core Ops, SparseCore 0:
  9.9 47.0 all-gather.2
  77.9 52.3 reduce-scatter.1
  144.8 58.9 all-gather.4

commit v9 on v7

--- a/solution.py
+++ b/solution.py
@@ -359,6 +359,7 @@
         (),
         (attn_all, proj, teacher_resid, teacher_part),
         (attn_all, proj, teacher_resid, teacher_part, jax.ShapeDtypeStruct((tokens, split), BF16)),
+        loose=(0,),
     )
     part = lax.psum_scatter(part, "z", scatter_dimension=0, tiled=True)
 

time: 217 us -> 221 us (1.018)
  local copies, waits for them, and re-layouts: 17.4 us -> 21 us
    unnamed x31 -> x43, local copies, waits for them, and re-layouts: 4.34 us -> 7.61 us
    reduce_scatter x1, waiting for transfers between devices: 5.14 us -> 2.93 us  [body(): part = lax.psum_scatter(part, 'z', scatter_dimension=0, tiled=True)]
  transfers between devices with their start and end apart: 33 -> 33, of which waited for: 15 -> 16; matrix products, arithmetic and copies ran while one was open for 12% -> 13% of each run, Pallas kernels for 7% -> 7%
where the time goes in v9:
time: 221 us; the launch traced here: 218 us
  waiting for transfers between devices  65.2 us (30%)
  starting transfers between devices  59.4 us (27%)
  Pallas kernels  26.9 us (12%)
  blocking collectives  21.2 us (10%)
  local copies, waits for them, and re-layouts  21 us (10%)
  between operations  14.2 us (6%)
  matrix products  8.39 us (4%)
  other arithmetic  2.34 us (1%)
    ppermute x15, waiting for transfers between devices, turn(): return lax.ppermute(array, 'z', [(i, (i + by) % n_z) for i in range(n_z)])  30.8 us
    pallas_call x7, Pallas kernels, call(): pl.pallas_call(kernel, out_shape=out_shape, out_specs=out_specs, in_specs...  26.9 us
    ppermute x15, starting transfers between devices, turn(): return lax.ppermute(array, 'z', [(i, (i + by) % n_z) for i in range(n_z)])  25.3 us
    ppermute x8, waiting for transfers between devices, shift(): return lax.ppermute(array, SP, pairs)  22.6 us
    all_to_all x1, blocking collectives, body(): lax.all_to_all(dattn_part.reshape(n_sp, rows, width), SP, 0, 0, tiled=True)  21.2 us
    ppermute x8, starting transfers between devices, shift(): return lax.ppermute(array, SP, pairs)  20.7 us
    all_to_all x2, starting transfers between devices, everywhere(): lax.all_to_all(copies, SP, 0, 0, tiled=True).reshape(-1, array.shape[1])  11.1 us
    dot_general x1, matrix products, dot(): return lax.dot_general(a, b, dims, preferred_element_type=F32)  8.39 us
  transfers between devices with their start and end apart: 33, of which 16 were waited for; matrix products, arithmetic and copies ran while one was open for 13% of the time, Pallas kernels for 7%

profile of v9, /device:TPU:4, one launch (start us, length us, event | category | flops | bytes accessed | tf_op | source)
XLA Modules:
  0.0 218.5 jit_solution(13253928891833629669)
XLA Ops:
  7.2 0.7 all-gather.3.cloned.1.call-update
  7.9 2.0 collective-permute-start
  9.9 4.0 %collective-permute-start.1 = (bf16[256,1024]{1,0:T(8,128)(2,1)}, bf16[256,1024]{1,0:T(8,128)(2,1)}, u32[]{:S(2)}, u32[]{:S(2)}) collective-permute-start(bf16[256,1024]{1,0:T(8,128)(2,1)} %refs_0_.1), channel_id=1, source_target_pairs={{0,224},{32,0},{64,32},{96,64},{128,96},{160,128},{192,160},{224,1... | collective-permute-start | bytes 1572872 | tf_op jit(solution)/shard_map/ppermute | solution.py:287
  13.9 0.8 constant_dynamic-update-slice_fusion.1
  14.8 0.8 constant_dynamic-update-slice_fusion.refs_0_.kv_hbm
  15.6 3.1 %collective-permute-start.2 = (bf16[128,512]{1,0:T(8,128)(2,1)S(1)}, bf16[128,512]{1,0:T(8,128)(2,1)S(1)}, u32[]{:S(2)}, u32[]{:S(2)}) collective-permute-start(bf16[128,512]{1,0:T(8,128)(2,1)S(1)} %constant_dynamic-update-slice_fusion.refs_0_.kv_hbm), channel_id=1, source_target_pairs={{0,2},{1,3},{2,4},{3,5},{4,6},{5,7},{6,8},{7,9},{8,10},{9,11},{10,... | collective-permute-start | bytes 393224 | tf_op jit(solution)/shard_map/ppermute | solution.py:276
  18.7 3.5 %collective-permute-start.3 = (bf16[128,512]{1,0:T(8,128)(2,1)S(1)}, bf16[128,512]{1,0:T(8,128)(2,1)S(1)}, u32[]{:S(2)}, u32[]{:S(2)}) collective-permute-start(bf16[128,512]{1,0:T(8,128)(2,1)S(1)} %constant_dynamic-update-slice_fusion.refs_0_.kv_hbm), channel_id=1, source_target_pairs={{0,4},{1,5},{2,6},{3,7},{4,8},{5,9},{6,10},{7,11},{8,12},{9,13},{1... | collective-permute-start | bytes 393224 | tf_op jit(solution)/shard_map/ppermute | solution.py:276
  22.2 4.5 %collective-permute-start.4 = (bf16[128,512]{1,0:T(8,128)(2,1)S(1)}, bf16[128,512]{1,0:T(8,128)(2,1)S(1)}, u32[]{:S(2)}, u32[]{:S(2)}) collective-permute-start(bf16[128,512]{1,0:T(8,128)(2,1)S(1)} %constant_dynamic-update-slice_fusion.refs_0_.kv_hbm), channel_id=1, source_target_pairs={{0,6},{1,7},{2,8},{3,9},{4,10},{5,11},{6,12},{7,13},{8,14},{9,15},... | collective-permute-start | bytes 393224 | tf_op jit(solution)/shard_map/ppermute | solution.py:276
  26.7 4.5 %collective-permute-start.5 = (bf16[128,512]{1,0:T(8,128)(2,1)S(1)}, bf16[128,512]{1,0:T(8,128)(2,1)S(1)}, u32[]{:S(2)}, u32[]{:S(2)}) collective-permute-start(bf16[128,512]{1,0:T(8,128)(2,1)S(1)} %constant_dynamic-update-slice_fusion.refs_0_.kv_hbm), channel_id=1, source_target_pairs={{0,8},{1,9},{2,10},{3,11},{4,12},{5,13},{6,14},{7,15},{16,24},{17,... | collective-permute-start | bytes 393224 | tf_op jit(solution)/shard_map/ppermute | solution.py:276
  31.9 0.7 constant_dynamic-update-slice_fusion.5
  32.6 0.7 constant_dynamic-update-slice_fusion.4
  33.3 0.7 constant_dynamic-update-slice_fusion.3
  34.0 3.6 %collective-permute-done.5.refs_4_ = bf16[128,512]{1,0:T(8,128)(2,1)S(1)} collective-permute-done((bf16[128,512]{1,0:T(8,128)(2,1)S(1)}, bf16[128,512]{1,0:T(8,128)(2,1)S(1)}, u32[]{:S(2)}, u32[]{:S(2)}) %collective-permute-start.5) | collective-permute-done | bytes 131104 | tf_op jit(solution)/shard_map/ppermute | solution.py:276
  37.6 0.7 constant_dynamic-update-slice_fusion.2
  38.4 1.8 collective-permute-start.9
  40.4 1.4 pad_dynamic-slice_fusion.2
  41.9 0.8 dynamic-slice_bitcast_fusion
  42.7 3.8 %shard_map.111 = (bf16[128,256]{1,0:T(8,128)(2,1)S(1)}, f32[2,128,1280]{2,1,0:T(8,128)}, bf16[128,384]{1,0:T(8,128)(2,1)S(1)}) custom-call(s32[1]{0:T(128)} %bitcast.core_ref, s32[128,1]{1,0:T(8,128)S(1)} %copy.13.qseg_ref, s32[1,1280]{1,0:T(1,128)S(1)} %broadcast_in_dim.37.kseg_ref, bf16[128,256]{1,0:T(8,128)(2,1)} %q_hbm.1, ...), custom_call_target="tpu_custom_call" | custom-call | tf_op jit(solution)/shard_map/pallas_call | solution.py:247
  47.2 1.1 broadcast_in_dim.38
  48.4 5.6 %all-to-all-start = ((bf16[16,128,256]{2,1,0:T(8,128)(2,1)}), bf16[16,128,256]{2,1,0:T(8,128)(2,1)S(1)}, u32[]{:S(2)}, u32[]{:S(2)}) async-start(bf16[16,128,256]{2,1,0:T(8,128)(2,1)} %broadcast_in_dim.38), calls=%async_computation | async-start | bytes 2097152 | tf_op jit(solution)/shard_map/all_to_all | solution.py:284
  54.1 3.2 %collective-permute-start.10 = (bf16[256,1024]{1,0:T(8,128)(2,1)}, bf16[256,1024]{1,0:T(8,128)(2,1)}, u32[]{:S(2)}, u32[]{:S(2)}) collective-permute-start(bf16[256,1024]{1,0:T(8,128)(2,1)} %collective-permute-done.9.refs_4_), channel_id=1, source_target_pairs={{0,224},{32,0},{64,32},{96,64},{128,96},{160,128},{192,160},{224,1... | collective-permute-start | bytes 1572872 | tf_op jit(solution)/shard_map/ppermute | solution.py:287
  57.3 8.4 %convolution_convert_fusion.teacher_hbm = bf16[2048,1024]{1,0:T(8,128)(2,1)} fusion(bf16[2048,1024]{1,0:T(8,128)(2,1)} %all-gather.3.cloned.1.call-done, bf16[1024,1024]{1,0:T(8,128)(2,1)S(1)} %copy-done), kind=kOutput, calls=%fused_computation | convolution fusion | flops 4297064448 | bytes 10485760 | tf_op jit(solution)/shard_map/dot_general | solution.py:24
  65.7 3.7 %collective-permute-done.10.refs_6_ = bf16[256,1024]{1,0:T(8,128)(2,1)} collective-permute-done((bf16[256,1024]{1,0:T(8,128)(2,1)}, bf16[256,1024]{1,0:T(8,128)(2,1)}, u32[]{:S(2)}, u32[]{:S(2)}) %collective-permute-start.10) | collective-permute-done | bytes 524320 | tf_op jit(solution)/shard_map/ppermute | solution.py:287
  69.4 3.4 %collective-permute-done.8.refs_5_ = bf16[256,1024]{1,0:T(8,128)(2,1)} collective-permute-done((bf16[256,1024]{1,0:T(8,128)(2,1)}, bf16[256,1024]{1,0:T(8,128)(2,1)}, u32[]{:S(2)}, u32[]{:S(2)}) %collective-permute-start.8) | collective-permute-done | bytes 524320 | tf_op jit(solution)/shard_map/ppermute | solution.py:287
  72.8 5.1 %shard_map.112 = (bf16[2048,768]{1,0:T(8,128)(2,1)}, bf16[256,256]{1,0:T(8,128)(2,1)S(1)}, bf16[256,256]{1,0:T(8,128)(2,1)S(1)}, bf16[256,256]{1,0:T(8,128)(2,1)...) custom-call(s32[1]{0:T(128)} %bitcast.3.z_ref, ...), custom_call_target="tpu_custom_call" | custom-call | tf_op jit(solution)/shard_map/pallas_call | solution.py:247
  78.6 0.7 copy-done.10
  79.2 0.7 copy-done.11
  79.9 0.7 copy-done.14
  81.5 3.2 %collective-permute-start.15 = (bf16[256,256]{1,0:T(8,128)(2,1)}, bf16[256,256]{1,0:T(8,128)(2,1)}, u32[]{:S(2)}, u32[]{:S(2)}) collective-permute-start(bf16[256,256]{1,0:T(8,128)(2,1)} %copy-done.14), channel_id=1, source_target_pairs={{0,224},{32,0},{64,32},{96,64},{128,96},{160,128},{192,160},{224,1... | collective-permute-start | bytes 393224 | tf_op jit(solution)/shard_map/ppermute | solution.py:287
  84.7 2.3 %broadcast_in_dim.41 = bf16[16,128,384]{2,1,0:T(8,128)(2,1)} broadcast(bf16[128,384]{1,0:T(8,128)(2,1)} %copy-done.13), dimensions={1,2} | broadcast | bytes 1671168 | tf_op jit(solution)/shard_map/broadcast_in_dim | solution.py:283
  87.0 5.5 %all-to-all-start.1 = ((bf16[16,128,384]{2,1,0:T(8,128)(2,1)}), bf16[16,128,384]{2,1,0:T(8,128)(2,1)}, u32[]{:S(2)}, u32[]{:S(2)}) async-start(bf16[16,128,384]{2,1,0:T(8,128)(2,1)} %broadcast_in_dim.41), calls=%async_computation.2 | async-start | bytes 3145728 | tf_op jit(solution)/shard_map/all_to_all | solution.py:284
  92.5 1.0 add_convert_fusion.5
  93.7 1.0 add_convert_fusion.2
  94.7 3.3 %collective-permute-start.16 = (bf16[256,256]{1,0:T(8,128)(2,1)S(1)}, bf16[256,256]{1,0:T(8,128)(2,1)S(1)}, u32[]{:S(2)}, u32[]{:S(2)}) collective-permute-start(bf16[256,256]{1,0:T(8,128)(2,1)S(1)} %add_convert_fusion.2), channel_id=1, source_target_pairs={{0,224},{32,0},{64,32},{96,64},{128,96},{160,128},{192,160},{224,1... | collective-permute-start | bytes 393224 | tf_op jit(solution)/shard_map/ppermute | solution.py:287
  98.0 5.8 %collective-permute-done.12 = bf16[256,256]{1,0:T(8,128)(2,1)S(1)} collective-permute-done((bf16[256,256]{1,0:T(8,128)(2,1)S(1)}, bf16[256,256]{1,0:T(8,128)(2,1)S(1)}, u32[]{:S(2)}, u32[]{:S(2)}) %collective-permute-start.12) | collective-permute-done | bytes 131104 | tf_op jit(solution)/shard_map/ppermute | solution.py:287
  104.3 3.8 %collective-permute-start.17 = (bf16[256,256]{1,0:T(8,128)(2,1)S(1)}, bf16[256,256]{1,0:T(8,128)(2,1)S(1)}, u32[]{:S(2)}, u32[]{:S(2)}) collective-permute-start(bf16[256,256]{1,0:T(8,128)(2,1)S(1)} %add_convert_fusion.1), channel_id=1, source_target_pairs={{0,224},{32,0},{64,32},{96,64},{128,96},{160,128},{192,160},{224,1... | collective-permute-start | bytes 393224 | tf_op jit(solution)/shard_map/ppermute | solution.py:287
  108.1 5.9 %collective-permute-done.13 = bf16[256,256]{1,0:T(8,128)(2,1)S(1)} collective-permute-done((bf16[256,256]{1,0:T(8,128)(2,1)S(1)}, bf16[256,256]{1,0:T(8,128)(2,1)S(1)}, u32[]{:S(2)}, u32[]{:S(2)}) %collective-permute-start.13) | collective-permute-done | bytes 131104 | tf_op jit(solution)/shard_map/ppermute | solution.py:287
  114.1 1.5 pad_dynamic-slice_fusion.1.attn_hbm
  115.6 1.0 slice.6
  116.6 1.0 slice.7
  117.6 6.4 %collective-permute-done.14 = bf16[256,256]{1,0:T(8,128)(2,1)S(1)} collective-permute-done((bf16[256,256]{1,0:T(8,128)(2,1)S(1)}, bf16[256,256]{1,0:T(8,128)(2,1)S(1)}, u32[]{:S(2)}, u32[]{:S(2)}) %collective-permute-start.14) | collective-permute-done | bytes 131104 | tf_op jit(solution)/shard_map/ppermute | solution.py:287
  124.0 0.9 collective-permute-start.18
  124.9 2.5 %pad_dynamic-slice_fusion.qx_hbm = bf16[1280,384]{1,0:T(8,128)(2,1)} fusion(s32[]{:T(128)S(6)} %select_n.10, bf16[2048,384]{1,0:T(8,128)(2,1)} %bitcast.5), kind=kLoop, calls=%fused_computation.1 | loop fusion | bytes 2555908 | tf_op jit(solution)/shard_map/dynamic_slice | solution.py:345
  127.4 3.2 %collective-permute-done.18.refs_1_ = bf16[256,256]{1,0:T(8,128)(2,1)S(1)} collective-permute-done((bf16[256,256]{1,0:T(8,128)(2,1)S(1)}, bf16[256,256]{1,0:T(8,128)(2,1)S(1)}, u32[]{:S(2)}, u32[]{:S(2)}) %collective-permute-start.18) | collective-permute-done | bytes 131104 | tf_op jit(solution)/shard_map/ppermute | solution.py:290
  130.6 2.9 %reduce-scatter.2.cloned.1.call-done.refs_2_ = bf16[256,768]{1,0:T(8,128)(2,1)} async-done(((bf16[2048,768]{1,0:T(8,128)(2,1)}), bf16[256,768]{1,0:T(8,128)(2,1)}) %reduce-scatter.2.cloned.1.call-update) | async-done | bytes 393232 | tf_op jit(solution)/shard_map/reduce_scatter | solution.py:364
  134.5 2.9 %collective-permute-start.21 = (bf16[128,1024]{1,0:T(8,128)(2,1)S(1)}, bf16[128,1024]{1,0:T(8,128)(2,1)S(1)}, u32[]{:S(2)}, u32[]{:S(2)}) collective-permute-start(bf16[128,1024]{1,0:T(8,128)(2,1)S(1)} %slice.7), channel_id=1, source_target_pairs={{0,224},{32,0},{64,32},{96,64},{128,96},{160,128},{192,160},{224,1... | collective-permute-start | bytes 786440 | tf_op jit(solution)/shard_map/ppermute | solution.py:287
  137.4 5.2 %collective-permute-done.20.refs_7_ = bf16[128,1024]{1,0:T(8,128)(2,1)S(1)} collective-permute-done((bf16[128,1024]{1,0:T(8,128)(2,1)S(1)}, bf16[128,1024]{1,0:T(8,128)(2,1)S(1)}, u32[]{:S(2)}, u32[]{:S(2)}) %collective-permute-start.20) | collective-permute-done | bytes 262176 | tf_op jit(solution)/shard_map/ppermute | solution.py:287
  142.6 3.1 %collective-permute-done.19.refs_3_ = bf16[256,768]{1,0:T(8,128)(2,1)S(1)} collective-permute-done((bf16[256,768]{1,0:T(8,128)(2,1)}, bf16[256,768]{1,0:T(8,128)(2,1)S(1)}, u32[]{:S(2)}, u32[]{:S(2)}) %collective-permute-start.19) | collective-permute-done | bytes 393248 | tf_op jit(solution)/shard_map/ppermute | solution.py:290
  145.7 2.4 %shard_map.113.dpred_hbm = bf16[256,1024]{1,0:T(8,128)(2,1)} custom-call(bf16[256,256]{1,0:T(8,128)(2,1)S(1)} %add_convert_fusion.refs_0_, bf16[256,256]{1,0:T(8,128)(2,1)S(1)} %collective-permute-done.18.refs_1_, bf16[256,768]{1,0:T(8,128)(2,1)} %reduce-scatter.2.cloned.1.call-done.refs_2_, bf16[256,768]{1,0:T(8,128)(2,1)S(1)} %collective-permute-done.19.refs_3_), custom_call_target="tpu_custom_call" | custom-call | tf_op jit(solution)/shard_map/pallas_call | solution.py:247
  148.1 3.8 %shard_map.115 = bf16[8,256,256]{2,1,0:T(8,128)(2,1)S(1)} custom-call(s32[1]{0:T(128)} %bitcast.3.z_ref, bf16[256,1024]{1,0:T(8,128)(2,1)} %shard_map.113.dpred_hbm, bf16[256,1024]{1,0:T(8,128)(2,1)} %refs_0_.1, bf16[256,1024]{1,0:T(8,128)(2,1)} %collective-permute-done.refs_1_, bf16[256,1024]{1,0:T(8,128)(2,1)} %collective-permute-done.1.refs_2_, ...), custom_call_target="tpu_custom_call" | custom-call | tf_op jit(solution)/shard_map/pallas_call | solution.py:247
  152.0 21.2 %all_to_all.15 = bf16[16,128,256]{2,1,0:T(8,128)(2,1)S(1)} all-to-all(bf16[16,128,256]{2,1,0:T(8,128)(2,1)S(1)} %bitcast.15), channel_id=1, replica_groups=mesh['z'=8,'xh'=2,'y'=4,'xl'=2,'core'=2] {'y','xl','core'}, dimensions={0} | all-to-all | bytes 2097152 | tf_op jit(solution)/shard_map/all_to_all | solution.py:403
  173.3 0.7 collective-permute-start.22
  174.0 1.3 collective-permute-start.23
  175.3 1.3 collective-permute-start.24
  176.6 1.3 collective-permute-start.25
  177.9 1.3 collective-permute-start.26
  179.2 10.3 %collective-permute-done.23.refs_1_ = bf16[128,256]{1,0:T(8,128)(2,1)S(1)} collective-permute-done((bf16[128,256]{1,0:T(8,128)(2,1)S(1)}, bf16[128,256]{1,0:T(8,128)(2,1)S(1)}, u32[]{:S(2)}, u32[]{:S(2)}) %collective-permute-start.23) | collective-permute-done | bytes 65568 | tf_op jit(solution)/shard_map/ppermute | solution.py:276
  189.4 3.4 %collective-permute-done.24.refs_2_ = bf16[128,256]{1,0:T(8,128)(2,1)S(1)} collective-permute-done((bf16[128,256]{1,0:T(8,128)(2,1)S(1)}, bf16[128,256]{1,0:T(8,128)(2,1)S(1)}, u32[]{:S(2)}, u32[]{:S(2)}) %collective-permute-start.24) | collective-permute-done | bytes 65568 | tf_op jit(solution)/shard_map/ppermute | solution.py:276
  192.8 1.9 collective-permute-done.25.refs_3_
  194.7 3.4 %collective-permute-done.26.refs_4_ = bf16[128,256]{1,0:T(8,128)(2,1)S(1)} collective-permute-done((bf16[128,256]{1,0:T(8,128)(2,1)S(1)}, bf16[128,256]{1,0:T(8,128)(2,1)S(1)}, u32[]{:S(2)}, u32[]{:S(2)}) %collective-permute-start.26) | collective-permute-done | bytes 65568 | tf_op jit(solution)/shard_map/ppermute | solution.py:276
  198.4 3.2 %shard_map.116 = bf16[128,256]{1,0:T(8,128)(2,1)} custom-call(s32[1]{0:T(128)} %bitcast.core_ref, bf16[128,256]{1,0:T(8,128)(2,1)S(1)} %collective-permute-done.22.dattn_hbm.refs_0_, bf16[128,256]{1,0:T(8,128)(2,1)} %copy-done.8, f32[2,128,1280]{2,1,0:T(8,128)} %get-tuple-element.61.probs_hbm, bf16[128,512]{1,0:T(8,128)(2,1)} %copy-done.2, ...), custom_call_target="tpu_custom_call" | custom-call | tf_op jit(solution)/shard_map/pallas_call | solution.py:247
  201.6 4.3 %shard_map.117 = (bf16[128,256]{1,0:T(8,128)(2,1)}, bf16[128,256]{1,0:T(8,128)(2,1)}) custom-call(s32[1]{0:T(128)} %bitcast.core_ref, s32[1280,1]{1,0:T(8,128)S(1)} %broadcast_in_dim.44.qseg_ref, s32[1,128]{1,0:T(1,128)S(1)} %get-tuple-element.68.kseg_ref, bf16[128,512]{1,0:T(8,128)(2,1)} %copy-done.2, bf16[1280,384]{1,0:T(8,128)(2,1)} %pad_dynamic-slice_fusion.qx_hbm, ...), custom_call_target="tpu_custom_call" | custom-call | tf_op jit(solution)/shard_map/pallas_call | solution.py:247
  205.9 1.7 all-gather.5.cloned.1.call-done.dpred_hbm
  207.6 4.3 %shard_map.114 = bf16[256,1024]{1,0:T(8,128)(2,1)} custom-call(bf16[2048,256]{1,0:T(8,128)(2,1)} %bitcast.14, bf16[2048,1024]{1,0:T(8,128)(2,1)} %all-gather.5.cloned.1.call-done.dpred_hbm), custom_call_target="tpu_custom_call" | custom-call | tf_op jit(solution)/shard_map/pallas_call | solution.py:247
  (78 shorter events, 5.6 us)
Async XLA Ops:
  7.2 50.1 %copy-start = (bf16[1024,1024]{1,0:T(8,128)(2,1)S(1)}, bf16[1024,1024]{1,0:T(8,128)(2,1)}, u32[]{:S(2)}) copy-start(bf16[1024,1024]{1,0:T(8,128)(2,1)} %param.9) | copy-start | bytes 6291460
  7.2 50.1 %all-gather.3.cloned.1.call-start = ((), (), s32[]{:S(2)}) async-start(), calls=%async_computation.4 | async-start | bytes 4456448 | tf_op jit(solution)/shard_map/all_gather | solution.py:292
  7.9 18.8 %collective-permute-start = (bf16[256,1024]{1,0:T(8,128)(2,1)}, bf16[256,1024]{1,0:T(8,128)(2,1)}, u32[]{:S(2)}, u32[]{:S(2)}) collective-permute-start(bf16[256,1024]{1,0:T(8,128)(2,1)} %refs_0_.1), channel_id=1, source_target_pairs={{0,32},{32,64},{64,96},{96,128},{128,160},{160,192},{192,224},{224... | collective-permute-start | bytes 1572872 | tf_op jit(solution)/shard_map/ppermute | solution.py:287
  9.9 21.3 %collective-permute-start.1 = (bf16[256,1024]{1,0:T(8,128)(2,1)}, bf16[256,1024]{1,0:T(8,128)(2,1)}, u32[]{:S(2)}, u32[]{:S(2)}) collective-permute-start(bf16[256,1024]{1,0:T(8,128)(2,1)} %refs_0_.1), channel_id=1, source_target_pairs={{0,224},{32,0},{64,32},{96,64},{128,96},{160,128},{192,160},{224,1... | collective-permute-start | bytes 1572872 | tf_op jit(solution)/shard_map/ppermute | solution.py:287
  15.6 32.7 %copy-start.2 = (bf16[128,512]{1,0:T(8,128)(2,1)}, bf16[128,512]{1,0:T(8,128)(2,1)S(1)}, u32[]{:S(2)}) copy-start(bf16[128,512]{1,0:T(8,128)(2,1)S(1)} %constant_dynamic-update-slice_fusion.refs_0_.kv_hbm) | copy-start | bytes 393220
  15.6 16.2 %collective-permute-start.2 = (bf16[128,512]{1,0:T(8,128)(2,1)S(1)}, bf16[128,512]{1,0:T(8,128)(2,1)S(1)}, u32[]{:S(2)}, u32[]{:S(2)}) collective-permute-start(bf16[128,512]{1,0:T(8,128)(2,1)S(1)} %constant_dynamic-update-slice_fusion.refs_0_.kv_hbm), channel_id=1, source_target_pairs={{0,2},{1,3},{2,4},{3,5},{4,6},{5,7},{6,8},{7,9},{8,10},{9,11},{10,... | collective-permute-start | bytes 393224 | tf_op jit(solution)/shard_map/ppermute | solution.py:276
  18.7 13.8 %collective-permute-start.3 = (bf16[128,512]{1,0:T(8,128)(2,1)S(1)}, bf16[128,512]{1,0:T(8,128)(2,1)S(1)}, u32[]{:S(2)}, u32[]{:S(2)}) collective-permute-start(bf16[128,512]{1,0:T(8,128)(2,1)S(1)} %constant_dynamic-update-slice_fusion.refs_0_.kv_hbm), channel_id=1, source_target_pairs={{0,4},{1,5},{2,6},{3,7},{4,8},{5,9},{6,10},{7,11},{8,12},{9,13},{1... | collective-permute-start | bytes 393224 | tf_op jit(solution)/shard_map/ppermute | solution.py:276
  22.2 11.1 %collective-permute-start.4 = (bf16[128,512]{1,0:T(8,128)(2,1)S(1)}, bf16[128,512]{1,0:T(8,128)(2,1)S(1)}, u32[]{:S(2)}, u32[]{:S(2)}) collective-permute-start(bf16[128,512]{1,0:T(8,128)(2,1)S(1)} %constant_dynamic-update-slice_fusion.refs_0_.kv_hbm), channel_id=1, source_target_pairs={{0,6},{1,7},{2,8},{3,9},{4,10},{5,11},{6,12},{7,13},{8,14},{9,15},... | collective-permute-start | bytes 393224 | tf_op jit(solution)/shard_map/ppermute | solution.py:276
  26.7 10.9 %collective-permute-start.5 = (bf16[128,512]{1,0:T(8,128)(2,1)S(1)}, bf16[128,512]{1,0:T(8,128)(2,1)S(1)}, u32[]{:S(2)}, u32[]{:S(2)}) collective-permute-start(bf16[128,512]{1,0:T(8,128)(2,1)S(1)} %constant_dynamic-update-slice_fusion.refs_0_.kv_hbm), channel_id=1, source_target_pairs={{0,8},{1,9},{2,10},{3,11},{4,12},{5,13},{6,14},{7,15},{16,24},{17,... | collective-permute-start | bytes 393224 | tf_op jit(solution)/shard_map/ppermute | solution.py:276
  31.9 16.5 %copy-start.4 = (bf16[128,512]{1,0:T(8,128)(2,1)}, bf16[128,512]{1,0:T(8,128)(2,1)S(1)}, u32[]{:S(2)}) copy-start(bf16[128,512]{1,0:T(8,128)(2,1)S(1)} %collective-permute-done.2.refs_1_) | copy-start | bytes 393220
  32.6 15.8 %copy-start.5 = (bf16[128,512]{1,0:T(8,128)(2,1)}, bf16[128,512]{1,0:T(8,128)(2,1)S(1)}, u32[]{:S(2)}) copy-start(bf16[128,512]{1,0:T(8,128)(2,1)S(1)} %collective-permute-done.3.refs_2_) | copy-start | bytes 393220
  33.3 15.0 %copy-start.6 = (bf16[128,512]{1,0:T(8,128)(2,1)}, bf16[128,512]{1,0:T(8,128)(2,1)S(1)}, u32[]{:S(2)}) copy-start(bf16[128,512]{1,0:T(8,128)(2,1)S(1)} %collective-permute-done.4.refs_3_) | copy-start | bytes 393220
  37.6 10.7 %copy-start.7 = (bf16[128,512]{1,0:T(8,128)(2,1)}, bf16[128,512]{1,0:T(8,128)(2,1)S(1)}, u32[]{:S(2)}) copy-start(bf16[128,512]{1,0:T(8,128)(2,1)S(1)} %collective-permute-done.5.refs_4_) | copy-start | bytes 393220
  38.4 4.4 %collective-permute-start.6 = (bf16[640,512]{1,0:T(8,128)(2,1)}, bf16[640,512]{1,0:T(8,128)(2,1)S(1)}, u32[]{:S(2)}, u32[]{:S(2)}) collective-permute-start(bf16[640,512]{1,0:T(8,128)(2,1)} %constant_dynamic-update-slice_fusion.2), channel_id=1, source_target_pairs={{0,1},{1,0},{2,3},{3,2},{4,5},{5,4},{6,7},{7,6},{8,9},{9,8},{10,11... | collective-permute-start | bytes 1966088 | tf_op jit(solution)/shard_map/ppermute | solution.py:280
  38.4 15.7 %collective-permute-start.9 = (bf16[256,1024]{1,0:T(8,128)(2,1)}, bf16[256,1024]{1,0:T(8,128)(2,1)}, u32[]{:S(2)}, u32[]{:S(2)}) collective-permute-start(bf16[256,1024]{1,0:T(8,128)(2,1)} %collective-permute-done.1.refs_2_), channel_id=1, source_target_pairs={{0,224},{32,0},{64,32},{96,64},{128,96},{160,128},{192,160},{224,1... | collective-permute-start | bytes 1572872 | tf_op jit(solution)/shard_map/ppermute | solution.py:287
  40.1 17.1 %collective-permute-start.7 = (bf16[256,1024]{1,0:T(8,128)(2,1)}, bf16[256,1024]{1,0:T(8,128)(2,1)}, u32[]{:S(2)}, u32[]{:S(2)}) collective-permute-start(bf16[256,1024]{1,0:T(8,128)(2,1)} %collective-permute-done.refs_1_), channel_id=1, source_target_pairs={{0,32},{32,64},{64,96},{96,128},{128,160},{160,192},{192,224},{224... | collective-permute-start | bytes 1572872 | tf_op jit(solution)/shard_map/ppermute | solution.py:287
  42.7 5.6 %copy-start.3 = (bf16[640,512]{1,0:T(8,128)(2,1)}, bf16[640,512]{1,0:T(8,128)(2,1)S(1)}, u32[]{:S(2)}) copy-start(bf16[640,512]{1,0:T(8,128)(2,1)S(1)} %collective-permute-done.6.refs_5_) | copy-start | bytes 1966084
  46.6 0.6 copy-start.13
  47.2 1.1 copy-start.8
  48.4 24.4 %all-to-all-start = ((bf16[16,128,256]{2,1,0:T(8,128)(2,1)}), bf16[16,128,256]{2,1,0:T(8,128)(2,1)S(1)}, u32[]{:S(2)}, u32[]{:S(2)}) async-start(bf16[16,128,256]{2,1,0:T(8,128)(2,1)} %broadcast_in_dim.38), calls=%async_computation | async-start | bytes 2097152 | tf_op jit(solution)/shard_map/all_to_all | solution.py:284
  54.0 79.5 %reduce-scatter.2.cloned.1.call-start = ((), (), s32[]{:S(2)}) async-start(), calls=%async_computation.5 | async-start | bytes 3538944 | tf_op jit(solution)/shard_map/reduce_scatter | solution.py:364
  54.1 15.3 %collective-permute-start.10 = (bf16[256,1024]{1,0:T(8,128)(2,1)}, bf16[256,1024]{1,0:T(8,128)(2,1)}, u32[]{:S(2)}, u32[]{:S(2)}) collective-permute-start(bf16[256,1024]{1,0:T(8,128)(2,1)} %collective-permute-done.9.refs_4_), channel_id=1, source_target_pairs={{0,224},{32,0},{64,32},{96,64},{128,96},{160,128},{192,160},{224,1... | collective-permute-start | bytes 1572872 | tf_op jit(solution)/shard_map/ppermute | solution.py:287
  57.3 15.5 %collective-permute-start.8 = (bf16[256,1024]{1,0:T(8,128)(2,1)}, bf16[256,1024]{1,0:T(8,128)(2,1)}, u32[]{:S(2)}, u32[]{:S(2)}) collective-permute-start(bf16[256,1024]{1,0:T(8,128)(2,1)} %collective-permute-done.7.refs_3_), channel_id=1, source_target_pairs={{0,32},{32,64},{64,96},{96,128},{128,160},{160,192},{192,224},{224... | collective-permute-start | bytes 1572872 | tf_op jit(solution)/shard_map/ppermute | solution.py:287
  72.8 41.3 %copy-start.1 = (bf16[16,128,256]{2,1,0:T(8,128)(2,1)}, bf16[16,128,256]{2,1,0:T(8,128)(2,1)S(1)}, u32[]{:S(2)}) copy-start(bf16[16,128,256]{2,1,0:T(8,128)(2,1)S(1)} %all-to-all-done) | copy-start | bytes 3145732
  77.9 0.7 copy-start.9
  78.6 0.7 copy-start.10
  79.2 0.7 copy-start.11
  79.9 0.7 copy-start.14
  80.5 0.7 copy-start.15
  81.2 11.3 %collective-permute-start.11 = (bf16[256,256]{1,0:T(8,128)(2,1)}, bf16[256,256]{1,0:T(8,128)(2,1)}, u32[]{:S(2)}, u32[]{:S(2)}) collective-permute-start(bf16[256,256]{1,0:T(8,128)(2,1)} %copy-done.15), channel_id=1, source_target_pairs={{0,32},{32,64},{64,96},{96,128},{128,160},{160,192},{192,224},{224... | collective-permute-start | bytes 393224 | tf_op jit(solution)/shard_map/ppermute | solution.py:287
  81.5 12.2 %collective-permute-start.15 = (bf16[256,256]{1,0:T(8,128)(2,1)}, bf16[256,256]{1,0:T(8,128)(2,1)}, u32[]{:S(2)}, u32[]{:S(2)}) collective-permute-start(bf16[256,256]{1,0:T(8,128)(2,1)} %copy-done.14), channel_id=1, source_target_pairs={{0,224},{32,0},{64,32},{96,64},{128,96},{160,128},{192,160},{224,1... | collective-permute-start | bytes 393224 | tf_op jit(solution)/shard_map/ppermute | solution.py:287
  87.0 37.9 %all-to-all-start.1 = ((bf16[16,128,384]{2,1,0:T(8,128)(2,1)}), bf16[16,128,384]{2,1,0:T(8,128)(2,1)}, u32[]{:S(2)}, u32[]{:S(2)}) async-start(bf16[16,128,384]{2,1,0:T(8,128)(2,1)} %broadcast_in_dim.41), calls=%async_computation.2 | async-start | bytes 3145728 | tf_op jit(solution)/shard_map/all_to_all | solution.py:284
  92.5 115.2 %all-gather.5.cloned.1.call-start = ((), (), s32[]{:S(2)}) async-start(), calls=%async_computation.6 | async-start | bytes 4718592 | tf_op jit(solution)/shard_map/all_gather | solution.py:418
  92.5 31.5 %copy-start.12 = (bf16[256,256]{1,0:T(8,128)(2,1)S(1)}, bf16[256,256]{1,0:T(8,128)(2,1)}, u32[]{:S(2)}) copy-start(bf16[256,256]{1,0:T(8,128)(2,1)} %copy-done.11) | copy-start | bytes 393220
  93.6 10.2 %collective-permute-start.12 = (bf16[256,256]{1,0:T(8,128)(2,1)S(1)}, bf16[256,256]{1,0:T(8,128)(2,1)S(1)}, u32[]{:S(2)}, u32[]{:S(2)}) collective-permute-start(bf16[256,256]{1,0:T(8,128)(2,1)S(1)} %add_convert_fusion.5), channel_id=1, source_target_pairs={{0,32},{32,64},{64,96},{96,128},{128,160},{160,192},{192,224},{224... | collective-permute-start | bytes 393224 | tf_op jit(solution)/shard_map/ppermute | solution.py:287
  94.7 9.6 %collective-permute-start.16 = (bf16[256,256]{1,0:T(8,128)(2,1)S(1)}, bf16[256,256]{1,0:T(8,128)(2,1)S(1)}, u32[]{:S(2)}, u32[]{:S(2)}) collective-permute-start(bf16[256,256]{1,0:T(8,128)(2,1)S(1)} %add_convert_fusion.2), channel_id=1, source_target_pairs={{0,224},{32,0},{64,32},{96,64},{128,96},{160,128},{192,160},{224,1... | collective-permute-start | bytes 393224 | tf_op jit(solution)/shard_map/ppermute | solution.py:287
  103.8 10.2 %collective-permute-start.13 = (bf16[256,256]{1,0:T(8,128)(2,1)S(1)}, bf16[256,256]{1,0:T(8,128)(2,1)S(1)}, u32[]{:S(2)}, u32[]{:S(2)}) collective-permute-start(bf16[256,256]{1,0:T(8,128)(2,1)S(1)} %add_convert_fusion.4), channel_id=1, source_target_pairs={{0,32},{32,64},{64,96},{96,128},{128,160},{160,192},{192,224},{224... | collective-permute-start | bytes 393224 | tf_op jit(solution)/shard_map/ppermute | solution.py:287
  104.3 13.3 %collective-permute-start.17 = (bf16[256,256]{1,0:T(8,128)(2,1)S(1)}, bf16[256,256]{1,0:T(8,128)(2,1)S(1)}, u32[]{:S(2)}, u32[]{:S(2)}) collective-permute-start(bf16[256,256]{1,0:T(8,128)(2,1)S(1)} %add_convert_fusion.1), channel_id=1, source_target_pairs={{0,224},{32,0},{64,32},{96,64},{128,96},{160,128},{192,160},{224,1... | collective-permute-start | bytes 393224 | tf_op jit(solution)/shard_map/ppermute | solution.py:287
  114.0 9.9 %collective-permute-start.14 = (bf16[256,256]{1,0:T(8,128)(2,1)S(1)}, bf16[256,256]{1,0:T(8,128)(2,1)S(1)}, u32[]{:S(2)}, u32[]{:S(2)}) collective-permute-start(bf16[256,256]{1,0:T(8,128)(2,1)S(1)} %add_convert_fusion.3), channel_id=1, source_target_pairs={{0,32},{32,64},{64,96},{96,128},{128,160},{160,192},{192,224},{224... | collective-permute-start | bytes 393224 | tf_op jit(solution)/shard_map/ppermute | solution.py:287
  124.0 6.6 %collective-permute-start.18 = (bf16[256,256]{1,0:T(8,128)(2,1)S(1)}, bf16[256,256]{1,0:T(8,128)(2,1)S(1)}, u32[]{:S(2)}, u32[]{:S(2)}) collective-permute-start(bf16[256,256]{1,0:T(8,128)(2,1)S(1)} %add_convert_fusion.refs_0_), channel_id=1, source_target_pairs={{0,16},{16,0},{1,17},{17,1},{2,18},{18,2},{3,19},{19,3},{4,20},{20... | collective-permute-start | bytes 393224 | tf_op jit(solution)/shard_map/ppermute | solution.py:290
  133.5 12.2 %collective-permute-start.19 = (bf16[256,768]{1,0:T(8,128)(2,1)}, bf16[256,768]{1,0:T(8,128)(2,1)S(1)}, u32[]{:S(2)}, u32[]{:S(2)}) collective-permute-start(bf16[256,768]{1,0:T(8,128)(2,1)} %reduce-scatter.2.cloned.1.call-done.refs_2_), channel_id=1, source_target_pairs={{0,16},{16,0},{1,17},{17,1},{2,18},{18,2},{3,19},{19,3},{4,20},{20... | collective-permute-start | bytes 1179656 | tf_op jit(solution)/shard_map/ppermute | solution.py:290
  134.2 8.5 %collective-permute-start.20 = (bf16[128,1024]{1,0:T(8,128)(2,1)S(1)}, bf16[128,1024]{1,0:T(8,128)(2,1)S(1)}, u32[]{:S(2)}, u32[]{:S(2)}) collective-permute-start(bf16[128,1024]{1,0:T(8,128)(2,1)S(1)} %slice.6), channel_id=1, source_target_pairs={{0,32},{32,64},{64,96},{96,128},{128,160},{160,192},{192,224},{224... | collective-permute-start | bytes 786440 | tf_op jit(solution)/shard_map/ppermute | solution.py:287
  134.5 8.1 %collective-permute-start.21 = (bf16[128,1024]{1,0:T(8,128)(2,1)S(1)}, bf16[128,1024]{1,0:T(8,128)(2,1)S(1)}, u32[]{:S(2)}, u32[]{:S(2)}) collective-permute-start(bf16[128,1024]{1,0:T(8,128)(2,1)S(1)} %slice.7), channel_id=1, source_target_pairs={{0,224},{32,0},{64,32},{96,64},{128,96},{160,128},{192,160},{224,1... | collective-permute-start | bytes 786440 | tf_op jit(solution)/shard_map/ppermute | solution.py:287
  151.9 46.2 %copy-start.16 = (s32[1280]{0:T(1024)S(1)}, s32[1280]{0:T(1024)}, u32[]{:S(2)}) copy-start(s32[1280]{0:T(1024)} %get-tuple-element.70) | copy-start | bytes 15364
  173.3 0.7 collective-permute-start.22
  174.0 15.5 %collective-permute-start.23 = (bf16[128,256]{1,0:T(8,128)(2,1)S(1)}, bf16[128,256]{1,0:T(8,128)(2,1)S(1)}, u32[]{:S(2)}, u32[]{:S(2)}) collective-permute-start(bf16[128,256]{1,0:T(8,128)(2,1)S(1)} %collective-permute-done.22.dattn_hbm.refs_0_), channel_id=1, source_target_pairs={{2,0},{3,1},{4,2},{5,3},{6,4},{7,5},{8,6},{9,7},{10,8},{11,9},{12,... | collective-permute-start | bytes 196616 | tf_op jit(solution)/shard_map/ppermute | solution.py:276
  175.3 17.6 %collective-permute-start.24 = (bf16[128,256]{1,0:T(8,128)(2,1)S(1)}, bf16[128,256]{1,0:T(8,128)(2,1)S(1)}, u32[]{:S(2)}, u32[]{:S(2)}) collective-permute-start(bf16[128,256]{1,0:T(8,128)(2,1)S(1)} %collective-permute-done.22.dattn_hbm.refs_0_), channel_id=1, source_target_pairs={{4,0},{5,1},{6,2},{7,3},{8,4},{9,5},{10,6},{11,7},{12,8},{13,9},{1... | collective-permute-start | bytes 196616 | tf_op jit(solution)/shard_map/ppermute | solution.py:276
  176.6 18.2 %collective-permute-start.25 = (bf16[128,256]{1,0:T(8,128)(2,1)S(1)}, bf16[128,256]{1,0:T(8,128)(2,1)S(1)}, u32[]{:S(2)}, u32[]{:S(2)}) collective-permute-start(bf16[128,256]{1,0:T(8,128)(2,1)S(1)} %collective-permute-done.22.dattn_hbm.refs_0_), channel_id=1, source_target_pairs={{6,0},{7,1},{8,2},{9,3},{10,4},{11,5},{12,6},{13,7},{14,8},{15,9},... | collective-permute-start | bytes 196616 | tf_op jit(solution)/shard_map/ppermute | solution.py:276
  177.9 20.2 %collective-permute-start.26 = (bf16[128,256]{1,0:T(8,128)(2,1)S(1)}, bf16[128,256]{1,0:T(8,128)(2,1)S(1)}, u32[]{:S(2)}, u32[]{:S(2)}) collective-permute-start(bf16[128,256]{1,0:T(8,128)(2,1)S(1)} %collective-permute-done.22.dattn_hbm.refs_0_), channel_id=1, source_target_pairs={{8,0},{9,1},{10,2},{11,3},{12,4},{13,5},{14,6},{15,7},{24,16},{25,... | collective-permute-start | bytes 196616 | tf_op jit(solution)/shard_map/ppermute | solution.py:276
  198.1 3.5 %collective-permute-start.27 = (bf16[640,256]{1,0:T(8,128)(2,1)S(1)}, bf16[640,256]{1,0:T(8,128)(2,1)S(1)}, u32[]{:S(2)}, u32[]{:S(2)}) collective-permute-start(bf16[640,256]{1,0:T(8,128)(2,1)S(1)} %constant_dynamic-update-slice_fusion.7), channel_id=1, source_target_pairs={{0,1},{1,0},{2,3},{3,2},{4,5},{5,4},{6,7},{7,6},{8,9},{9,8},{10,11... | collective-permute-start | bytes 983048 | tf_op jit(solution)/shard_map/ppermute | solution.py:280
Sparse Core Ops, SparseCore 0:
  9.9 47.0 all-gather.2
  81.3 52.1 reduce-scatter.1
  148.3 59.3 all-gather.4
